TPU v7x, 32 devices: a whole 2x2x4 slice. The times are simulated.
32 devices in a mesh: dp: 8 (over y, x, core), tensor: 4 (over z).
Axes of the slice: x: 2, y: 2, z: 4, core: 2. Of those that a mesh axis runs over, the one named last changes fastest.
Arguments:
- tokens: bfloat16 [8192, 2048], P(('dp', 'tensor')), may hold values from -6 to 6
- lengths: int32 [8], P('dp'), may hold values from 256 to 1024, as said below
- cotangent: bfloat16 [8192, 2048], P(('dp', 'tensor')), may hold values from -6 to 6
- gain_one: float32 [2048], replicated, may hold values from 0.5 to 1.5
- gain_two: float32 [2048], replicated, may hold values from 0.5 to 1.5
- w_query: float32 [2048, 2048], P('dp', 'tensor'), may hold values from -0.125 to 0.125
- w_key: float32 [2048, 2048], P('dp', 'tensor'), may hold values from -0.125 to 0.125
- w_value: float32 [2048, 3456], P('dp', 'tensor'), may hold values from -0.125 to 0.125
- w_gate: float32 [2048, 3456], P('dp', 'tensor'), may hold values from -0.125 to 0.125
- w_out: float32 [2048, 3456], P('dp', 'tensor'), may hold values from -0.109375 to 0.109375
- w_mgate: float32 [2048, 3456], P('dp', 'tensor'), may hold values from -0.125 to 0.125
- w_mup: float32 [2048, 3456], P('dp', 'tensor'), may hold values from -0.125 to 0.125
- w_down: float32 [2048, 3456], P('dp', 'tensor'), may hold values from -0.109375 to 0.109375
Outputs:
- output: bfloat16 [8192, 2048], P(('dp', 'tensor'))
- grad_tokens: bfloat16 [8192, 2048], P(('dp', 'tensor'))
- grad_gain_one: float32 [2048], replicated
- grad_gain_two: float32 [2048], replicated
- grad_w_query: float32 [2048, 2048], P('dp', 'tensor')
- grad_w_key: float32 [2048, 2048], P('dp', 'tensor')
- grad_w_value: float32 [2048, 3456], P('dp', 'tensor')
- grad_w_gate: float32 [2048, 3456], P('dp', 'tensor')
- grad_w_out: float32 [2048, 3456], P('dp', 'tensor')
- grad_w_mgate: float32 [2048, 3456], P('dp', 'tensor')
- grad_w_mup: float32 [2048, 3456], P('dp', 'tensor')
- grad_w_down: float32 [2048, 3456], P('dp', 'tensor')
Inputs may be any that keep to these rules, and one draw needn't show every extreme that they name: Valid slots of sequence s are 0 to lengths[s] - 1; some sequence has all 1024 slots valid and some other has 256.
All inputs are finite; a program needn't handle non-finite values.
Results may differ from a plain program's by a relative error of at most 0.019.
Values may be sent and summed in bfloat16 or wider, within the bound.
No kernel may reach another device: no remote copies, remote signals or barrier semaphores. Data moves between devices by JAX's collectives and lax.ppermute only.
A program may use at most 256 MiB of HBM per device.

v0:
```python
from functools import partial

import jax
import jax.numpy as jnp
from jax import lax
from jax.sharding import PartitionSpec as P

KEY = 256
VAL = 432


EPS = 1e-05
HEAD_EPS = 1.0


def times_plain(left, right):
    return jnp.dot(left, right, preferred_element_type=jnp.float32)


def times_left(left, right):
    return lax.dot_general(
        left, right, (((0,), (0,)), ((), ())), preferred_element_type=jnp.float32
    )


def times_right(left, right):
    return lax.dot_general(
        left, right, (((1,), (1,)), ((), ())), preferred_element_type=jnp.float32
    )


def layer_norm(features, gain_vec):
    centred = features - jnp.mean(features, -1, keepdims=True)
    variance = jnp.mean(centred * centred, -1, keepdims=True)
    return centred * lax.rsqrt(variance + EPS) * gain_vec


def rotation_tables(seq_slots, width):
    half_width = width // 2
    freqs = 10000.0 ** (-jnp.arange(half_width, dtype=jnp.float32) / half_width)
    angles = jnp.arange(seq_slots, dtype=jnp.float32)[:, None] * freqs[None, :]
    angles = jnp.concatenate([angles, angles], -1)[:, None, :]
    return (jnp.cos(angles), jnp.sin(angles))


def rotate(features, cosines, sines):
    half_width = features.shape[-1] // 2
    turned = jnp.concatenate([-features[..., half_width:], features[..., :half_width]], -1)
    return features * cosines + turned * sines


def rotate_scaled(features, cosines, sines):
    return rotate(features, cosines, sines) * KEY ** (-0.5)


def decay_block(offset, block_rows, seq_slots, log_decay):
    query_pos = jnp.arange(block_rows, dtype=jnp.int32) + offset
    key_pos = jnp.arange(seq_slots, dtype=jnp.int32)
    spacing = query_pos[:, None] - key_pos[None, :]
    behind = spacing >= 0
    factor = jnp.exp(
        log_decay[:, None, None] * jnp.where(behind, spacing, 0).astype(jnp.float32)[None]
    )
    return jnp.where(behind[None], factor, 0.0)


def head_norm(retained):
    centred = retained - jnp.mean(retained, -1, keepdims=True)
    variance = jnp.mean(centred * centred, -1, keepdims=True)
    return centred * lax.rsqrt(variance + HEAD_EPS)


def gated_heads(gate_pre, retained):
    return jax.nn.silu(gate_pre) * head_norm(retained)


def gelu_gated(mgate_pre, mup_pre):
    return jax.nn.gelu(mgate_pre, approximate=False) * mup_pre


def per_device(
    tokens,
    lengths,
    cotangent,
    gain_one,
    gain_two,
    w_query,
    w_key,
    w_value,
    w_gate,
    w_out,
    w_mgate,
    w_mup,
    w_down,
):
    local_rows = tokens.shape[0]
    seq_slots = local_rows * lax.axis_size("tensor")
    heads_here = w_query.shape[1] // KEY
    block_rows = min(512, seq_slots)
    block_count = seq_slots // block_rows
    first_row = lax.axis_index("tensor") * local_rows
    valid = (first_row + jnp.arange(local_rows, dtype=jnp.int32) < lengths[0])[:, None]
    head_ids = (
        lax.axis_index("tensor") * heads_here + jnp.arange(heads_here, dtype=jnp.int32)
    ).astype(jnp.float32)
    log_decay = jnp.log(1.0 - jnp.exp2(-5.0 - head_ids))
    cosines, sines = rotation_tables(seq_slots, KEY)
    offsets = jnp.arange(block_count, dtype=jnp.int32) * block_rows
    features = tokens.astype(jnp.float32)
    first_norm = layer_norm(features, gain_one).astype(jnp.bfloat16)
    rows_one = lax.all_gather(first_norm, "tensor", axis=0, tiled=True)
    query_low, key_low, value_low, gate_low, out_low = (
        lax.all_gather(w_query.astype(jnp.bfloat16), "dp", axis=0, tiled=True),
        lax.all_gather(w_key.astype(jnp.bfloat16), "dp", axis=0, tiled=True),
        lax.all_gather(w_value.astype(jnp.bfloat16), "dp", axis=0, tiled=True),
        lax.all_gather(w_gate.astype(jnp.bfloat16), "dp", axis=0, tiled=True),
        lax.all_gather(w_out.astype(jnp.bfloat16), "dp", axis=0, tiled=True),
    )
    queries = times_plain(rows_one, query_low).reshape(seq_slots, heads_here, KEY)
    key_rows = times_plain(rows_one, key_low).reshape(seq_slots, heads_here, KEY)
    value_rows = (
        times_plain(rows_one, value_low).reshape(seq_slots, heads_here, VAL).astype(jnp.bfloat16)
    )
    gate_pre = times_plain(rows_one, gate_low).reshape(seq_slots, heads_here, VAL)
    query_turned = rotate(queries, cosines, sines).astype(jnp.bfloat16)
    key_turned = rotate_scaled(key_rows, cosines, sines).astype(jnp.bfloat16)

    def retain(offset):
        query_block = lax.dynamic_slice_in_dim(query_turned, offset, block_rows, 0)
        scores = jnp.einsum(
            "qhk,shk->hqs", query_block, key_turned, preferred_element_type=jnp.float32
        )
        weights = (scores * decay_block(offset, block_rows, seq_slots, log_decay)).astype(
            jnp.bfloat16
        )
        return jnp.einsum("hqs,shv->qhv", weights, value_rows, preferred_element_type=jnp.float32)

    retained = lax.map(retain, offsets).reshape(seq_slots, heads_here, VAL)
    mixed = (
        gated_heads(gate_pre, retained).astype(jnp.bfloat16).reshape(seq_slots, heads_here * VAL)
    )
    middle = features + lax.psum_scatter(
        times_right(mixed, out_low), "tensor", scatter_dimension=0, tiled=True
    )
    second_norm = layer_norm(middle, gain_two).astype(jnp.bfloat16)
    rows_two = lax.all_gather(second_norm, "tensor", axis=0, tiled=True)
    mgate_low, mup_low, down_low = (
        lax.all_gather(w_mgate.astype(jnp.bfloat16), "dp", axis=0, tiled=True),
        lax.all_gather(w_mup.astype(jnp.bfloat16), "dp", axis=0, tiled=True),
        lax.all_gather(w_down.astype(jnp.bfloat16), "dp", axis=0, tiled=True),
    )
    mgate_pre = times_plain(rows_two, mgate_low)
    mup_pre = times_plain(rows_two, mup_low)
    hidden = gelu_gated(mgate_pre, mup_pre).astype(jnp.bfloat16)
    final = middle + lax.psum_scatter(
        times_right(hidden, down_low).astype(jnp.bfloat16),
        "tensor",
        scatter_dimension=0,
        tiled=True,
    ).astype(jnp.float32)
    output = jnp.where(valid, final, 0.0).astype(jnp.bfloat16)
    grad_final = jnp.where(valid, cotangent.astype(jnp.float32), 0.0)
    grad_mlp_rows = lax.all_gather(grad_final.astype(jnp.bfloat16), "tensor", axis=0, tiled=True)
    grad_hidden = times_plain(grad_mlp_rows, down_low)
    grad_down = times_left(grad_mlp_rows, hidden)
    _, pull_mlp = jax.vjp(gelu_gated, mgate_pre, mup_pre)
    grad_mgate_f, grad_mup_f = pull_mlp(grad_hidden)
    grad_mgate_low = grad_mgate_f.astype(jnp.bfloat16)
    grad_mup_low = grad_mup_f.astype(jnp.bfloat16)
    grad_mgate = times_left(rows_two, grad_mgate_low)
    grad_mup = times_left(rows_two, grad_mup_low)
    grad_second = lax.psum_scatter(
        times_right(grad_mgate_low, mgate_low) + times_right(grad_mup_low, mup_low),
        "tensor",
        scatter_dimension=0,
        tiled=True,
    )
    _, pull_two = jax.vjp(layer_norm, middle, gain_two)
    grad_middle_norm, grad_gain_two_here = pull_two(grad_second)
    grad_middle = grad_final + grad_middle_norm
    grad_attn_rows = lax.all_gather(grad_middle.astype(jnp.bfloat16), "tensor", axis=0, tiled=True)
    grad_mixed = times_plain(grad_attn_rows, out_low).reshape(seq_slots, heads_here, VAL)
    grad_out = times_left(grad_attn_rows, mixed)
    _, pull_heads = jax.vjp(gated_heads, gate_pre, retained)
    grad_gate_f, grad_ret_f = pull_heads(grad_mixed)
    grad_gate_low = grad_gate_f.astype(jnp.bfloat16).reshape(seq_slots, heads_here * VAL)
    grad_ret = grad_ret_f.astype(jnp.bfloat16)

    def retain_back(carry, offset):
        key_total, value_total = carry
        query_block = lax.dynamic_slice_in_dim(query_turned, offset, block_rows, 0)
        grad_block = lax.dynamic_slice_in_dim(grad_ret, offset, block_rows, 0)
        factor = decay_block(offset, block_rows, seq_slots, log_decay)
        scores = jnp.einsum(
            "qhk,shk->hqs", query_block, key_turned, preferred_element_type=jnp.float32
        )
        weights = (scores * factor).astype(jnp.bfloat16)
        grad_weights = jnp.einsum(
            "qhv,shv->hqs", grad_block, value_rows, preferred_element_type=jnp.float32
        )
        grad_scores = (grad_weights * factor).astype(jnp.bfloat16)
        value_total = value_total + jnp.einsum(
            "hqs,qhv->shv", weights, grad_block, preferred_element_type=jnp.float32
        )
        key_total = key_total + jnp.einsum(
            "hqs,qhk->shk", grad_scores, query_block, preferred_element_type=jnp.float32
        )
        grad_query_block = jnp.einsum(
            "hqs,shk->qhk", grad_scores, key_turned, preferred_element_type=jnp.float32
        )
        return ((key_total, value_total), grad_query_block)

    start_carry = (
        jnp.zeros((seq_slots, heads_here, KEY), jnp.float32),
        jnp.zeros((seq_slots, heads_here, VAL), jnp.float32),
    )
    (grad_key_turned, grad_value_f), grad_query_blocks = lax.scan(retain_back, start_carry, offsets)
    grad_query_turned = grad_query_blocks.reshape(seq_slots, heads_here, KEY)
    _, pull_query = jax.vjp(partial(rotate, cosines=cosines, sines=sines), queries)
    _, pull_key = jax.vjp(partial(rotate_scaled, cosines=cosines, sines=sines), key_rows)
    grad_query_low = (
        pull_query(grad_query_turned)[0].astype(jnp.bfloat16).reshape(seq_slots, heads_here * KEY)
    )
    grad_key_low = (
        pull_key(grad_key_turned)[0].astype(jnp.bfloat16).reshape(seq_slots, heads_here * KEY)
    )
    grad_value_low = grad_value_f.astype(jnp.bfloat16).reshape(seq_slots, heads_here * VAL)
    grad_query = times_left(rows_one, grad_query_low)
    grad_key = times_left(rows_one, grad_key_low)
    grad_value = times_left(rows_one, grad_value_low)
    grad_gate = times_left(rows_one, grad_gate_low)
    total = times_right(grad_query_low, query_low)
    total = total + times_right(grad_key_low, key_low)
    total = total + times_right(grad_value_low, value_low)
    grad_first = lax.psum_scatter(
        total + times_right(grad_gate_low, gate_low), "tensor", scatter_dimension=0, tiled=True
    )
    _, pull_one = jax.vjp(layer_norm, features, gain_one)
    grad_features_norm, grad_gain_one_here = pull_one(grad_first)
    grad_tokens = (grad_middle + grad_features_norm).astype(jnp.bfloat16)
    sum_gain_one, sum_gain_two = lax.psum(
        (grad_gain_one_here, grad_gain_two_here), ("dp", "tensor")
    )
    sum_query, sum_key, sum_value, sum_gate, sum_out, sum_mgate, sum_mup, sum_down = (
        lax.psum_scatter(
            grad_query.astype(jnp.bfloat16), "dp", scatter_dimension=0, tiled=True
        ).astype(jnp.float32),
        lax.psum_scatter(
            grad_key.astype(jnp.bfloat16), "dp", scatter_dimension=0, tiled=True
        ).astype(jnp.float32),
        lax.psum_scatter(
            grad_value.astype(jnp.bfloat16), "dp", scatter_dimension=0, tiled=True
        ).astype(jnp.float32),
        lax.psum_scatter(
            grad_gate.astype(jnp.bfloat16), "dp", scatter_dimension=0, tiled=True
        ).astype(jnp.float32),
        lax.psum_scatter(
            grad_out.astype(jnp.bfloat16), "dp", scatter_dimension=0, tiled=True
        ).astype(jnp.float32),
        lax.psum_scatter(
            grad_mgate.astype(jnp.bfloat16), "dp", scatter_dimension=0, tiled=True
        ).astype(jnp.float32),
        lax.psum_scatter(
            grad_mup.astype(jnp.bfloat16), "dp", scatter_dimension=0, tiled=True
        ).astype(jnp.float32),
        lax.psum_scatter(
            grad_down.astype(jnp.bfloat16), "dp", scatter_dimension=0, tiled=True
        ).astype(jnp.float32),
    )
    return (
        output,
        grad_tokens,
        sum_gain_one,
        sum_gain_two,
        sum_query,
        sum_key,
        sum_value,
        sum_gate,
        sum_out,
        sum_mgate,
        sum_mup,
        sum_down,
    )


def solution(mesh):
    placed = (
        P(("dp", "tensor"), None),
        P("dp"),
        P(("dp", "tensor"), None),
        P(),
        P(),
        P("dp", "tensor"),
        P("dp", "tensor"),
        P("dp", "tensor"),
        P("dp", "tensor"),
        P("dp", "tensor"),
        P("dp", "tensor"),
        P("dp", "tensor"),
        P("dp", "tensor"),
    )
    return jax.shard_map(
        per_device,
        mesh=mesh,
        in_specs=placed,
        out_specs=(
            P(("dp", "tensor"), None),
            P(("dp", "tensor"), None),
            P(),
            P(),
            P("dp", "tensor"),
            P("dp", "tensor"),
            P("dp", "tensor"),
            P("dp", "tensor"),
            P("dp", "tensor"),
            P("dp", "tensor"),
            P("dp", "tensor"),
            P("dp", "tensor"),
        ),
        check_vma=False,
    )
```

profile of v0, /device:TPU:0, one launch (start us, length us, event | category | flops | bytes accessed | tf_op | source)
XLA Modules:
  0.0 1631.8 jit_solution(9255726333543230482)
XLA Ops:
  23.2 17.9 %all-gather.19.cloned.1.call-done = bf16[2048,512]{1,0:T(8,128)(2,1)} async-done(((bf16[256,512]{1,0:T(8,128)(2,1)}), bf16[2048,512]{1,0:T(8,128)(2,1)}) %all-gather.19.cloned.1.call-update) | async-done | bytes 2097168 | tf_op jit(solution)/shard_map/all_gather | solution.py:114
  41.1 82.9 %all-gather.13.cloned.1.call-done = bf16[1024,2048]{1,0:T(8,128)(2,1)} async-done(((bf16[256,2048]{1,0:T(8,128)(2,1)}), bf16[1024,2048]{1,0:T(8,128)(2,1)}) %all-gather.13.cloned.1.call-update) | async-done | bytes 4194320 | tf_op jit(solution)/shard_map/all_gather | solution.py:111
  124.1 6.6 fusion.65
  133.6 19.4 %all-gather.17.cloned.1.call-done = bf16[2048,512]{1,0:T(8,128)(2,1)} async-done(((bf16[256,512]{1,0:T(8,128)(2,1)}), bf16[2048,512]{1,0:T(8,128)(2,1)}) %all-gather.17.cloned.1.call-update) | async-done | bytes 2097168 | tf_op jit(solution)/shard_map/all_gather | solution.py:113
  153.0 6.6 fusion.64
  168.0 21.9 %all-gather.21.cloned.1.call-done = bf16[2048,864]{0,1:T(8,128)(2,1)} async-done(((bf16[256,864]{0,1:T(8,128)(2,1)}), bf16[2048,864]{0,1:T(8,128)(2,1)}) %all-gather.21.cloned.1.call-update) | async-done | bytes 3538960 | tf_op jit(solution)/shard_map/all_gather | solution.py:115
  189.9 8.4 convolution_convert_fusion.9
  198.2 22.2 %while.26 = (s32[]{:T(128)}, f32[2,512,2,432]{1,3,2,0:T(8,128)S(1)}, s32[2]{0:T(128)S(1)}, bf16[1024,2,256]{2,0,1:T(8,128)(2,1)}, bf16[1024,2,256]{2,0,1:T(8,128...) while((s32[]{:T(128)}, ...), condition=%wide.region_3.4_spmd.clone, body=%wide.region_2.3_spmd.clone.sunk | while | flops 1450181120 | bytes 10362023 | solution.py:138
  230.0 10.9 multiply_convert_fusion.5
  240.9 22.8 %all-gather.23.cloned.1.call-done = bf16[2048,864]{0,1:T(8,128)(2,1)} async-done(((bf16[256,864]{0,1:T(8,128)(2,1)}), bf16[2048,864]{0,1:T(8,128)(2,1)}) %all-gather.23.cloned.1.call-update) | async-done | bytes 3538960 | tf_op jit(solution)/shard_map/all_gather | solution.py:117
  263.7 10.6 fusion.66
  276.4 142.5 %reduce-scatter.13.cloned.1.call-done = f32[256,2048]{1,0:T(8,128)} async-done(((f32[1024,2048]{1,0:T(8,128)}), f32[256,2048]{1,0:T(8,128)}) %reduce-scatter.13.cloned.1.call-update) | async-done | bytes 2097168 | tf_op jit(solution)/shard_map/reduce_scatter | solution.py:142
  432.2 24.5 %all-gather.27.cloned.1.call-done = bf16[2048,864]{0,1:T(8,128)(2,1)} async-done(((bf16[256,864]{0,1:T(8,128)(2,1)}), bf16[2048,864]{0,1:T(8,128)(2,1)}) %all-gather.27.cloned.1.call-update) | async-done | bytes 3538960 | tf_op jit(solution)/shard_map/all_gather | solution.py:148
  456.7 82.9 %all-gather.25.cloned.1.call-done = bf16[1024,2048]{1,0:T(8,128)(2,1)} async-done(((bf16[256,2048]{1,0:T(8,128)(2,1)}), bf16[1024,2048]{1,0:T(8,128)(2,1)}) %all-gather.25.cloned.1.call-update) | async-done | bytes 4194320 | tf_op jit(solution)/shard_map/all_gather | solution.py:146
  539.6 8.9 fusion.67
  548.5 26.5 %all-gather.31.cloned.1.call-done = bf16[2048,864]{0,1:T(8,128)(2,1)} async-done(((bf16[256,864]{0,1:T(8,128)(2,1)}), bf16[2048,864]{0,1:T(8,128)(2,1)}) %all-gather.31.cloned.1.call-update) | async-done | bytes 3538960 | tf_op jit(solution)/shard_map/all_gather | solution.py:150
  575.0 82.4 %all-gather.33.cloned.1.call-done = bf16[1024,2048]{1,0:T(8,128)(2,1)} async-done(((bf16[256,2048]{1,0:T(8,128)(2,1)}), bf16[1024,2048]{1,0:T(8,128)(2,1)}) %all-gather.33.cloned.1.call-update) | async-done | bytes 4194320 | tf_op jit(solution)/shard_map/all_gather | solution.py:163
  657.4 16.5 %multiply_convert_fusion.3 = (bf16[1024,864]{0,1:T(8,128)(2,1)}, f32[1024,864]{0,1:T(8,128)}, f32[1024,864]{0,1:T(8,128)}) fusion(f32[1024,864]{0,1:T(8,128)} %fusion.67, bf16[1024,2048]{1,0:T(8,128)(2,1)} %all-gather.33.cloned.1.call-done, bf16[2048,864]{0,1:T(8,128)(2,1)} %all-gather.31.cloned.1.call-done), kind=kOutput, calls=%fused_computation.48 | convolution fusion | flops 3682271232 | bytes 20119552 | tf_op jit(solution)/shard_map/dot_general | solution.py:17
  674.0 18.9 %all-gather.29.cloned.1.call-done = bf16[2048,864]{0,1:T(8,128)(2,1)} async-done(((bf16[256,864]{0,1:T(8,128)(2,1)}), bf16[2048,864]{0,1:T(8,128)(2,1)}) %all-gather.29.cloned.1.call-update) | async-done | bytes 3538960 | tf_op jit(solution)/shard_map/all_gather | solution.py:149
  692.8 12.8 add_convert_fusion.1
  710.3 7.1 convolution_add_fusion
  717.8 9.1 convolution_convert_fusion
  727.0 135.0 %reduce-scatter.17.cloned.1.call-done = f32[256,2048]{1,0:T(8,128)} async-done(((f32[1024,2048]{1,0:T(8,128)}), f32[256,2048]{1,0:T(8,128)}) %reduce-scatter.17.cloned.1.call-update) | async-done | bytes 2097168 | tf_op jit(solution)/shard_map/reduce_scatter | solution.py:172
  866.0 75.6 %reduce-scatter.15.cloned.1.call-done = bf16[256,2048]{1,0:T(8,128)(2,1)} async-done(((bf16[1024,2048]{1,0:T(8,128)(2,1)}), bf16[256,2048]{1,0:T(8,128)(2,1)}) %reduce-scatter.15.cloned.1.call-update) | async-done | bytes 1048592 | tf_op jit(solution)/shard_map/reduce_scatter | solution.py:155
  948.9 8.3 convolution_convert_fusion.3
  957.3 8.7 convolution_convert_fusion.2
  971.4 5.8 reshape.312
  981.2 5.3 convolution_convert_fusion.1
  986.6 43.7 %all-gather.35.cloned.1.call-done = bf16[1024,2048]{1,0:T(8,128)(2,1)} async-done(((bf16[256,2048]{1,0:T(8,128)(2,1)}), bf16[1024,2048]{1,0:T(8,128)(2,1)}) %all-gather.35.cloned.1.call-update) | async-done | bytes 4194320 | tf_op jit(solution)/shard_map/all_gather | solution.py:181
  1030.3 12.4 fusion.25
  1042.7 6.1 reshape.313
  1058.9 44.1 %while.27 = (s32[]{:T(128)}, f32[1024,2,256]{0,2,1:T(8,128)}, f32[1024,2,432]{0,2,1:T(8,128)}, f32[2,512,2,256]{3,1,0,2:T(8,128)}, s32[2]{0:T(128)S(1)}, /*index...) while((s32[]{:T(128)}, f32[1024,2,256]{0,2,1:T(8,128)}, ...), condition=%wide.region_16.17_spmd.clone, body=%wide.region_15.16_spmd.clone.sunk | while | flops 3436904960 | bytes 60432208 | solution.py:217
  1073.3 6.3 bitcast_add_fusion.5
  1094.7 7.8 bitcast_add_fusion.5
  1115.6 6.4 convolution_convert_fusion.8
  1126.0 5.2 convolution_convert_fusion.6
  1132.8 7.4 convolution_convert_fusion.4
  1141.7 7.6 convolution_convert_fusion.5
  1154.1 6.9 fusion.70
  1161.0 6.9 fusion.71
  1167.9 12.2 add_add_fusion
  1186.5 42.8 %reduce-scatter.23.cloned.1.call-done = bf16[256,512]{1,0:T(8,128)(2,1)} async-done(((bf16[2048,512]{1,0:T(8,128)(2,1)}), bf16[256,512]{1,0:T(8,128)(2,1)}) %reduce-scatter.23.cloned.1.call-update) | async-done | bytes 262160 | tf_op jit(solution)/shard_map/reduce_scatter | solution.py:248
  1231.1 42.6 %reduce-scatter.21.cloned.1.call-done = bf16[256,512]{1,0:T(8,128)(2,1)} async-done(((bf16[2048,512]{1,0:T(8,128)(2,1)}), bf16[256,512]{1,0:T(8,128)(2,1)}) %reduce-scatter.21.cloned.1.call-update) | async-done | bytes 262160 | tf_op jit(solution)/shard_map/reduce_scatter | solution.py:245
  1275.5 50.2 %reduce-scatter.25.cloned.1.call-done = bf16[256,864]{0,1:T(8,128)(2,1)} async-done(((bf16[2048,864]{0,1:T(8,128)(2,1)}), bf16[256,864]{0,1:T(8,128)(2,1)}) %reduce-scatter.25.cloned.1.call-update) | async-done | bytes 442384 | tf_op jit(solution)/shard_map/reduce_scatter | solution.py:251
  1327.7 50.0 %reduce-scatter.29.cloned.1.call-done = bf16[256,864]{0,1:T(8,128)(2,1)} async-done(((bf16[2048,864]{0,1:T(8,128)(2,1)}), bf16[256,864]{0,1:T(8,128)(2,1)}) %reduce-scatter.29.cloned.1.call-update) | async-done | bytes 442384 | tf_op jit(solution)/shard_map/reduce_scatter | solution.py:257
  1379.7 50.0 %reduce-scatter.27.cloned.1.call-done = bf16[256,864]{0,1:T(8,128)(2,1)} async-done(((bf16[2048,864]{0,1:T(8,128)(2,1)}), bf16[256,864]{0,1:T(8,128)(2,1)}) %reduce-scatter.27.cloned.1.call-update) | async-done | bytes 442384 | tf_op jit(solution)/shard_map/reduce_scatter | solution.py:254
  1431.6 144.8 %reduce-scatter.19.cloned.1.call-done = f32[256,2048]{1,0:T(8,128)} async-done(((f32[1024,2048]{1,0:T(8,128)}), f32[256,2048]{1,0:T(8,128)}) %reduce-scatter.19.cloned.1.call-update) | async-done | bytes 2097168 | tf_op jit(solution)/shard_map/reduce_scatter | solution.py:235
  1579.7 41.1 %all-reduce.4 = (f32[2048]{0:T(1024)}, f32[2048]{0:T(1024)}) all-reduce(f32[2048]{0:T(1024)S(1)} %get-tuple-element.206, f32[2048]{0:T(1024)S(1)} %copy-done.45), channel_id=1, replica_groups=mesh['dp'=8,'tensor'=4] {'dp','tensor'}, use_global_device_ids=true, to_apply=%region_21.22 | all-reduce | flops 4096 | bytes 32768 | tf_op jit(solution)/shard_map/psum | solution.py:241
  (301 shorter events, 177.8 us)
Async XLA Ops:
  7.2 5.3 copy-start.4
  7.2 7.4 copy-start.38
  7.2 8.2 copy-start.35
  7.2 33.9 %all-gather.19.cloned.1.call-start = ((), (), s32[]{:S(2)}) async-start(), calls=%async_computation.15 | async-start | bytes 2359296 | tf_op jit(solution)/shard_map/all_gather | solution.py:114
  9.2 114.9 %all-gather.13.cloned.1.call-start = ((), (), s32[]{:S(2)}) async-start(), calls=%async_computation.12 | async-start | bytes 5242880 | tf_op jit(solution)/shard_map/all_gather | solution.py:111
  10.7 5.6 copy-start.36
  10.7 6.4 copy-start.43
  14.6 138.4 %all-gather.17.cloned.1.call-start = ((), (), s32[]{:S(2)}) async-start(), calls=%async_computation.14 | async-start | bytes 2359296 | tf_op jit(solution)/shard_map/all_gather | solution.py:113
  15.4 174.5 %all-gather.21.cloned.1.call-start = ((), (), s32[]{:S(2)}) async-start(), calls=%async_computation.16 | async-start | bytes 3981312 | tf_op jit(solution)/shard_map/all_gather | solution.py:115
  16.3 213.7 %all-gather.15.cloned.1.call-start = ((), (), s32[]{:S(2)}) async-start(), calls=%async_computation.13 | async-start | bytes 3981312 | tf_op jit(solution)/shard_map/all_gather | solution.py:116
  17.2 246.5 %all-gather.23.cloned.1.call-start = ((), (), s32[]{:S(2)}) async-start(), calls=%async_computation.17 | async-start | bytes 3981312 | tf_op jit(solution)/shard_map/all_gather | solution.py:117
  18.1 400.8 %reduce-scatter.13.cloned.1.call-start = ((), (), s32[]{:S(2)}) async-start(), calls=%async_computation.18 | async-start | bytes 10485760 | tf_op jit(solution)/shard_map/reduce_scatter | solution.py:142
  274.3 182.4 %all-gather.27.cloned.1.call-start = ((), (), s32[]{:S(2)}) async-start(), calls=%async_computation.20 | async-start | bytes 3981312 | tf_op jit(solution)/shard_map/all_gather | solution.py:148
  276.3 263.3 %all-gather.25.cloned.1.call-start = ((), (), s32[]{:S(2)}) async-start(), calls=%async_computation.19 | async-start | bytes 5242880 | tf_op jit(solution)/shard_map/all_gather | solution.py:146
  424.3 150.7 %all-gather.31.cloned.1.call-start = ((), (), s32[]{:S(2)}) async-start(), calls=%async_computation.22 | async-start | bytes 3981312 | tf_op jit(solution)/shard_map/all_gather | solution.py:150
  426.3 231.1 %all-gather.33.cloned.1.call-start = ((), (), s32[]{:S(2)}) async-start(), calls=%async_computation.24 | async-start | bytes 5242880 | tf_op jit(solution)/shard_map/all_gather | solution.py:163
  430.1 262.8 %all-gather.29.cloned.1.call-start = ((), (), s32[]{:S(2)}) async-start(), calls=%async_computation.21 | async-start | bytes 3981312 | tf_op jit(solution)/shard_map/all_gather | solution.py:149
  432.1 429.9 %reduce-scatter.17.cloned.1.call-start = ((), (), s32[]{:S(2)}) async-start(), calls=%async_computation.25 | async-start | bytes 10485760 | tf_op jit(solution)/shard_map/reduce_scatter | solution.py:172
  692.8 12.8 copy-start.61
  717.4 224.3 %reduce-scatter.15.cloned.1.call-start = ((), (), s32[]{:S(2)}) async-start(), calls=%async_computation.23 | async-start | bytes 5242880 | tf_op jit(solution)/shard_map/reduce_scatter | solution.py:155
  726.9 303.3 %all-gather.35.cloned.1.call-start = ((), (), s32[]{:S(2)}) async-start(), calls=%async_computation.26 | async-start | bytes 5242880 | tf_op jit(solution)/shard_map/all_gather | solution.py:181
  941.7 5.8 copy-start.16
  941.7 5.8 copy-start.57
  948.9 231.4 %reduce-scatter.31.cloned.1.call-start = ((), (), s32[]{:S(2)}) async-start(), calls=%async_computation.33 | async-start | bytes 3981312 | tf_op jit(solution)/shard_map/reduce_scatter | solution.py:260
  957.2 225.0 %reduce-scatter.33.cloned.1.call-start = ((), (), s32[]{:S(2)}) async-start(), calls=%async_computation.34 | async-start | bytes 3981312 | tf_op jit(solution)/shard_map/reduce_scatter | solution.py:263
  966.0 218.4 %reduce-scatter.35.cloned.1.call-start = ((), (), s32[]{:S(2)}) async-start(), calls=%async_computation.35 | async-start | bytes 3981312 | tf_op jit(solution)/shard_map/reduce_scatter | solution.py:266
  986.5 242.8 %reduce-scatter.23.cloned.1.call-start = ((), (), s32[]{:S(2)}) async-start(), calls=%async_computation.29 | async-start | bytes 2359296 | tf_op jit(solution)/shard_map/reduce_scatter | solution.py:248
  1048.8 5.1 copy-start.1
  1048.8 5.2 copy-start.7
  1048.8 6.6 copy-start.13
  1112.1 161.6 %reduce-scatter.21.cloned.1.call-start = ((), (), s32[]{:S(2)}) async-start(), calls=%async_computation.28 | async-start | bytes 2359296 | tf_op jit(solution)/shard_map/reduce_scatter | solution.py:245
  1115.6 6.4 copy-start.34
  1122.0 203.7 %reduce-scatter.25.cloned.1.call-start = ((), (), s32[]{:S(2)}) async-start(), calls=%async_computation.30 | async-start | bytes 3981312 | tf_op jit(solution)/shard_map/reduce_scatter | solution.py:251
  1131.3 246.4 %reduce-scatter.29.cloned.1.call-start = ((), (), s32[]{:S(2)}) async-start(), calls=%async_computation.32 | async-start | bytes 3981312 | tf_op jit(solution)/shard_map/reduce_scatter | solution.py:257
  1140.2 289.5 %reduce-scatter.27.cloned.1.call-start = ((), (), s32[]{:S(2)}) async-start(), calls=%async_computation.31 | async-start | bytes 3981312 | tf_op jit(solution)/shard_map/reduce_scatter | solution.py:254
  1149.3 427.2 %reduce-scatter.19.cloned.1.call-start = ((), (), s32[]{:S(2)}) async-start(), calls=%async_computation.27 | async-start | bytes 10485760 | tf_op jit(solution)/shard_map/reduce_scatter | solution.py:235
  1154.1 6.9 copy-start.27
  1154.1 6.9 copy-start.31
  1161.0 6.9 copy-start.28
  1184.2 392.3 %copy-start.5 = (bf16[256,2048]{1,0:T(8,128)(2,1)S(1)}, bf16[256,2048]{1,0:T(8,128)(2,1)}, u32[]{:S(2)}) copy-start(bf16[256,2048]{1,0:T(8,128)(2,1)} %param.17) | copy-start | bytes 3145732
  1184.2 392.3 %copy-start.39 = (f32[2048]{0:T(1024)S(1)}, f32[2048]{0:T(1024)}, u32[]{:S(2)}) copy-start(f32[2048]{0:T(1024)} %param.20) | copy-start | bytes 24580
  1184.2 392.3 %copy-start.44 = (f32[256]{0:T(256)S(1)}, f32[256]{0:T(256)}, u32[]{:S(2)}) copy-start(f32[256]{0:T(256)} %copy-done.43) | copy-start | bytes 3076
  1275.5 303.2 %copy-start.55 = (f32[256]{0:T(256)S(1)}, f32[256]{0:T(256)}, u32[]{:S(2)}) copy-start(f32[256]{0:T(256)} %copy-done.54) | copy-start | bytes 3076
  1275.5 303.3 %copy-start.48 = (f32[256]{0:T(256)S(1)}, f32[256]{0:T(256)}, u32[]{:S(2)}) copy-start(f32[256]{0:T(256)} %copy-done.47) | copy-start | bytes 3076
  1379.6 200.1 %copy-start.45 = (f32[2048]{0:T(1024)S(1)}, f32[2048]{0:T(1024)}, u32[]{:S(2)}) copy-start(f32[2048]{0:T(1024)} %get-tuple-element.204) | copy-start | bytes 24580
  1379.7 241.2 %copy-start.9 = (f32[256,2048]{1,0:T(8,128)S(1)}, f32[256,2048]{1,0:T(8,128)}, u32[]{:S(2)}) copy-start(f32[256,2048]{1,0:T(8,128)} %copy-done.8) | copy-start | bytes 6291460
  1379.7 241.2 %copy-start.53 = (f32[256]{0:T(256)S(1)}, f32[256]{0:T(256)}, u32[]{:S(2)}) copy-start(f32[256]{0:T(256)} %copy-done.52) | copy-start | bytes 3076
  1379.7 241.2 %copy-start.58 = (pred[256]{0:T(512)(128)(4,1)S(1)}, pred[256]{0:T(512)(128)(4,1)}, u32[]{:S(2)}) copy-start(pred[256]{0:T(512)(128)(4,1)} %copy-done.56) | copy-start | bytes 772
  (48 other events, 127.6 us)
Sparse Core Ops, SparseCore 0:
  10.5 30.5 all-gather.18
  43.3 80.7 all-gather.12
  126.5 26.4 all-gather.16
  155.3 34.5 all-gather.20
  192.2 34.5 all-gather.14
  229.1 34.5 all-gather.22
  274.4 144.4 reduce-scatter.12
  421.4 35.2 all-gather.26
  458.8 80.7 all-gather.24
  541.9 33.0 all-gather.30
  576.6 80.7 all-gather.32
  659.7 33.0 all-gather.28
  717.5 144.4 reduce-scatter.16
  864.2 77.4 reduce-scatter.14
  949.0 81.2 all-gather.34
  1034.0 46.6 reduce-scatter.30
  1084.5 48.0 reduce-scatter.32
  1136.3 48.0 reduce-scatter.34
  1188.1 41.1 reduce-scatter.22
  1232.4 41.1 reduce-scatter.20
  1277.5 48.0 reduce-scatter.24
  1329.6 48.0 reduce-scatter.28
  1381.5 48.0 reduce-scatter.26
  1432.0 144.4 reduce-scatter.18
where the time goes:
time: 1640 us; the launch traced here: 1630 us
  waiting for transfers between devices  1180 us (72%)
  matrix products  238 us (15%)
  other arithmetic  91.4 us (6%)
  local copies, waits for them, and re-layouts  56.6 us (3%)
  blocking collectives  41.1 us (3%)
    reduce_scatter x1, waiting for transfers between devices, per_device(): lax.psum_scatter(total + times_right(grad_gate_low, gate_low), 'tensor',...  145 us
    reduce_scatter x1, waiting for transfers between devices, per_device(): lax.psum_scatter(times_right(mixed, out_low), 'tensor', scatter_dimension...  143 us
    reduce_scatter x1, waiting for transfers between devices, per_device(): lax.psum_scatter(times_right(grad_mgate_low, mgate_low) + times_right(gra...  135 us
    dot_general x8, matrix products, times_plain(): return jnp.dot(left, right, preferred_element_type=jnp.float32)  83 us
    all_gather x1, waiting for transfers between devices, per_device(): rows_two = lax.all_gather(second_norm, 'tensor', axis=0, tiled=True)  82.9 us
    all_gather x1, waiting for transfers between devices, per_device(): rows_one = lax.all_gather(first_norm, 'tensor', axis=0, tiled=True)  82.9 us
    all_gather x1, waiting for transfers between devices, per_device(): lax.all_gather(grad_final.astype(jnp.bfloat16), 'tensor', axis=0, tiled=T...  82.4 us
    reduce_scatter x1, waiting for transfers between devices, per_device(): lax.psum_scatter(times_right(hidden, down_low).astype(jnp.bfloat16), 'ten...  75.6 us
  transfers between devices with their start and end apart: 24, of which 21 were waited for; matrix products, arithmetic and copies ran while one was open for 19% of the time, Pallas kernels for 0%

commit v1 on v0

v1 whole, which is shorter than its diff:
```python
from functools import partial

import jax
import jax.numpy as jnp
from jax import lax
from jax.experimental import pallas as pl
from jax.experimental.pallas import tpu as pltpu
from jax.sharding import PartitionSpec as P

KEY = 256
VAL = 432
VPAD = 512
EPS = 1e-05
HEAD_EPS = 1.0
F32 = jnp.float32
BF16 = jnp.bfloat16
VMEM_LIMIT = 48 * 1024 * 1024


def times_plain(left, right):
    return jnp.dot(left, right, preferred_element_type=F32)


def times_left(left, right):
    return lax.dot_general(left, right, (((0,), (0,)), ((), ())), preferred_element_type=F32)


def times_right(left, right):
    return lax.dot_general(left, right, (((1,), (1,)), ((), ())), preferred_element_type=F32)


def after(array, *earlier):
    return lax.optimization_barrier((array, *earlier))[0]


def norm_parts(features):
    centred = features - jnp.mean(features, -1, keepdims=True)
    inverse = lax.rsqrt(jnp.mean(centred * centred, -1, keepdims=True) + EPS)
    return centred * inverse, inverse


def norm_back(normed, inverse, grad, gain):
    scaled = grad * gain
    return inverse * (
        scaled
        - jnp.mean(scaled, -1, keepdims=True)
        - normed * jnp.mean(scaled * normed, -1, keepdims=True)
    )


def decay_rows(log_decay, rows, width):
    query = lax.broadcasted_iota(jnp.int32, (rows, width), 0) + (width - rows)
    key = lax.broadcasted_iota(jnp.int32, (rows, width), 1)
    spacing = query - key
    factor = jnp.exp(log_decay * jnp.maximum(spacing, 0).astype(F32))
    return jnp.where(spacing >= 0, factor, 0.0)


def retain_kernel(slots, rows, place_ref, decay_ref, *refs):
    ins, (cos_ref, sin_ref), outs = refs[: 4 * slots], refs[4 * slots : 4 * slots + 2], refs[4 * slots + 2 :]
    query_ref, key_ref, value_ref, normed_ref, scale_ref, mixed_ref, factor_ref, kept_ref = outs
    head = pl.program_id(0)
    place = place_ref[0]
    seq = slots * rows
    half = KEY // 2
    for slot in range(slots):
        start = pl.multiple_of((slot ^ place) * rows, rows)
        cosines, sines = cos_ref[pl.ds(start, rows), :], sin_ref[pl.ds(start, rows), :]
        for source, target, scale in ((ins[slot], query_ref, 1.0), (ins[slots + slot], key_ref, KEY**-0.5)):
            low = source[:, :half].astype(F32)
            high = source[:, half:].astype(F32)
            target[pl.ds(start, rows), :half] = ((low * cosines - high * sines) * scale).astype(BF16)
            target[pl.ds(start, rows), half:] = ((high * cosines + low * sines) * scale).astype(BF16)
        value_ref[pl.ds(start, rows), :] = ins[2 * slots + slot][...]
    factor_ref[...] = decay_rows(decay_ref[head], rows, seq)
    for block in range(slots):
        width = (block + 1) * rows
        scores = times_right(query_ref[block * rows : width, :], key_ref[:width, :])
        weights = (scores * factor_ref[:, seq - width :]).astype(BF16)
        kept_ref[block * rows : width, :] = times_plain(weights, value_ref[:width, :])
    inside = lax.broadcasted_iota(jnp.int32, (rows, VPAD), 1) < VAL
    for slot in range(slots):
        start = pl.multiple_of((slot ^ place) * rows, rows)
        kept = kept_ref[pl.ds(start, rows), :]
        mean = jnp.sum(kept, -1, keepdims=True) / VAL
        centred = jnp.where(inside, kept - mean, 0.0)
        inverse = lax.rsqrt(jnp.sum(centred * centred, -1, keepdims=True) / VAL + HEAD_EPS)
        normed = centred * inverse
        gate = ins[3 * slots + slot][...].astype(F32)
        mixed = gate * jax.nn.sigmoid(gate) * normed
        mixed_ref[slot * rows : (slot + 1) * rows, :] = mixed.astype(BF16)
        normed_ref[slot * rows : (slot + 1) * rows, :] = normed.astype(BF16)
        scale_ref[slot * rows : (slot + 1) * rows, :] = jnp.broadcast_to(inverse, (rows, 128))


def slot_specs(rows, heads):
    first_value = 2 * heads * KEY // VPAD
    return (
        pl.BlockSpec((rows, KEY), lambda h, *_: (0, h)),
        pl.BlockSpec((rows, KEY), lambda h, *_: (0, heads + h)),
        pl.BlockSpec((rows, VPAD), lambda h, *_: (0, first_value + h)),
        pl.BlockSpec((rows, VPAD), lambda h, *_: (0, first_value + heads + h)),
    )


def retain(projected, place, log_decay, cosines, sines, heads):
    slots, rows = len(projected), projected[0].shape[0]
    seq = slots * rows
    specs = slot_specs(rows, heads)
    table = pl.BlockSpec((seq, KEY // 2), lambda h, *_: (0, 0))

    def column(width):
        return pl.BlockSpec((seq, width), lambda h, *_: (0, h))

    return pl.pallas_call(
        partial(retain_kernel, slots, rows),
        out_shape=(
            jax.ShapeDtypeStruct((seq, heads * KEY), BF16),
            jax.ShapeDtypeStruct((seq, heads * KEY), BF16),
            jax.ShapeDtypeStruct((seq, heads * VPAD), BF16),
            jax.ShapeDtypeStruct((seq, heads * VPAD), BF16),
            jax.ShapeDtypeStruct((seq, heads * 128), F32),
            jax.ShapeDtypeStruct((seq, heads * VPAD), BF16),
        ),
        grid_spec=pltpu.PrefetchScalarGridSpec(
            num_scalar_prefetch=2,
            grid=(heads,),
            in_specs=[spec for spec in specs for _ in range(slots)] + [table, table],
            out_specs=[column(KEY), column(KEY), column(VPAD), column(VPAD), column(128), column(VPAD)],
            scratch_shapes=[pltpu.VMEM((rows, seq), F32), pltpu.VMEM((seq, VPAD), F32)],
        ),
        compiler_params=pltpu.CompilerParams(vmem_limit_bytes=VMEM_LIMIT),
        cost_estimate=pl.CostEstimate(
            flops=heads * seq * seq * (KEY + VPAD), bytes_accessed=heads * seq * 9000, transcendentals=heads * seq * 800
        ),
    )(place, log_decay, *(projected * 4), cosines, sines)


def retain_back_kernel(slots, rows, heads, place_ref, decay_ref, *refs):
    grads, gates, rest = refs[:slots], refs[slots : 2 * slots], refs[2 * slots :]
    (normed_ref, scale_ref, query_ref, key_ref, value_ref, cos_ref, sin_ref, out_ref, factor_ref, ret_ref, key_sum, value_sum) = rest
    head = pl.program_id(0)
    place = place_ref[0]
    seq = slots * rows
    half = KEY // 2
    query_col = pl.multiple_of(head * KEY, KEY)
    key_col = pl.multiple_of((heads + head) * KEY, KEY)
    value_col = pl.multiple_of(2 * heads * KEY + head * VPAD, VPAD)
    gate_col = pl.multiple_of(2 * heads * KEY + (heads + head) * VPAD, VPAD)
    inside = lax.broadcasted_iota(jnp.int32, (rows, VPAD), 1) < VAL
    for slot in range(slots):
        start = pl.multiple_of((slot ^ place) * rows, rows)
        span = slice(slot * rows, (slot + 1) * rows)
        grad, gate = grads[slot][...].astype(F32), gates[slot][...].astype(F32)
        normed, inverse = normed_ref[span, :].astype(F32), scale_ref[span, :1]
        sig = jax.nn.sigmoid(gate)
        out_ref[span, pl.ds(gate_col, VPAD)] = (grad * normed * sig * (1.0 + gate * (1.0 - sig))).astype(BF16)
        grad_normed = grad * gate * sig
        mean = jnp.sum(grad_normed, -1, keepdims=True) / VAL
        along = jnp.sum(grad_normed * normed, -1, keepdims=True) / VAL
        grad_ret = inverse * (grad_normed - mean - normed * along)
        ret_ref[pl.ds(start, rows), :] = jnp.where(inside, grad_ret, 0.0).astype(BF16)
    factor_ref[...] = decay_rows(decay_ref[head], rows, seq)
    key_sum[...] = jnp.zeros_like(key_sum)
    value_sum[...] = jnp.zeros_like(value_sum)
    for block in range(slots):
        width = (block + 1) * rows
        span = slice(block * rows, width)
        query, ret, keys = query_ref[span, :], ret_ref[span, :], key_ref[:width, :]
        factor = factor_ref[:, seq - width :]
        weights = (times_right(query, keys) * factor).astype(BF16)
        grad_scores = (times_right(ret, value_ref[:width, :]) * factor).astype(BF16)
        value_sum[:width, :] += times_left(weights, ret)
        key_sum[:width, :] += times_left(grad_scores, query)
        grad_query = times_plain(grad_scores, keys)
        row = pl.multiple_of((block ^ place) * rows, rows)
        cosines, sines = cos_ref[span, :], sin_ref[span, :]
        low, high = grad_query[:, :half], grad_query[:, half:]
        out_ref[pl.ds(row, rows), pl.ds(query_col, half)] = (low * cosines + high * sines).astype(BF16)
        out_ref[pl.ds(row, rows), pl.ds(pl.multiple_of(query_col + half, half), half)] = (
            high * cosines - low * sines
        ).astype(BF16)
    for block in range(slots):
        span = slice(block * rows, (block + 1) * rows)
        row = pl.multiple_of((block ^ place) * rows, rows)
        cosines, sines = cos_ref[span, :], sin_ref[span, :]
        low, high = key_sum[span, :half] * KEY**-0.5, key_sum[span, half:] * KEY**-0.5
        out_ref[pl.ds(row, rows), pl.ds(key_col, half)] = (low * cosines + high * sines).astype(BF16)
        out_ref[pl.ds(row, rows), pl.ds(pl.multiple_of(key_col + half, half), half)] = (
            high * cosines - low * sines
        ).astype(BF16)
        out_ref[pl.ds(row, rows), pl.ds(value_col, VPAD)] = value_sum[span, :].astype(BF16)


def retain_back(grads, projected, normed, scale, query, key, value, place, log_decay, cosines, sines, heads):
    slots, rows = len(projected), projected[0].shape[0]
    seq = slots * rows
    columns = 2 * heads * (KEY + VPAD)
    table = pl.BlockSpec((seq, KEY // 2), lambda h, *_: (0, 0))

    def column(width):
        return pl.BlockSpec((seq, width), lambda h, *_: (0, h))

    return pl.pallas_call(
        partial(retain_back_kernel, slots, rows, heads),
        out_shape=jax.ShapeDtypeStruct((seq, columns), BF16),
        grid_spec=pltpu.PrefetchScalarGridSpec(
            num_scalar_prefetch=2,
            grid=(heads,),
            in_specs=[pl.BlockSpec((rows, VPAD), lambda h, *_: (0, h))] * slots
            + [slot_specs(rows, heads)[3]] * slots
            + [column(VPAD), column(128), column(KEY), column(KEY), column(VPAD), table, table],
            out_specs=pl.BlockSpec((seq, columns), lambda h, *_: (0, 0)),
            scratch_shapes=[
                pltpu.VMEM((rows, seq), F32),
                pltpu.VMEM((seq, VPAD), BF16),
                pltpu.VMEM((seq, KEY), F32),
                pltpu.VMEM((seq, VPAD), F32),
            ],
        ),
        compiler_params=pltpu.CompilerParams(vmem_limit_bytes=VMEM_LIMIT),
        cost_estimate=pl.CostEstimate(
            flops=heads * seq * seq * (3 * KEY + 2 * VPAD), bytes_accessed=heads * seq * 10000, transcendentals=heads * seq * 800
        ),
    )(place, log_decay, *grads, *projected, normed, scale, query, key, value, cosines, sines)


def per_device(
    dp_size,
    tensor_size,
    tokens,
    lengths,
    cotangent,
    gain_one,
    gain_two,
    w_query,
    w_key,
    w_value,
    w_gate,
    w_out,
    w_mgate,
    w_mup,
    w_down,
):
    rows, width = tokens.shape
    seq = rows * tensor_size
    heads = w_query.shape[1] // KEY
    units = w_mgate.shape[1]
    shard_rows = w_query.shape[0]
    half_rows = shard_rows // 2
    bits = dp_size.bit_length() - 1
    mine, place = lax.axis_index("dp"), lax.axis_index("tensor")
    inner = (place == 1) | (place == 2)
    odd = (mine & 1) == 1
    up_bits = list(range(1, bits))
    down_bits = up_bits[::-1]

    def swap_dp(array, mask):
        return lax.ppermute(array, "dp", [(i, i ^ mask) for i in range(dp_size)])

    def move_tensor(array, pairs):
        return lax.ppermute(array, "tensor", pairs)

    def swap_tensor(array, mask):
        return move_tensor(array, [(i, i ^ mask) for i in range(tensor_size)])

    across = [(1, 2), (2, 1)]
    outward = [(1, 0), (2, 3)]
    inward = [(0, 1), (3, 2)]

    def line_gather(own):
        beside = swap_tensor(own, 1)
        middle = move_tensor(own, across)
        far_ends = move_tensor(middle, outward)
        far_inner = move_tensor(beside, across)
        last = move_tensor(far_inner, outward)
        return own, beside, jnp.where(inner, far_inner, far_ends), jnp.where(inner, middle, last)

    def line_scatter(part):
        third, second = part(3), part(2)
        from_ends = move_tensor(third.astype(BF16), inward)
        from_ends_two = move_tensor(second.astype(BF16), inward)
        second_sum = (second + from_ends.astype(F32)).astype(BF16)
        third_sum = (third + from_ends_two.astype(F32)).astype(BF16)
        first = part(1) + move_tensor(second_sum, across).astype(F32)
        beside = swap_tensor(first.astype(BF16), 1)
        middle = move_tensor(third_sum, across)
        return part(0) + middle.astype(F32) + beside.astype(F32)

    def gather_half(piece, order):
        pieces = [piece]
        for bit in order:
            pieces = pieces + [swap_dp(p, 1 << bit) for p in pieces]
        return pieces

    def scatter_half(low, high, order):
        for bit in order[::-1]:
            total = low + swap_dp(high.astype(BF16), 1 << bit).astype(F32)
            middle = total.shape[-2] // 2
            low, high = total[..., :middle, :], total[..., middle:, :]
        return total

    blocks = [
        (chip << 1 | core, part)
        for core in range(2)
        for part, order in ((0, up_bits), (1, down_bits))
        for chip in [sum((i >> j & 1) << (b - 1) for j, b in enumerate(order)) for i in range(dp_size // 2)]
    ]

    def to_relative(array):
        return jnp.concatenate(
            [
                lax.dynamic_slice_in_dim(array, (mine ^ mask) * shard_rows + part * half_rows, half_rows, -1)
                for mask, part in blocks
            ],
            -1,
        )

    def to_global(array):
        found = []
        for shard in range(dp_size):
            mask = mine ^ shard
            for part, order in ((0, up_bits), (1, down_bits)):
                chip = sum((mask >> b & 1) << j for j, b in enumerate(order))
                index = (mask & 1) * dp_size + part * (dp_size // 2) + chip
                found.append(lax.dynamic_slice_in_dim(array, index * half_rows, half_rows, -1))
        return jnp.concatenate(found, -1)

    def pad_heads(array):
        split = array.reshape(shard_rows, heads, VAL)
        return jnp.pad(split, ((0, 0), (0, 0), (0, VPAD - VAL))).reshape(shard_rows, heads * VPAD)

    def cut_heads(array):
        return array.reshape(shard_rows, heads, VPAD)[:, :, :VAL].reshape(shard_rows, heads * VAL)

    first_row = place * rows
    valid = (first_row + jnp.arange(rows, dtype=jnp.int32) < lengths[0])[:, None]
    head_ids = (place * heads + jnp.arange(heads, dtype=jnp.int32)).astype(F32)
    log_decay = jnp.log(1.0 - jnp.exp2(-5.0 - head_ids))
    place_arg = place.astype(jnp.int32).reshape(1)
    freqs = 10000.0 ** (-jnp.arange(KEY // 2, dtype=F32) / (KEY // 2))
    angles = jnp.arange(seq, dtype=F32)[:, None] * freqs[None, :]
    cosines, sines = jnp.cos(angles), jnp.sin(angles)

    gain_first, gain_second = to_relative(gain_one), to_relative(gain_two)
    features = to_relative(tokens).astype(F32)
    normed_one, inverse_one = norm_parts(features)
    first_slots = line_gather((normed_one * gain_first).astype(BF16))

    local_one = jnp.concatenate(
        [w_query.astype(BF16), w_key.astype(BF16), pad_heads(w_value.astype(BF16)), pad_heads(w_gate.astype(BF16))], -1
    )

    def gather_weight(local):
        own = gather_half(local[:half_rows], up_bits) + gather_half(local[half_rows:], down_bits)
        other = [swap_dp(p, 1) for p in own]
        return jnp.concatenate(own + other, 0)

    proj_low = gather_weight(local_one)
    out_low = gather_weight(pad_heads(w_out.astype(BF16)))

    local_two = jnp.concatenate([w_mgate.astype(BF16), w_mup.astype(BF16), w_down.astype(BF16)], -1)

    def pair(dp_index, tensor_index):
        return dp_index * tensor_size + tensor_index

    top = tensor_size - 1
    to_even = [(pair(m | 1, t), pair(m, t)) for m in range(0, dp_size, 2) for t in range(tensor_size)]
    to_odd = [(pair(m, t), pair(m | 1, t ^ top)) for m in range(0, dp_size, 2) for t in range(tensor_size)]
    odd_turn = [(pair(m | 1, t), pair(m | 1, t ^ top)) for m in range(0, dp_size, 2) for t in range(tensor_size)]
    both = ("dp", "tensor")
    from_core = lax.ppermute(local_two, both, to_even + to_odd)
    turned = lax.ppermute(local_two, both, odd_turn)
    pair_local = jnp.stack([jnp.where(odd, turned, local_two), from_core])
    mlp_pieces = gather_half(pair_local[:, :half_rows], up_bits) + gather_half(pair_local[:, half_rows:], down_bits)
    mgate_low, mup_low, down_low = (
        jnp.concatenate([p[:, :, i * units : (i + 1) * units] for p in mlp_pieces], 1).reshape(width, units)
        for i in range(3)
    )

    def turn_cores(array):
        return jnp.concatenate([array[:, width // 2 :], array[:, : width // 2]], 1)

    def pair_gather(own):
        chips = jnp.concatenate([own, swap_tensor(own, 1)], 0)
        return jnp.concatenate([chips, turn_cores(swap_dp(chips, 1))], 0)

    def pair_scatter(part):
        core = turn_cores(swap_dp(part(1).astype(BF16), 1))
        total = part(0) + core.astype(F32)
        beside = swap_tensor(total[rows:].astype(BF16), 1)
        return total[:rows] + beside.astype(F32)

    grad_final = jnp.where(valid, to_relative(cotangent).astype(F32), 0.0)
    grad_mlp_rows = pair_gather(grad_final.astype(BF16))

    projected = [times_plain(slot, proj_low).astype(BF16) for slot in first_slots]
    query, key, value, normed_head, scale_head, mixed = retain(
        projected, place_arg, log_decay, cosines, sines, heads
    )
    middle = features + line_scatter(lambda s: times_right(mixed[s * rows : (s + 1) * rows], out_low))

    normed_two, inverse_two = norm_parts(middle)
    rows_two = pair_gather((normed_two * gain_second).astype(BF16))
    grad_hidden = times_plain(grad_mlp_rows, down_low)
    mgate_pre = times_plain(rows_two, mgate_low)
    mup_pre = times_plain(rows_two, mup_low)
    below = 0.5 * lax.erfc(-mgate_pre * (0.5**0.5))
    density = jnp.exp(-0.5 * mgate_pre * mgate_pre) * 0.3989422804014327
    hidden = (mgate_pre * below * mup_pre).astype(BF16)
    grad_mgate_low = (grad_hidden * mup_pre * (below + mgate_pre * density)).astype(BF16)
    grad_mup_low = (grad_hidden * mgate_pre * below).astype(BF16)

    grad_second = pair_scatter(
        lambda c: times_right(grad_mgate_low[2 * c * rows : 2 * (c + 1) * rows], mgate_low)
        + times_right(grad_mup_low[2 * c * rows : 2 * (c + 1) * rows], mup_low)
    )
    grad_middle = grad_final + norm_back(normed_two, inverse_two, grad_second, gain_second)
    grad_gain_two = jnp.sum(grad_second * normed_two, 0)

    attn_slots = line_gather(grad_middle.astype(BF16))

    final = middle + pair_scatter(lambda c: times_right(hidden[2 * c * rows : 2 * (c + 1) * rows], down_low))
    output = to_global(jnp.where(valid, final, 0.0).astype(BF16))

    def mlp_grad(left, right):
        left = left.reshape(left.shape[0], 2, 2, 2, width // 8)

        def group(part, end):
            return jnp.stack([times_left(left[:, core, part, end], right) for core in range(2)])

        total = jnp.concatenate(
            [
                scatter_half(group(0, 0), group(0, 1), up_bits),
                scatter_half(group(1, 0), group(1, 1), down_bits),
            ],
            1,
        )
        low = total.astype(BF16)
        core = lax.ppermute(low[1], both, [(b, a) for a, b in to_even + to_odd])
        turn = lax.ppermute(low[0], both, [(b, a) for a, b in odd_turn])
        return jnp.where(odd, turn.astype(F32), total[0]) + core.astype(F32)

    sum_down = mlp_grad(grad_mlp_rows, hidden)
    sum_mgate = mlp_grad(rows_two, grad_mgate_low)
    sum_mup = mlp_grad(rows_two, grad_mup_low)

    grad_mixed = [times_plain(slot, out_low).astype(BF16) for slot in attn_slots]
    grad_proj = retain_back(
        grad_mixed, projected, normed_head, scale_head, query, key, value, place_arg, log_decay, cosines, sines, heads
    )

    def attn_grad(left, right):
        other = swap_dp(times_left(left[:, width // 2 :], right).astype(BF16), 1)
        total = times_left(left[:, : width // 2], right) + other.astype(F32)
        quarter = width // 8
        return jnp.concatenate(
            [
                scatter_half(total[:quarter], total[quarter : 2 * quarter], up_bits),
                scatter_half(total[2 * quarter : 3 * quarter], total[3 * quarter :], down_bits),
            ],
            0,
        )

    sum_out = cut_heads(attn_grad(jnp.concatenate(attn_slots, 0), mixed))
    totals = [times_right(grad_proj[s * rows : (s + 1) * rows], proj_low) for s in range(tensor_size)]
    gain_one_parts = sum(jnp.sum(t * a.astype(F32), 0) for t, a in zip(totals, first_slots)) / gain_first
    grad_first = line_scatter(lambda s: totals[s])
    grad_tokens = grad_middle + norm_back(normed_one, inverse_one, grad_first, gain_first)
    grad_tokens = to_global(grad_tokens.astype(BF16))

    sum_proj = attn_grad(jnp.concatenate(first_slots, 0), grad_proj)
    cuts = [heads * KEY, 2 * heads * KEY, 2 * heads * KEY + heads * VPAD]
    sum_query, sum_key, sum_value, sum_gate = jnp.split(sum_proj, cuts, -1)

    gains = to_global(jnp.stack([gain_one_parts, grad_gain_two]))
    gains = gains + swap_tensor(gains, 1)
    gains = gains + swap_tensor(gains, 2)
    for bit in range(bits):
        gains = gains + swap_dp(gains, 1 << bit)
    return (
        output,
        grad_tokens,
        gains[0],
        gains[1],
        sum_query,
        sum_key,
        cut_heads(sum_value),
        cut_heads(sum_gate),
        sum_out,
        sum_mgate,
        sum_mup,
        sum_down,
    )


def solution(mesh):
    rows = P(("dp", "tensor"), None)
    block = P("dp", "tensor")
    return jax.shard_map(
        partial(per_device, mesh.shape["dp"], mesh.shape["tensor"]),
        mesh=mesh,
        in_specs=(rows, P("dp"), rows, P(), P()) + (block,) * 8,
        out_specs=(rows, rows, P(), P()) + (block,) * 8,
        check_vma=False,
    )
```

time: 1640 us -> 1050 us (0.64)
  waiting for transfers between devices: 1180 us -> 441 us
  starting transfers between devices: 1.75 us -> 122 us
  local copies, waits for them, and re-layouts: 56.6 us -> 150 us
  blocking collectives: 41.1 us -> 0 us
  Pallas kernels: 0 us -> 26.5 us
  matrix products: 238 us -> 212 us
    reduce_scatter x12 -> x0, waiting for transfers between devices: 734 us -> none  [the longest x1 145 us: per_device(): lax.psum_scatter(total + times_right(grad_gate_low, gate_low), 'tensor',...]
    all_gather x12 -> x0, waiting for transfers between devices: 444 us -> none  [the longest x1 82.9 us: per_device(): rows_two = lax.all_gather(second_norm, 'tensor', axis=0, tiled=True)]
    ppermute x0 -> x97, waiting for transfers between devices: none -> 441 us  [the longest x26 237 us: move_tensor(): return lax.ppermute(array, 'tensor', pairs)]
    ppermute x0 -> x97, starting transfers between devices: none -> 122 us  [the longest x26 58.1 us: move_tensor(): return lax.ppermute(array, 'tensor', pairs)]
    unnamed x129 -> x338, local copies, waits for them, and re-layouts: 19.1 us -> 74.6 us
    psum x1 -> x0, blocking collectives: 41.1 us -> none  [per_device(): lax.psum((grad_gain_one_here, grad_gain_two_here), ('dp', 'tensor'))]
    dot_general x18 -> x11, matrix products: 124 us -> 87 us  [times_plain(): return jnp.dot(left, right, preferred_element_type=F32)]
    slice x0 -> x26, local copies, waits for them, and re-layouts: none -> 32.5 us  [the longest x2 18.5 us: group(): left[:, core, part, end]]
  transfers between devices with their start and end apart: 24 -> 97, of which waited for: 21 -> 40; matrix products, arithmetic and copies ran while one was open for 19% -> 32% of each run, Pallas kernels for 0% -> 1%
where the time goes in v1:
time: 1050 us; the launch traced here: 1040 us
  waiting for transfers between devices  441 us (42%)
  matrix products  212 us (20%)
  local copies, waits for them, and re-layouts  150 us (14%)
  starting transfers between devices  122 us (12%)
  other arithmetic  79.7 us (8%)
  Pallas kernels  26.5 us (3%)
    ppermute x26, waiting for transfers between devices, move_tensor(): return lax.ppermute(array, 'tensor', pairs)  237 us
    ppermute x63, waiting for transfers between devices, swap_dp(): return lax.ppermute(array, 'dp', [(i, i ^ mask) for i in range(dp_size)])  204 us
    dot_general x11, matrix products, times_plain(): return jnp.dot(left, right, preferred_element_type=F32)  87 us
    dot_general x14, matrix products, times_right(): lax.dot_general(left, right, (((1,), (1,)), ((), ())), preferred_element_...  78.1 us
    unnamed x338, local copies, waits for them, and re-layouts  74.6 us
    ppermute x26, starting transfers between devices, move_tensor(): return lax.ppermute(array, 'tensor', pairs)  58.1 us
    ppermute x63, starting transfers between devices, swap_dp(): return lax.ppermute(array, 'dp', [(i, i ^ mask) for i in range(dp_size)])  54.1 us
    dot_general x28, matrix products, times_left(): lax.dot_general(left, right, (((0,), (0,)), ((), ())), preferred_element_...  46.8 us
  transfers between devices with their start and end apart: 97, of which 40 were waited for; matrix products, arithmetic and copies ran while one was open for 32% of the time, Pallas kernels for 1%

profile of v1, /device:TPU:0, one launch (start us, length us, event | category | flops | bytes accessed | tf_op | source)
XLA Modules:
  0.0 1035.5 jit_solution(10226615823246306468)
XLA Ops:
  76.9 12.0 %collective-permute-done.3 = bf16[128,3072]{0,1:T(8,128)(2,1)S(1)} collective-permute-done((bf16[128,3072]{0,1:T(8,128)(2,1)S(1)}, bf16[128,3072]{0,1:T(8,128)(2,1)S(1)}, u32[]{:S(2)}, u32[]{:S(2)}) %collective-permute-start.3) | collective-permute-done | bytes 786464 | tf_op jit(solution)/shard_map/ppermute | solution.py:259
  88.9 15.6 %collective-permute-done.2 = bf16[128,3072]{0,1:T(8,128)(2,1)S(1)} collective-permute-done((bf16[128,3072]{0,1:T(8,128)(2,1)}, bf16[128,3072]{0,1:T(8,128)(2,1)S(1)}, u32[]{:S(2)}, u32[]{:S(2)}) %collective-permute-start.2) | collective-permute-done | bytes 786464 | tf_op jit(solution)/shard_map/ppermute | solution.py:259
  109.9 12.9 %collective-permute-done.5 = bf16[128,3072]{0,1:T(8,128)(2,1)S(1)} collective-permute-done((bf16[128,3072]{0,1:T(8,128)(2,1)S(1)}, bf16[128,3072]{0,1:T(8,128)(2,1)S(1)}, u32[]{:S(2)}, u32[]{:S(2)}) %collective-permute-start.5) | collective-permute-done | bytes 786464 | tf_op jit(solution)/shard_map/ppermute | solution.py:259
  134.4 48.9 %collective-permute-done.17 = bf16[256,2048]{1,0:T(8,128)(2,1)S(1)} collective-permute-done((bf16[256,2048]{1,0:T(8,128)(2,1)S(1)}, bf16[256,2048]{1,0:T(8,128)(2,1)S(1)}, u32[]{:S(2)}, u32[]{:S(2)}) %collective-permute-start.17) | collective-permute-done | bytes 1048608 | tf_op jit(solution)/shard_map/ppermute | solution.py:262
  192.4 14.0 %convolution_convert_fusion.2.refs_2_.refs_6_.refs_10_.refs_14_ = bf16[256,3072]{1,0:T(8,128)(2,1)} fusion(bf16[256,2048]{1,0:T(8,128)(2,1)S(1)} %broadcast_select_fusion.3, bf16[2048,3072]{0,1:T(8,128)(2,1)} %constant_dynamic-update-slice_fusion.17), kind=kOutput, calls=%fused_computation.27 | convolution fusion | flops 3222011904 | bytes 15204352 | tf_op jit(solution)/shard_map/dot_general | solution.py:21
  206.4 14.0 %convolution_convert_fusion.3.refs_1_.refs_5_.refs_9_.refs_13_ = bf16[256,3072]{1,0:T(8,128)(2,1)} fusion(bf16[256,2048]{1,0:T(8,128)(2,1)S(1)} %collective-permute-done.14, bf16[2048,3072]{0,1:T(8,128)(2,1)} %constant_dynamic-update-slice_fusion.17), kind=kOutput, calls=%fused_computation.28 | convolution fusion | flops 3222011904 | bytes 15204352 | tf_op jit(solution)/shard_map/dot_general | solution.py:21
  220.4 8.2 convolution_convert_fusion.4.refs_0_.refs_4_.refs_8_.refs_12_
  234.5 14.4 %convolution_convert_fusion.1.refs_3_.refs_7_.refs_11_.refs_15_ = bf16[256,3072]{1,0:T(8,128)(2,1)} fusion(bf16[256,2048]{1,0:T(8,128)(2,1)S(1)} %broadcast_select_fusion.2, bf16[2048,3072]{0,1:T(8,128)(2,1)} %constant_dynamic-update-slice_fusion.17), kind=kOutput, calls=%fused_computation.26 | convolution fusion | flops 3222011904 | bytes 15204352 | tf_op jit(solution)/shard_map/dot_general | solution.py:21
  248.9 10.5 %shard_map.220 = (bf16[1024,512]{1,0:T(8,128)(2,1)S(1)}, bf16[1024,512]{1,0:T(8,128)(2,1)S(1)}, bf16[1024,1024]{1,0:T(8,128)(2,1)}, bf16[1024,1024]{1,0:T(8,128)...) custom-call(s32[1]{0:T(128)} %bitcast.1.place_ref, f32[2]{0:T(128)S(1)} %subtract_log_fusion.decay_ref, ...), custom_call_target="tpu_custom_call" | custom-call | flops 1610612736 | bytes 18432000 | tf_op jit(solution)/shard_map/pallas_call | solution.py:115
  270.2 17.6 %collective-permute-done.33 = bf16[256,2048]{1,0:T(8,128)(2,1)} collective-permute-done((bf16[256,2048]{1,0:T(8,128)(2,1)}, bf16[256,2048]{1,0:T(8,128)(2,1)}, u32[]{:S(2)}, u32[]{:S(2)}) %collective-permute-start.33) | collective-permute-done | bytes 1048608 | tf_op jit(solution)/shard_map/ppermute | solution.py:262
  305.4 12.4 %collective-permute-done.35 = bf16[256,2048]{1,0:T(8,128)(2,1)} collective-permute-done((bf16[256,2048]{1,0:T(8,128)(2,1)}, bf16[256,2048]{1,0:T(8,128)(2,1)}, u32[]{:S(2)}, u32[]{:S(2)}) %collective-permute-start.35) | collective-permute-done | bytes 1048608 | tf_op jit(solution)/shard_map/ppermute | solution.py:262
  322.9 9.9 collective-permute-done.42
  338.0 26.0 %collective-permute-done.45 = bf16[2,128,2592]{1,2,0:T(8,128)(2,1)} collective-permute-done((bf16[2,128,2592]{1,2,0:T(8,128)(2,1)}, bf16[2,128,2592]{1,2,0:T(8,128)(2,1)}, u32[]{:S(2)}, u32[]{:S(2)}) %collective-permute-start.45) | collective-permute-done | bytes 1327136 | tf_op jit(solution)/shard_map/ppermute | solution.py:259
  373.7 10.4 %maximum_maximum_fusion.1 = bf16[1024,2048]{1,0:T(8,128)(2,1)} fusion(bf16[512,1024]{1,0:T(8,128)(2,1)S(1)} %get-tuple-element.85, bf16[512,1024]{1,0:T(8,128)(2,1)S(1)} %get-tuple-element.84, bf16[256,2048]{1,0:T(8,128)(2,1)} %collective-permute-done.50, bf16[256,2048]{1,0:T(8,128)(2,1)} %fusion.37), kind=kLoop, calls=%fused_computation.19 | loop fusion | flops 16777216 | bytes 8388608 | tf_op jit(solution)/shard_map/concatenate | solution.py:386
  384.1 7.8 reshape.387
  391.9 11.3 %fusion.127 = (bf16[1024,1,1,1,256]{4,3,2,1,0:T(2,128)(2,1)}, bf16[1024,1,1,1,256]{4,3,2,1,0:T(2,128)(2,1)}, bf16[1024,1,1,1,256]{4,3,2,1,0:T(2,128)(2,1)}, bf16...) fusion(bf16[1024,2,2,2,256]{4,3,2,1,0:T(2,128)(2,1)} %reshape.387), kind=kLoop, calls=%fused_computation.525 | loop fusion | bytes 8388608 | tf_op jit(solution)/shard_map/slice | solution.py:430
  421.7 9.3 collective-permute-done.38
  455.5 6.4 copy.32
  461.9 8.9 fusion.146
  473.0 9.4 maximum_maximum_fusion
  482.3 7.8 reshape.386
  490.1 6.9 fusion.145
  497.1 7.2 fusion.128
  504.3 15.5 %fusion.7 = (bf16[1024,864]{0,1:T(8,128)(2,1)}, f32[1024,864]{0,1:T(8,128)}, f32[1024,864]{0,1:T(8,128)}) fusion(f32[1024,864]{0,1:T(8,128)S(1)} %copy-done.45, f32[1024,864]{0,1:T(8,128)S(1)} %fusion.145, bf16[1024,2048]{1,0:T(8,128)(2,1)S(1)} %copy-done.11, bf16[2048,864]{1,0:T(8,128)(2,1)S(1)} %bitcast.263), kind=kOutput, calls=%fused_computation.37 | convolution fusion | flops 3686694912 | bytes 23658496 | tf_op jit(solution)/shard_map/dot_general | solution.py:21
  581.3 15.3 %collective-permute-done.87 = bf16[2,256,864]{1,2,0:T(8,128)(2,1)} collective-permute-done((bf16[2,256,864]{1,2,0:T(8,128)(2,1)S(1)}, bf16[2,256,864]{1,2,0:T(8,128)(2,1)}, u32[]{:S(2)}, u32[]{:S(2)}) %collective-permute-start.87) | collective-permute-done | bytes 884768 | tf_op jit(solution)/shard_map/ppermute | solution.py:259
  603.0 12.0 %collective-permute-done.81 = bf16[2,256,864]{1,2,0:T(8,128)(2,1)S(1)} collective-permute-done((bf16[2,256,864]{1,2,0:T(8,128)(2,1)S(1)}, bf16[2,256,864]{1,2,0:T(8,128)(2,1)S(1)}, u32[]{:S(2)}, u32[]{:S(2)}) %collective-permute-start.81) | collective-permute-done | bytes 884768 | tf_op jit(solution)/shard_map/ppermute | solution.py:259
  620.6 7.7 collective-permute-done.94
  631.0 6.8 collective-permute-done.88
  640.1 6.5 collective-permute-done.82
  661.8 9.8 collective-permute-start.49
  672.6 15.7 %collective-permute-done.53 = bf16[256,2048]{1,0:T(8,128)(2,1)S(1)} collective-permute-done((bf16[256,2048]{1,0:T(8,128)(2,1)S(1)}, bf16[256,2048]{1,0:T(8,128)(2,1)S(1)}, u32[]{:S(2)}, u32[]{:S(2)}) %collective-permute-start.53) | collective-permute-done | bytes 1048608 | tf_op jit(solution)/shard_map/ppermute | solution.py:262
  691.5 23.9 %collective-permute-done.49 = bf16[256,2048]{1,0:T(8,128)(2,1)S(1)} collective-permute-done((bf16[256,2048]{1,0:T(8,128)(2,1)S(1)}, bf16[256,2048]{1,0:T(8,128)(2,1)S(1)}, u32[]{:S(2)}, u32[]{:S(2)}) %collective-permute-start.49) | collective-permute-done | bytes 1048608 | tf_op jit(solution)/shard_map/ppermute | solution.py:262
  722.1 21.3 %collective-permute-done.54 = bf16[256,2048]{1,0:T(8,128)(2,1)S(1)} collective-permute-done((bf16[256,2048]{1,0:T(8,128)(2,1)S(1)}, bf16[256,2048]{1,0:T(8,128)(2,1)S(1)}, u32[]{:S(2)}, u32[]{:S(2)}) %collective-permute-start.54) | collective-permute-done | bytes 1048608 | tf_op jit(solution)/shard_map/ppermute | solution.py:262
  749.8 22.8 %collective-permute-done.57 = bf16[256,2048]{1,0:T(8,128)(2,1)S(1)} collective-permute-done((bf16[256,2048]{1,0:T(8,128)(2,1)S(1)}, bf16[256,2048]{1,0:T(8,128)(2,1)S(1)}, u32[]{:S(2)}, u32[]{:S(2)}) %collective-permute-start.57) | collective-permute-done | bytes 1048608 | tf_op jit(solution)/shard_map/ppermute | solution.py:262
  774.0 21.1 %collective-permute-done.58 = bf16[256,2048]{1,0:T(8,128)(2,1)S(1)} collective-permute-done((bf16[256,2048]{1,0:T(8,128)(2,1)S(1)}, bf16[256,2048]{1,0:T(8,128)(2,1)S(1)}, u32[]{:S(2)}, u32[]{:S(2)}) %collective-permute-start.58) | collective-permute-done | bytes 1048608 | tf_op jit(solution)/shard_map/ppermute | solution.py:262
  796.4 16.0 %shard_map.221 = bf16[1024,3072]{1,0:T(8,128)(2,1)} custom-call(s32[1]{0:T(128)} %bitcast.1.place_ref, f32[2]{0:T(128)S(1)} %subtract_log_fusion.decay_ref, bf16[256,1024]{1,0:T(8,128)(2,1)S(1)} %convolution_convert_fusion.9.refs_0_, bf16[256,1024]{1,0:T(8,128)(2,1)S(1)} %convolution_convert_fusion.8.refs_1_, ...), custom_call_target="tpu_custom_call" | custom-call | flops 3758096384 | bytes 20480000 | tf_op jit(solution)/shard_map/pallas_call | solution.py:204
  812.4 6.9 multiply_reduce_fusion.1
  825.5 16.6 %collective-permute-done.61 = bf16[256,2048]{1,0:T(8,128)(2,1)S(1)} collective-permute-done((bf16[256,2048]{1,0:T(8,128)(2,1)S(1)}, bf16[256,2048]{1,0:T(8,128)(2,1)S(1)}, u32[]{:S(2)}, u32[]{:S(2)}) %collective-permute-start.61) | collective-permute-done | bytes 1048608 | tf_op jit(solution)/shard_map/ppermute | solution.py:262
  842.1 9.3 multiply_reduce_fusion.2
  855.8 8.9 convolution_convert_fusion
  879.2 9.3 multiply_reduce_fusion.3
  888.5 12.7 %collective-permute-start.63 = (bf16[256,2048]{1,0:T(8,128)(2,1)}, bf16[256,2048]{1,0:T(8,128)(2,1)}, u32[]{:S(2)}, u32[]{:S(2)}) collective-permute-start(bf16[256,2048]{1,0:T(8,128)(2,1)} %get-tuple-element.73), channel_id=1, source_target_pairs={{0,1},{1,0},{2,3},{3,2},{4,5},{5,4},{6,7},{7,6},{8,9},{9,8},{10,11... | collective-permute-start | bytes 3145736 | tf_op jit(solution)/shard_map/ppermute | solution.py:262
  911.9 12.3 %collective-permute-done.63 = bf16[256,2048]{1,0:T(8,128)(2,1)} collective-permute-done((bf16[256,2048]{1,0:T(8,128)(2,1)}, bf16[256,2048]{1,0:T(8,128)(2,1)}, u32[]{:S(2)}, u32[]{:S(2)}) %collective-permute-start.63) | collective-permute-done | bytes 1048608 | tf_op jit(solution)/shard_map/ppermute | solution.py:262
  924.2 10.9 %fusion.123 = (f32[256]{0:T(256)S(1)}, f32[256]{0:T(256)S(1)}, f32[256,2048]{1,0:T(8,128)}, f32[2048]{0:T(1024)S(1)}) fusion(f32[256]{0:T(256)S(1)} %copy-done.84, f32[256]{0:T(256)S(1)} %copy-done.82, bf16[256,2048]{1,0:T(8,128)(2,1)S(1)} %copy-done.10, f32[2048]{0:T(1024)S(1)} %copy-done.86, bf16[256,2048]{1,0:T(8,128)(2,1)} %collective-permute-done.63, ...), kind=kOutput, calls=%fused_computation.522 | convolution fusion | flops 3229611520 | bytes 19419136 | tf_op jit(solution)/shard_map/dot_general | solution.py:29
  938.3 13.2 %fusion.138 = (bf16[1024,3072]{1,0:T(8,128)(2,1)}, f32[1024,3072]{1,0:T(8,128)S(1)}) fusion(bf16[1024,3072]{1,0:T(8,128)(2,1)} %collective-permute-done.69, bf16[1024,3072]{1,0:T(8,128)(2,1)} %shard_map.221, bf16[1024,2048]{1,0:T(8,128)(2,1)S(1)} %copy-done.25), kind=kOutput, calls=%fused_computation.536 | convolution fusion | flops 6451888128 | bytes 33554432 | tf_op jit(solution)/shard_map/dot_general | solution.py:25
  962.0 26.2 %collective-permute-done.70 = bf16[256,3072]{1,0:T(8,128)(2,1)S(1)} collective-permute-done((bf16[256,3072]{1,0:T(8,128)(2,1)S(1)}, bf16[256,3072]{1,0:T(8,128)(2,1)S(1)}, u32[]{:S(2)}, u32[]{:S(2)}) %collective-permute-start.70) | collective-permute-done | bytes 1572896 | tf_op jit(solution)/shard_map/ppermute | solution.py:259
  995.8 14.7 %collective-permute-done.67 = f32[2,2048]{1,0:T(2,128)S(1)} collective-permute-done((f32[2,2048]{1,0:T(2,128)S(1)}, f32[2,2048]{1,0:T(2,128)S(1)}, u32[]{:S(2)}, u32[]{:S(2)}) %collective-permute-start.67) | collective-permute-done | bytes 16416 | tf_op jit(solution)/shard_map/ppermute | solution.py:259
  1017.1 12.4 %collective-permute-done.73 = bf16[128,3072]{1,0:T(8,128)(2,1)S(1)} collective-permute-done((bf16[128,3072]{1,0:T(8,128)(2,1)S(1)}, bf16[128,3072]{1,0:T(8,128)(2,1)S(1)}, u32[]{:S(2)}, u32[]{:S(2)}) %collective-permute-start.73) | collective-permute-done | bytes 786464 | tf_op jit(solution)/shard_map/ppermute | solution.py:259
  (698 shorter events, 382.1 us)
Async XLA Ops:
  5.5 64.5 %collective-permute-start = (bf16[128,3072]{0,1:T(8,128)(2,1)}, bf16[128,3072]{0,1:T(8,128)(2,1)}, u32[]{:S(2)}, u32[]{:S(2)}) collective-permute-start(bf16[128,3072]{0,1:T(8,128)(2,1)} %get-tuple-element.92), channel_id=1, source_target_pairs={{0,8},{4,12},{8,0},{12,4},{16,24},{20,28},{24,16},{28,20},{1,9},{5... | collective-permute-start | bytes 2359304 | tf_op jit(solution)/shard_map/ppermute | solution.py:259
  8.4 65.0 %collective-permute-start.1 = (bf16[128,3072]{0,1:T(8,128)(2,1)}, bf16[128,3072]{0,1:T(8,128)(2,1)}, u32[]{:S(2)}, u32[]{:S(2)}) collective-permute-start(bf16[128,3072]{0,1:T(8,128)(2,1)} %get-tuple-element.92), channel_id=1, source_target_pairs={{0,16},{4,20},{8,24},{12,28},{16,0},{20,4},{24,8},{28,12},{1,17},{... | collective-permute-start | bytes 2359304 | tf_op jit(solution)/shard_map/ppermute | solution.py:259
  10.8 33.2 %collective-permute-start.19 = (bf16[128,1024]{0,1:T(8,128)(2,1)}, bf16[128,1024]{0,1:T(8,128)(2,1)}, u32[]{:S(2)}, u32[]{:S(2)}) collective-permute-start(bf16[128,1024]{0,1:T(8,128)(2,1)} %bitcast.7), channel_id=1, source_target_pairs={{0,8},{4,12},{8,0},{12,4},{16,24},{20,28},{24,16},{28,20},{1,9},{5... | collective-permute-start | bytes 786440 | tf_op jit(solution)/shard_map/ppermute | solution.py:259
  11.3 34.7 %collective-permute-start.20 = (bf16[128,1024]{0,1:T(8,128)(2,1)}, bf16[128,1024]{0,1:T(8,128)(2,1)}, u32[]{:S(2)}, u32[]{:S(2)}) collective-permute-start(bf16[128,1024]{0,1:T(8,128)(2,1)} %bitcast.7), channel_id=1, source_target_pairs={{0,16},{4,20},{8,24},{12,28},{16,0},{20,4},{24,8},{28,12},{1,17},{... | collective-permute-start | bytes 786440 | tf_op jit(solution)/shard_map/ppermute | solution.py:259
  11.3 38.2 %collective-permute-start.22 = (bf16[128,1024]{0,1:T(8,128)(2,1)S(1)}, bf16[128,1024]{0,1:T(8,128)(2,1)}, u32[]{:S(2)}, u32[]{:S(2)}) collective-permute-start(bf16[128,1024]{0,1:T(8,128)(2,1)S(1)} %bitcast.290), channel_id=1, source_target_pairs={{0,16},{4,20},{8,24},{12,28},{16,0},{20,4},{24,8},{28,12},{1,17},{... | collective-permute-start | bytes 786440 | tf_op jit(solution)/shard_map/ppermute | solution.py:259
  64.6 59.7 %collective-permute-start.14 = (bf16[256,2048]{1,0:T(8,128)(2,1)}, bf16[256,2048]{1,0:T(8,128)(2,1)S(1)}, u32[]{:S(2)}, u32[]{:S(2)}) collective-permute-start(bf16[256,2048]{1,0:T(8,128)(2,1)} %fusion.21), channel_id=1, source_target_pairs={{0,1},{1,0},{2,3},{3,2},{4,5},{5,4},{6,7},{7,6},{8,9},{9,8},{10,11... | collective-permute-start | bytes 3145736 | tf_op jit(solution)/shard_map/ppermute | solution.py:262
  67.0 58.0 %collective-permute-start.16 = (bf16[256,2048]{1,0:T(8,128)(2,1)S(1)}, bf16[256,2048]{1,0:T(8,128)(2,1)S(1)}, u32[]{:S(2)}, u32[]{:S(2)}) collective-permute-start(bf16[256,2048]{1,0:T(8,128)(2,1)S(1)} %copy-done.26), channel_id=1, source_target_pairs={{1,2},{2,1},{5,6},{6,5},{9,10},{10,9},{13,14},{14,13},{17,18},{18,... | collective-permute-start | bytes 3145736 | tf_op jit(solution)/shard_map/ppermute | solution.py:262
  70.0 34.5 %collective-permute-start.2 = (bf16[128,3072]{0,1:T(8,128)(2,1)}, bf16[128,3072]{0,1:T(8,128)(2,1)S(1)}, u32[]{:S(2)}, u32[]{:S(2)}) collective-permute-start(bf16[128,3072]{0,1:T(8,128)(2,1)} %collective-permute-done), channel_id=1, source_target_pairs={{0,16},{4,20},{8,24},{12,28},{16,0},{20,4},{24,8},{28,12},{1,17},{... | collective-permute-start | bytes 2359304 | tf_op jit(solution)/shard_map/ppermute | solution.py:259
  73.4 35.5 %collective-permute-start.4 = (bf16[128,3072]{0,1:T(8,128)(2,1)S(1)}, bf16[128,3072]{0,1:T(8,128)(2,1)S(1)}, u32[]{:S(2)}, u32[]{:S(2)}) collective-permute-start(bf16[128,3072]{0,1:T(8,128)(2,1)S(1)} %copy-done.71), channel_id=1, source_target_pairs={{0,8},{4,12},{8,0},{12,4},{16,24},{20,28},{24,16},{28,20},{1,9},{5... | collective-permute-start | bytes 2359304 | tf_op jit(solution)/shard_map/ppermute | solution.py:259
  88.9 34.9 %collective-permute-start.6 = (bf16[128,3072]{0,1:T(8,128)(2,1)}, bf16[128,3072]{0,1:T(8,128)(2,1)S(1)}, u32[]{:S(2)}, u32[]{:S(2)}) collective-permute-start(bf16[128,3072]{0,1:T(8,128)(2,1)} %get-tuple-element.92), channel_id=1, source_target_pairs={{0,4},{4,0},{8,12},{12,8},{16,20},{20,16},{24,28},{28,24},{1,5},{5... | collective-permute-start | bytes 2359304 | tf_op jit(solution)/shard_map/ppermute | solution.py:259
  123.8 61.3 %collective-permute-start.10 = (bf16[128,3072]{0,1:T(8,128)(2,1)S(1)}, bf16[128,3072]{0,1:T(8,128)(2,1)S(1)}, u32[]{:S(2)}, u32[]{:S(2)}) collective-permute-start(bf16[128,3072]{0,1:T(8,128)(2,1)S(1)} %copy-done.71), channel_id=1, source_target_pairs={{0,4},{4,0},{8,12},{12,8},{16,20},{20,16},{24,28},{28,24},{1,5},{5... | collective-permute-start | bytes 2359304 | tf_op jit(solution)/shard_map/ppermute | solution.py:259
  125.0 58.3 %collective-permute-start.17 = (bf16[256,2048]{1,0:T(8,128)(2,1)S(1)}, bf16[256,2048]{1,0:T(8,128)(2,1)S(1)}, u32[]{:S(2)}, u32[]{:S(2)}) collective-permute-start(bf16[256,2048]{1,0:T(8,128)(2,1)S(1)} %collective-permute-done.16), channel_id=1, source_target_pairs={{1,0},{2,3},{5,4},{6,7},{9,8},{10,11},{13,12},{14,15},{17,16},{18,... | collective-permute-start | bytes 3145736 | tf_op jit(solution)/shard_map/ppermute | solution.py:262
  127.3 169.8 %collective-permute-start.40 = (bf16[256,2592]{0,1:T(8,128)(2,1)}, bf16[256,2592]{0,1:T(8,128)(2,1)}, u32[]{:S(2)}, u32[]{:S(2)}) collective-permute-start(bf16[256,2592]{0,1:T(8,128)(2,1)} %pad_maximum_fusion.8), channel_id=1, source_target_pairs={{4,7},{5,6},{6,5},{7,4},{12,15},{13,14},{14,13},{15,12},{20,23},{2... | collective-permute-start | bytes 3981320 | tf_op jit(solution)/shard_map/ppermute | solution.py:373
  130.1 53.3 %collective-permute-start.9 = (bf16[128,3072]{0,1:T(8,128)(2,1)S(1)}, bf16[128,3072]{0,1:T(8,128)(2,1)S(1)}, u32[]{:S(2)}, u32[]{:S(2)}) collective-permute-start(bf16[128,3072]{0,1:T(8,128)(2,1)S(1)} %collective-permute-done.2), channel_id=1, source_target_pairs={{0,4},{4,0},{8,12},{12,8},{16,20},{20,16},{24,28},{28,24},{1,5},{5... | collective-permute-start | bytes 2359304 | tf_op jit(solution)/shard_map/ppermute | solution.py:259
  133.5 164.1 %collective-permute-start.41 = (bf16[256,2592]{0,1:T(8,128)(2,1)}, bf16[256,2592]{0,1:T(8,128)(2,1)}, u32[]{:S(2)}, u32[]{:S(2)}) collective-permute-start(bf16[256,2592]{0,1:T(8,128)(2,1)} %pad_maximum_fusion.8), channel_id=1, source_target_pairs={{4,0},{5,1},{6,2},{7,3},{12,8},{13,9},{14,10},{15,11},{20,16},{21,... | collective-permute-start | bytes 3981320 | tf_op jit(solution)/shard_map/ppermute | solution.py:372
  186.2 80.5 %collective-permute-start.50 = (bf16[256,2048]{1,0:T(8,128)(2,1)}, bf16[256,2048]{1,0:T(8,128)(2,1)}, u32[]{:S(2)}, u32[]{:S(2)}) collective-permute-start(bf16[256,2048]{1,0:T(8,128)(2,1)} %fusion.37), channel_id=1, source_target_pairs={{0,1},{1,0},{2,3},{3,2},{4,5},{5,4},{6,7},{7,6},{8,9},{9,8},{10,11... | collective-permute-start | bytes 3145736 | tf_op jit(solution)/shard_map/ppermute | solution.py:262
  188.9 45.5 %collective-permute-start.18 = (bf16[256,2048]{1,0:T(8,128)(2,1)S(1)}, bf16[256,2048]{1,0:T(8,128)(2,1)S(1)}, u32[]{:S(2)}, u32[]{:S(2)}) collective-permute-start(bf16[256,2048]{1,0:T(8,128)(2,1)S(1)} %collective-permute-done.15), channel_id=1, source_target_pairs={{1,0},{2,3},{5,4},{6,7},{9,8},{10,11},{13,12},{14,15},{17,16},{18,... | collective-permute-start | bytes 3145736 | tf_op jit(solution)/shard_map/ppermute | solution.py:262
  270.2 96.7 %collective-permute-start.51 = (bf16[512,2048]{1,0:T(8,128)(2,1)}, bf16[512,2048]{1,0:T(8,128)(2,1)}, u32[]{:S(2)}, u32[]{:S(2)}) collective-permute-start(bf16[512,2048]{1,0:T(8,128)(2,1)} %pad_maximum_fusion.6), channel_id=1, source_target_pairs={{0,4},{4,0},{8,12},{12,8},{16,20},{20,16},{24,28},{28,24},{1,5},{5... | collective-permute-start | bytes 6291464 | tf_op jit(solution)/shard_map/ppermute | solution.py:259
  301.6 31.2 %collective-permute-start.42 = (bf16[2,128,2592]{1,2,0:T(8,128)(2,1)}, bf16[2,128,2592]{1,2,0:T(8,128)(2,1)}, u32[]{:S(2)}, u32[]{:S(2)}) collective-permute-start(bf16[2,128,2592]{1,2,0:T(8,128)(2,1)} %get-tuple-element.68), channel_id=1, source_target_pairs={{0,8},{4,12},{8,0},{12,4},{16,24},{20,28},{24,16},{28,20},{1,9},{5... | collective-permute-start | bytes 3981320 | tf_op jit(solution)/shard_map/ppermute | solution.py:259
  303.1 33.3 %collective-permute-start.43 = (bf16[2,128,2592]{1,2,0:T(8,128)(2,1)}, bf16[2,128,2592]{1,2,0:T(8,128)(2,1)}, u32[]{:S(2)}, u32[]{:S(2)}) collective-permute-start(bf16[2,128,2592]{1,2,0:T(8,128)(2,1)} %get-tuple-element.68), channel_id=1, source_target_pairs={{0,16},{4,20},{8,24},{12,28},{16,0},{20,4},{24,8},{28,12},{1,17},{... | collective-permute-start | bytes 3981320 | tf_op jit(solution)/shard_map/ppermute | solution.py:259
  304.7 59.3 %collective-permute-start.45 = (bf16[2,128,2592]{1,2,0:T(8,128)(2,1)}, bf16[2,128,2592]{1,2,0:T(8,128)(2,1)}, u32[]{:S(2)}, u32[]{:S(2)}) collective-permute-start(bf16[2,128,2592]{1,2,0:T(8,128)(2,1)} %get-tuple-element.67), channel_id=1, source_target_pairs={{0,16},{4,20},{8,24},{12,28},{16,0},{20,4},{24,8},{28,12},{1,17},{... | collective-permute-start | bytes 3981320 | tf_op jit(solution)/shard_map/ppermute | solution.py:259
  320.0 50.3 %collective-permute-start.36 = (bf16[256,2048]{1,0:T(8,128)(2,1)S(1)}, bf16[256,2048]{1,0:T(8,128)(2,1)S(1)}, u32[]{:S(2)}, u32[]{:S(2)}) collective-permute-start(bf16[256,2048]{1,0:T(8,128)(2,1)S(1)} %add_convert_fusion.4), channel_id=1, source_target_pairs={{1,2},{2,1},{5,6},{6,5},{9,10},{10,9},{13,14},{14,13},{17,18},{18,... | collective-permute-start | bytes 3145736 | tf_op jit(solution)/shard_map/ppermute | solution.py:262
  332.8 105.9 %collective-permute-start.46 = (bf16[2,128,2592]{1,2,0:T(8,128)(2,1)}, bf16[2,128,2592]{1,2,0:T(8,128)(2,1)}, u32[]{:S(2)}, u32[]{:S(2)}) collective-permute-start(bf16[2,128,2592]{1,2,0:T(8,128)(2,1)} %get-tuple-element.67), channel_id=1, source_target_pairs={{0,8},{4,12},{8,0},{12,4},{16,24},{20,28},{24,16},{28,20},{1,9},{5... | collective-permute-start | bytes 3981320 | tf_op jit(solution)/shard_map/ppermute | solution.py:259
  336.5 76.9 %collective-permute-start.44 = (bf16[2,128,2592]{1,2,0:T(8,128)(2,1)}, bf16[2,128,2592]{1,2,0:T(8,128)(2,1)}, u32[]{:S(2)}, u32[]{:S(2)}) collective-permute-start(bf16[2,128,2592]{1,2,0:T(8,128)(2,1)} %collective-permute-done.42), channel_id=1, source_target_pairs={{0,16},{4,20},{8,24},{12,28},{16,0},{20,4},{24,8},{28,12},{1,17},{... | collective-permute-start | bytes 3981320 | tf_op jit(solution)/shard_map/ppermute | solution.py:259
  364.0 77.2 %collective-permute-start.47 = (bf16[2,128,2592]{1,2,0:T(8,128)(2,1)}, bf16[2,128,2592]{1,2,0:T(8,128)(2,1)}, u32[]{:S(2)}, u32[]{:S(2)}) collective-permute-start(bf16[2,128,2592]{1,2,0:T(8,128)(2,1)} %collective-permute-done.45), channel_id=1, source_target_pairs={{0,8},{4,12},{8,0},{12,4},{16,24},{20,28},{24,16},{28,20},{1,9},{5... | collective-permute-start | bytes 3981320 | tf_op jit(solution)/shard_map/ppermute | solution.py:259
  368.6 34.6 %collective-permute-start.34 = (bf16[256,2048]{1,0:T(8,128)(2,1)}, bf16[256,2048]{1,0:T(8,128)(2,1)}, u32[]{:S(2)}, u32[]{:S(2)}) collective-permute-start(bf16[256,2048]{1,0:T(8,128)(2,1)} %get-tuple-element.88), channel_id=1, source_target_pairs={{1,2},{2,1},{5,6},{6,5},{9,10},{10,9},{13,14},{14,13},{17,18},{18,... | collective-permute-start | bytes 3145736 | tf_op jit(solution)/shard_map/ppermute | solution.py:262
  432.6 38.2 %collective-permute-start.39 = (bf16[512,2048]{1,0:T(8,128)(2,1)}, bf16[512,2048]{1,0:T(8,128)(2,1)}, u32[]{:S(2)}, u32[]{:S(2)}) collective-permute-start(bf16[512,2048]{1,0:T(8,128)(2,1)} %pad_maximum_fusion.5), channel_id=1, source_target_pairs={{0,4},{4,0},{8,12},{12,8},{16,20},{20,16},{24,28},{28,24},{1,5},{5... | collective-permute-start | bytes 6291464 | tf_op jit(solution)/shard_map/ppermute | solution.py:259
  560.1 36.5 %collective-permute-start.87 = (bf16[2,256,864]{1,2,0:T(8,128)(2,1)S(1)}, bf16[2,256,864]{1,2,0:T(8,128)(2,1)}, u32[]{:S(2)}, u32[]{:S(2)}) collective-permute-start(bf16[2,256,864]{1,2,0:T(8,128)(2,1)S(1)} %pad_maximum_fusion.15), channel_id=1, source_target_pairs={{0,8},{4,12},{8,0},{12,4},{16,24},{20,28},{24,16},{28,20},{1,9},{5... | collective-permute-start | bytes 2654216 | tf_op jit(solution)/shard_map/ppermute | solution.py:259
  560.9 39.1 %collective-permute-start.85 = (bf16[2,256,864]{1,2,0:T(8,128)(2,1)S(1)}, bf16[2,256,864]{1,2,0:T(8,128)(2,1)}, u32[]{:S(2)}, u32[]{:S(2)}) collective-permute-start(bf16[2,256,864]{1,2,0:T(8,128)(2,1)S(1)} %pad_maximum_fusion.14), channel_id=1, source_target_pairs={{0,16},{4,20},{8,24},{12,28},{16,0},{20,4},{24,8},{28,12},{1,17},{... | collective-permute-start | bytes 2654216 | tf_op jit(solution)/shard_map/ppermute | solution.py:259
  561.6 53.4 %collective-permute-start.81 = (bf16[2,256,864]{1,2,0:T(8,128)(2,1)S(1)}, bf16[2,256,864]{1,2,0:T(8,128)(2,1)S(1)}, u32[]{:S(2)}, u32[]{:S(2)}) collective-permute-start(bf16[2,256,864]{1,2,0:T(8,128)(2,1)S(1)} %pad_maximum_fusion.13), channel_id=1, source_target_pairs={{0,8},{4,12},{8,0},{12,4},{16,24},{20,28},{24,16},{28,20},{1,9},{5... | collective-permute-start | bytes 2654216 | tf_op jit(solution)/shard_map/ppermute | solution.py:259
  577.5 41.4 %collective-permute-start.79 = (bf16[2,256,864]{1,2,0:T(8,128)(2,1)S(1)}, bf16[2,256,864]{1,2,0:T(8,128)(2,1)S(1)}, u32[]{:S(2)}, u32[]{:S(2)}) collective-permute-start(bf16[2,256,864]{1,2,0:T(8,128)(2,1)S(1)} %pad_maximum_fusion.12), channel_id=1, source_target_pairs={{0,16},{4,20},{8,24},{12,28},{16,0},{20,4},{24,8},{28,12},{1,17},{... | collective-permute-start | bytes 2654216 | tf_op jit(solution)/shard_map/ppermute | solution.py:259
  581.0 77.1 %collective-permute-start.48 = (bf16[512,2048]{1,0:T(8,128)(2,1)}, bf16[512,2048]{1,0:T(8,128)(2,1)S(1)}, u32[]{:S(2)}, u32[]{:S(2)}) collective-permute-start(bf16[512,2048]{1,0:T(8,128)(2,1)} %convolution_convert_fusion.5), channel_id=1, source_target_pairs={{0,4},{4,0},{8,12},{12,8},{16,20},{20,16},{24,28},{28,24},{1,5},{5... | collective-permute-start | bytes 6291464 | tf_op jit(solution)/shard_map/ppermute | solution.py:259
  596.6 53.0 %collective-permute-start.52 = (bf16[512,2048]{1,0:T(8,128)(2,1)S(1)}, bf16[512,2048]{1,0:T(8,128)(2,1)S(1)}, u32[]{:S(2)}, u32[]{:S(2)}) collective-permute-start(bf16[512,2048]{1,0:T(8,128)(2,1)S(1)} %copy-done.95), channel_id=1, source_target_pairs={{0,4},{4,0},{8,12},{12,8},{16,20},{20,16},{24,28},{28,24},{1,5},{5... | collective-permute-start | bytes 6291464 | tf_op jit(solution)/shard_map/ppermute | solution.py:259
  648.6 69.7 %collective-permute-start.89 = (bf16[256,864]{0,1:T(8,128)(2,1)S(1)}, bf16[256,864]{0,1:T(8,128)(2,1)S(1)}, u32[]{:S(2)}, u32[]{:S(2)}) collective-permute-start(bf16[256,864]{0,1:T(8,128)(2,1)S(1)} %get-tuple-element.110), channel_id=1, source_target_pairs={{7,4},{6,5},{5,6},{4,7},{15,12},{14,13},{13,14},{12,15},{23,20},{2... | collective-permute-start | bytes 1327112 | tf_op jit(solution)/shard_map/ppermute | solution.py:441
  649.6 68.8 %collective-permute-start.90 = (bf16[256,864]{0,1:T(8,128)(2,1)S(1)}, bf16[256,864]{0,1:T(8,128)(2,1)S(1)}, u32[]{:S(2)}, u32[]{:S(2)}) collective-permute-start(bf16[256,864]{0,1:T(8,128)(2,1)S(1)} %get-tuple-element.111), channel_id=1, source_target_pairs={{0,4},{1,5},{2,6},{3,7},{8,12},{9,13},{10,14},{11,15},{16,20},{17,... | collective-permute-start | bytes 1327112 | tf_op jit(solution)/shard_map/ppermute | solution.py:440
  661.0 58.4 %collective-permute-start.83 = (bf16[256,864]{0,1:T(8,128)(2,1)S(1)}, bf16[256,864]{0,1:T(8,128)(2,1)S(1)}, u32[]{:S(2)}, u32[]{:S(2)}) collective-permute-start(bf16[256,864]{0,1:T(8,128)(2,1)S(1)} %get-tuple-element.112), channel_id=1, source_target_pairs={{7,4},{6,5},{5,6},{4,7},{15,12},{14,13},{13,14},{12,15},{23,20},{2... | collective-permute-start | bytes 1327112 | tf_op jit(solution)/shard_map/ppermute | solution.py:441
  661.8 53.6 %collective-permute-start.49 = (bf16[256,2048]{1,0:T(8,128)(2,1)S(1)}, bf16[256,2048]{1,0:T(8,128)(2,1)S(1)}, u32[]{:S(2)}, u32[]{:S(2)}) collective-permute-start(bf16[256,2048]{1,0:T(8,128)(2,1)S(1)} %slice.830), channel_id=1, source_target_pairs={{0,1},{1,0},{2,3},{3,2},{4,5},{5,4},{6,7},{7,6},{8,9},{9,8},{10,11... | collective-permute-start | bytes 3145736 | tf_op jit(solution)/shard_map/ppermute | solution.py:262
  688.3 31.9 %collective-permute-start.84 = (bf16[256,864]{0,1:T(8,128)(2,1)S(1)}, bf16[256,864]{0,1:T(8,128)(2,1)S(1)}, u32[]{:S(2)}, u32[]{:S(2)}) collective-permute-start(bf16[256,864]{0,1:T(8,128)(2,1)S(1)} %get-tuple-element.113), channel_id=1, source_target_pairs={{0,4},{1,5},{2,6},{3,7},{8,12},{9,13},{10,14},{11,15},{16,20},{17,... | collective-permute-start | bytes 1327112 | tf_op jit(solution)/shard_map/ppermute | solution.py:440
  747.2 47.8 %collective-permute-start.58 = (bf16[256,2048]{1,0:T(8,128)(2,1)S(1)}, bf16[256,2048]{1,0:T(8,128)(2,1)S(1)}, u32[]{:S(2)}, u32[]{:S(2)}) collective-permute-start(bf16[256,2048]{1,0:T(8,128)(2,1)S(1)} %collective-permute-done.55), channel_id=1, source_target_pairs={{1,0},{2,3},{5,4},{6,7},{9,8},{10,11},{13,12},{14,15},{17,16},{18,... | collective-permute-start | bytes 3145736 | tf_op jit(solution)/shard_map/ppermute | solution.py:262
  825.4 40.1 %collective-permute-start.74 = (bf16[1024,1024]{1,0:T(8,128)(2,1)S(1)}, bf16[1024,1024]{1,0:T(8,128)(2,1)S(1)}, u32[]{:S(2)}, u32[]{:S(2)}) collective-permute-start(bf16[1024,1024]{1,0:T(8,128)(2,1)S(1)} %fusion.40), channel_id=1, source_target_pairs={{0,4},{4,0},{8,12},{12,8},{16,20},{20,16},{24,28},{28,24},{1,5},{5... | collective-permute-start | bytes 6291464 | tf_op jit(solution)/shard_map/ppermute | solution.py:259
  864.8 73.5 %collective-permute-start.69 = (bf16[1024,3072]{1,0:T(8,128)(2,1)}, bf16[1024,3072]{1,0:T(8,128)(2,1)}, u32[]{:S(2)}, u32[]{:S(2)}) collective-permute-start(bf16[1024,3072]{1,0:T(8,128)(2,1)} %convolution_convert_fusion), channel_id=1, source_target_pairs={{0,4},{4,0},{8,12},{12,8},{16,20},{20,16},{24,28},{28,24},{1,5},{5... | collective-permute-start | bytes 18874376 | tf_op jit(solution)/shard_map/ppermute | solution.py:259
  868.1 33.1 %collective-permute-start.75 = (bf16[256,1024]{1,0:T(8,128)(2,1)S(1)}, bf16[256,1024]{1,0:T(8,128)(2,1)S(1)}, u32[]{:S(2)}, u32[]{:S(2)}) collective-permute-start(bf16[256,1024]{1,0:T(8,128)(2,1)S(1)} %get-tuple-element.70), channel_id=1, source_target_pairs={{0,16},{4,20},{8,24},{12,28},{16,0},{20,4},{24,8},{28,12},{1,17},{... | collective-permute-start | bytes 1572872 | tf_op jit(solution)/shard_map/ppermute | solution.py:259
  869.7 31.5 %collective-permute-start.77 = (bf16[256,1024]{1,0:T(8,128)(2,1)S(1)}, bf16[256,1024]{1,0:T(8,128)(2,1)S(1)}, u32[]{:S(2)}, u32[]{:S(2)}) collective-permute-start(bf16[256,1024]{1,0:T(8,128)(2,1)S(1)} %get-tuple-element.71), channel_id=1, source_target_pairs={{0,8},{4,12},{8,0},{12,4},{16,24},{20,28},{24,16},{28,20},{1,9},{5... | collective-permute-start | bytes 1572872 | tf_op jit(solution)/shard_map/ppermute | solution.py:259
  877.4 34.5 %collective-permute-start.60 = (bf16[256,2048]{1,0:T(8,128)(2,1)}, bf16[256,2048]{1,0:T(8,128)(2,1)}, u32[]{:S(2)}, u32[]{:S(2)}) collective-permute-start(bf16[256,2048]{1,0:T(8,128)(2,1)} %add_convert_fusion.3), channel_id=1, source_target_pairs={{1,2},{2,1},{5,6},{6,5},{9,10},{10,9},{13,14},{14,13},{17,18},{18,... | collective-permute-start | bytes 3145736 | tf_op jit(solution)/shard_map/ppermute | solution.py:262
  888.5 35.7 %collective-permute-start.63 = (bf16[256,2048]{1,0:T(8,128)(2,1)}, bf16[256,2048]{1,0:T(8,128)(2,1)}, u32[]{:S(2)}, u32[]{:S(2)}) collective-permute-start(bf16[256,2048]{1,0:T(8,128)(2,1)} %get-tuple-element.73), channel_id=1, source_target_pairs={{0,1},{1,0},{2,3},{3,2},{4,5},{5,4},{6,7},{7,6},{8,9},{9,8},{10,11... | collective-permute-start | bytes 3145736 | tf_op jit(solution)/shard_map/ppermute | solution.py:262
  953.7 34.5 %collective-permute-start.70 = (bf16[256,3072]{1,0:T(8,128)(2,1)S(1)}, bf16[256,3072]{1,0:T(8,128)(2,1)S(1)}, u32[]{:S(2)}, u32[]{:S(2)}) collective-permute-start(bf16[256,3072]{1,0:T(8,128)(2,1)S(1)} %get-tuple-element.38), channel_id=1, source_target_pairs={{0,16},{4,20},{8,24},{12,28},{16,0},{20,4},{24,8},{28,12},{1,17},{... | collective-permute-start | bytes 4718600 | tf_op jit(solution)/shard_map/ppermute | solution.py:259
  955.3 34.2 %collective-permute-start.72 = (bf16[256,3072]{1,0:T(8,128)(2,1)S(1)}, bf16[256,3072]{1,0:T(8,128)(2,1)S(1)}, u32[]{:S(2)}, u32[]{:S(2)}) collective-permute-start(bf16[256,3072]{1,0:T(8,128)(2,1)S(1)} %get-tuple-element.39), channel_id=1, source_target_pairs={{0,8},{4,12},{8,0},{12,4},{16,24},{20,28},{24,16},{28,20},{1,9},{5... | collective-permute-start | bytes 4718600 | tf_op jit(solution)/shard_map/ppermute | solution.py:259
  961.9 32.4 %collective-permute-start.66 = (f32[2,2048]{1,0:T(2,128)S(1)}, f32[2,2048]{1,0:T(2,128)S(1)}, u32[]{:S(2)}, u32[]{:S(2)}) collective-permute-start(f32[2,2048]{1,0:T(2,128)S(1)} %add.778), channel_id=1, source_target_pairs={{0,4},{4,0},{8,12},{12,8},{16,20},{20,16},{24,28},{28,24},{1,5},{5... | collective-permute-start | bytes 49160 | tf_op jit(solution)/shard_map/ppermute | solution.py:259
  (148 other events, 3098.0 us)

commit v2 on v1

--- a/solution.py
+++ b/solution.py
@@ -2,6 +2,7 @@
 
 import jax
 import jax.numpy as jnp
+import numpy as np
 from jax import lax
 from jax.experimental import pallas as pl
 from jax.experimental.pallas import tpu as pltpu
@@ -10,6 +11,7 @@
 KEY = 256
 VAL = 432
 VPAD = 512
+LANES = 128
 EPS = 1e-05
 HEAD_EPS = 1.0
 F32 = jnp.float32
@@ -31,6 +33,14 @@
 
 def after(array, *earlier):
     return lax.optimization_barrier((array, *earlier))[0]
+
+
+def params(**more):
+    return pltpu.CompilerParams(vmem_limit_bytes=VMEM_LIMIT, **more)
+
+
+def cost(flops, moved):
+    return pl.CostEstimate(flops=flops // 4, bytes_accessed=moved // 4, transcendentals=0)
 
 
 def norm_parts(features):
@@ -130,9 +140,7 @@
             scratch_shapes=[pltpu.VMEM((rows, seq), F32), pltpu.VMEM((seq, VPAD), F32)],
         ),
         compiler_params=pltpu.CompilerParams(vmem_limit_bytes=VMEM_LIMIT),
-        cost_estimate=pl.CostEstimate(
-            flops=heads * seq * seq * (KEY + VPAD), bytes_accessed=heads * seq * 9000, transcendentals=heads * seq * 800
-        ),
+        cost_estimate=cost(heads * seq * seq * (KEY + VPAD), heads * seq * 9000),
     )(place, log_decay, *(projected * 4), cosines, sines)
 
 
@@ -219,10 +227,377 @@
             ],
         ),
         compiler_params=pltpu.CompilerParams(vmem_limit_bytes=VMEM_LIMIT),
-        cost_estimate=pl.CostEstimate(
-            flops=heads * seq * seq * (3 * KEY + 2 * VPAD), bytes_accessed=heads * seq * 10000, transcendentals=heads * seq * 800
+        cost_estimate=cost(heads * seq * seq * (3 * KEY + 2 * VPAD), heads * seq * 10000),
+    )(place, log_decay, *grads, *projected, normed, scale, query, key, value, cosines, sines)
+
+
+def rows_kernel(slots, pieces, *refs):
+    lefts, weights, outs = refs[:slots], refs[slots : slots + pieces], refs[slots + pieces :]
+    left = jnp.concatenate([ref[...] for ref in lefts], 0)
+    result = times_plain(left, jnp.concatenate([ref[...] for ref in weights], 0)).astype(BF16)
+    rows = lefts[0].shape[0]
+    for slot in range(slots):
+        outs[slot][...] = result[slot * rows : (slot + 1) * rows]
+
+
+def rows_times(lefts, pieces, first, columns, tile=512):
+    rows, width = lefts[0].shape
+    return pl.pallas_call(
+        partial(rows_kernel, len(lefts), len(pieces)),
+        out_shape=[jax.ShapeDtypeStruct((rows, columns), BF16)] * len(lefts),
+        grid=(columns // tile,),
+        in_specs=[pl.BlockSpec((rows, width), lambda n: (0, 0))] * len(lefts)
+        + [pl.BlockSpec((p.shape[0], tile), lambda n: (0, n + first // tile)) for p in pieces],
+        out_specs=[pl.BlockSpec((rows, tile), lambda n: (0, n))] * len(lefts),
+        compiler_params=params(),
+        cost_estimate=cost(2 * len(lefts) * rows * width * columns, 2 * width * columns),
+    )(*lefts, *pieces)
+
+
+def rows_back_kernel(slots, pieces, weigh, *refs):
+    lefts, weights, rest = refs[:slots], refs[slots : slots + pieces], refs[slots + pieces :]
+    total = rest[-1]
+    step = pl.program_id(0)
+    left = jnp.concatenate([ref[...] for ref in lefts], 0)
+    part = times_right(left, jnp.concatenate([ref[...] for ref in weights], 0))
+
+    @pl.when(step == 0)
+    def _():
+        total[...] = part
+
+    @pl.when(step > 0)
+    def _():
+        total[...] += part
+
+    @pl.when(step == pl.num_programs(0) - 1)
+    def _():
+        rows = lefts[0].shape[0]
+        for slot in range(slots):
+            rest[weigh * slots + slot][...] = total[slot * rows : (slot + 1) * rows, :].astype(BF16)
+        if weigh:
+            other = jnp.concatenate([ref[...] for ref in rest[:slots]], 0).astype(F32)
+            along = jnp.sum(total[...] * other, 0, keepdims=True)
+            rest[2 * slots][...] = jnp.broadcast_to(along, (8, along.shape[1]))
+
+
+def rows_back(left, slots, pieces, first=0, weigh=(), tile=512):
+    rows = left.shape[0] // 4
+    columns = left.shape[1]
+    width = sum(p.shape[0] for p in pieces)
+    whole = pl.BlockSpec((rows, width), lambda k: (0, 0))
+    return pl.pallas_call(
+        partial(rows_back_kernel, len(slots), len(pieces), 1 if weigh else 0),
+        out_shape=[jax.ShapeDtypeStruct((rows, width), BF16)] * len(slots)
+        + ([jax.ShapeDtypeStruct((8, width), F32)] if weigh else []),
+        grid=(columns // tile,),
+        in_specs=[pl.BlockSpec((rows, tile), partial(lambda s, k: (s, k), s)) for s in slots]
+        + [pl.BlockSpec((p.shape[0], tile), lambda k: (0, k + first // tile)) for p in pieces]
+        + [whole] * len(weigh),
+        out_specs=[whole] * len(slots) + ([pl.BlockSpec((8, width), lambda k: (0, 0))] if weigh else []),
+        scratch_shapes=[pltpu.VMEM((len(slots) * rows, width), F32)],
+        compiler_params=params(),
+        cost_estimate=cost(2 * len(slots) * rows * width * columns, 2 * width * columns),
+    )(*([left] * len(slots)), *pieces, *weigh)
+
+
+def turn(array):
+    middle = array.shape[1] // 2
+    return jnp.concatenate([array[:, middle:], array[:, :middle]], 1)
+
+
+def mlp_kernel(pieces, units, own_ref, other_ref, own_grad_ref, other_grad_ref, *refs):
+    sources, outs = refs[:pieces], refs[pieces : pieces + 8]
+    gate_ref, up_ref, down_ref, semaphores = refs[pieces + 8 :]
+    rows = own_ref.shape[0]
+    height = sources[0].shape[1]
+    copies = []
+    for part, target in enumerate((gate_ref, up_ref, down_ref)):
+        for core in range(2):
+            for index, source in enumerate(sources):
+                place = core * pieces + index
+                copy = pltpu.make_async_copy(
+                    source.at[core, :, pl.ds(part * units, units)],
+                    target.at[pl.ds(place * height, height), :],
+                    semaphores.at[part, place],
+                )
+                copy.start()
+                copies.append(copy)
+    third = 2 * pieces
+    left = jnp.concatenate([own_ref[...], turn(other_ref[...])], 0)
+    grad = jnp.concatenate([own_grad_ref[...], turn(other_grad_ref[...])], 0)
+    for copy in copies[:third]:
+        copy.wait()
+    gate = times_plain(left, gate_ref[...])
+    for copy in copies[third : 2 * third]:
+        copy.wait()
+    up = times_plain(left, up_ref[...])
+    for copy in copies[2 * third :]:
+        copy.wait()
+    grad_hidden = times_plain(grad, down_ref[...])
+    below = 0.5 + 0.5 * lax.erf(gate * (0.5**0.5))
+    density = jnp.exp(-0.5 * gate * gate) * 0.3989422804014327
+    smooth = gate * below
+    hidden = (smooth * up).astype(BF16)
+    grad_gate = (grad_hidden * up * (below + gate * density)).astype(BF16)
+    grad_up = (grad_hidden * smooth).astype(BF16)
+    for slot in range(2):
+        span = slice(slot * rows, (slot + 1) * rows)
+        outs[slot][...] = hidden[span]
+        outs[2 + slot][...] = grad_gate[span]
+        outs[4 + slot][...] = grad_up[span]
+    back = times_right(grad_gate, gate_ref[...]) + times_right(grad_up, up_ref[...])
+    outs[6][...] = back[:rows].astype(BF16)
+    outs[7][...] = turn(back[rows:]).astype(BF16)
+
+
+def mlp(own, other, own_grad, other_grad, pieces):
+    rows, width = own.shape
+    units = pieces[0].shape[2] // 3
+    whole = pl.BlockSpec(memory_space=pltpu.VMEM)
+    small, large = jax.ShapeDtypeStruct((rows, units), BF16), jax.ShapeDtypeStruct((rows, width), BF16)
+    return pl.pallas_call(
+        partial(mlp_kernel, len(pieces), units),
+        out_shape=[small] * 6 + [large] * 2,
+        in_specs=[whole] * 4 + [pl.BlockSpec(memory_space=pl.ANY)] * len(pieces),
+        out_specs=[whole] * 8,
+        scratch_shapes=[pltpu.VMEM((width, units), BF16)] * 3 + [pltpu.SemaphoreType.DMA((3, 2 * len(pieces)))],
+        compiler_params=params(),
+        cost_estimate=cost(2 * 2 * rows * width * units * 5, 6 * width * units),
+    )(own, other, own_grad, other_grad, *pieces)
+
+
+def down_kernel(pieces, *refs):
+    lefts, weights, outs = refs[:4], refs[4 : 4 + pieces], refs[4 + pieces :]
+    rows = lefts[0].shape[0]
+    weight = jnp.concatenate([ref[core] for core in range(2) for ref in weights], 0)
+    for core in range(2):
+        left = jnp.concatenate([lefts[2 * core][...], lefts[2 * core + 1][...]], 0)
+        result = times_right(left, weight)
+        outs[core][...] = (turn(result) if core else result).astype(BF16)
+
+
+def mlp_down(hidden, pieces):
+    rows, units = hidden[0].shape
+    width = 2 * sum(p.shape[1] for p in pieces)
+    whole = pl.BlockSpec((rows, units), lambda n: (0, 0))
+    out = pl.BlockSpec((2 * rows, width), lambda n: (0, 0))
+    return pl.pallas_call(
+        partial(down_kernel, len(pieces)),
+        out_shape=[jax.ShapeDtypeStruct((2 * rows, width), BF16)] * 2,
+        grid=(1,),
+        in_specs=[whole] * 4 + [pl.BlockSpec((2, p.shape[1], units), lambda n: (0, 0, 2)) for p in pieces],
+        out_specs=[out] * 2,
+        compiler_params=params(),
+        cost_estimate=cost(8 * rows * width * units, 2 * width * units),
+    )(*hidden, *pieces)
+
+
+def mlp_grad_kernel(*refs):
+    lefts, grads, rights, outs = refs[:4], refs[4:8], refs[8:20], refs[20:]
+    left = jnp.concatenate([ref[...] for ref in lefts], 0)
+    grad = jnp.concatenate([ref[...] for ref in grads], 0)
+    parts = []
+    for index, rows in enumerate((left, left, grad)):
+        right = jnp.concatenate([ref[...] for ref in rights[4 * index : 4 * index + 4]], 0)
+        parts.append(times_left(rows, right).astype(BF16))
+    result = jnp.concatenate(parts, 1)
+    for part in range(2):
+
+        @pl.when(pl.program_id(0) == part)
+        def _():
+            outs[part][...] = result
+
+
+def mlp_grads(end, core, lefts, grads, grad_gate, grad_up, hidden):
+    rows, width = lefts[0].shape
+    units = hidden[0].shape[1]
+    tile = width // 8
+
+    def column(other, step):
+        return (0, (core ^ other) * 4 + step * 2 + end)
+
+    narrow = [pl.BlockSpec((rows, tile), partial(column, other)) for other in (0, 0, 1, 1)]
+    whole = pl.BlockSpec((rows, units), lambda i: (0, 0))
+    return pl.pallas_call(
+        mlp_grad_kernel,
+        out_shape=[jax.ShapeDtypeStruct((tile, 3 * units), BF16)] * 2,
+        grid=(2,),
+        in_specs=narrow * 2 + [whole] * 12,
+        out_specs=[pl.BlockSpec((tile, 3 * units), lambda i: (0, 0))] * 2,
+        compiler_params=params(),
+        cost_estimate=cost(2 * rows * width * units * 3, 2 * width * units),
+    )(*lefts, *grads, *grad_gate, *grad_up, *hidden)
+
+
+def attn_grad_kernel(*refs):
+    left = jnp.concatenate([ref[...] for ref in refs[:4]], 0)
+    refs[5][...] = times_left(left, refs[4][...]).astype(BF16)
+
+
+def attn_grad_add_kernel(*refs):
+    left = jnp.concatenate([ref[...] for ref in refs[:4]], 0)
+    result = (times_left(left, refs[4][...]) + refs[5][...].astype(F32)).astype(BF16)
+    for part in range(2):
+
+        @pl.when(pl.program_id(0) == part)
+        def _():
+            refs[6 + part][...] = result
+
+
+def attn_grads(end, lefts, right, other=None):
+    rows, width = lefts[0].shape
+    columns = right.shape[1]
+    tile = width // 8
+    core = 1 if other is None else 0
+    narrow = pl.BlockSpec((rows, tile), lambda i: (0, core * 4 + 2 * i + end))
+    block = pl.BlockSpec((tile, columns), lambda i: (i, 0))
+    whole = pl.BlockSpec((tile, columns), lambda i: (0, 0))
+    return pl.pallas_call(
+        attn_grad_kernel if core else attn_grad_add_kernel,
+        out_shape=jax.ShapeDtypeStruct((2 * tile, columns), BF16)
+        if core
+        else [jax.ShapeDtypeStruct((tile, columns), BF16)] * 2,
+        grid=(2,),
+        in_specs=[narrow] * 4 + [pl.BlockSpec(right.shape, lambda i: (0, 0))] + ([] if core else [block]),
+        out_specs=block if core else [whole] * 2,
+        compiler_params=params(),
+        cost_estimate=cost(2 * rows * width * columns, width * columns),
+    )(*lefts, right, *([] if core else [other]))
+
+
+def own_order_kernel(blocks, sizes, mine_ref, *refs):
+    (shard_rows, half_rows), count = sizes, len(refs) // 2
+    for index, (mask, part) in enumerate(blocks):
+        start = pl.multiple_of((mine_ref[0] ^ mask) * shard_rows + part * half_rows, half_rows)
+        for source, target in zip(refs[:count], refs[count:]):
+            target[:, index * half_rows : (index + 1) * half_rows] = source[:, pl.ds(start, half_rows)]
+
+
+def global_order_kernel(blocks, sizes, mine_ref, source, target):
+    shard_rows, half_rows = sizes
+    for index, (mask, part) in enumerate(blocks):
+        start = pl.multiple_of((mine_ref[0] ^ mask) * shard_rows + part * half_rows, half_rows)
+        target[:, pl.ds(start, half_rows)] = source[:, index * half_rows : (index + 1) * half_rows]
+
+
+def reorder(kernel, blocks, sizes, mine, arrays):
+    specs = [pl.BlockSpec(a.shape, lambda i, *_: (0, 0)) for a in arrays]
+    return pl.pallas_call(
+        partial(kernel, blocks, sizes),
+        out_shape=[jax.ShapeDtypeStruct(a.shape, a.dtype) for a in arrays],
+        grid_spec=pltpu.PrefetchScalarGridSpec(num_scalar_prefetch=1, grid=(1,), in_specs=specs, out_specs=specs),
+        compiler_params=params(),
+    )(mine, *arrays)
+
+
+def widen(array, height):
+    return jnp.concatenate([array, jnp.zeros((height - array.shape[0], array.shape[1]), array.dtype)], 0)
+
+
+def send_attn_kernel(heads, *refs):
+    sources, targets = refs[:5], refs[5:]
+    half = targets[0].shape[0]
+    spans = [slice(part * half, (part + 1) * half) for part in range(2)]
+    for index, source in enumerate(sources):
+        if index < 2:
+            for span, target in zip(spans, targets):
+                target[:, index * heads * KEY : (index + 1) * heads * KEY] = source[span, :].astype(BF16)
+        else:
+            for head in range(heads):
+                column = 2 * heads * KEY + ((index - 2) * heads + head) * VPAD
+                block = widen(source[head * VAL : (head + 1) * VAL, :], VPAD).T.astype(BF16)
+                for span, target in zip(spans, targets):
+                    target[:, column : column + VPAD] = block[span, :]
+
+
+def send_attn(weights, heads):
+    half = weights[0].shape[0] // 2
+    columns = heads * (2 * KEY + 3 * VPAD)
+    arrays = [*weights[:2], *(w.T for w in weights[2:])]
+    return pl.pallas_call(
+        partial(send_attn_kernel, heads),
+        out_shape=[jax.ShapeDtypeStruct((half, columns), BF16)] * 2,
+        grid=(1,),
+        in_specs=[pl.BlockSpec(w.shape, lambda i: (0, 0)) for w in arrays],
+        out_specs=[pl.BlockSpec((half, columns), lambda i: (0, 0))] * 2,
+        compiler_params=params(),
+        cost_estimate=cost(0, half * columns * 12),
+    )(*arrays)
+
+
+def send_mlp_kernel(padded, *refs):
+    target = refs[-1]
+    for index, source in enumerate(refs[:-1]):
+        target[:, index * padded : (index + 1) * padded] = widen(source[...], padded).T.astype(BF16)
+
+
+def send_mlp(weights, padded):
+    rows, units = weights[0].shape
+    return pl.pallas_call(
+        partial(send_mlp_kernel, padded),
+        out_shape=jax.ShapeDtypeStruct((rows, len(weights) * padded), BF16),
+        grid=(1,),
+        in_specs=[pl.BlockSpec((units, rows), lambda i: (0, 0))] * len(weights),
+        out_specs=pl.BlockSpec((rows, len(weights) * padded), lambda i: (0, 0)),
+        compiler_params=params(),
+        cost_estimate=cost(0, rows * padded * 18),
+    )(*(w.T for w in weights))
+
+
+def receive_kernel(narrow, heads, *refs):
+    targets = refs[4:]
+    total = jnp.concatenate(
+        [refs[2 * part][...].astype(F32) + refs[2 * part + 1][...].astype(F32) for part in range(2)], 0
+    )
+    column = 0
+    for index, target in enumerate(targets):
+        if index < narrow:
+            target[...] = total[:, column : column + heads * KEY]
+            column += heads * KEY
+        else:
+            for head in range(heads):
+                target[head * VAL : (head + 1) * VAL, :] = total[:, column : column + VPAD].T[:VAL]
+                column += VPAD
+
+
+def receive_attn(parts, narrow, wide, heads):
+    rows = 2 * parts[0].shape[0]
+    shapes = [(rows, heads * KEY)] * narrow + [(heads * VAL, rows)] * wide
+    found = pl.pallas_call(
+        partial(receive_kernel, narrow, heads),
+        out_shape=[jax.ShapeDtypeStruct(s, F32) for s in shapes],
+        grid=(1,),
+        in_specs=[pl.BlockSpec(p.shape, lambda i: (0, 0)) for p in parts],
+        out_specs=[pl.BlockSpec(s, lambda i: (0, 0)) for s in shapes],
+        compiler_params=params(),
+        cost_estimate=cost(0, rows * sum(s[0] for s in shapes) * 4),
+    )(*parts)
+    return [*found[:narrow], *(f.T for f in found[narrow:])]
+
+
+def receive_mlp_kernel(padded, odd_ref, kept, turned, core, *targets):
+    first = jnp.where(odd_ref[0] == 1, turned[...], kept[...]).astype(F32)
+    total = first + core[...].astype(F32)
+    for index, target in enumerate(targets):
+        target[...] = total[:, index * padded : (index + 1) * padded].T[: target.shape[0]]
+
+
+def receive_mlp(odd, kept, turned, core, units):
+    rows, columns = kept.shape
+    whole = pl.BlockSpec((rows, columns), lambda i, *_: (0, 0))
+    found = pl.pallas_call(
+        partial(receive_mlp_kernel, columns // 3),
+        out_shape=[jax.ShapeDtypeStruct((units, rows), F32)] * 3,
+        grid_spec=pltpu.PrefetchScalarGridSpec(
+            num_scalar_prefetch=1,
+            grid=(1,),
+            in_specs=[whole] * 3,
+            out_specs=[pl.BlockSpec((units, rows), lambda i, *_: (0, 0))] * 3,
         ),
-    )(place, log_decay, *grads, *projected, normed, scale, query, key, value, cosines, sines)
+        compiler_params=params(),
+        cost_estimate=cost(0, rows * columns * 10),
+    )(odd, kept, turned, core)
+    return [f.T for f in found]
 
 
 def per_device(
@@ -255,6 +630,9 @@
     up_bits = list(range(1, bits))
     down_bits = up_bits[::-1]
 
+    def add(*arrays):
+        return sum(array.astype(F32) for array in arrays)
+
     def swap_dp(array, mask):
         return lax.ppermute(array, "dp", [(i, i ^ mask) for i in range(dp_size)])
 
@@ -268,37 +646,52 @@
     outward = [(1, 0), (2, 3)]
     inward = [(0, 1), (3, 2)]
 
-    def line_gather(own):
-        beside = swap_tensor(own, 1)
-        middle = move_tensor(own, across)
-        far_ends = move_tensor(middle, outward)
-        far_inner = move_tensor(beside, across)
-        last = move_tensor(far_inner, outward)
+    def pair(dp_index, tensor_index):
+        return dp_index * tensor_size + tensor_index
+
+    top = tensor_size - 1
+    to_even = [(pair(m | 1, t), pair(m, t)) for m in range(0, dp_size, 2) for t in range(tensor_size)]
+    to_odd = [(pair(m, t), pair(m | 1, t ^ top)) for m in range(0, dp_size, 2) for t in range(tensor_size)]
+    odd_turn = [(pair(m | 1, t), pair(m | 1, t ^ top)) for m in range(0, dp_size, 2) for t in range(tensor_size)]
+    both = ("dp", "tensor")
+
+    def hold(array):
+        return after(array, token[0])
+
+    def close(*results):
+        token[0] = after(token[0], *results)
+
+    def line_out(slots, beside, middle):
+        return move_tensor(hold(beside), across), move_tensor(hold(middle), outward)
+
+    def line_all(own, beside, middle, far_inner, far_ends, last):
         return own, beside, jnp.where(inner, far_inner, far_ends), jnp.where(inner, middle, last)
 
-    def line_scatter(part):
-        third, second = part(3), part(2)
-        from_ends = move_tensor(third.astype(BF16), inward)
-        from_ends_two = move_tensor(second.astype(BF16), inward)
-        second_sum = (second + from_ends.astype(F32)).astype(BF16)
-        third_sum = (third + from_ends_two.astype(F32)).astype(BF16)
-        first = part(1) + move_tensor(second_sum, across).astype(F32)
-        beside = swap_tensor(first.astype(BF16), 1)
-        middle = move_tensor(third_sum, across)
-        return part(0) + middle.astype(F32) + beside.astype(F32)
-
-    def gather_half(piece, order):
-        pieces = [piece]
-        for bit in order:
+    def first_level(piece, order):
+        return swap_dp(piece, 1 << order[0])
+
+    def second_level(piece, order):
+        return swap_dp(hold(piece), 1 << order[1])
+
+    def further(pieces, order):
+        for bit in order[2:]:
             pieces = pieces + [swap_dp(p, 1 << bit) for p in pieces]
         return pieces
 
-    def scatter_half(low, high, order):
-        for bit in order[::-1]:
-            total = low + swap_dp(high.astype(BF16), 1 << bit).astype(F32)
-            middle = total.shape[-2] // 2
-            low, high = total[..., :middle, :], total[..., middle:, :]
-        return total
+    def to_core(piece):
+        return swap_dp(hold(piece), 1)
+
+    def sum_start(high, order):
+        return swap_dp(hold(high), 1 << order[-1])
+
+    def sum_split(low, come):
+        middle = low.shape[0] // 2
+        return [add(low[span], come[span]).astype(BF16) for span in (slice(0, middle), slice(middle, 2 * middle))]
+
+    def sum_end(low, high, order):
+        for bit in order[-2:0:-1]:
+            low, high = sum_split(low, swap_dp(hold(high), 1 << bit))
+        return low, swap_dp(hold(high), 1 << order[0])
 
     blocks = [
         (chip << 1 | core, part)
@@ -307,16 +700,27 @@
         for chip in [sum((i >> j & 1) << (b - 1) for j, b in enumerate(order)) for i in range(dp_size // 2)]
     ]
 
-    def to_relative(array):
-        return jnp.concatenate(
-            [
-                lax.dynamic_slice_in_dim(array, (mine ^ mask) * shard_rows + part * half_rows, half_rows, -1)
-                for mask, part in blocks
-            ],
-            -1,
-        )
+    sizes = (shard_rows, half_rows)
+    aligned = half_rows % LANES == 0
+    mine_arg = mine.astype(jnp.int32).reshape(1)
+
+    def to_relative(*arrays):
+        if aligned:
+            return reorder(own_order_kernel, blocks, sizes, mine_arg, arrays)
+        return [
+            jnp.concatenate(
+                [
+                    lax.dynamic_slice_in_dim(a, (mine ^ mask) * shard_rows + part * half_rows, half_rows, -1)
+                    for mask, part in blocks
+                ],
+                -1,
+            )
+            for a in arrays
+        ]
 
     def to_global(array):
+        if aligned:
+            return reorder(global_order_kernel, blocks, sizes, mine_arg, [array])[0]
         found = []
         for shard in range(dp_size):
             mask = mine ^ shard
@@ -326,158 +730,206 @@
                 found.append(lax.dynamic_slice_in_dim(array, index * half_rows, half_rows, -1))
         return jnp.concatenate(found, -1)
 
-    def pad_heads(array):
-        split = array.reshape(shard_rows, heads, VAL)
-        return jnp.pad(split, ((0, 0), (0, 0), (0, VPAD - VAL))).reshape(shard_rows, heads * VPAD)
-
-    def cut_heads(array):
-        return array.reshape(shard_rows, heads, VPAD)[:, :, :VAL].reshape(shard_rows, heads * VAL)
-
     first_row = place * rows
     valid = (first_row + jnp.arange(rows, dtype=jnp.int32) < lengths[0])[:, None]
     head_ids = (place * heads + jnp.arange(heads, dtype=jnp.int32)).astype(F32)
     log_decay = jnp.log(1.0 - jnp.exp2(-5.0 - head_ids))
     place_arg = place.astype(jnp.int32).reshape(1)
-    freqs = 10000.0 ** (-jnp.arange(KEY // 2, dtype=F32) / (KEY // 2))
-    angles = jnp.arange(seq, dtype=F32)[:, None] * freqs[None, :]
-    cosines, sines = jnp.cos(angles), jnp.sin(angles)
-
-    gain_first, gain_second = to_relative(gain_one), to_relative(gain_two)
-    features = to_relative(tokens).astype(F32)
+    freqs = np.float32(10000.0) ** (-np.arange(KEY // 2, dtype=np.float32) / np.float32(KEY // 2))
+    angles = np.arange(seq, dtype=np.float32)[:, None] * freqs[None, :]
+    cosines, sines = jnp.asarray(np.cos(angles)), jnp.asarray(np.sin(angles))
+
+    token = [mine_arg]
+    proj_columns, out_columns = 2 * heads * (KEY + VPAD), heads * VPAD
+    padded = -(-units // LANES) * LANES
+
+    sent_up, sent_down = send_attn((w_query, w_key, w_value, w_gate, w_out), heads)
+    features_low, gain_first = to_relative(tokens, gain_one[None])
+    features = features_low.astype(F32)
     normed_one, inverse_one = norm_parts(features)
-    first_slots = line_gather((normed_one * gain_first).astype(BF16))
-
-    local_one = jnp.concatenate(
-        [w_query.astype(BF16), w_key.astype(BF16), pad_heads(w_value.astype(BF16)), pad_heads(w_gate.astype(BF16))], -1
-    )
-
-    def gather_weight(local):
-        own = gather_half(local[:half_rows], up_bits) + gather_half(local[half_rows:], down_bits)
-        other = [swap_dp(p, 1) for p in own]
-        return jnp.concatenate(own + other, 0)
-
-    proj_low = gather_weight(local_one)
-    out_low = gather_weight(pad_heads(w_out.astype(BF16)))
-
-    local_two = jnp.concatenate([w_mgate.astype(BF16), w_mup.astype(BF16), w_down.astype(BF16)], -1)
-
-    def pair(dp_index, tensor_index):
-        return dp_index * tensor_size + tensor_index
-
-    top = tensor_size - 1
-    to_even = [(pair(m | 1, t), pair(m, t)) for m in range(0, dp_size, 2) for t in range(tensor_size)]
-    to_odd = [(pair(m, t), pair(m | 1, t ^ top)) for m in range(0, dp_size, 2) for t in range(tensor_size)]
-    odd_turn = [(pair(m | 1, t), pair(m | 1, t ^ top)) for m in range(0, dp_size, 2) for t in range(tensor_size)]
-    both = ("dp", "tensor")
-    from_core = lax.ppermute(local_two, both, to_even + to_odd)
-    turned = lax.ppermute(local_two, both, odd_turn)
-    pair_local = jnp.stack([jnp.where(odd, turned, local_two), from_core])
-    mlp_pieces = gather_half(pair_local[:, :half_rows], up_bits) + gather_half(pair_local[:, half_rows:], down_bits)
-    mgate_low, mup_low, down_low = (
-        jnp.concatenate([p[:, :, i * units : (i + 1) * units] for p in mlp_pieces], 1).reshape(width, units)
-        for i in range(3)
-    )
-
-    def turn_cores(array):
-        return jnp.concatenate([array[:, width // 2 :], array[:, : width // 2]], 1)
-
-    def pair_gather(own):
-        chips = jnp.concatenate([own, swap_tensor(own, 1)], 0)
-        return jnp.concatenate([chips, turn_cores(swap_dp(chips, 1))], 0)
-
-    def pair_scatter(part):
-        core = turn_cores(swap_dp(part(1).astype(BF16), 1))
-        total = part(0) + core.astype(F32)
-        beside = swap_tensor(total[rows:].astype(BF16), 1)
-        return total[:rows] + beside.astype(F32)
-
-    grad_final = jnp.where(valid, to_relative(cotangent).astype(F32), 0.0)
-    grad_mlp_rows = pair_gather(grad_final.astype(BF16))
-
-    projected = [times_plain(slot, proj_low).astype(BF16) for slot in first_slots]
+    first_own = (normed_one * gain_first).astype(BF16)
+    close(sent_up, sent_down, first_own)
+
+    up_one = first_level(hold(sent_up), up_bits)
+    down_one = first_level(hold(sent_down), down_bits)
+    first_beside = swap_tensor(hold(first_own), 1)
+    first_middle = move_tensor(hold(first_own), across)
+    local_two = send_mlp((w_mgate, w_mup, hold(w_down)), padded)
+    cotangent_low, gain_second = to_relative(hold(cotangent), gain_two[None])
+    grad_own = jnp.where(valid, cotangent_low, 0.0)
+    grad_final = grad_own.astype(F32)
+    close(up_one, down_one, first_beside, first_middle, local_two, grad_own)
+
+    up_two, down_two = second_level(sent_up, up_bits), second_level(sent_down, down_bits)
+    first_far = line_out(None, first_beside, first_middle)
+    core_one = [to_core(p) for p in (sent_up, sent_down)]
+    close(up_two, down_two, *first_far, *core_one)
+
+    up_three, down_three = second_level(up_one, up_bits), second_level(down_one, down_bits)
+    first_last = move_tensor(hold(first_far[0]), outward)
+    core_two = [to_core(p) for p in (up_one, down_one)]
+    close(up_three, down_three, first_last, *core_two)
+
+    up_all = further([sent_up, up_one, up_two, up_three], up_bits)
+    down_all = further([sent_down, down_one, down_two, down_three], down_bits)
+    up_core = [core_one[0], core_two[0]] + [to_core(p) for p in up_all[2:]]
+    down_core = [core_one[1], core_two[1]] + [to_core(p) for p in down_all[2:]]
+    close(*up_core, *down_core)
+    attn_low = up_all + down_all + up_core + down_core
+    first_slots = line_all(first_own, first_beside, first_middle, *first_far, first_last)
+
+    turned = lax.ppermute(hold(local_two), both, odd_turn)
+    grad_beside = swap_tensor(hold(grad_own), 1)
+    grad_core = to_core(grad_own)
+    projected = rows_times([hold(first_slots[0]), *first_slots[1:]], attn_low, 0, proj_columns)
     query, key, value, normed_head, scale_head, mixed = retain(
         projected, place_arg, log_decay, cosines, sines, heads
     )
-    middle = features + line_scatter(lambda s: times_right(mixed[s * rows : (s + 1) * rows], out_low))
-
+    close(turned, grad_beside, grad_core, mixed)
+
+    from_core = lax.ppermute(hold(local_two), both, to_even + to_odd)
+    grad_rows = [grad_own, grad_beside, grad_core, to_core(grad_beside)]
+    mixed_second, mixed_third = rows_back(hold(mixed), (2, 3), attn_low, proj_columns)
+    from_ends = move_tensor(mixed_third, inward)
+    mixed_own, mixed_first = rows_back(after(mixed, mixed_third), (0, 1), attn_low, proj_columns)
+    mixed_partial = add(mixed_second, from_ends).astype(BF16)
+    close(from_core, grad_rows[3], mixed_partial, mixed_own)
+
+    def pair_half(span):
+        return jnp.stack([jnp.where(odd, turned[span], local_two[span]), hold(from_core)[span]])
+
+    mlp_up, mlp_across = pair_half(slice(0, half_rows)), pair_half(slice(half_rows, shard_rows))
+    mlp_up_one, mlp_across_one = first_level(mlp_up, up_bits), first_level(mlp_across, down_bits)
+    from_inner = move_tensor(hold(mixed_partial), across)
+    from_ends = move_tensor(hold(mixed_second), inward)
+    close(mlp_up_one, mlp_across_one, from_inner, from_ends)
+
+    mlp_up_two, mlp_across_two = second_level(mlp_up, up_bits), second_level(mlp_across, down_bits)
+    from_beside = swap_tensor(add(mixed_first, hold(from_inner)).astype(BF16), 1)
+    from_middle = move_tensor(add(mixed_third, hold(from_ends)).astype(BF16), across)
+    middle = features + add(mixed_own, from_beside, from_middle)
     normed_two, inverse_two = norm_parts(middle)
-    rows_two = pair_gather((normed_two * gain_second).astype(BF16))
-    grad_hidden = times_plain(grad_mlp_rows, down_low)
-    mgate_pre = times_plain(rows_two, mgate_low)
-    mup_pre = times_plain(rows_two, mup_low)
-    below = 0.5 * lax.erfc(-mgate_pre * (0.5**0.5))
-    density = jnp.exp(-0.5 * mgate_pre * mgate_pre) * 0.3989422804014327
-    hidden = (mgate_pre * below * mup_pre).astype(BF16)
-    grad_mgate_low = (grad_hidden * mup_pre * (below + mgate_pre * density)).astype(BF16)
-    grad_mup_low = (grad_hidden * mgate_pre * below).astype(BF16)
-
-    grad_second = pair_scatter(
-        lambda c: times_right(grad_mgate_low[2 * c * rows : 2 * (c + 1) * rows], mgate_low)
-        + times_right(grad_mup_low[2 * c * rows : 2 * (c + 1) * rows], mup_low)
-    )
+    second_own = (normed_two * gain_second).astype(BF16)
+    close(mlp_up_two, mlp_across_two, second_own)
+
+    mlp_up_three, mlp_across_three = second_level(mlp_up_one, up_bits), second_level(mlp_across_one, down_bits)
+    second_beside = swap_tensor(hold(second_own), 1)
+    second_core = to_core(second_own)
+    close(mlp_up_three, mlp_across_three, second_beside, second_core)
+    mlp_pieces = further([mlp_up, mlp_up_one, mlp_up_two, mlp_up_three], up_bits) + further(
+        [mlp_across, mlp_across_one, mlp_across_two, mlp_across_three], down_bits
+    )
+
+    first_part = mlp(hold(second_own), second_core, grad_rows[0], grad_rows[2], mlp_pieces)
+    second_far = to_core(second_beside)
+    second_rows = [second_own, second_beside, second_core, second_far]
+    close(first_part[7], second_far)
+
+    second_part = mlp(hold(second_beside), second_far, grad_rows[1], grad_rows[3], mlp_pieces)
+    near_core = to_core(first_part[7])
+    close(second_part[7], near_core)
+    hidden, grad_gate, grad_up = (
+        [first_part[2 * i], second_part[2 * i], first_part[2 * i + 1], second_part[2 * i + 1]] for i in range(3)
+    )
+
+    far = add(second_part[6], to_core(second_part[7])).astype(BF16)
+    near = add(first_part[6], near_core)
+    close(far)
+
+    def mlp_grad(end, core):
+        return mlp_grads(end, core, [hold(second_rows[0]), *second_rows[1:]], grad_rows, grad_gate, grad_up, hidden)
+
+    second_back = swap_tensor(hold(far), 1)
+    high = [mlp_grad(1, 0), mlp_grad(1, 1)]
+    down_own, down_other = mlp_down([hold(hidden[0]), *hidden[1:]], mlp_pieces)
+    close(second_back, *high[0], *high[1], down_own)
+
+    grad_second = near + hold(second_back).astype(F32)
     grad_middle = grad_final + norm_back(normed_two, inverse_two, grad_second, gain_second)
     grad_gain_two = jnp.sum(grad_second * normed_two, 0)
-
-    attn_slots = line_gather(grad_middle.astype(BF16))
-
-    final = middle + pair_scatter(lambda c: times_right(hidden[2 * c * rows : 2 * (c + 1) * rows], down_low))
-    output = to_global(jnp.where(valid, final, 0.0).astype(BF16))
-
-    def mlp_grad(left, right):
-        left = left.reshape(left.shape[0], 2, 2, 2, width // 8)
-
-        def group(part, end):
-            return jnp.stack([times_left(left[:, core, part, end], right) for core in range(2)])
-
-        total = jnp.concatenate(
-            [
-                scatter_half(group(0, 0), group(0, 1), up_bits),
-                scatter_half(group(1, 0), group(1, 1), down_bits),
-            ],
-            1,
-        )
-        low = total.astype(BF16)
-        core = lax.ppermute(low[1], both, [(b, a) for a, b in to_even + to_odd])
-        turn = lax.ppermute(low[0], both, [(b, a) for a, b in odd_turn])
-        return jnp.where(odd, turn.astype(F32), total[0]) + core.astype(F32)
-
-    sum_down = mlp_grad(grad_mlp_rows, hidden)
-    sum_mgate = mlp_grad(rows_two, grad_mgate_low)
-    sum_mup = mlp_grad(rows_two, grad_mup_low)
-
-    grad_mixed = [times_plain(slot, out_low).astype(BF16) for slot in attn_slots]
+    attn_own = grad_middle.astype(BF16)
+    attn_beside = swap_tensor(attn_own, 1)
+    attn_middle = move_tensor(attn_own, across)
+    come = [[sum_start(high[0][0], up_bits), sum_start(high[0][1], down_bits)]]
+    low = [mlp_grad(0, 0), mlp_grad(0, 1)]
+    close(attn_beside, attn_middle, *come[0], *low[0], *low[1])
+
+    attn_far = line_out(None, attn_beside, attn_middle)
+    come.append([sum_start(high[1][0], up_bits), sum_start(high[1][1], down_bits)])
+    down_core = to_core(down_other)
+    close(*attn_far, *come[1], down_core)
+
+    attn_last = move_tensor(hold(attn_far[0]), outward)
+    mlp_total = []
+    for core in range(2):
+        ends = []
+        for part, order in enumerate((up_bits, down_bits)):
+            ends.append(add(*sum_end(*sum_split(low[core][part], hold(come[core][part])), order)).astype(BF16))
+        mlp_total.append(jnp.concatenate(ends, 0))
+    down_sum = add(down_own, hold(down_core))
+    down_sent = down_sum[rows:].astype(BF16)
+    close(attn_last, *mlp_total, down_sent)
+    attn_slots = line_all(attn_own, attn_beside, attn_middle, *attn_far, attn_last)
+
+    grad_turn = lax.ppermute(hold(mlp_total[0]), both, [(b, a) for a, b in odd_turn])
+    down_beside = swap_tensor(hold(down_sent), 1)
+    grad_mixed = rows_times([hold(attn_slots[0]), *attn_slots[1:]], attn_low, proj_columns, out_columns)
     grad_proj = retain_back(
         grad_mixed, projected, normed_head, scale_head, query, key, value, place_arg, log_decay, cosines, sines, heads
     )
-
-    def attn_grad(left, right):
-        other = swap_dp(times_left(left[:, width // 2 :], right).astype(BF16), 1)
-        total = times_left(left[:, : width // 2], right) + other.astype(F32)
-        quarter = width // 8
-        return jnp.concatenate(
-            [
-                scatter_half(total[:quarter], total[quarter : 2 * quarter], up_bits),
-                scatter_half(total[2 * quarter : 3 * quarter], total[3 * quarter :], down_bits),
-            ],
-            0,
-        )
-
-    sum_out = cut_heads(attn_grad(jnp.concatenate(attn_slots, 0), mixed))
-    totals = [times_right(grad_proj[s * rows : (s + 1) * rows], proj_low) for s in range(tensor_size)]
-    gain_one_parts = sum(jnp.sum(t * a.astype(F32), 0) for t, a in zip(totals, first_slots)) / gain_first
-    grad_first = line_scatter(lambda s: totals[s])
+    back_second, back_third, gain_far = rows_back(grad_proj, (2, 3), attn_low, 0, first_slots[2:])
+    close(grad_turn, down_beside, back_third)
+
+    grad_core = lax.ppermute(hold(mlp_total[1]), both, [(b, a) for a, b in to_even + to_odd])
+    from_ends = move_tensor(hold(back_third), inward)
+    other_high = attn_grads(1, first_slots, hold(grad_proj))
+    other_low = attn_grads(0, first_slots, after(grad_proj, other_high))
+    core_high = swap_dp(other_high, 1)
+    close(grad_core, from_ends, core_high, other_low)
+
+    from_inner = move_tensor(add(back_second, hold(from_ends)).astype(BF16), across)
+    from_ends = move_tensor(hold(back_second), inward)
+    core_low = to_core(other_low)
+    up_high, down_high = attn_grads(1, first_slots, hold(grad_proj), core_high)
+    back_own, back_first, gain_near = rows_back(after(grad_proj, up_high), (0, 1), attn_low, 0, first_slots[:2])
+    close(from_inner, from_ends, core_low, back_own)
+
+    from_beside = swap_tensor(add(back_first, hold(from_inner)).astype(BF16), 1)
+    from_middle = move_tensor(add(back_third, hold(from_ends)).astype(BF16), across)
+    proj_come = sum_start(up_high, up_bits), sum_start(down_high, down_bits)
+    up_low, down_low = attn_grads(0, first_slots, hold(grad_proj), core_low)
+    out_other_high = attn_grads(1, attn_slots, after(mixed, up_low))
+    out_other_low = attn_grads(0, attn_slots, after(mixed, out_other_high))
+    out_up_high, out_down_high = attn_grads(1, attn_slots, after(mixed, out_other_low), swap_dp(out_other_high, 1))
+    out_up_low, out_down_low = attn_grads(0, attn_slots, after(mixed, out_up_high), swap_dp(out_other_low, 1))
+    close(from_beside, from_middle, *proj_come, out_up_low)
+
+    gains = to_global(jnp.stack([hold(gain_far[0] + gain_near[0]) / gain_first[0], grad_gain_two]))
+    gains = gains + swap_tensor(gains, 1)
+    gains = gains + swap_tensor(gains, 2)
+    gains = gains + swap_dp(gains, 1)
+    proj_up = sum_end(*sum_split(up_low, hold(proj_come[0])), up_bits)
+    proj_down = sum_end(*sum_split(down_low, hold(proj_come[1])), down_bits)
+    out_come = sum_start(out_up_high, up_bits), sum_start(out_down_high, down_bits)
+    grad_first = add(back_own, hold(from_beside), from_middle)
     grad_tokens = grad_middle + norm_back(normed_one, inverse_one, grad_first, gain_first)
     grad_tokens = to_global(grad_tokens.astype(BF16))
-
-    sum_proj = attn_grad(jnp.concatenate(first_slots, 0), grad_proj)
-    cuts = [heads * KEY, 2 * heads * KEY, 2 * heads * KEY + heads * VPAD]
-    sum_query, sum_key, sum_value, sum_gate = jnp.split(sum_proj, cuts, -1)
-
-    gains = to_global(jnp.stack([gain_one_parts, grad_gain_two]))
-    gains = gains + swap_tensor(gains, 1)
-    gains = gains + swap_tensor(gains, 2)
-    for bit in range(bits):
+    final = middle + down_sum[:rows] + hold(down_beside).astype(F32)
+    output = to_global(jnp.where(valid, final, 0.0).astype(BF16))
+    sum_mgate, sum_mup, sum_down = receive_mlp(
+        (mine & 1).astype(jnp.int32).reshape(1), hold(mlp_total[0]), grad_turn, grad_core, units
+    )
+    close(gains, *proj_up, *proj_down, *out_come, grad_tokens, output, sum_mgate)
+
+    out_up = sum_end(*sum_split(out_up_low, hold(out_come[0])), up_bits)
+    out_down = sum_end(*sum_split(out_down_low, hold(out_come[1])), down_bits)
+    gains = hold(gains)
+    for bit in range(1, bits):
         gains = gains + swap_dp(gains, 1 << bit)
+    sum_query, sum_key, sum_value, sum_gate = receive_attn(
+        (hold(proj_up[0]), proj_up[1], *proj_down), 2, 2, heads
+    )
+    (sum_out,) = receive_attn((*out_up, *out_down), 0, 1, heads)
     return (
         output,
         grad_tokens,
@@ -485,8 +937,8 @@
         gains[1],
         sum_query,
         sum_key,
-        cut_heads(sum_value),
-        cut_heads(sum_gate),
+        sum_value,
+        sum_gate,
         sum_out,
         sum_mgate,
         sum_mup,

time: 1050 us -> 713 us (0.68)
  matrix products: 212 us -> 0 us
  Pallas kernels: 26.5 us -> 219 us
  waiting for transfers between devices: 441 us -> 295 us
  local copies, waits for them, and re-layouts: 150 us -> 24.4 us
  other arithmetic: 79.7 us -> 44 us
    dot_general x53 -> x0, matrix products: 212 us -> none  [the longest x11 87 us: times_plain(): return jnp.dot(left, right, preferred_element_type=F32)]
    pallas_call x0 -> x31, Pallas kernels: none -> 193 us  [the longest x8 49.2 us: attn_grads(): pl.pallas_call(attn_grad_kernel if core else attn_grad_add_kernel, out_sh...]
    ppermute x26, waiting for transfers between devices: 237 us -> 146 us  [move_tensor(): return lax.ppermute(array, 'tensor', pairs)]
    ppermute x63 -> x50, waiting for transfers between devices: 204 us -> 129 us  [swap_dp(): return lax.ppermute(array, 'dp', [(i, i ^ mask) for i in range(dp_size)])]
    unnamed x338 -> x202, local copies, waits for them, and re-layouts: 74.6 us -> 22.5 us
    slice x25 -> x1, local copies, waits for them, and re-layouts: 31.9 us -> 1.25 us  [per_device(): down_sent = down_sum[rows:].astype(BF16)]
    concatenate x11 -> x2, other arithmetic: 29.2 us -> 1.24 us  [per_device(): mlp_total.append(jnp.concatenate(ends, 0))]
    concatenate x13 -> x0, local copies, waits for them, and re-layouts: 23.7 us -> none  [the longest x4 20.7 us: per_device(): jnp.concatenate([p[:, :, i * units:(i + 1) * units] for p in mlp_pieces], 1)]
  transfers between devices with their start and end apart: 97 -> 80, of which waited for: 40 -> 42; matrix products, arithmetic and copies ran while one was open for 32% -> 4% of each run, Pallas kernels for 1% -> 27%
where the time goes in v2:
time: 713 us; the launch traced here: 704 us
  waiting for transfers between devices  295 us (41%)
  Pallas kernels  219 us (31%)
  starting transfers between devices  119 us (17%)
  other arithmetic  44 us (6%)
  local copies, waits for them, and re-layouts  24.4 us (3%)
    ppermute x26, waiting for transfers between devices, move_tensor(): return lax.ppermute(array, 'tensor', pairs)  146 us
    ppermute x50, waiting for transfers between devices, swap_dp(): return lax.ppermute(array, 'dp', [(i, i ^ mask) for i in range(dp_size)])  129 us
    ppermute x26, starting transfers between devices, move_tensor(): return lax.ppermute(array, 'tensor', pairs)  55.9 us
    pallas_call x8, Pallas kernels, attn_grads(): pl.pallas_call(attn_grad_kernel if core else attn_grad_add_kernel, out_sh...  49.2 us
    ppermute x50, starting transfers between devices, swap_dp(): return lax.ppermute(array, 'dp', [(i, i ^ mask) for i in range(dp_size)])  46.6 us
    pallas_call x4, Pallas kernels, rows_back(): pl.pallas_call(partial(rows_back_kernel, len(slots), len(pieces), 1 if we...  40.3 us
    pallas_call x2, Pallas kernels, mlp(): pl.pallas_call(partial(mlp_kernel, len(pieces), units), out_shape=[small]...  32.9 us
    pallas_call x4, Pallas kernels, mlp_grads(): pl.pallas_call(mlp_grad_kernel, out_shape=[jax.ShapeDtypeStruct((tile, 3...  27.8 us
  transfers between devices with their start and end apart: 80, of which 42 were waited for; matrix products, arithmetic and copies ran while one was open for 4% of the time, Pallas kernels for 27%

profile of v2, /device:TPU:0, one launch (start us, length us, event | category | flops | bytes accessed | tf_op | source)
XLA Modules:
  0.0 704.4 jit_solution(7659373025738783584)
XLA Ops:
  23.6 8.8 %collective-permute-done.refs_5_.refs_3_ = bf16[128,4096]{1,0:T(8,128)(2,1)} collective-permute-done((bf16[128,4096]{1,0:T(8,128)(2,1)S(1)}, bf16[128,4096]{1,0:T(8,128)(2,1)}, u32[]{:S(2)}, u32[]{:S(2)}) %collective-permute-start) | collective-permute-done | bytes 1048608 | tf_op jit(solution)/shard_map/ppermute | solution.py:637
  33.9 4.4 collective-permute-done.2.refs_1_.refs_19_
  42.2 21.7 %collective-permute-done.4.refs_6_.refs_4_ = bf16[128,4096]{1,0:T(8,128)(2,1)} collective-permute-done((bf16[128,4096]{1,0:T(8,128)(2,1)S(1)}, bf16[128,4096]{1,0:T(8,128)(2,1)}, u32[]{:S(2)}, u32[]{:S(2)}) %collective-permute-start.4) | collective-permute-done | bytes 1048608 | tf_op jit(solution)/shard_map/ppermute | solution.py:637
  64.4 3.7 collective-permute-done.7
  72.7 21.3 %collective-permute-done.10.refs_7_.refs_5_ = bf16[128,4096]{1,0:T(8,128)(2,1)S(1)} collective-permute-done((bf16[128,4096]{1,0:T(8,128)(2,1)}, bf16[128,4096]{1,0:T(8,128)(2,1)S(1)}, u32[]{:S(2)}, u32[]{:S(2)}) %collective-permute-start.10) | collective-permute-done | bytes 1048608 | tf_op jit(solution)/shard_map/ppermute | solution.py:637
  109.8 17.8 %shard_map.242 = (bf16[256,3072]{1,0:T(8,128)(2,1)}, bf16[256,3072]{1,0:T(8,128)(2,1)}, bf16[256,3072]{1,0:T(8,128)(2,1)}, bf16[256,3072]{1,0:T(8,128)(2,1)}) custom-call(bf16[256,2048]{1,0:T(8,128)(2,1)S(1)} %fusion.5.refs_0_.refs_18_, bf16[256,2048]{1,0:T(8,128)(2,1)} %collective-permute-done.2.refs_1_.refs_19_, ...), custom_call_target="tpu_custom_call" | custom-call | flops 3221225472 | bytes 3145728 | tf_op jit(solution)/shard_map/pallas_call | solution.py:245
  129.0 10.3 %shard_map.243 = (bf16[1024,512]{1,0:T(8,128)(2,1)S(1)}, bf16[1024,512]{1,0:T(8,128)(2,1)S(1)}, bf16[1024,1024]{1,0:T(8,128)(2,1)}, bf16[1024,1024]{1,0:T(8,128)...) custom-call(s32[1]{0:T(128)} %bitcast.3.place_ref, f32[2]{0:T(128)S(1)} %subtract_log_fusion.decay_ref, ...), custom_call_target="tpu_custom_call" | custom-call | flops 402653184 | bytes 4608000 | tf_op jit(solution)/shard_map/pallas_call | solution.py:125
  142.3 7.0 shard_map.244
  150.3 5.2 collective-permute-start.22
  155.5 14.4 %collective-permute-start.23 = (bf16[256,2688]{1,0:T(8,128)(2,1)S(1)}, bf16[256,2688]{1,0:T(8,128)(2,1)}, u32[]{:S(2)}, u32[]{:S(2)}) collective-permute-start(bf16[256,2688]{1,0:T(8,128)(2,1)S(1)} %copy-done.26), channel_id=1, source_target_pairs={{4,0},{5,1},{6,2},{7,3},{12,8},{13,9},{14,10},{15,11},{20,16},{21,... | collective-permute-start | bytes 4128776 | tf_op jit(solution)/shard_map/ppermute | solution.py:790
  170.0 5.2 shard_map.245
  178.4 14.7 %collective-permute-done.23 = bf16[256,2688]{1,0:T(8,128)(2,1)} collective-permute-done((bf16[256,2688]{1,0:T(8,128)(2,1)S(1)}, bf16[256,2688]{1,0:T(8,128)(2,1)}, u32[]{:S(2)}, u32[]{:S(2)}) %collective-permute-start.23) | collective-permute-done | bytes 1376288 | tf_op jit(solution)/shard_map/ppermute | solution.py:790
  197.0 10.3 %collective-permute-start.28 = (bf16[256,2048]{1,0:T(8,128)(2,1)S(1)}, bf16[256,2048]{1,0:T(8,128)(2,1)S(1)}, u32[]{:S(2)}, u32[]{:S(2)}) collective-permute-start(bf16[256,2048]{1,0:T(8,128)(2,1)S(1)} %copy-done.49), channel_id=1, source_target_pairs={{0,1},{3,2},{4,5},{7,6},{8,9},{11,10},{12,13},{15,14},{16,17},{19,... | collective-permute-start | bytes 3145736 | tf_op jit(solution)/shard_map/ppermute | solution.py:640
  207.3 22.5 %collective-permute-done.28 = bf16[256,2048]{1,0:T(8,128)(2,1)S(1)} collective-permute-done((bf16[256,2048]{1,0:T(8,128)(2,1)S(1)}, bf16[256,2048]{1,0:T(8,128)(2,1)S(1)}, u32[]{:S(2)}, u32[]{:S(2)}) %collective-permute-start.28) | collective-permute-done | bytes 1048608 | tf_op jit(solution)/shard_map/ppermute | solution.py:640
  232.6 3.7 collective-permute-start.29
  239.2 21.0 %collective-permute-done.29 = bf16[256,2048]{1,0:T(8,128)(2,1)S(1)} collective-permute-done((bf16[256,2048]{1,0:T(8,128)(2,1)S(1)}, bf16[256,2048]{1,0:T(8,128)(2,1)S(1)}, u32[]{:S(2)}, u32[]{:S(2)}) %collective-permute-start.29) | collective-permute-done | bytes 1048608 | tf_op jit(solution)/shard_map/ppermute | solution.py:640
  261.7 7.7 %collective-permute-done.31.refs_2_.refs_6_ = bf16[2,128,2688]{2,1,0:T(8,128)(2,1)S(1)} collective-permute-done((bf16[2,128,2688]{2,1,0:T(8,128)(2,1)S(1)}, bf16[2,128,2688]{2,1,0:T(8,128)(2,1)S(1)}, u32[]{:S(2)}, u32[]{:S(2)}) %collective-permute-start.31) | collective-permute-done | bytes 1376288 | tf_op jit(solution)/shard_map/ppermute | solution.py:637
  275.3 23.5 %collective-permute-done.35.own_ref.refs_1_ = bf16[256,2048]{1,0:T(8,128)(2,1)S(1)} collective-permute-done((bf16[256,2048]{1,0:T(8,128)(2,1)S(1)}, bf16[256,2048]{1,0:T(8,128)(2,1)S(1)}, u32[]{:S(2)}, u32[]{:S(2)}) %collective-permute-start.35) | collective-permute-done | bytes 1048608 | tf_op jit(solution)/shard_map/ppermute | solution.py:640
  303.2 16.2 %shard_map.246 = (bf16[256,896]{1,0:T(8,128)(2,1)S(1)}, bf16[256,896]{1,0:T(8,128)(2,1)S(1)}, bf16[256,896]{1,0:T(8,128)(2,1)S(1)}, bf16[256,896]{1,0:T(8,128)(2...) custom-call(bf16[256,2048]{1,0:T(8,128)(2,1)S(1)} %multiply_convert_, ...), custom_call_target="tpu_custom_call" | custom-call | flops 2348810240 | bytes 2752512 | tf_op jit(solution)/shard_map/pallas_call | solution.py:358
  322.1 16.7 %shard_map.247 = (bf16[256,896]{1,0:T(8,128)(2,1)S(1)}, bf16[256,896]{1,0:T(8,128)(2,1)S(1)}, bf16[256,896]{1,0:T(8,128)(2,1)S(1)}, bf16[256,896]{1,0:T(8,128)(2...) custom-call(bf16[256,2048]{1,0:T(8,128)(2,1)S(1)} %collective-permut, ...), custom_call_target="tpu_custom_call" | custom-call | flops 2348810240 | bytes 2752512 | tf_op jit(solution)/shard_map/pallas_call | solution.py:358
  344.8 6.8 shard_map.250
  351.7 7.0 shard_map.249
  358.8 8.0 %shard_map.248 = (bf16[512,2048]{1,0:T(8,128)(2,1)}, bf16[512,2048]{1,0:T(8,128)(2,1)}) custom-call(bf16[256,896]{1,0:T(8,128)(2,1)S(1)} %get-tuple-element.272.refs_0_.refs_16_, bf16[256,896]{1,0:T(8,128)(2,1)S(1)} %get-tuple-element.273.refs_1_.refs_17_, bf16[256,896]{1,0:T(8,128)(2,1)S(1)} %get-tuple-element.274.refs_2_.refs_18_, ...), custom_call_target="tpu_custom_call" | custom-call | flops 939524096 | bytes 917504 | tf_op jit(solution)/shard_map/pallas_call | solution.py:384
  373.8 3.9 fusion.18
  378.4 4.5 collective-permute-start.41
  382.9 7.1 %shard_map.252 = (bf16[256,2688]{1,0:T(8,128)(2,1)}, bf16[256,2688]{1,0:T(8,128)(2,1)}) custom-call(bf16[256,2048]{1,0:T(8,128)(2,1)} %copy-done.15, bf16[256,2048]{1,0:T(8,128)(2,1)} %copy-done.16, bf16[256,2048]{1,0:T(8,128)(2,1)} %copy-done.75, bf16[256,2048]{1,0:T(8,128)(2,1)} %copy-done.76, bf16[256,2048]{1,0:T(8,128)(2,1)} %broadcast_select_fusion.own_grad_ref.refs_4_, ...), custom_call_target="tpu_custom_call" | custom-call | flops 704643072 | bytes 917504 | tf_op jit(solution)/shard_map/pallas_call | solution.py:421
  389.9 6.9 shard_map.251
  396.8 7.9 %collective-permute-done.41.refs_1_ = bf16[256,2048]{1,0:T(8,128)(2,1)S(1)} collective-permute-done((bf16[256,2048]{1,0:T(8,128)(2,1)S(1)}, bf16[256,2048]{1,0:T(8,128)(2,1)S(1)}, u32[]{:S(2)}, u32[]{:S(2)}) %collective-permute-start.41) | collective-permute-done | bytes 1048608 | tf_op jit(solution)/shard_map/ppermute | solution.py:640
  408.0 27.3 %collective-permute-done.47 = bf16[256,2048]{1,0:T(8,128)(2,1)S(1)} collective-permute-done((bf16[256,2048]{1,0:T(8,128)(2,1)S(1)}, bf16[256,2048]{1,0:T(8,128)(2,1)S(1)}, u32[]{:S(2)}, u32[]{:S(2)}) %collective-permute-start.47) | collective-permute-done | bytes 1048608 | tf_op jit(solution)/shard_map/ppermute | solution.py:640
  448.5 10.7 %collective-permute-done.54 = bf16[128,2688]{1,0:T(8,128)(2,1)S(1)} collective-permute-done((bf16[128,2688]{1,0:T(8,128)(2,1)S(1)}, bf16[128,2688]{1,0:T(8,128)(2,1)S(1)}, u32[]{:S(2)}, u32[]{:S(2)}) %collective-permute-start.54) | collective-permute-done | bytes 688160 | tf_op jit(solution)/shard_map/ppermute | solution.py:637
  462.2 10.1 %collective-permute-done.52 = bf16[128,2688]{1,0:T(8,128)(2,1)S(1)} collective-permute-done((bf16[128,2688]{1,0:T(8,128)(2,1)S(1)}, bf16[128,2688]{1,0:T(8,128)(2,1)S(1)}, u32[]{:S(2)}, u32[]{:S(2)}) %collective-permute-start.52) | collective-permute-done | bytes 688160 | tf_op jit(solution)/shard_map/ppermute | solution.py:637
  477.9 7.2 %shard_map.253 = (bf16[256,1024]{1,0:T(8,128)(2,1)S(1)}, bf16[256,1024]{1,0:T(8,128)(2,1)S(1)}, bf16[256,1024]{1,0:T(8,128)(2,1)S(1)}, bf16[256,1024]{1,0:T(8,128)(2,1)S(1)}) custom-call(bf16[256,2048]{1,0:T(8,128)(2,1)S(1)} %get-tuple-element.322.refs_0_, bf16[256,2048]{1,0:T(8,128)(2,1)S(1)} %collective-permute-done.41.refs_1_, ...), custom_call_target="tpu_custom_call" | custom-call | flops 1073741824 | bytes 1048576 | tf_op jit(solution)/shard_map/pallas_call | solution.py:245
  485.2 16.0 %shard_map.254.refs_0_.refs_1_.refs_4_ = bf16[1024,3072]{1,0:T(8,128)(2,1)} custom-call(s32[1]{0:T(128)} %bitcast.3.place_ref, f32[2]{0:T(128)S(1)} %subtract_log_fusion.decay_ref, bf16[256,1024]{1,0:T(8,128)(2,1)S(1)} %get-tuple-element.323.refs_0_, bf16[256,1024]{1,0:T(8,128)(2,1)S(1)} %get-tuple-element.324.refs_1_, ...), custom_call_target="tpu_custom_call" | custom-call | flops 939524096 | bytes 5120000 | tf_op jit(solution)/shard_map/pallas_call | solution.py:212
  501.2 14.6 %shard_map.255 = (bf16[256,2048]{1,0:T(8,128)(2,1)}, bf16[256,2048]{1,0:T(8,128)(2,1)S(1)}, f32[8,2048]{1,0:T(8,128)S(1)}) custom-call(bf16[1024,3072]{1,0:T(8,128)(2,1)} %shard_map.254.refs_0_.refs_1_.refs_4_, bf16[1024,3072]{1,0:T(8,128)(2,1)} %shard_map.254.refs_0_.refs_1_.refs_4_, bf16[128,4096]{1,0:T(8,128)(2,1)S(1)} %copy-done.10, ...), custom_call_target="tpu_custom_call" | custom-call | flops 1610612736 | bytes 3145728 | tf_op jit(solution)/shard_map/pallas_call | solution.py:288
  515.9 8.6 %shard_map.256 = bf16[512,3072]{1,0:T(8,128)(2,1)} custom-call(bf16[256,2048]{1,0:T(8,128)(2,1)S(1)} %fusion.5.refs_0_.refs_18_, bf16[256,2048]{1,0:T(8,128)(2,1)} %collective-permute-done.2.refs_1_.refs_19_, bf16[256,2048]{1,0:T(8,128)(2,1)S(1)} %copy-done.3, bf16[256,2048]{1,0:T(8,128)(2,1)S(1)} %copy-done.5, ...), custom_call_target="tpu_custom_call" | custom-call | flops 805306368 | bytes 1572864 | tf_op jit(solution)/shard_map/pallas_call | solution.py:455
  527.2 8.1 %shard_map.257 = bf16[512,3072]{1,0:T(8,128)(2,1)} custom-call(bf16[256,2048]{1,0:T(8,128)(2,1)S(1)} %fusion.5.refs_0_.refs_18_, bf16[256,2048]{1,0:T(8,128)(2,1)} %collective-permute-done.2.refs_1_.refs_19_, bf16[256,2048]{1,0:T(8,128)(2,1)S(1)} %copy-done.3, bf16[256,2048]{1,0:T(8,128)(2,1)S(1)} %copy-done.5, ...), custom_call_target="tpu_custom_call" | custom-call | flops 805306368 | bytes 1572864 | tf_op jit(solution)/shard_map/pallas_call | solution.py:455
  535.4 15.3 %collective-permute-done.58 = bf16[256,2048]{1,0:T(8,128)(2,1)S(1)} collective-permute-done((bf16[256,2048]{1,0:T(8,128)(2,1)S(1)}, bf16[256,2048]{1,0:T(8,128)(2,1)S(1)}, u32[]{:S(2)}, u32[]{:S(2)}) %collective-permute-start.58) | collective-permute-done | bytes 1048608 | tf_op jit(solution)/shard_map/ppermute | solution.py:640
  550.6 5.3 collective-permute-done.57.core
  555.9 9.3 %collective-permute-start.62 = (bf16[512,3072]{1,0:T(8,128)(2,1)}, bf16[512,3072]{1,0:T(8,128)(2,1)}, u32[]{:S(2)}, u32[]{:S(2)}) collective-permute-start(bf16[512,3072]{1,0:T(8,128)(2,1)} %shard_map.257), channel_id=1, source_target_pairs={{0,4},{4,0},{8,12},{12,8},{16,20},{20,16},{24,28},{28,24},{1,5},{5... | collective-permute-start | bytes 9437192 | tf_op jit(solution)/shard_map/ppermute | solution.py:637
  568.5 6.1 collective-permute-start.61
  574.6 8.5 %shard_map.258 = (bf16[256,3072]{1,0:T(8,128)(2,1)S(1)}, bf16[256,3072]{1,0:T(8,128)(2,1)}) custom-call(bf16[256,2048]{1,0:T(8,128)(2,1)S(1)} %fusion.5.refs_0_.refs_18_, bf16[256,2048]{1,0:T(8,128)(2,1)} %collective-permute-done.2.refs_1_.refs_19_, bf16[256,2048]{1,0:T(8,128)(2,1)S(1)} %copy-done.3, bf16[256,2048]{1,0:T(8,128)(2,1)S(1)} %copy-done.5, ...), custom_call_target="tpu_custom_call" | custom-call | flops 805306368 | bytes 1572864 | tf_op jit(solution)/shard_map/pallas_call | solution.py:455
  584.3 13.5 %shard_map.259 = (bf16[256,2048]{1,0:T(8,128)(2,1)S(1)}, bf16[256,2048]{1,0:T(8,128)(2,1)S(1)}, f32[8,2048]{1,0:T(8,128)S(1)}) custom-call(bf16[1024,3072]{1,0:T(8,128)(2,1)} %shard_map.254.refs_0_.refs_1_.refs_4_, bf16[1024,3072]{1,0:T(8,128)(2,1)} %shard_map.254.refs_0_.refs_1_.refs_4_, bf16[128,4096]{1,0:T(8,128)(2,1)S(1)} %copy-done.10, ...), custom_call_target="tpu_custom_call" | custom-call | flops 1610612736 | bytes 3145728 | tf_op jit(solution)/shard_map/pallas_call | solution.py:288
  598.9 9.3 %shard_map.260 = (bf16[256,3072]{1,0:T(8,128)(2,1)S(1)}, bf16[256,3072]{1,0:T(8,128)(2,1)}) custom-call(bf16[256,2048]{1,0:T(8,128)(2,1)S(1)} %copy-done.1, bf16[256,2048]{1,0:T(8,128)(2,1)} %collective-permute-done.2.refs_1_.refs_19_, bf16[256,2048]{1,0:T(8,128)(2,1)S(1)} %copy-done.3, bf16[256,2048]{1,0:T(8,128)(2,1)S(1)} %copy-done.5, ...), custom_call_target="tpu_custom_call" | custom-call | flops 805306368 | bytes 1572864 | tf_op jit(solution)/shard_map/pallas_call | solution.py:455
  625.6 4.6 shard_map.263
  630.2 3.6 shard_map.264
  633.8 14.3 %collective-permute-done.63 = bf16[256,2048]{1,0:T(8,128)(2,1)S(1)} collective-permute-done((bf16[256,2048]{1,0:T(8,128)(2,1)}, bf16[256,2048]{1,0:T(8,128)(2,1)S(1)}, u32[]{:S(2)}, u32[]{:S(2)}) %collective-permute-start.63) | collective-permute-done | bytes 1048608 | tf_op jit(solution)/shard_map/ppermute | solution.py:640
  648.1 4.9 collective-permute-done.65
  674.4 16.6 %collective-permute-done.74 = bf16[256,1024]{1,0:T(8,128)(2,1)S(1)} collective-permute-done((bf16[256,1024]{1,0:T(8,128)(2,1)}, bf16[256,1024]{1,0:T(8,128)(2,1)S(1)}, u32[]{:S(2)}, u32[]{:S(2)}) %collective-permute-start.74) | collective-permute-done | bytes 524320 | tf_op jit(solution)/shard_map/ppermute | solution.py:637
  (408 shorter events, 179.4 us)
Async XLA Ops:
  6.1 26.3 %collective-permute-start = (bf16[128,4096]{1,0:T(8,128)(2,1)S(1)}, bf16[128,4096]{1,0:T(8,128)(2,1)}, u32[]{:S(2)}, u32[]{:S(2)}) collective-permute-start(bf16[128,4096]{1,0:T(8,128)(2,1)S(1)} %get-tuple-element.214.refs_4_.refs_2_), channel_id=1, source_target_pairs={{0,8},{4,12},{8,0},{12,4},{16,24},{20,28},{24,16},{28,20},{1,9},{5... | collective-permute-start | bytes 3145736 | tf_op jit(solution)/shard_map/ppermute | solution.py:637
  12.3 25.9 %collective-permute-start.2 = (bf16[256,2048]{1,0:T(8,128)(2,1)S(1)}, bf16[256,2048]{1,0:T(8,128)(2,1)}, u32[]{:S(2)}, u32[]{:S(2)}) collective-permute-start(bf16[256,2048]{1,0:T(8,128)(2,1)S(1)} %fusion.5.refs_0_.refs_18_), channel_id=1, source_target_pairs={{0,1},{1,0},{2,3},{3,2},{4,5},{5,4},{6,7},{7,6},{8,9},{9,8},{10,11... | collective-permute-start | bytes 3145736 | tf_op jit(solution)/shard_map/ppermute | solution.py:640
  38.2 25.7 %collective-permute-start.4 = (bf16[128,4096]{1,0:T(8,128)(2,1)S(1)}, bf16[128,4096]{1,0:T(8,128)(2,1)}, u32[]{:S(2)}, u32[]{:S(2)}) collective-permute-start(bf16[128,4096]{1,0:T(8,128)(2,1)S(1)} %get-tuple-element.214.refs_4_.refs_2_), channel_id=1, source_target_pairs={{0,16},{4,20},{8,24},{12,28},{16,0},{20,4},{24,8},{28,12},{1,17},{... | collective-permute-start | bytes 3145736 | tf_op jit(solution)/shard_map/ppermute | solution.py:637
  38.7 25.2 %collective-permute-start.9 = (bf16[128,4096]{1,0:T(8,128)(2,1)S(1)}, bf16[128,4096]{1,0:T(8,128)(2,1)S(1)}, u32[]{:S(2)}, u32[]{:S(2)}) collective-permute-start(bf16[128,4096]{1,0:T(8,128)(2,1)S(1)} %get-tuple-element.215.refs_8_.refs_6_), channel_id=1, source_target_pairs={{0,4},{4,0},{8,12},{12,8},{16,20},{20,16},{24,28},{28,24},{1,5},{5... | collective-permute-start | bytes 3145736 | tf_op jit(solution)/shard_map/ppermute | solution.py:637
  39.0 25.5 %collective-permute-start.5 = (bf16[128,4096]{1,0:T(8,128)(2,1)S(1)}, bf16[128,4096]{1,0:T(8,128)(2,1)}, u32[]{:S(2)}, u32[]{:S(2)}) collective-permute-start(bf16[128,4096]{1,0:T(8,128)(2,1)S(1)} %get-tuple-element.215.refs_8_.refs_6_), channel_id=1, source_target_pairs={{0,8},{4,12},{8,0},{12,4},{16,24},{20,28},{24,16},{28,20},{1,9},{5... | collective-permute-start | bytes 3145736 | tf_op jit(solution)/shard_map/ppermute | solution.py:637
  39.5 24.9 %collective-permute-start.6 = (bf16[256,2048]{1,0:T(8,128)(2,1)}, bf16[256,2048]{1,0:T(8,128)(2,1)S(1)}, u32[]{:S(2)}, u32[]{:S(2)}) collective-permute-start(bf16[256,2048]{1,0:T(8,128)(2,1)} %collective-permute-done.2.refs_1_.refs_19_), channel_id=1, source_target_pairs={{1,2},{2,1},{5,6},{6,5},{9,10},{10,9},{13,14},{14,13},{17,18},{18,... | collective-permute-start | bytes 3145736 | tf_op jit(solution)/shard_map/ppermute | solution.py:640
  40.9 27.3 %collective-permute-start.7 = (bf16[256,2048]{1,0:T(8,128)(2,1)}, bf16[256,2048]{1,0:T(8,128)(2,1)S(1)}, u32[]{:S(2)}, u32[]{:S(2)}) collective-permute-start(bf16[256,2048]{1,0:T(8,128)(2,1)} %collective-permute-done.3), channel_id=1, source_target_pairs={{1,0},{2,3},{5,4},{6,7},{9,8},{10,11},{13,12},{14,15},{17,16},{18,... | collective-permute-start | bytes 3145736 | tf_op jit(solution)/shard_map/ppermute | solution.py:640
  68.2 25.8 %collective-permute-start.10 = (bf16[128,4096]{1,0:T(8,128)(2,1)}, bf16[128,4096]{1,0:T(8,128)(2,1)S(1)}, u32[]{:S(2)}, u32[]{:S(2)}) collective-permute-start(bf16[128,4096]{1,0:T(8,128)(2,1)} %collective-permute-done.refs_5_.refs_3_), channel_id=1, source_target_pairs={{0,16},{4,20},{8,24},{12,28},{16,0},{20,4},{24,8},{28,12},{1,17},{... | collective-permute-start | bytes 3145736 | tf_op jit(solution)/shard_map/ppermute | solution.py:637
  69.9 25.7 %collective-permute-start.11 = (bf16[128,4096]{1,0:T(8,128)(2,1)}, bf16[128,4096]{1,0:T(8,128)(2,1)}, u32[]{:S(2)}, u32[]{:S(2)}) collective-permute-start(bf16[128,4096]{1,0:T(8,128)(2,1)} %collective-permute-done.1.refs_9_.refs_7_), channel_id=1, source_target_pairs={{0,8},{4,12},{8,0},{12,4},{16,24},{20,28},{24,16},{28,20},{1,9},{5... | collective-permute-start | bytes 3145736 | tf_op jit(solution)/shard_map/ppermute | solution.py:637
  71.4 27.0 %collective-permute-start.12 = (bf16[256,2048]{1,0:T(8,128)(2,1)S(1)}, bf16[256,2048]{1,0:T(8,128)(2,1)S(1)}, u32[]{:S(2)}, u32[]{:S(2)}) collective-permute-start(bf16[256,2048]{1,0:T(8,128)(2,1)S(1)} %collective-permute-done.6), channel_id=1, source_target_pairs={{1,0},{2,3},{5,4},{6,7},{9,8},{10,11},{13,12},{14,15},{17,16},{18,... | collective-permute-start | bytes 3145736 | tf_op jit(solution)/shard_map/ppermute | solution.py:640
  105.9 36.4 %collective-permute-start.21 = (bf16[256,2048]{1,0:T(8,128)(2,1)}, bf16[256,2048]{1,0:T(8,128)(2,1)S(1)}, u32[]{:S(2)}, u32[]{:S(2)}) collective-permute-start(bf16[256,2048]{1,0:T(8,128)(2,1)} %broadcast_select_fusion.own_grad_ref.refs_4_), channel_id=1, source_target_pairs={{0,4},{4,0},{8,12},{12,8},{16,20},{20,16},{24,28},{28,24},{1,5},{5... | collective-permute-start | bytes 3145736 | tf_op jit(solution)/shard_map/ppermute | solution.py:637
  106.1 36.2 %collective-permute-start.20 = (bf16[256,2048]{1,0:T(8,128)(2,1)}, bf16[256,2048]{1,0:T(8,128)(2,1)}, u32[]{:S(2)}, u32[]{:S(2)}) collective-permute-start(bf16[256,2048]{1,0:T(8,128)(2,1)} %broadcast_select_fusion.own_grad_ref.refs_4_), channel_id=1, source_target_pairs={{0,1},{1,0},{2,3},{3,2},{4,5},{5,4},{6,7},{7,6},{8,9},{9,8},{10,11... | collective-permute-start | bytes 3145736 | tf_op jit(solution)/shard_map/ppermute | solution.py:640
  106.1 36.2 %collective-permute-start.19 = (bf16[256,2688]{1,0:T(8,128)(2,1)}, bf16[256,2688]{1,0:T(8,128)(2,1)S(1)}, u32[]{:S(2)}, u32[]{:S(2)}) collective-permute-start(bf16[256,2688]{1,0:T(8,128)(2,1)} %copy-done.25), channel_id=1, source_target_pairs={{4,7},{5,6},{6,5},{7,4},{12,15},{13,14},{14,13},{15,12},{20,23},{2... | collective-permute-start | bytes 4128776 | tf_op jit(solution)/shard_map/ppermute | solution.py:781
  150.3 26.5 %collective-permute-start.22 = (bf16[256,2048]{1,0:T(8,128)(2,1)}, bf16[256,2048]{1,0:T(8,128)(2,1)}, u32[]{:S(2)}, u32[]{:S(2)}) collective-permute-start(bf16[256,2048]{1,0:T(8,128)(2,1)} %get-tuple-element.238), channel_id=1, source_target_pairs={{0,1},{3,2},{4,5},{7,6},{8,9},{11,10},{12,13},{15,14},{16,17},{19,... | collective-permute-start | bytes 3145736 | tf_op jit(solution)/shard_map/ppermute | solution.py:640
  155.5 37.5 %collective-permute-start.23 = (bf16[256,2688]{1,0:T(8,128)(2,1)S(1)}, bf16[256,2688]{1,0:T(8,128)(2,1)}, u32[]{:S(2)}, u32[]{:S(2)}) collective-permute-start(bf16[256,2688]{1,0:T(8,128)(2,1)S(1)} %copy-done.26), channel_id=1, source_target_pairs={{4,0},{5,1},{6,2},{7,3},{12,8},{13,9},{14,10},{15,11},{20,16},{21,... | collective-permute-start | bytes 4128776 | tf_op jit(solution)/shard_map/ppermute | solution.py:790
  194.9 34.9 %collective-permute-start.26 = (bf16[2,128,2688]{2,1,0:T(8,128)(2,1)S(1)}, bf16[2,128,2688]{2,1,0:T(8,128)(2,1)S(1)}, u32[]{:S(2)}, u32[]{:S(2)}) collective-permute-start(bf16[2,128,2688]{2,1,0:T(8,128)(2,1)S(1)} %pad_maximum_fusion.refs_0_.refs_4_), channel_id=1, source_target_pairs={{0,8},{4,12},{8,0},{12,4},{16,24},{20,28},{24,16},{28,20},{1,9},{5... | collective-permute-start | bytes 4128776 | tf_op jit(solution)/shard_map/ppermute | solution.py:637
  195.6 34.2 %collective-permute-start.27 = (bf16[2,128,2688]{2,1,0:T(8,128)(2,1)S(1)}, bf16[2,128,2688]{2,1,0:T(8,128)(2,1)S(1)}, u32[]{:S(2)}, u32[]{:S(2)}) collective-permute-start(bf16[2,128,2688]{2,1,0:T(8,128)(2,1)S(1)} %pad_maximum_fusion.1.refs_4_.refs_8_), channel_id=1, source_target_pairs={{0,16},{4,20},{8,24},{12,28},{16,0},{20,4},{24,8},{28,12},{1,17},{... | collective-permute-start | bytes 4128776 | tf_op jit(solution)/shard_map/ppermute | solution.py:637
  197.0 32.8 %collective-permute-start.28 = (bf16[256,2048]{1,0:T(8,128)(2,1)S(1)}, bf16[256,2048]{1,0:T(8,128)(2,1)S(1)}, u32[]{:S(2)}, u32[]{:S(2)}) collective-permute-start(bf16[256,2048]{1,0:T(8,128)(2,1)S(1)} %copy-done.49), channel_id=1, source_target_pairs={{0,1},{3,2},{4,5},{7,6},{8,9},{11,10},{12,13},{15,14},{16,17},{19,... | collective-permute-start | bytes 3145736 | tf_op jit(solution)/shard_map/ppermute | solution.py:640
  232.6 27.5 %collective-permute-start.29 = (bf16[256,2048]{1,0:T(8,128)(2,1)S(1)}, bf16[256,2048]{1,0:T(8,128)(2,1)S(1)}, u32[]{:S(2)}, u32[]{:S(2)}) collective-permute-start(bf16[256,2048]{1,0:T(8,128)(2,1)S(1)} %add_convert_fusion.5), channel_id=1, source_target_pairs={{0,1},{1,0},{2,3},{3,2},{4,5},{5,4},{6,7},{7,6},{8,9},{9,8},{10,11... | collective-permute-start | bytes 3145736 | tf_op jit(solution)/shard_map/ppermute | solution.py:640
  237.0 32.4 %collective-permute-start.31 = (bf16[2,128,2688]{2,1,0:T(8,128)(2,1)S(1)}, bf16[2,128,2688]{2,1,0:T(8,128)(2,1)S(1)}, u32[]{:S(2)}, u32[]{:S(2)}) collective-permute-start(bf16[2,128,2688]{2,1,0:T(8,128)(2,1)S(1)} %pad_maximum_fusion.refs_0_.refs_4_), channel_id=1, source_target_pairs={{0,16},{4,20},{8,24},{12,28},{16,0},{20,4},{24,8},{28,12},{1,17},{... | collective-permute-start | bytes 4128776 | tf_op jit(solution)/shard_map/ppermute | solution.py:637
  237.7 32.0 %collective-permute-start.32 = (bf16[2,128,2688]{2,1,0:T(8,128)(2,1)S(1)}, bf16[2,128,2688]{2,1,0:T(8,128)(2,1)S(1)}, u32[]{:S(2)}, u32[]{:S(2)}) collective-permute-start(bf16[2,128,2688]{2,1,0:T(8,128)(2,1)S(1)} %pad_maximum_fusion.1.refs_4_.refs_8_), channel_id=1, source_target_pairs={{0,8},{4,12},{8,0},{12,4},{16,24},{20,28},{24,16},{28,20},{1,9},{5... | collective-permute-start | bytes 4128776 | tf_op jit(solution)/shard_map/ppermute | solution.py:637
  269.7 31.4 %collective-permute-start.33 = (bf16[2,128,2688]{2,1,0:T(8,128)(2,1)S(1)}, bf16[2,128,2688]{2,1,0:T(8,128)(2,1)S(1)}, u32[]{:S(2)}, u32[]{:S(2)}) collective-permute-start(bf16[2,128,2688]{2,1,0:T(8,128)(2,1)S(1)} %collective-permute-done.26.refs_1_.refs_5_), channel_id=1, source_target_pairs={{0,16},{4,20},{8,24},{12,28},{16,0},{20,4},{24,8},{28,12},{1,17},{... | collective-permute-start | bytes 4128776 | tf_op jit(solution)/shard_map/ppermute | solution.py:637
  271.2 30.9 %collective-permute-start.34 = (bf16[2,128,2688]{2,1,0:T(8,128)(2,1)S(1)}, bf16[2,128,2688]{2,1,0:T(8,128)(2,1)S(1)}, u32[]{:S(2)}, u32[]{:S(2)}) collective-permute-start(bf16[2,128,2688]{2,1,0:T(8,128)(2,1)S(1)} %collective-permute-done.27.refs_5_.refs_9_), channel_id=1, source_target_pairs={{0,8},{4,12},{8,0},{12,4},{16,24},{20,28},{24,16},{28,20},{1,9},{5... | collective-permute-start | bytes 4128776 | tf_op jit(solution)/shard_map/ppermute | solution.py:637
  272.7 26.1 %collective-permute-start.35 = (bf16[256,2048]{1,0:T(8,128)(2,1)S(1)}, bf16[256,2048]{1,0:T(8,128)(2,1)S(1)}, u32[]{:S(2)}, u32[]{:S(2)}) collective-permute-start(bf16[256,2048]{1,0:T(8,128)(2,1)S(1)} %multiply_convert_fusion.own_ref.refs_0_), channel_id=1, source_target_pairs={{0,1},{1,0},{2,3},{3,2},{4,5},{5,4},{6,7},{7,6},{8,9},{9,8},{10,11... | collective-permute-start | bytes 3145736 | tf_op jit(solution)/shard_map/ppermute | solution.py:640
  342.9 25.7 %collective-permute-start.40 = (bf16[256,2048]{1,0:T(8,128)(2,1)}, bf16[256,2048]{1,0:T(8,128)(2,1)}, u32[]{:S(2)}, u32[]{:S(2)}) collective-permute-start(bf16[256,2048]{1,0:T(8,128)(2,1)} %add_convert_fusion.3), channel_id=1, source_target_pairs={{0,1},{1,0},{2,3},{3,2},{4,5},{5,4},{6,7},{7,6},{8,9},{9,8},{10,11... | collective-permute-start | bytes 3145736 | tf_op jit(solution)/shard_map/ppermute | solution.py:640
  371.1 33.6 %collective-permute-start.43 = (bf16[256,2688]{1,0:T(8,128)(2,1)}, bf16[256,2688]{1,0:T(8,128)(2,1)S(1)}, u32[]{:S(2)}, u32[]{:S(2)}) collective-permute-start(bf16[256,2688]{1,0:T(8,128)(2,1)} %get-tuple-element.295), channel_id=1, source_target_pairs={{0,16},{4,20},{8,24},{12,28},{16,0},{20,4},{24,8},{28,12},{1,17},{... | collective-permute-start | bytes 4128776 | tf_op jit(solution)/shard_map/ppermute | solution.py:637
  372.5 32.1 %collective-permute-start.44 = (bf16[256,2688]{1,0:T(8,128)(2,1)}, bf16[256,2688]{1,0:T(8,128)(2,1)}, u32[]{:S(2)}, u32[]{:S(2)}) collective-permute-start(bf16[256,2688]{1,0:T(8,128)(2,1)} %get-tuple-element.296), channel_id=1, source_target_pairs={{0,8},{4,12},{8,0},{12,4},{16,24},{20,28},{24,16},{28,20},{1,9},{5... | collective-permute-start | bytes 4128776 | tf_op jit(solution)/shard_map/ppermute | solution.py:637
  378.4 26.3 %collective-permute-start.41 = (bf16[256,2048]{1,0:T(8,128)(2,1)S(1)}, bf16[256,2048]{1,0:T(8,128)(2,1)S(1)}, u32[]{:S(2)}, u32[]{:S(2)}) collective-permute-start(bf16[256,2048]{1,0:T(8,128)(2,1)S(1)} %get-tuple-element.322.refs_0_), channel_id=1, source_target_pairs={{0,1},{1,0},{2,3},{3,2},{4,5},{5,4},{6,7},{7,6},{8,9},{9,8},{10,11... | collective-permute-start | bytes 3145736 | tf_op jit(solution)/shard_map/ppermute | solution.py:640
  404.6 33.2 %collective-permute-start.45 = (bf16[512,2048]{1,0:T(8,128)(2,1)}, bf16[512,2048]{1,0:T(8,128)(2,1)S(1)}, u32[]{:S(2)}, u32[]{:S(2)}) collective-permute-start(bf16[512,2048]{1,0:T(8,128)(2,1)} %get-tuple-element.303), channel_id=1, source_target_pairs={{0,4},{4,0},{8,12},{12,8},{16,20},{20,16},{24,28},{28,24},{1,5},{5... | collective-permute-start | bytes 6291464 | tf_op jit(solution)/shard_map/ppermute | solution.py:637
  404.7 32.8 %collective-permute-start.48 = (bf16[256,2688]{1,0:T(8,128)(2,1)}, bf16[256,2688]{1,0:T(8,128)(2,1)S(1)}, u32[]{:S(2)}, u32[]{:S(2)}) collective-permute-start(bf16[256,2688]{1,0:T(8,128)(2,1)} %get-tuple-element.306), channel_id=1, source_target_pairs={{0,16},{4,20},{8,24},{12,28},{16,0},{20,4},{24,8},{28,12},{1,17},{... | collective-permute-start | bytes 4128776 | tf_op jit(solution)/shard_map/ppermute | solution.py:637
  405.4 32.5 %collective-permute-start.49 = (bf16[256,2688]{1,0:T(8,128)(2,1)}, bf16[256,2688]{1,0:T(8,128)(2,1)S(1)}, u32[]{:S(2)}, u32[]{:S(2)}) collective-permute-start(bf16[256,2688]{1,0:T(8,128)(2,1)} %get-tuple-element.307), channel_id=1, source_target_pairs={{0,8},{4,12},{8,0},{12,4},{16,24},{20,28},{24,16},{28,20},{1,9},{5... | collective-permute-start | bytes 4128776 | tf_op jit(solution)/shard_map/ppermute | solution.py:637
  406.7 28.6 %collective-permute-start.47 = (bf16[256,2048]{1,0:T(8,128)(2,1)S(1)}, bf16[256,2048]{1,0:T(8,128)(2,1)S(1)}, u32[]{:S(2)}, u32[]{:S(2)}) collective-permute-start(bf16[256,2048]{1,0:T(8,128)(2,1)S(1)} %collective-permute-done.42), channel_id=1, source_target_pairs={{1,0},{2,3},{5,4},{6,7},{9,8},{10,11},{13,12},{14,15},{17,16},{18,... | collective-permute-start | bytes 3145736 | tf_op jit(solution)/shard_map/ppermute | solution.py:640
  443.0 29.2 %collective-permute-start.52 = (bf16[128,2688]{1,0:T(8,128)(2,1)S(1)}, bf16[128,2688]{1,0:T(8,128)(2,1)S(1)}, u32[]{:S(2)}, u32[]{:S(2)}) collective-permute-start(bf16[128,2688]{1,0:T(8,128)(2,1)S(1)} %add_convert_fusion.18), channel_id=1, source_target_pairs={{0,16},{4,20},{8,24},{12,28},{16,0},{20,4},{24,8},{28,12},{1,17},{... | collective-permute-start | bytes 2064392 | tf_op jit(solution)/shard_map/ppermute | solution.py:637
  443.7 30.0 %collective-permute-start.51 = (bf16[128,2688]{1,0:T(8,128)(2,1)S(1)}, bf16[128,2688]{1,0:T(8,128)(2,1)S(1)}, u32[]{:S(2)}, u32[]{:S(2)}) collective-permute-start(bf16[128,2688]{1,0:T(8,128)(2,1)S(1)} %add_convert_fusion.21), channel_id=1, source_target_pairs={{0,8},{4,12},{8,0},{12,4},{16,24},{20,28},{24,16},{28,20},{1,9},{5... | collective-permute-start | bytes 2064392 | tf_op jit(solution)/shard_map/ppermute | solution.py:637
  447.2 26.9 %collective-permute-start.50 = (bf16[256,2048]{1,0:T(8,128)(2,1)S(1)}, bf16[256,2048]{1,0:T(8,128)(2,1)S(1)}, u32[]{:S(2)}, u32[]{:S(2)}) collective-permute-start(bf16[256,2048]{1,0:T(8,128)(2,1)S(1)} %collective-permute-done.46), channel_id=1, source_target_pairs={{1,0},{2,3},{5,4},{6,7},{9,8},{10,11},{13,12},{14,15},{17,16},{18,... | collective-permute-start | bytes 3145736 | tf_op jit(solution)/shard_map/ppermute | solution.py:640
  474.1 41.7 %collective-permute-start.55 = (bf16[256,2048]{1,0:T(8,128)(2,1)}, bf16[256,2048]{1,0:T(8,128)(2,1)}, u32[]{:S(2)}, u32[]{:S(2)}) collective-permute-start(bf16[256,2048]{1,0:T(8,128)(2,1)} %slice.237), channel_id=1, source_target_pairs={{0,1},{1,0},{2,3},{3,2},{4,5},{5,4},{6,7},{7,6},{8,9},{9,8},{10,11... | collective-permute-start | bytes 3145736 | tf_op jit(solution)/shard_map/ppermute | solution.py:640
  475.9 40.0 %collective-permute-start.56 = (bf16[256,2688]{1,0:T(8,128)(2,1)S(1)}, bf16[256,2688]{1,0:T(8,128)(2,1)S(1)}, u32[]{:S(2)}, u32[]{:S(2)}) collective-permute-start(bf16[256,2688]{1,0:T(8,128)(2,1)S(1)} %pad_maximum_fusion.2.kept), channel_id=1, source_target_pairs={{7,4},{6,5},{5,6},{4,7},{15,12},{14,13},{13,14},{12,15},{23,20},{2... | collective-permute-start | bytes 4128776 | tf_op jit(solution)/shard_map/ppermute | solution.py:874
  524.5 31.5 %collective-permute-start.59 = (bf16[512,3072]{1,0:T(8,128)(2,1)}, bf16[512,3072]{1,0:T(8,128)(2,1)}, u32[]{:S(2)}, u32[]{:S(2)}) collective-permute-start(bf16[512,3072]{1,0:T(8,128)(2,1)} %shard_map.256), channel_id=1, source_target_pairs={{0,4},{4,0},{8,12},{12,8},{16,20},{20,16},{24,28},{28,24},{1,5},{5... | collective-permute-start | bytes 9437192 | tf_op jit(solution)/shard_map/ppermute | solution.py:637
  525.1 30.8 %collective-permute-start.57 = (bf16[256,2688]{1,0:T(8,128)(2,1)S(1)}, bf16[256,2688]{1,0:T(8,128)(2,1)S(1)}, u32[]{:S(2)}, u32[]{:S(2)}) collective-permute-start(bf16[256,2688]{1,0:T(8,128)(2,1)S(1)} %copy-done.91), channel_id=1, source_target_pairs={{0,4},{1,5},{2,6},{3,7},{8,12},{9,13},{10,14},{11,15},{16,20},{17,... | collective-permute-start | bytes 4128776 | tf_op jit(solution)/shard_map/ppermute | solution.py:883
  525.2 25.4 %collective-permute-start.58 = (bf16[256,2048]{1,0:T(8,128)(2,1)S(1)}, bf16[256,2048]{1,0:T(8,128)(2,1)S(1)}, u32[]{:S(2)}, u32[]{:S(2)}) collective-permute-start(bf16[256,2048]{1,0:T(8,128)(2,1)S(1)} %get-tuple-element.335), channel_id=1, source_target_pairs={{0,1},{3,2},{4,5},{7,6},{8,9},{11,10},{12,13},{15,14},{16,17},{19,... | collective-permute-start | bytes 3145736 | tf_op jit(solution)/shard_map/ppermute | solution.py:640
  555.9 42.9 %collective-permute-start.62 = (bf16[512,3072]{1,0:T(8,128)(2,1)}, bf16[512,3072]{1,0:T(8,128)(2,1)}, u32[]{:S(2)}, u32[]{:S(2)}) collective-permute-start(bf16[512,3072]{1,0:T(8,128)(2,1)} %shard_map.257), channel_id=1, source_target_pairs={{0,4},{4,0},{8,12},{12,8},{16,20},{20,16},{24,28},{28,24},{1,5},{5... | collective-permute-start | bytes 9437192 | tf_op jit(solution)/shard_map/ppermute | solution.py:637
  567.8 31.0 %collective-permute-start.60 = (bf16[256,2048]{1,0:T(8,128)(2,1)}, bf16[256,2048]{1,0:T(8,128)(2,1)S(1)}, u32[]{:S(2)}, u32[]{:S(2)}) collective-permute-start(bf16[256,2048]{1,0:T(8,128)(2,1)} %add_convert_fusion.2), channel_id=1, source_target_pairs={{1,2},{2,1},{5,6},{6,5},{9,10},{10,9},{13,14},{14,13},{17,18},{18,... | collective-permute-start | bytes 3145736 | tf_op jit(solution)/shard_map/ppermute | solution.py:640
  568.5 30.3 %collective-permute-start.61 = (bf16[256,2048]{1,0:T(8,128)(2,1)}, bf16[256,2048]{1,0:T(8,128)(2,1)S(1)}, u32[]{:S(2)}, u32[]{:S(2)}) collective-permute-start(bf16[256,2048]{1,0:T(8,128)(2,1)} %get-tuple-element.341), channel_id=1, source_target_pairs={{0,1},{3,2},{4,5},{7,6},{8,9},{11,10},{12,13},{15,14},{16,17},{19,... | collective-permute-start | bytes 3145736 | tf_op jit(solution)/shard_map/ppermute | solution.py:640
  616.5 36.5 %collective-permute-start.65 = (bf16[256,3072]{1,0:T(8,128)(2,1)S(1)}, bf16[256,3072]{1,0:T(8,128)(2,1)}, u32[]{:S(2)}, u32[]{:S(2)}) collective-permute-start(bf16[256,3072]{1,0:T(8,128)(2,1)S(1)} %copy-done.66), channel_id=1, source_target_pairs={{0,16},{4,20},{8,24},{12,28},{16,0},{20,4},{24,8},{28,12},{1,17},{... | collective-permute-start | bytes 4718600 | tf_op jit(solution)/shard_map/ppermute | solution.py:637
  617.9 36.3 %collective-permute-start.66 = (bf16[256,3072]{1,0:T(8,128)(2,1)}, bf16[256,3072]{1,0:T(8,128)(2,1)S(1)}, u32[]{:S(2)}, u32[]{:S(2)}) collective-permute-start(bf16[256,3072]{1,0:T(8,128)(2,1)} %get-tuple-element.353), channel_id=1, source_target_pairs={{0,8},{4,12},{8,0},{12,4},{16,24},{20,28},{24,16},{28,20},{1,9},{5... | collective-permute-start | bytes 4718600 | tf_op jit(solution)/shard_map/ppermute | solution.py:637
  660.4 30.7 %collective-permute-start.72 = (bf16[128,3072]{1,0:T(8,128)(2,1)}, bf16[128,3072]{1,0:T(8,128)(2,1)S(1)}, u32[]{:S(2)}, u32[]{:S(2)}) collective-permute-start(bf16[128,3072]{1,0:T(8,128)(2,1)} %get-tuple-element.369), channel_id=1, source_target_pairs={{0,8},{4,12},{8,0},{12,4},{16,24},{20,28},{24,16},{28,20},{1,9},{5... | collective-permute-start | bytes 2359304 | tf_op jit(solution)/shard_map/ppermute | solution.py:637
  661.8 29.3 %collective-permute-start.73 = (bf16[128,3072]{1,0:T(8,128)(2,1)}, bf16[128,3072]{1,0:T(8,128)(2,1)S(1)}, u32[]{:S(2)}, u32[]{:S(2)}) collective-permute-start(bf16[128,3072]{1,0:T(8,128)(2,1)} %get-tuple-element.372), channel_id=1, source_target_pairs={{0,16},{4,20},{8,24},{12,28},{16,0},{20,4},{24,8},{28,12},{1,17},{... | collective-permute-start | bytes 2359304 | tf_op jit(solution)/shard_map/ppermute | solution.py:637
  664.8 26.2 %collective-permute-start.74 = (bf16[256,1024]{1,0:T(8,128)(2,1)}, bf16[256,1024]{1,0:T(8,128)(2,1)S(1)}, u32[]{:S(2)}, u32[]{:S(2)}) collective-permute-start(bf16[256,1024]{1,0:T(8,128)(2,1)} %get-tuple-element.373), channel_id=1, source_target_pairs={{0,16},{4,20},{8,24},{12,28},{16,0},{20,4},{24,8},{28,12},{1,17},{... | collective-permute-start | bytes 1572872 | tf_op jit(solution)/shard_map/ppermute | solution.py:637
  (133 other events, 2346.2 us)

commit v3 on v2

--- a/solution.py
+++ b/solution.py
@@ -40,7 +40,7 @@
 
 
 def cost(flops, moved):
-    return pl.CostEstimate(flops=flops // 4, bytes_accessed=moved // 4, transcendentals=0)
+    return pl.CostEstimate(flops=flops // 64, bytes_accessed=moved // 64, transcendentals=0)
 
 
 def norm_parts(features):
@@ -309,20 +309,20 @@
     sources, outs = refs[:pieces], refs[pieces : pieces + 8]
     gate_ref, up_ref, down_ref, semaphores = refs[pieces + 8 :]
     rows = own_ref.shape[0]
-    height = sources[0].shape[1]
     copies = []
     for part, target in enumerate((gate_ref, up_ref, down_ref)):
-        for core in range(2):
-            for index, source in enumerate(sources):
-                place = core * pieces + index
-                copy = pltpu.make_async_copy(
-                    source.at[core, :, pl.ds(part * units, units)],
-                    target.at[pl.ds(place * height, height), :],
-                    semaphores.at[part, place],
-                )
-                copy.start()
-                copies.append(copy)
-    third = 2 * pieces
+        place = 0
+        for index, source in enumerate(sources):
+            height = source.shape[0]
+            copy = pltpu.make_async_copy(
+                source.at[:, pl.ds(part * units, units)],
+                target.at[pl.ds(place, height), :],
+                semaphores.at[part, index],
+            )
+            copy.start()
+            copies.append(copy)
+            place += height
+    third = pieces
     left = jnp.concatenate([own_ref[...], turn(other_ref[...])], 0)
     grad = jnp.concatenate([own_grad_ref[...], turn(other_grad_ref[...])], 0)
     for copy in copies[:third]:
@@ -352,15 +352,17 @@
 
 def mlp(own, other, own_grad, other_grad, pieces):
     rows, width = own.shape
-    units = pieces[0].shape[2] // 3
-    whole = pl.BlockSpec(memory_space=pltpu.VMEM)
+    units = pieces[0].shape[1] // 3
+    narrow = pl.BlockSpec((rows, units), lambda i: (0, 0))
+    wide = pl.BlockSpec((rows, width), lambda i: (0, 0))
     small, large = jax.ShapeDtypeStruct((rows, units), BF16), jax.ShapeDtypeStruct((rows, width), BF16)
     return pl.pallas_call(
         partial(mlp_kernel, len(pieces), units),
         out_shape=[small] * 6 + [large] * 2,
-        in_specs=[whole] * 4 + [pl.BlockSpec(memory_space=pl.ANY)] * len(pieces),
-        out_specs=[whole] * 8,
-        scratch_shapes=[pltpu.VMEM((width, units), BF16)] * 3 + [pltpu.SemaphoreType.DMA((3, 2 * len(pieces)))],
+        grid=(1,),
+        in_specs=[wide] * 4 + [pl.BlockSpec(memory_space=pl.ANY)] * len(pieces),
+        out_specs=[narrow] * 6 + [wide] * 2,
+        scratch_shapes=[pltpu.VMEM((width, units), BF16)] * 3 + [pltpu.SemaphoreType.DMA((3, len(pieces)))],
         compiler_params=params(),
         cost_estimate=cost(2 * 2 * rows * width * units * 5, 6 * width * units),
     )(own, other, own_grad, other_grad, *pieces)
@@ -369,7 +371,7 @@
 def down_kernel(pieces, *refs):
     lefts, weights, outs = refs[:4], refs[4 : 4 + pieces], refs[4 + pieces :]
     rows = lefts[0].shape[0]
-    weight = jnp.concatenate([ref[core] for core in range(2) for ref in weights], 0)
+    weight = jnp.concatenate([ref[...] for ref in weights], 0)
     for core in range(2):
         left = jnp.concatenate([lefts[2 * core][...], lefts[2 * core + 1][...]], 0)
         result = times_right(left, weight)
@@ -378,14 +380,14 @@
 
 def mlp_down(hidden, pieces):
     rows, units = hidden[0].shape
-    width = 2 * sum(p.shape[1] for p in pieces)
+    width = sum(p.shape[0] for p in pieces)
     whole = pl.BlockSpec((rows, units), lambda n: (0, 0))
     out = pl.BlockSpec((2 * rows, width), lambda n: (0, 0))
     return pl.pallas_call(
         partial(down_kernel, len(pieces)),
         out_shape=[jax.ShapeDtypeStruct((2 * rows, width), BF16)] * 2,
         grid=(1,),
-        in_specs=[whole] * 4 + [pl.BlockSpec((2, p.shape[1], units), lambda n: (0, 0, 2)) for p in pieces],
+        in_specs=[whole] * 4 + [pl.BlockSpec((p.shape[0], units), lambda n: (0, 2)) for p in pieces],
         out_specs=[out] * 2,
         compiler_params=params(),
         cost_estimate=cost(8 * rows * width * units, 2 * width * units),
@@ -488,6 +490,40 @@
         grid_spec=pltpu.PrefetchScalarGridSpec(num_scalar_prefetch=1, grid=(1,), in_specs=specs, out_specs=specs),
         compiler_params=params(),
     )(mine, *arrays)
+
+
+def middle_back_kernel(near, come, middle, grad_final, gain, low, full, gain_sum):
+    grad = near[...] + come[...].astype(F32)
+    normed, inverse = norm_parts(middle[...])
+    total = grad_final[...].astype(F32) + norm_back(normed, inverse, grad, gain[...])
+    low[...] = total.astype(BF16)
+    full[...] = total
+
+    @pl.when(pl.program_id(0) == 0)
+    def _():
+        gain_sum[...] = jnp.zeros_like(gain_sum)
+
+    gain_sum[...] += jnp.sum(grad * normed, 0, keepdims=True)
+
+
+def middle_back(near, come, middle, grad_final, gain):
+    rows, width = near.shape
+    tile = 64
+    block = pl.BlockSpec((tile, width), lambda i: (i, 0))
+    vector = pl.BlockSpec((1, width), lambda i: (0, 0))
+    return pl.pallas_call(
+        middle_back_kernel,
+        out_shape=[
+            jax.ShapeDtypeStruct((rows, width), BF16),
+            jax.ShapeDtypeStruct((rows, width), F32),
+            jax.ShapeDtypeStruct((1, width), F32),
+        ],
+        grid=(rows // tile,),
+        in_specs=[block] * 4 + [vector],
+        out_specs=[block, block, vector],
+        compiler_params=params(),
+        cost_estimate=cost(0, rows * width * 18),
+    )(near, come, middle, grad_final, gain)
 
 
 def widen(array, height):
@@ -758,11 +794,12 @@
     cotangent_low, gain_second = to_relative(hold(cotangent), gain_two[None])
     grad_own = jnp.where(valid, cotangent_low, 0.0)
     grad_final = grad_own.astype(F32)
-    close(up_one, down_one, first_beside, first_middle, local_two, grad_own)
+    core_one = [to_core(sent_up)]
+    close(up_one, down_one, first_beside, first_middle, local_two, grad_own, core_one[0])
 
     up_two, down_two = second_level(sent_up, up_bits), second_level(sent_down, down_bits)
     first_far = line_out(None, first_beside, first_middle)
-    core_one = [to_core(p) for p in (sent_up, sent_down)]
+    core_one.append(to_core(sent_down))
     close(up_two, down_two, *first_far, *core_one)
 
     up_three, down_three = second_level(up_one, up_bits), second_level(down_one, down_bits)
@@ -774,67 +811,81 @@
     down_all = further([sent_down, down_one, down_two, down_three], down_bits)
     up_core = [core_one[0], core_two[0]] + [to_core(p) for p in up_all[2:]]
     down_core = [core_one[1], core_two[1]] + [to_core(p) for p in down_all[2:]]
+    turned = lax.ppermute(hold(local_two), both, odd_turn)
+    grad_beside = swap_tensor(hold(grad_own), 1)
     close(*up_core, *down_core)
     attn_low = up_all + down_all + up_core + down_core
     first_slots = line_all(first_own, first_beside, first_middle, *first_far, first_last)
 
-    turned = lax.ppermute(hold(local_two), both, odd_turn)
-    grad_beside = swap_tensor(hold(grad_own), 1)
+    spans = slice(0, half_rows), slice(half_rows, shard_rows)
+    orders = up_bits, down_bits
+
+    def level_one(halves):
+        return [first_level(half, order) for half, order in zip(halves, orders)]
+
+    def level_two(halves, come):
+        found = []
+        for half, other, order in zip(halves, come, orders):
+            both_pieces = jnp.concatenate([half, hold(other)], 0)
+            found += further_two([both_pieces, swap_dp(both_pieces, 1 << order[1])], order)
+        return found
+
+    def further_two(pieces, order):
+        for bit in order[2:]:
+            pieces = pieces + [swap_dp(p, 1 << bit) for p in pieces]
+        return pieces
+
     grad_core = to_core(grad_own)
     projected = rows_times([hold(first_slots[0]), *first_slots[1:]], attn_low, 0, proj_columns)
+    close(turned, projected[0], grad_core)
+
+    mlp_zero = [jnp.where(odd, hold(turned)[span], local_two[span]) for span in spans]
+    zero_come = level_one(mlp_zero)
+    mlp_one = [lax.ppermute(hold(local_two)[spans[0]], both, to_even + to_odd)]
     query, key, value, normed_head, scale_head, mixed = retain(
-        projected, place_arg, log_decay, cosines, sines, heads
+        [hold(projected[0]), *projected[1:]], place_arg, log_decay, cosines, sines, heads
     )
-    close(turned, grad_beside, grad_core, mixed)
-
-    from_core = lax.ppermute(hold(local_two), both, to_even + to_odd)
+    (mixed_third,) = rows_back(mixed, (3,), attn_low, proj_columns)
+    close(*zero_come, mlp_one[0], grad_beside, mixed_third)
+
+    from_ends = move_tensor(hold(mixed_third), inward)
+    mlp_one.append(lax.ppermute(hold(local_two)[spans[1]], both, to_even + to_odd))
+    zero_pieces = level_two(mlp_zero, zero_come)
+    mixed_second, mixed_first, mixed_own = rows_back(hold(mixed), (2, 1, 0), attn_low, proj_columns)
+    mixed_partial = add(mixed_second, from_ends).astype(BF16)
     grad_rows = [grad_own, grad_beside, grad_core, to_core(grad_beside)]
-    mixed_second, mixed_third = rows_back(hold(mixed), (2, 3), attn_low, proj_columns)
-    from_ends = move_tensor(mixed_third, inward)
-    mixed_own, mixed_first = rows_back(after(mixed, mixed_third), (0, 1), attn_low, proj_columns)
-    mixed_partial = add(mixed_second, from_ends).astype(BF16)
-    close(from_core, grad_rows[3], mixed_partial, mixed_own)
-
-    def pair_half(span):
-        return jnp.stack([jnp.where(odd, turned[span], local_two[span]), hold(from_core)[span]])
-
-    mlp_up, mlp_across = pair_half(slice(0, half_rows)), pair_half(slice(half_rows, shard_rows))
-    mlp_up_one, mlp_across_one = first_level(mlp_up, up_bits), first_level(mlp_across, down_bits)
+    close(mlp_one[1], *zero_pieces, mixed_partial, grad_rows[3])
+
     from_inner = move_tensor(hold(mixed_partial), across)
     from_ends = move_tensor(hold(mixed_second), inward)
-    close(mlp_up_one, mlp_across_one, from_inner, from_ends)
-
-    mlp_up_two, mlp_across_two = second_level(mlp_up, up_bits), second_level(mlp_across, down_bits)
+    one_come = level_one([hold(half) for half in mlp_one])
+    close(*one_come, from_inner, from_ends)
+
     from_beside = swap_tensor(add(mixed_first, hold(from_inner)).astype(BF16), 1)
     from_middle = move_tensor(add(mixed_third, hold(from_ends)).astype(BF16), across)
+    mlp_pieces = zero_pieces + level_two(mlp_one, one_come)
     middle = features + add(mixed_own, from_beside, from_middle)
     normed_two, inverse_two = norm_parts(middle)
     second_own = (normed_two * gain_second).astype(BF16)
-    close(mlp_up_two, mlp_across_two, second_own)
-
-    mlp_up_three, mlp_across_three = second_level(mlp_up_one, up_bits), second_level(mlp_across_one, down_bits)
+    close(*mlp_pieces, second_own)
+
     second_beside = swap_tensor(hold(second_own), 1)
     second_core = to_core(second_own)
-    close(mlp_up_three, mlp_across_three, second_beside, second_core)
-    mlp_pieces = further([mlp_up, mlp_up_one, mlp_up_two, mlp_up_three], up_bits) + further(
-        [mlp_across, mlp_across_one, mlp_across_two, mlp_across_three], down_bits
-    )
-
     first_part = mlp(hold(second_own), second_core, grad_rows[0], grad_rows[2], mlp_pieces)
+    near_core = swap_dp(first_part[7], 1)
+    close(second_beside, near_core)
+
     second_far = to_core(second_beside)
     second_rows = [second_own, second_beside, second_core, second_far]
-    close(first_part[7], second_far)
-
     second_part = mlp(hold(second_beside), second_far, grad_rows[1], grad_rows[3], mlp_pieces)
-    near_core = to_core(first_part[7])
-    close(second_part[7], near_core)
+    far_core = swap_dp(second_part[7], 1)
     hidden, grad_gate, grad_up = (
         [first_part[2 * i], second_part[2 * i], first_part[2 * i + 1], second_part[2 * i + 1]] for i in range(3)
     )
 
-    far = add(second_part[6], to_core(second_part[7])).astype(BF16)
+    far = add(second_part[6], far_core).astype(BF16)
     near = add(first_part[6], near_core)
-    close(far)
+    close(far, near)
 
     def mlp_grad(end, core):
         return mlp_grads(end, core, [hold(second_rows[0]), *second_rows[1:]], grad_rows, grad_gate, grad_up, hidden)
@@ -844,10 +895,7 @@
     down_own, down_other = mlp_down([hold(hidden[0]), *hidden[1:]], mlp_pieces)
     close(second_back, *high[0], *high[1], down_own)
 
-    grad_second = near + hold(second_back).astype(F32)
-    grad_middle = grad_final + norm_back(normed_two, inverse_two, grad_second, gain_second)
-    grad_gain_two = jnp.sum(grad_second * normed_two, 0)
-    attn_own = grad_middle.astype(BF16)
+    attn_own, grad_middle, grad_gain_two = middle_back(near, hold(second_back), middle, grad_own, gain_second)
     attn_beside = swap_tensor(attn_own, 1)
     attn_middle = move_tensor(attn_own, across)
     come = [[sum_start(high[0][0], up_bits), sum_start(high[0][1], down_bits)]]
@@ -857,75 +905,87 @@
     attn_far = line_out(None, attn_beside, attn_middle)
     come.append([sum_start(high[1][0], up_bits), sum_start(high[1][1], down_bits)])
     down_core = to_core(down_other)
-    close(*attn_far, *come[1], down_core)
+    splits = [[sum_split(low[0][part], hold(come[0][part])) for part in range(2)]]
+    close(*attn_far, *come[1], down_core, *splits[0][0], *splits[0][1])
 
     attn_last = move_tensor(hold(attn_far[0]), outward)
-    mlp_total = []
-    for core in range(2):
-        ends = []
-        for part, order in enumerate((up_bits, down_bits)):
-            ends.append(add(*sum_end(*sum_split(low[core][part], hold(come[core][part])), order)).astype(BF16))
-        mlp_total.append(jnp.concatenate(ends, 0))
+    splits.append([sum_split(low[1][part], hold(come[1][part])) for part in range(2)])
+
+    def mlp_end(core):
+        return [add(*sum_end(*splits[core][part], orders[part])).astype(BF16) for part in range(2)]
+
+    mlp_total = [mlp_end(0)]
+    attn_third = attn_far[0], attn_far[1]
+    attn_second = jnp.where(inner, *attn_third)
+    grad_mixed = rows_times([hold(attn_own), attn_beside, attn_second], attn_low, proj_columns, out_columns)
     down_sum = add(down_own, hold(down_core))
     down_sent = down_sum[rows:].astype(BF16)
-    close(attn_last, *mlp_total, down_sent)
-    attn_slots = line_all(attn_own, attn_beside, attn_middle, *attn_far, attn_last)
-
-    grad_turn = lax.ppermute(hold(mlp_total[0]), both, [(b, a) for a, b in odd_turn])
-    down_beside = swap_tensor(hold(down_sent), 1)
-    grad_mixed = rows_times([hold(attn_slots[0]), *attn_slots[1:]], attn_low, proj_columns, out_columns)
+    close(attn_last, *mlp_total[0], grad_mixed[0])
+    attn_slots = attn_own, attn_beside, attn_second, jnp.where(inner, attn_middle, hold(attn_last))
+
+    grad_turn = lax.ppermute(jnp.concatenate([hold(t) for t in mlp_total[0]], 0), both, [(b, a) for a, b in odd_turn])
+    grad_mixed = grad_mixed + rows_times([attn_slots[3]], attn_low, proj_columns, out_columns)
     grad_proj = retain_back(
         grad_mixed, projected, normed_head, scale_head, query, key, value, place_arg, log_decay, cosines, sines, heads
     )
-    back_second, back_third, gain_far = rows_back(grad_proj, (2, 3), attn_low, 0, first_slots[2:])
-    close(grad_turn, down_beside, back_third)
-
-    grad_core = lax.ppermute(hold(mlp_total[1]), both, [(b, a) for a, b in to_even + to_odd])
+    back_third, gain_third = rows_back(grad_proj, (3,), attn_low, 0, first_slots[3:])
+    mlp_total.append(mlp_end(1))
+    close(grad_turn, back_third, *mlp_total[1])
+
     from_ends = move_tensor(hold(back_third), inward)
+    to_owner = [(b, a) for a, b in to_even + to_odd]
+    grad_core = [lax.ppermute(hold(mlp_total[1][0]), both, to_owner)]
     other_high = attn_grads(1, first_slots, hold(grad_proj))
-    other_low = attn_grads(0, first_slots, after(grad_proj, other_high))
-    core_high = swap_dp(other_high, 1)
-    close(grad_core, from_ends, core_high, other_low)
-
-    from_inner = move_tensor(add(back_second, hold(from_ends)).astype(BF16), across)
+    back_second, gain_second_part = rows_back(after(grad_proj, other_high), (2,), attn_low, 0, first_slots[2:3])
+    other_low = attn_grads(0, first_slots, after(grad_proj, back_second))
+    back_partial = add(back_second, from_ends).astype(BF16)
+    close(back_partial, other_low, grad_core[0])
+
+    from_inner = move_tensor(hold(back_partial), across)
     from_ends = move_tensor(hold(back_second), inward)
-    core_low = to_core(other_low)
-    up_high, down_high = attn_grads(1, first_slots, hold(grad_proj), core_high)
+    core_high, core_low = to_core(other_high), to_core(other_low)
+    out_other_high = attn_grads(1, attn_slots, hold(mixed))
+    out_other_low = attn_grads(0, attn_slots, after(mixed, out_other_high))
+    up_high, down_high = attn_grads(1, first_slots, after(grad_proj, out_other_low), core_high)
+    proj_come = swap_dp(up_high, 1 << up_bits[-1]), swap_dp(down_high, 1 << down_bits[-1])
     back_own, back_first, gain_near = rows_back(after(grad_proj, up_high), (0, 1), attn_low, 0, first_slots[:2])
-    close(from_inner, from_ends, core_low, back_own)
+    close(from_inner, from_ends, back_own, core_low, out_other_low)
 
     from_beside = swap_tensor(add(back_first, hold(from_inner)).astype(BF16), 1)
     from_middle = move_tensor(add(back_third, hold(from_ends)).astype(BF16), across)
-    proj_come = sum_start(up_high, up_bits), sum_start(down_high, down_bits)
+    out_core_high, out_core_low = to_core(out_other_high), to_core(out_other_low)
     up_low, down_low = attn_grads(0, first_slots, hold(grad_proj), core_low)
-    out_other_high = attn_grads(1, attn_slots, after(mixed, up_low))
-    out_other_low = attn_grads(0, attn_slots, after(mixed, out_other_high))
-    out_up_high, out_down_high = attn_grads(1, attn_slots, after(mixed, out_other_low), swap_dp(out_other_high, 1))
-    out_up_low, out_down_low = attn_grads(0, attn_slots, after(mixed, out_up_high), swap_dp(out_other_low, 1))
-    close(from_beside, from_middle, *proj_come, out_up_low)
-
-    gains = to_global(jnp.stack([hold(gain_far[0] + gain_near[0]) / gain_first[0], grad_gain_two]))
-    gains = gains + swap_tensor(gains, 1)
-    gains = gains + swap_tensor(gains, 2)
+    out_up_high, out_down_high = attn_grads(1, attn_slots, after(mixed, up_low), out_core_high)
+    out_up_low, out_down_low = attn_grads(0, attn_slots, after(mixed, out_up_high), out_core_low)
+    gain_parts = gain_third[0] + gain_second_part[0] + hold(gain_near)[0]
+    gains = to_global(jnp.stack([gain_parts / gain_first[0], grad_gain_two[0]]))
     gains = gains + swap_dp(gains, 1)
+    close(from_beside, from_middle, *proj_come, gains, up_low, out_up_low)
+
+    down_beside = swap_tensor(hold(down_sent), 1)
     proj_up = sum_end(*sum_split(up_low, hold(proj_come[0])), up_bits)
     proj_down = sum_end(*sum_split(down_low, hold(proj_come[1])), down_bits)
     out_come = sum_start(out_up_high, up_bits), sum_start(out_down_high, down_bits)
+    grad_core.append(lax.ppermute(after(mlp_total[1][1], out_come[0]), both, to_owner))
     grad_first = add(back_own, hold(from_beside), from_middle)
     grad_tokens = grad_middle + norm_back(normed_one, inverse_one, grad_first, gain_first)
     grad_tokens = to_global(grad_tokens.astype(BF16))
+    close(*proj_up, *proj_down, *out_come, grad_core[1], down_beside, grad_tokens)
+
     final = middle + down_sum[:rows] + hold(down_beside).astype(F32)
     output = to_global(jnp.where(valid, final, 0.0).astype(BF16))
     sum_mgate, sum_mup, sum_down = receive_mlp(
-        (mine & 1).astype(jnp.int32).reshape(1), hold(mlp_total[0]), grad_turn, grad_core, units
+        (mine & 1).astype(jnp.int32).reshape(1),
+        jnp.concatenate([hold(t) for t in mlp_total[0]], 0),
+        grad_turn,
+        jnp.concatenate(grad_core, 0),
+        units,
     )
-    close(gains, *proj_up, *proj_down, *out_come, grad_tokens, output, sum_mgate)
-
     out_up = sum_end(*sum_split(out_up_low, hold(out_come[0])), up_bits)
     out_down = sum_end(*sum_split(out_down_low, hold(out_come[1])), down_bits)
     gains = hold(gains)
-    for bit in range(1, bits):
-        gains = gains + swap_dp(gains, 1 << bit)
+    gains = gains + sum(swap_dp(gains, 2 * chip) for chip in range(1, dp_size // 2))
+    gains = gains + sum(swap_tensor(gains, other) for other in range(1, tensor_size))
     sum_query, sum_key, sum_value, sum_gate = receive_attn(
         (hold(proj_up[0]), proj_up[1], *proj_down), 2, 2, heads
     )

time: 713 us -> 656 us (0.920)
  waiting for transfers between devices: 295 us -> 233 us
  Pallas kernels: 219 us -> 239 us
  starting transfers between devices: 119 us -> 100 us
  other arithmetic: 44 us -> 53.1 us
    ppermute x26 -> x27, waiting for transfers between devices: 146 us -> 87.4 us  [move_tensor(): return lax.ppermute(array, 'tensor', pairs)]
    pallas_call x2, Pallas kernels: 32.9 us -> 43.2 us  [mlp(): pl.pallas_call(partial(mlp_kernel, len(pieces), units), out_shape=[small]...]
    ppermute x3 -> x5, waiting for transfers between devices: 20 us -> 10.8 us  [the longest x1 7.09 us: per_device(): lax.ppermute(hold(local_two)[spans[1]], both, to_even + to_odd)]
    ppermute x26 -> x27, starting transfers between devices: 55.9 us -> 47.7 us  [move_tensor(): return lax.ppermute(array, 'tensor', pairs)]
    unnamed x202 -> x220, local copies, waits for them, and re-layouts: 22.5 us -> 14.5 us
    ppermute x50 -> x53, starting transfers between devices: 46.6 us -> 40.2 us  [swap_dp(): return lax.ppermute(array, 'dp', [(i, i ^ mask) for i in range(dp_size)])]
    ppermute x50 -> x53, waiting for transfers between devices: 129 us -> 135 us  [swap_dp(): return lax.ppermute(array, 'dp', [(i, i ^ mask) for i in range(dp_size)])]
    ppermute x3 -> x5, starting transfers between devices: 15.2 us -> 10.8 us  [the longest x1 7.29 us: per_device(): mlp_one = [lax.ppermute(hold(local_two)[spans[0]], both, to_even + to_odd)]]
  transfers between devices with their start and end apart: 80 -> 86, of which waited for: 42 -> 39; matrix products, arithmetic and copies ran while one was open for 4% -> 8% of each run, Pallas kernels for 27% -> 32%
where the time goes in v3:
time: 656 us; the launch traced here: 651 us
  Pallas kernels  239 us (36%)
  waiting for transfers between devices  233 us (36%)
  starting transfers between devices  100 us (15%)
  other arithmetic  53.1 us (8%)
  local copies, waits for them, and re-layouts  22.4 us (3%)
    ppermute x53, waiting for transfers between devices, swap_dp(): return lax.ppermute(array, 'dp', [(i, i ^ mask) for i in range(dp_size)])  135 us
    ppermute x27, waiting for transfers between devices, move_tensor(): return lax.ppermute(array, 'tensor', pairs)  87.4 us
    pallas_call x8, Pallas kernels, attn_grads(): pl.pallas_call(attn_grad_kernel if core else attn_grad_add_kernel, out_sh...  47.7 us
    ppermute x27, starting transfers between devices, move_tensor(): return lax.ppermute(array, 'tensor', pairs)  47.7 us
    pallas_call x5, Pallas kernels, rows_back(): pl.pallas_call(partial(rows_back_kernel, len(slots), len(pieces), 1 if we...  43.6 us
    pallas_call x2, Pallas kernels, mlp(): pl.pallas_call(partial(mlp_kernel, len(pieces), units), out_shape=[small]...  43.2 us
    ppermute x53, starting transfers between devices, swap_dp(): return lax.ppermute(array, 'dp', [(i, i ^ mask) for i in range(dp_size)])  40.2 us
    pallas_call x4, Pallas kernels, mlp_grads(): pl.pallas_call(mlp_grad_kernel, out_shape=[jax.ShapeDtypeStruct((tile, 3...  27.8 us
  transfers between devices with their start and end apart: 86, of which 39 were waited for; matrix products, arithmetic and copies ran while one was open for 8% of the time, Pallas kernels for 32%

profile of v3, /device:TPU:0, one launch (start us, length us, event | category | flops | bytes accessed | tf_op | source)
XLA Modules:
  0.0 651.0 jit_solution(13957597291120242384)
XLA Ops:
  24.2 8.8 %collective-permute-done.refs_5_.refs_2_.refs_4_.refs_3_ = bf16[128,4096]{1,0:T(8,128)(2,1)S(1)} collective-permute-done((bf16[128,4096]{1,0:T(8,128)(2,1)S(1)}, bf16[128,4096]{1,0:T(8,128)(2,1)S(1)}, u32[]{:S(2)}, u32[]{:S(2)}) %collective-permute-start) | collective-permute-done | bytes 1048608 | tf_op jit(solution)/shard_map/ppermute | solution.py:673
  34.6 4.5 collective-permute-done.2.refs_1_.refs_19_
  42.2 22.9 %collective-permute-done.5.refs_6_.refs_3_.refs_5_.refs_4_ = bf16[128,4096]{1,0:T(8,128)(2,1)} collective-permute-done((bf16[128,4096]{1,0:T(8,128)(2,1)S(1)}, bf16[128,4096]{1,0:T(8,128)(2,1)}, u32[]{:S(2)}, u32[]{:S(2)}) %collective-permute-start.5) | collective-permute-done | bytes 1048608 | tf_op jit(solution)/shard_map/ppermute | solution.py:673
  65.1 3.8 collective-permute-done.8
  73.4 21.0 %collective-permute-done.10.refs_7_.refs_4_.refs_6_.refs_5_ = bf16[128,4096]{1,0:T(8,128)(2,1)S(1)} collective-permute-done((bf16[128,4096]{1,0:T(8,128)(2,1)S(1)}, bf16[128,4096]{1,0:T(8,128)(2,1)S(1)}, u32[]{:S(2)}, u32[]{:S(2)}) %collective-permute-start.10) | collective-permute-done | bytes 1048608 | tf_op jit(solution)/shard_map/ppermute | solution.py:673
  108.3 18.0 %shard_map.242 = (bf16[256,3072]{1,0:T(8,128)(2,1)}, bf16[256,3072]{1,0:T(8,128)(2,1)}, bf16[256,3072]{1,0:T(8,128)(2,1)}, bf16[256,3072]{1,0:T(8,128)(2,1)}) custom-call(bf16[256,2048]{1,0:T(8,128)(2,1)} %fusion.5.refs_0_.refs_18_, bf16[256,2048]{1,0:T(8,128)(2,1)} %collective-permute-done.2.refs_1_.refs_19_, ...), custom_call_target="tpu_custom_call" | custom-call | flops 201326592 | bytes 196608 | tf_op jit(solution)/shard_map/pallas_call | solution.py:245
  128.7 7.3 %collective-permute-start.23 = (bf16[128,2688]{1,0:T(8,128)(2,1)}, bf16[128,2688]{1,0:T(8,128)(2,1)}, u32[]{:S(2)}, u32[]{:S(2)}) collective-permute-start(bf16[128,2688]{1,0:T(8,128)(2,1)} %slice.140), channel_id=1, source_target_pairs={{4,0},{5,1},{6,2},{7,3},{12,8},{13,9},{14,10},{15,11},{20,16},{21,... | collective-permute-start | bytes 2064392 | tf_op jit(solution)/shard_map/ppermute | solution.py:844
  141.1 10.1 %shard_map.243 = (bf16[1024,512]{1,0:T(8,128)(2,1)S(1)}, bf16[1024,512]{1,0:T(8,128)(2,1)S(1)}, bf16[1024,1024]{1,0:T(8,128)(2,1)}, bf16[1024,1024]{1,0:T(8,128)...) custom-call(s32[1]{0:T(128)} %bitcast.3.place_ref, f32[2]{0:T(128)S(1)} %subtract_log_fusion.decay_ref, ...), custom_call_target="tpu_custom_call" | custom-call | flops 25165824 | bytes 288000 | tf_op jit(solution)/shard_map/pallas_call | solution.py:125
  153.2 3.9 shard_map.244
  158.6 3.9 collective-permute-start.25
  170.4 6.7 %shard_map.245 = (bf16[256,2048]{1,0:T(8,128)(2,1)S(1)}, bf16[256,2048]{1,0:T(8,128)(2,1)S(1)}, bf16[256,2048]{1,0:T(8,128)(2,1)S(1)}) custom-call(bf16[1024,1024]{1,0:T(8,128)(2,1)} %get-tuple-element.374.refs_0_.refs_1_.refs_2_.refs_4_, bf16[1024,1024]{1,0:T(8,128)(2,1)} %get-tuple-element.374.refs_0_.refs_1_.refs_2_.refs_4_, ...), custom_call_target="tpu_custom_call" | custom-call | flops 50331648 | bytes 65536 | tf_op jit(solution)/shard_map/pallas_call | solution.py:288
  177.1 6.0 collective-permute-done.25
  183.5 7.1 %collective-permute-done.26 = bf16[128,2688]{1,0:T(8,128)(2,1)S(1)} collective-permute-done((bf16[128,2688]{1,0:T(8,128)(2,1)}, bf16[128,2688]{1,0:T(8,128)(2,1)S(1)}, u32[]{:S(2)}, u32[]{:S(2)}) %collective-permute-start.26) | collective-permute-done | bytes 688160 | tf_op jit(solution)/shard_map/ppermute | solution.py:852
  196.1 4.3 collective-permute-start.33
  203.7 12.2 %collective-permute-done.31 = bf16[128,2688]{1,0:T(8,128)(2,1)S(1)} collective-permute-done((bf16[128,2688]{1,0:T(8,128)(2,1)}, bf16[128,2688]{1,0:T(8,128)(2,1)S(1)}, u32[]{:S(2)}, u32[]{:S(2)}) %collective-permute-start.31) | collective-permute-done | bytes 688160 | tf_op jit(solution)/shard_map/ppermute | solution.py:673
  216.9 4.1 collective-permute-done.33
  227.6 17.3 %collective-permute-done.34 = bf16[256,2048]{1,0:T(8,128)(2,1)S(1)} collective-permute-done((bf16[256,2048]{1,0:T(8,128)(2,1)S(1)}, bf16[256,2048]{1,0:T(8,128)(2,1)S(1)}, u32[]{:S(2)}, u32[]{:S(2)}) %collective-permute-start.34) | collective-permute-done | bytes 1048608 | tf_op jit(solution)/shard_map/ppermute | solution.py:676
  246.9 7.3 %collective-permute-done.36.refs_5_.refs_9_ = bf16[256,2688]{1,0:T(8,128)(2,1)S(1)} collective-permute-done((bf16[256,2688]{1,0:T(8,128)(2,1)S(1)}, bf16[256,2688]{1,0:T(8,128)(2,1)S(1)}, u32[]{:S(2)}, u32[]{:S(2)}) %collective-permute-start.36) | collective-permute-done | bytes 1376288 | tf_op jit(solution)/shard_map/ppermute | solution.py:673
  258.4 15.8 %shard_map.246 = (bf16[256,896]{1,0:T(8,128)(2,1)S(1)}, bf16[256,896]{1,0:T(8,128)(2,1)S(1)}, bf16[256,896]{1,0:T(8,128)(2,1)S(1)}, bf16[256,896]{1,0:T(8,128)(2...) custom-call(bf16[256,2048]{1,0:T(8,128)(2,1)S(1)} %multiply_convert_, ...), custom_call_target="tpu_custom_call" | custom-call | flops 146800640 | bytes 172032 | tf_op jit(solution)/shard_map/pallas_call | solution.py:359
  274.5 5.8 collective-permute-done.39.own_ref.refs_1_
  284.1 27.3 %shard_map.247 = (bf16[256,896]{1,0:T(8,128)(2,1)S(1)}, bf16[256,896]{1,0:T(8,128)(2,1)S(1)}, bf16[256,896]{1,0:T(8,128)(2,1)S(1)}, bf16[256,896]{1,0:T(8,128)(2...) custom-call(bf16[256,2048]{1,0:T(8,128)(2,1)S(1)} %collective-permut, ...), custom_call_target="tpu_custom_call" | custom-call | flops 146800640 | bytes 172032 | tf_op jit(solution)/shard_map/pallas_call | solution.py:359
  316.3 7.0 %shard_map.250 = (bf16[256,2688]{1,0:T(8,128)(2,1)}, bf16[256,2688]{1,0:T(8,128)(2,1)}) custom-call(bf16[256,2048]{1,0:T(8,128)(2,1)} %copy-done.15, bf16[256,2048]{1,0:T(8,128)(2,1)} %copy-done.16, bf16[256,2048]{1,0:T(8,128)(2,1)} %copy-done.73, bf16[256,2048]{1,0:T(8,128)(2,1)} %copy-done.74, ...), custom_call_target="tpu_custom_call" | custom-call | flops 44040192 | bytes 57344 | tf_op jit(solution)/shard_map/pallas_call | solution.py:423
  323.4 7.1 %shard_map.249 = (bf16[256,2688]{1,0:T(8,128)(2,1)}, bf16[256,2688]{1,0:T(8,128)(2,1)}) custom-call(bf16[256,2048]{1,0:T(8,128)(2,1)} %copy-done.15, bf16[256,2048]{1,0:T(8,128)(2,1)} %copy-done.16, bf16[256,2048]{1,0:T(8,128)(2,1)} %copy-done.73, bf16[256,2048]{1,0:T(8,128)(2,1)} %copy-done.74, ...), custom_call_target="tpu_custom_call" | custom-call | flops 44040192 | bytes 57344 | tf_op jit(solution)/shard_map/pallas_call | solution.py:423
  330.4 8.0 %shard_map.248 = (bf16[512,2048]{1,0:T(8,128)(2,1)}, bf16[512,2048]{1,0:T(8,128)(2,1)}) custom-call(bf16[256,896]{1,0:T(8,128)(2,1)S(1)} %get-tuple-element.280.refs_0_.refs_16_, bf16[256,896]{1,0:T(8,128)(2,1)S(1)} %get-tuple-element.281.refs_1_.refs_17_, bf16[256,896]{1,0:T(8,128)(2,1)S(1)} %get-tuple-element.282.refs_2_.refs_18_, ...), custom_call_target="tpu_custom_call" | custom-call | flops 58720256 | bytes 57344 | tf_op jit(solution)/shard_map/pallas_call | solution.py:386
  342.9 4.2 shard_map.251
  348.9 3.6 collective-permute-start.44
  352.5 6.9 %shard_map.253 = (bf16[256,2688]{1,0:T(8,128)(2,1)}, bf16[256,2688]{1,0:T(8,128)(2,1)}) custom-call(bf16[256,2048]{1,0:T(8,128)(2,1)} %copy-done.15, bf16[256,2048]{1,0:T(8,128)(2,1)} %copy-done.16, bf16[256,2048]{1,0:T(8,128)(2,1)} %copy-done.73, bf16[256,2048]{1,0:T(8,128)(2,1)} %copy-done.74, ...), custom_call_target="tpu_custom_call" | custom-call | flops 44040192 | bytes 57344 | tf_op jit(solution)/shard_map/pallas_call | solution.py:423
  359.4 6.9 %shard_map.252 = (bf16[256,2688]{1,0:T(8,128)(2,1)}, bf16[256,2688]{1,0:T(8,128)(2,1)}) custom-call(bf16[256,2048]{1,0:T(8,128)(2,1)} %copy-done.15, bf16[256,2048]{1,0:T(8,128)(2,1)} %copy-done.16, bf16[256,2048]{1,0:T(8,128)(2,1)} %copy-done.73, bf16[256,2048]{1,0:T(8,128)(2,1)} %copy-done.74, ...), custom_call_target="tpu_custom_call" | custom-call | flops 44040192 | bytes 57344 | tf_op jit(solution)/shard_map/pallas_call | solution.py:423
  366.3 8.0 %collective-permute-done.44.refs_1_ = bf16[256,2048]{1,0:T(8,128)(2,1)S(1)} collective-permute-done((bf16[256,2048]{1,0:T(8,128)(2,1)S(1)}, bf16[256,2048]{1,0:T(8,128)(2,1)S(1)}, u32[]{:S(2)}, u32[]{:S(2)}) %collective-permute-start.44) | collective-permute-done | bytes 1048608 | tf_op jit(solution)/shard_map/ppermute | solution.py:676
  379.2 3.8 add_convert_fusion.19
  383.1 20.5 %collective-permute-done.50 = bf16[256,2048]{1,0:T(8,128)(2,1)S(1)} collective-permute-done((bf16[256,2048]{1,0:T(8,128)(2,1)}, bf16[256,2048]{1,0:T(8,128)(2,1)S(1)}, u32[]{:S(2)}, u32[]{:S(2)}) %collective-permute-start.50) | collective-permute-done | bytes 1048608 | tf_op jit(solution)/shard_map/ppermute | solution.py:676
  403.7 6.9 %collective-permute-done.51 = bf16[256,2688]{1,0:T(8,128)(2,1)} collective-permute-done((bf16[256,2688]{1,0:T(8,128)(2,1)}, bf16[256,2688]{1,0:T(8,128)(2,1)}, u32[]{:S(2)}, u32[]{:S(2)}) %collective-permute-start.51) | collective-permute-done | bytes 1376288 | tf_op jit(solution)/shard_map/ppermute | solution.py:673
  416.7 5.4 shard_map.254
  422.2 8.4 %collective-permute-done.54 = bf16[128,2688]{1,0:T(8,128)(2,1)} collective-permute-done((bf16[128,2688]{1,0:T(8,128)(2,1)}, bf16[128,2688]{1,0:T(8,128)(2,1)}, u32[]{:S(2)}, u32[]{:S(2)}) %collective-permute-start.54) | collective-permute-done | bytes 688160 | tf_op jit(solution)/shard_map/ppermute | solution.py:673
  432.1 9.6 %collective-permute-done.53 = bf16[256,2048]{1,0:T(8,128)(2,1)S(1)} collective-permute-done((bf16[256,2048]{1,0:T(8,128)(2,1)}, bf16[256,2048]{1,0:T(8,128)(2,1)S(1)}, u32[]{:S(2)}, u32[]{:S(2)}) %collective-permute-start.53) | collective-permute-done | bytes 1048608 | tf_op jit(solution)/shard_map/ppermute | solution.py:676
  450.1 16.1 %shard_map.256.refs_0_.refs_4_.refs_1_ = bf16[1024,3072]{1,0:T(8,128)(2,1)} custom-call(s32[1]{0:T(128)} %bitcast.3.place_ref, f32[2]{0:T(128)S(1)} %subtract_log_fusion.decay_ref, bf16[256,1024]{1,0:T(8,128)(2,1)S(1)} %get-tuple-element.324.refs_0_, bf16[256,1024]{1,0:T(8,128)(2,1)S(1)} %get-tuple-element.328.refs_1_, ...), custom_call_target="tpu_custom_call" | custom-call | flops 58720256 | bytes 320000 | tf_op jit(solution)/shard_map/pallas_call | solution.py:212
  466.2 9.4 %shard_map.257 = (bf16[256,2048]{1,0:T(8,128)(2,1)S(1)}, f32[8,2048]{1,0:T(8,128)S(1)}) custom-call(bf16[1024,3072]{1,0:T(8,128)(2,1)} %shard_map.256.refs_0_.refs_4_.refs_1_, bf16[128,4096]{1,0:T(8,128)(2,1)S(1)} %get-tuple-element.222.refs_4_.refs_1_.refs_3_.refs_2_, bf16[128,4096]{1,0:T(8,128)(2,1)S(1)} %copy-done.3, ...), custom_call_target="tpu_custom_call" | custom-call | flops 50331648 | bytes 196608 | tf_op jit(solution)/shard_map/pallas_call | solution.py:288
  480.8 3.7 collective-permute-start.59
  484.7 7.8 %shard_map.258 = bf16[512,3072]{1,0:T(8,128)(2,1)} custom-call(bf16[256,2048]{1,0:T(8,128)(2,1)} %fusion.5.refs_0_.refs_18_, bf16[256,2048]{1,0:T(8,128)(2,1)} %collective-permute-done.2.refs_1_.refs_19_, bf16[256,2048]{1,0:T(8,128)(2,1)S(1)} %copy-done.8, bf16[256,2048]{1,0:T(8,128)(2,1)S(1)} %copy-done.11, ...), custom_call_target="tpu_custom_call" | custom-call | flops 50331648 | bytes 98304 | tf_op jit(solution)/shard_map/pallas_call | solution.py:457
  492.5 10.2 %shard_map.259 = (bf16[256,2048]{1,0:T(8,128)(2,1)}, f32[8,2048]{1,0:T(8,128)S(1)}) custom-call(bf16[1024,3072]{1,0:T(8,128)(2,1)} %shard_map.256.refs_0_.refs_4_.refs_1_, bf16[128,4096]{1,0:T(8,128)(2,1)S(1)} %get-tuple-element.222.refs_4_.refs_1_.refs_3_.refs_2_, bf16[128,4096]{1,0:T(8,128)(2,1)S(1)} %copy-done.3, ...), custom_call_target="tpu_custom_call" | custom-call | flops 50331648 | bytes 196608 | tf_op jit(solution)/shard_map/pallas_call | solution.py:288
  502.8 7.8 %shard_map.260 = bf16[512,3072]{1,0:T(8,128)(2,1)} custom-call(bf16[256,2048]{1,0:T(8,128)(2,1)} %fusion.5.refs_0_.refs_18_, bf16[256,2048]{1,0:T(8,128)(2,1)} %collective-permute-done.2.refs_1_.refs_19_, bf16[256,2048]{1,0:T(8,128)(2,1)S(1)} %copy-done.9, bf16[256,2048]{1,0:T(8,128)(2,1)S(1)} %copy-done.11, ...), custom_call_target="tpu_custom_call" | custom-call | flops 50331648 | bytes 98304 | tf_op jit(solution)/shard_map/pallas_call | solution.py:457
  523.0 4.3 shard_map.262
  527.3 9.1 %shard_map.263 = (bf16[256,3072]{1,0:T(8,128)(2,1)}, bf16[256,3072]{1,0:T(8,128)(2,1)}) custom-call(bf16[256,2048]{1,0:T(8,128)(2,1)} %fusion.5.refs_0_.refs_18_, bf16[256,2048]{1,0:T(8,128)(2,1)} %collective-permute-done.2.refs_1_.refs_19_, bf16[256,2048]{1,0:T(8,128)(2,1)S(1)} %copy-done.9, bf16[256,2048]{1,0:T(8,128)(2,1)S(1)} %copy-done.11, ...), custom_call_target="tpu_custom_call" | custom-call | flops 50331648 | bytes 98304 | tf_op jit(solution)/shard_map/pallas_call | solution.py:457
  537.7 13.5 %shard_map.264 = (bf16[256,2048]{1,0:T(8,128)(2,1)S(1)}, bf16[256,2048]{1,0:T(8,128)(2,1)S(1)}, f32[8,2048]{1,0:T(8,128)S(1)}) custom-call(bf16[1024,3072]{1,0:T(8,128)(2,1)} %shard_map.256.refs_0_.refs_4_.refs_1_, bf16[1024,3072]{1,0:T(8,128)(2,1)} %shard_map.256.refs_0_.refs_4_.refs_1_, ...), custom_call_target="tpu_custom_call" | custom-call | flops 100663296 | bytes 196608 | tf_op jit(solution)/shard_map/pallas_call | solution.py:288
  564.8 8.5 %shard_map.266 = (bf16[256,3072]{1,0:T(8,128)(2,1)S(1)}, bf16[256,3072]{1,0:T(8,128)(2,1)}) custom-call(bf16[256,2048]{1,0:T(8,128)(2,1)} %fusion.5.refs_0_.refs_18_, bf16[256,2048]{1,0:T(8,128)(2,1)} %collective-permute-done.2.refs_1_.refs_19_, bf16[256,2048]{1,0:T(8,128)(2,1)S(1)} %copy-done.9, bf16[256,2048]{1,0:T(8,128)(2,1)S(1)} %copy-done.11, ...), custom_call_target="tpu_custom_call" | custom-call | flops 50331648 | bytes 98304 | tf_op jit(solution)/shard_map/pallas_call | solution.py:457
  583.9 4.2 collective-permute-done.68
  598.1 10.7 %collective-permute-done.75 = bf16[256,1024]{1,0:T(8,128)(2,1)S(1)} collective-permute-done((bf16[256,1024]{1,0:T(8,128)(2,1)S(1)}, bf16[256,1024]{1,0:T(8,128)(2,1)S(1)}, u32[]{:S(2)}, u32[]{:S(2)}) %collective-permute-start.75) | collective-permute-done | bytes 524320 | tf_op jit(solution)/shard_map/ppermute | solution.py:673
  611.7 13.2 %collective-permute-done.76 = bf16[256,1024]{1,0:T(8,128)(2,1)S(1)} collective-permute-done((bf16[256,1024]{1,0:T(8,128)(2,1)S(1)}, bf16[256,1024]{1,0:T(8,128)(2,1)S(1)}, u32[]{:S(2)}, u32[]{:S(2)}) %collective-permute-start.76) | collective-permute-done | bytes 524320 | tf_op jit(solution)/shard_map/ppermute | solution.py:673
  (439 shorter events, 205.0 us)
Async XLA Ops:
  6.7 26.3 %collective-permute-start = (bf16[128,4096]{1,0:T(8,128)(2,1)S(1)}, bf16[128,4096]{1,0:T(8,128)(2,1)S(1)}, u32[]{:S(2)}, u32[]{:S(2)}) collective-permute-start(bf16[128,4096]{1,0:T(8,128)(2,1)S(1)} %get-tuple-element.222.refs_4_.refs_1_.refs_3_.refs_2_), channel_id=1, source_target_pairs={{0,8},{4,12},{8,0},{12,4},{16,24},{20,28},{24,16},{28,20},{1,9},{5... | collective-permute-start | bytes 3145736 | tf_op jit(solution)/shard_map/ppermute | solution.py:673
  9.3 25.3 %collective-permute-start.1 = (bf16[128,4096]{1,0:T(8,128)(2,1)S(1)}, bf16[128,4096]{1,0:T(8,128)(2,1)}, u32[]{:S(2)}, u32[]{:S(2)}) collective-permute-start(bf16[128,4096]{1,0:T(8,128)(2,1)S(1)} %get-tuple-element.223.refs_8_.refs_5_.refs_7_.refs_6_), channel_id=1, source_target_pairs={{0,16},{4,20},{8,24},{12,28},{16,0},{20,4},{24,8},{28,12},{1,17},{... | collective-permute-start | bytes 3145736 | tf_op jit(solution)/shard_map/ppermute | solution.py:673
  10.8 23.8 %collective-permute-start.3 = (bf16[256,2048]{1,0:T(8,128)(2,1)}, bf16[256,2048]{1,0:T(8,128)(2,1)}, u32[]{:S(2)}, u32[]{:S(2)}) collective-permute-start(bf16[256,2048]{1,0:T(8,128)(2,1)} %fusion.5.refs_0_.refs_18_), channel_id=1, source_target_pairs={{1,2},{2,1},{5,6},{6,5},{9,10},{10,9},{13,14},{14,13},{17,18},{18,... | collective-permute-start | bytes 3145736 | tf_op jit(solution)/shard_map/ppermute | solution.py:676
  12.4 26.7 %collective-permute-start.2 = (bf16[256,2048]{1,0:T(8,128)(2,1)}, bf16[256,2048]{1,0:T(8,128)(2,1)}, u32[]{:S(2)}, u32[]{:S(2)}) collective-permute-start(bf16[256,2048]{1,0:T(8,128)(2,1)} %fusion.5.refs_0_.refs_18_), channel_id=1, source_target_pairs={{0,1},{1,0},{2,3},{3,2},{4,5},{5,4},{6,7},{7,6},{8,9},{9,8},{10,11... | collective-permute-start | bytes 3145736 | tf_op jit(solution)/shard_map/ppermute | solution.py:676
  39.1 25.9 %collective-permute-start.9 = (bf16[128,4096]{1,0:T(8,128)(2,1)S(1)}, bf16[128,4096]{1,0:T(8,128)(2,1)S(1)}, u32[]{:S(2)}, u32[]{:S(2)}) collective-permute-start(bf16[128,4096]{1,0:T(8,128)(2,1)S(1)} %get-tuple-element.223.refs_8_.refs_5_.refs_7_.refs_6_), channel_id=1, source_target_pairs={{0,4},{4,0},{8,12},{12,8},{16,20},{20,16},{24,28},{28,24},{1,5},{5... | collective-permute-start | bytes 3145736 | tf_op jit(solution)/shard_map/ppermute | solution.py:673
  39.1 25.9 %collective-permute-start.6 = (bf16[128,4096]{1,0:T(8,128)(2,1)S(1)}, bf16[128,4096]{1,0:T(8,128)(2,1)}, u32[]{:S(2)}, u32[]{:S(2)}) collective-permute-start(bf16[128,4096]{1,0:T(8,128)(2,1)S(1)} %get-tuple-element.223.refs_8_.refs_5_.refs_7_.refs_6_), channel_id=1, source_target_pairs={{0,8},{4,12},{8,0},{12,4},{16,24},{20,28},{24,16},{28,20},{1,9},{5... | collective-permute-start | bytes 3145736 | tf_op jit(solution)/shard_map/ppermute | solution.py:673
  39.7 25.4 %collective-permute-start.5 = (bf16[128,4096]{1,0:T(8,128)(2,1)S(1)}, bf16[128,4096]{1,0:T(8,128)(2,1)}, u32[]{:S(2)}, u32[]{:S(2)}) collective-permute-start(bf16[128,4096]{1,0:T(8,128)(2,1)S(1)} %get-tuple-element.222.refs_4_.refs_1_.refs_3_.refs_2_), channel_id=1, source_target_pairs={{0,16},{4,20},{8,24},{12,28},{16,0},{20,4},{24,8},{28,12},{1,17},{... | collective-permute-start | bytes 3145736 | tf_op jit(solution)/shard_map/ppermute | solution.py:673
  40.2 24.9 %collective-permute-start.7 = (bf16[256,2048]{1,0:T(8,128)(2,1)}, bf16[256,2048]{1,0:T(8,128)(2,1)S(1)}, u32[]{:S(2)}, u32[]{:S(2)}) collective-permute-start(bf16[256,2048]{1,0:T(8,128)(2,1)} %collective-permute-done.2.refs_1_.refs_19_), channel_id=1, source_target_pairs={{1,2},{2,1},{5,6},{6,5},{9,10},{10,9},{13,14},{14,13},{17,18},{18,... | collective-permute-start | bytes 3145736 | tf_op jit(solution)/shard_map/ppermute | solution.py:676
  40.9 27.9 %collective-permute-start.8 = (bf16[256,2048]{1,0:T(8,128)(2,1)}, bf16[256,2048]{1,0:T(8,128)(2,1)}, u32[]{:S(2)}, u32[]{:S(2)}) collective-permute-start(bf16[256,2048]{1,0:T(8,128)(2,1)} %collective-permute-done.3), channel_id=1, source_target_pairs={{1,0},{2,3},{5,4},{6,7},{9,8},{10,11},{13,12},{14,15},{17,16},{18,... | collective-permute-start | bytes 3145736 | tf_op jit(solution)/shard_map/ppermute | solution.py:676
  68.9 25.6 %collective-permute-start.10 = (bf16[128,4096]{1,0:T(8,128)(2,1)S(1)}, bf16[128,4096]{1,0:T(8,128)(2,1)S(1)}, u32[]{:S(2)}, u32[]{:S(2)}) collective-permute-start(bf16[128,4096]{1,0:T(8,128)(2,1)S(1)} %collective-permute-done.refs_5_.refs_2_.refs_4_.refs_3_), channel_id=1, source_target_pairs={{0,16},{4,20},{8,24},{12,28},{16,0},{20,4},{24,8},{28,12},{1,17},{... | collective-permute-start | bytes 3145736 | tf_op jit(solution)/shard_map/ppermute | solution.py:673
  70.4 24.1 %collective-permute-start.14 = (bf16[128,4096]{1,0:T(8,128)(2,1)}, bf16[128,4096]{1,0:T(8,128)(2,1)S(1)}, u32[]{:S(2)}, u32[]{:S(2)}) collective-permute-start(bf16[128,4096]{1,0:T(8,128)(2,1)} %collective-permute-done.1.refs_9_.refs_6_.refs_8_.refs_7_), channel_id=1, source_target_pairs={{0,4},{4,0},{8,12},{12,8},{16,20},{20,16},{24,28},{28,24},{1,5},{5... | collective-permute-start | bytes 3145736 | tf_op jit(solution)/shard_map/ppermute | solution.py:673
  70.6 25.7 %collective-permute-start.11 = (bf16[128,4096]{1,0:T(8,128)(2,1)}, bf16[128,4096]{1,0:T(8,128)(2,1)}, u32[]{:S(2)}, u32[]{:S(2)}) collective-permute-start(bf16[128,4096]{1,0:T(8,128)(2,1)} %collective-permute-done.1.refs_9_.refs_6_.refs_8_.refs_7_), channel_id=1, source_target_pairs={{0,8},{4,12},{8,0},{12,4},{16,24},{20,28},{24,16},{28,20},{1,9},{5... | collective-permute-start | bytes 3145736 | tf_op jit(solution)/shard_map/ppermute | solution.py:673
  72.1 26.9 %collective-permute-start.12 = (bf16[256,2048]{1,0:T(8,128)(2,1)S(1)}, bf16[256,2048]{1,0:T(8,128)(2,1)S(1)}, u32[]{:S(2)}, u32[]{:S(2)}) collective-permute-start(bf16[256,2048]{1,0:T(8,128)(2,1)S(1)} %collective-permute-done.7), channel_id=1, source_target_pairs={{1,0},{2,3},{5,4},{6,7},{9,8},{10,11},{13,12},{14,15},{17,16},{18,... | collective-permute-start | bytes 3145736 | tf_op jit(solution)/shard_map/ppermute | solution.py:676
  100.1 26.2 %collective-permute-start.19 = (bf16[256,2688]{1,0:T(8,128)(2,1)}, bf16[256,2688]{1,0:T(8,128)(2,1)}, u32[]{:S(2)}, u32[]{:S(2)}) collective-permute-start(bf16[256,2688]{1,0:T(8,128)(2,1)} %shard_map.240), channel_id=1, source_target_pairs={{4,7},{5,6},{6,5},{7,4},{12,15},{13,14},{14,13},{15,12},{20,23},{2... | collective-permute-start | bytes 4128776 | tf_op jit(solution)/shard_map/ppermute | solution.py:814
  108.0 49.1 %collective-permute-start.24 = (bf16[256,2048]{1,0:T(8,128)(2,1)}, bf16[256,2048]{1,0:T(8,128)(2,1)}, u32[]{:S(2)}, u32[]{:S(2)}) collective-permute-start(bf16[256,2048]{1,0:T(8,128)(2,1)} %broadcast_select_fusion.own_grad_ref.refs_4_.grad_final), channel_id=1, source_target_pairs={{0,1},{1,0},{2,3},{3,2},{4,5},{5,4},{6,7},{7,6},{8,9},{9,8},{10,11... | collective-permute-start | bytes 3145736 | tf_op jit(solution)/shard_map/ppermute | solution.py:676
  128.7 28.4 %collective-permute-start.23 = (bf16[128,2688]{1,0:T(8,128)(2,1)}, bf16[128,2688]{1,0:T(8,128)(2,1)}, u32[]{:S(2)}, u32[]{:S(2)}) collective-permute-start(bf16[128,2688]{1,0:T(8,128)(2,1)} %slice.140), channel_id=1, source_target_pairs={{4,0},{5,1},{6,2},{7,3},{12,8},{13,9},{14,10},{15,11},{20,16},{21,... | collective-permute-start | bytes 2064392 | tf_op jit(solution)/shard_map/ppermute | solution.py:844
  158.6 24.6 %collective-permute-start.25 = (bf16[256,2048]{1,0:T(8,128)(2,1)S(1)}, bf16[256,2048]{1,0:T(8,128)(2,1)S(1)}, u32[]{:S(2)}, u32[]{:S(2)}) collective-permute-start(bf16[256,2048]{1,0:T(8,128)(2,1)S(1)} %shard_map.244), channel_id=1, source_target_pairs={{0,1},{3,2},{4,5},{7,6},{8,9},{11,10},{12,13},{15,14},{16,17},{19,... | collective-permute-start | bytes 3145736 | tf_op jit(solution)/shard_map/ppermute | solution.py:676
  163.9 30.3 %collective-permute-start.27 = (bf16[256,2688]{1,0:T(8,128)(2,1)S(1)}, bf16[256,2688]{1,0:T(8,128)(2,1)S(1)}, u32[]{:S(2)}, u32[]{:S(2)}) collective-permute-start(bf16[256,2688]{1,0:T(8,128)(2,1)S(1)} %pad_maximum_fusion.refs_0_.refs_4_), channel_id=1, source_target_pairs={{0,16},{4,20},{8,24},{12,28},{16,0},{20,4},{24,8},{28,12},{1,17},{... | collective-permute-start | bytes 4128776 | tf_op jit(solution)/shard_map/ppermute | solution.py:673
  165.5 29.9 %collective-permute-start.28 = (bf16[256,2688]{1,0:T(8,128)(2,1)S(1)}, bf16[256,2688]{1,0:T(8,128)(2,1)S(1)}, u32[]{:S(2)}, u32[]{:S(2)}) collective-permute-start(bf16[256,2688]{1,0:T(8,128)(2,1)S(1)} %pad_maximum_fusion.1.refs_2_.refs_6_), channel_id=1, source_target_pairs={{0,8},{4,12},{8,0},{12,4},{16,24},{20,28},{24,16},{28,20},{1,9},{5... | collective-permute-start | bytes 4128776 | tf_op jit(solution)/shard_map/ppermute | solution.py:673
  196.1 24.9 %collective-permute-start.33 = (bf16[256,2048]{1,0:T(8,128)(2,1)S(1)}, bf16[256,2048]{1,0:T(8,128)(2,1)S(1)}, u32[]{:S(2)}, u32[]{:S(2)}) collective-permute-start(bf16[256,2048]{1,0:T(8,128)(2,1)S(1)} %get-tuple-element.263), channel_id=1, source_target_pairs={{0,1},{3,2},{4,5},{7,6},{8,9},{11,10},{12,13},{15,14},{16,17},{19,... | collective-permute-start | bytes 3145736 | tf_op jit(solution)/shard_map/ppermute | solution.py:676
  225.3 29.0 %collective-permute-start.36 = (bf16[256,2688]{1,0:T(8,128)(2,1)S(1)}, bf16[256,2688]{1,0:T(8,128)(2,1)S(1)}, u32[]{:S(2)}, u32[]{:S(2)}) collective-permute-start(bf16[256,2688]{1,0:T(8,128)(2,1)S(1)} %constant_dynamic-update-slice_fusion.refs_4_.refs_8_), channel_id=1, source_target_pairs={{0,16},{4,20},{8,24},{12,28},{16,0},{20,4},{24,8},{28,12},{1,17},{... | collective-permute-start | bytes 4128776 | tf_op jit(solution)/shard_map/ppermute | solution.py:673
  226.0 28.8 %collective-permute-start.37 = (bf16[256,2688]{1,0:T(8,128)(2,1)S(1)}, bf16[256,2688]{1,0:T(8,128)(2,1)S(1)}, u32[]{:S(2)}, u32[]{:S(2)}) collective-permute-start(bf16[256,2688]{1,0:T(8,128)(2,1)S(1)} %constant_dynamic-update-slice_fusion.2.refs_6_.refs_10_), channel_id=1, source_target_pairs={{0,8},{4,12},{8,0},{12,4},{16,24},{20,28},{24,16},{28,20},{1,9},{5... | collective-permute-start | bytes 4128776 | tf_op jit(solution)/shard_map/ppermute | solution.py:673
  254.8 25.6 %collective-permute-start.39 = (bf16[256,2048]{1,0:T(8,128)(2,1)S(1)}, bf16[256,2048]{1,0:T(8,128)(2,1)S(1)}, u32[]{:S(2)}, u32[]{:S(2)}) collective-permute-start(bf16[256,2048]{1,0:T(8,128)(2,1)S(1)} %multiply_convert_fusion.own_ref.refs_0_), channel_id=1, source_target_pairs={{0,1},{1,0},{2,3},{3,2},{4,5},{5,4},{6,7},{7,6},{8,9},{9,8},{10,11... | collective-permute-start | bytes 3145736 | tf_op jit(solution)/shard_map/ppermute | solution.py:676
  314.6 25.3 %collective-permute-start.43 = (bf16[256,2048]{1,0:T(8,128)(2,1)S(1)}, bf16[256,2048]{1,0:T(8,128)(2,1)S(1)}, u32[]{:S(2)}, u32[]{:S(2)}) collective-permute-start(bf16[256,2048]{1,0:T(8,128)(2,1)S(1)} %add_convert_fusion.3), channel_id=1, source_target_pairs={{0,1},{1,0},{2,3},{3,2},{4,5},{5,4},{6,7},{7,6},{8,9},{9,8},{10,11... | collective-permute-start | bytes 3145736 | tf_op jit(solution)/shard_map/ppermute | solution.py:676
  339.9 34.4 %collective-permute-start.46 = (bf16[256,2688]{1,0:T(8,128)(2,1)}, bf16[256,2688]{1,0:T(8,128)(2,1)S(1)}, u32[]{:S(2)}, u32[]{:S(2)}) collective-permute-start(bf16[256,2688]{1,0:T(8,128)(2,1)} %get-tuple-element.303), channel_id=1, source_target_pairs={{0,16},{4,20},{8,24},{12,28},{16,0},{20,4},{24,8},{28,12},{1,17},{... | collective-permute-start | bytes 4128776 | tf_op jit(solution)/shard_map/ppermute | solution.py:673
  341.4 32.9 %collective-permute-start.47 = (bf16[256,2688]{1,0:T(8,128)(2,1)}, bf16[256,2688]{1,0:T(8,128)(2,1)}, u32[]{:S(2)}, u32[]{:S(2)}) collective-permute-start(bf16[256,2688]{1,0:T(8,128)(2,1)} %get-tuple-element.304), channel_id=1, source_target_pairs={{0,8},{4,12},{8,0},{12,4},{16,24},{20,28},{24,16},{28,20},{1,9},{5... | collective-permute-start | bytes 4128776 | tf_op jit(solution)/shard_map/ppermute | solution.py:673
  348.9 25.4 %collective-permute-start.44 = (bf16[256,2048]{1,0:T(8,128)(2,1)S(1)}, bf16[256,2048]{1,0:T(8,128)(2,1)S(1)}, u32[]{:S(2)}, u32[]{:S(2)}) collective-permute-start(bf16[256,2048]{1,0:T(8,128)(2,1)S(1)} %get-tuple-element.323.refs_0_), channel_id=1, source_target_pairs={{0,1},{1,0},{2,3},{3,2},{4,5},{5,4},{6,7},{7,6},{8,9},{9,8},{10,11... | collective-permute-start | bytes 3145736 | tf_op jit(solution)/shard_map/ppermute | solution.py:676
  374.3 36.6 %collective-permute-start.48 = (bf16[512,2048]{1,0:T(8,128)(2,1)}, bf16[512,2048]{1,0:T(8,128)(2,1)S(1)}, u32[]{:S(2)}, u32[]{:S(2)}) collective-permute-start(bf16[512,2048]{1,0:T(8,128)(2,1)} %get-tuple-element.311), channel_id=1, source_target_pairs={{0,4},{4,0},{8,12},{12,8},{16,20},{20,16},{24,28},{28,24},{1,5},{5... | collective-permute-start | bytes 6291464 | tf_op jit(solution)/shard_map/ppermute | solution.py:673
  375.9 27.6 %collective-permute-start.50 = (bf16[256,2048]{1,0:T(8,128)(2,1)}, bf16[256,2048]{1,0:T(8,128)(2,1)S(1)}, u32[]{:S(2)}, u32[]{:S(2)}) collective-permute-start(bf16[256,2048]{1,0:T(8,128)(2,1)} %collective-permute-done.45), channel_id=1, source_target_pairs={{1,0},{2,3},{5,4},{6,7},{9,8},{10,11},{13,12},{14,15},{17,16},{18,... | collective-permute-start | bytes 3145736 | tf_op jit(solution)/shard_map/ppermute | solution.py:676
  377.6 33.0 %collective-permute-start.51 = (bf16[256,2688]{1,0:T(8,128)(2,1)}, bf16[256,2688]{1,0:T(8,128)(2,1)}, u32[]{:S(2)}, u32[]{:S(2)}) collective-permute-start(bf16[256,2688]{1,0:T(8,128)(2,1)} %get-tuple-element.314), channel_id=1, source_target_pairs={{0,16},{4,20},{8,24},{12,28},{16,0},{20,4},{24,8},{28,12},{1,17},{... | collective-permute-start | bytes 4128776 | tf_op jit(solution)/shard_map/ppermute | solution.py:673
  378.3 32.5 %collective-permute-start.52 = (bf16[256,2688]{1,0:T(8,128)(2,1)}, bf16[256,2688]{1,0:T(8,128)(2,1)S(1)}, u32[]{:S(2)}, u32[]{:S(2)}) collective-permute-start(bf16[256,2688]{1,0:T(8,128)(2,1)} %get-tuple-element.315), channel_id=1, source_target_pairs={{0,8},{4,12},{8,0},{12,4},{16,24},{20,28},{24,16},{28,20},{1,9},{5... | collective-permute-start | bytes 4128776 | tf_op jit(solution)/shard_map/ppermute | solution.py:673
  415.4 26.3 %collective-permute-start.53 = (bf16[256,2048]{1,0:T(8,128)(2,1)}, bf16[256,2048]{1,0:T(8,128)(2,1)S(1)}, u32[]{:S(2)}, u32[]{:S(2)}) collective-permute-start(bf16[256,2048]{1,0:T(8,128)(2,1)} %collective-permute-done.49), channel_id=1, source_target_pairs={{1,0},{2,3},{5,4},{6,7},{9,8},{10,11},{13,12},{14,15},{17,16},{18,... | collective-permute-start | bytes 3145736 | tf_op jit(solution)/shard_map/ppermute | solution.py:676
  441.7 33.9 %collective-permute-start.57 = (bf16[128,2688]{1,0:T(8,128)(2,1)}, bf16[128,2688]{1,0:T(8,128)(2,1)}, u32[]{:S(2)}, u32[]{:S(2)}) collective-permute-start(bf16[128,2688]{1,0:T(8,128)(2,1)} %add_convert_fusion.15), channel_id=1, source_target_pairs={{0,8},{4,12},{8,0},{12,4},{16,24},{20,28},{24,16},{28,20},{1,9},{5... | collective-permute-start | bytes 2064392 | tf_op jit(solution)/shard_map/ppermute | solution.py:673
  442.9 35.5 %collective-permute-start.58 = (bf16[128,2688]{1,0:T(8,128)(2,1)S(1)}, bf16[128,2688]{1,0:T(8,128)(2,1)}, u32[]{:S(2)}, u32[]{:S(2)}) collective-permute-start(bf16[128,2688]{1,0:T(8,128)(2,1)S(1)} %add_convert_fusion.12), channel_id=1, source_target_pairs={{0,16},{4,20},{8,24},{12,28},{16,0},{20,4},{24,8},{28,12},{1,17},{... | collective-permute-start | bytes 2064392 | tf_op jit(solution)/shard_map/ppermute | solution.py:673
  444.8 36.0 %collective-permute-start.56 = (bf16[256,2688]{1,0:T(8,128)(2,1)}, bf16[256,2688]{1,0:T(8,128)(2,1)}, u32[]{:S(2)}, u32[]{:S(2)}) collective-permute-start(bf16[256,2688]{1,0:T(8,128)(2,1)} %pad_maximum_fusion.2), channel_id=1, source_target_pairs={{7,4},{6,5},{5,6},{4,7},{15,12},{14,13},{13,14},{12,15},{23,20},{2... | collective-permute-start | bytes 4128776 | tf_op jit(solution)/shard_map/ppermute | solution.py:926
  480.8 29.8 %collective-permute-start.59 = (bf16[256,2048]{1,0:T(8,128)(2,1)S(1)}, bf16[256,2048]{1,0:T(8,128)(2,1)}, u32[]{:S(2)}, u32[]{:S(2)}) collective-permute-start(bf16[256,2048]{1,0:T(8,128)(2,1)S(1)} %get-tuple-element.345), channel_id=1, source_target_pairs={{0,1},{3,2},{4,5},{7,6},{8,9},{11,10},{12,13},{15,14},{16,17},{19,... | collective-permute-start | bytes 3145736 | tf_op jit(solution)/shard_map/ppermute | solution.py:676
  484.5 29.8 %collective-permute-start.60 = (bf16[128,2688]{1,0:T(8,128)(2,1)}, bf16[128,2688]{1,0:T(8,128)(2,1)}, u32[]{:S(2)}, u32[]{:S(2)}) collective-permute-start(bf16[128,2688]{1,0:T(8,128)(2,1)} %add_convert_fusion.14), channel_id=1, source_target_pairs={{0,4},{1,5},{2,6},{3,7},{8,12},{9,13},{10,14},{11,15},{16,20},{17,... | collective-permute-start | bytes 2064392 | tf_op jit(solution)/shard_map/ppermute | solution.py:937
  515.8 35.4 %collective-permute-start.64 = (bf16[512,3072]{1,0:T(8,128)(2,1)}, bf16[512,3072]{1,0:T(8,128)(2,1)}, u32[]{:S(2)}, u32[]{:S(2)}) collective-permute-start(bf16[512,3072]{1,0:T(8,128)(2,1)} %shard_map.260), channel_id=1, source_target_pairs={{0,4},{4,0},{8,12},{12,8},{16,20},{20,16},{24,28},{28,24},{1,5},{5... | collective-permute-start | bytes 9437192 | tf_op jit(solution)/shard_map/ppermute | solution.py:673
  515.9 35.3 %collective-permute-start.61 = (bf16[256,2048]{1,0:T(8,128)(2,1)}, bf16[256,2048]{1,0:T(8,128)(2,1)}, u32[]{:S(2)}, u32[]{:S(2)}) collective-permute-start(bf16[256,2048]{1,0:T(8,128)(2,1)} %add_convert_fusion.2), channel_id=1, source_target_pairs={{1,2},{2,1},{5,6},{6,5},{9,10},{10,9},{13,14},{14,13},{17,18},{18,... | collective-permute-start | bytes 3145736 | tf_op jit(solution)/shard_map/ppermute | solution.py:676
  517.6 33.7 %collective-permute-start.62 = (bf16[256,2048]{1,0:T(8,128)(2,1)}, bf16[256,2048]{1,0:T(8,128)(2,1)}, u32[]{:S(2)}, u32[]{:S(2)}) collective-permute-start(bf16[256,2048]{1,0:T(8,128)(2,1)} %get-tuple-element.350), channel_id=1, source_target_pairs={{0,1},{3,2},{4,5},{7,6},{8,9},{11,10},{12,13},{15,14},{16,17},{19,... | collective-permute-start | bytes 3145736 | tf_op jit(solution)/shard_map/ppermute | solution.py:676
  536.4 51.7 %collective-permute-start.67 = (bf16[256,3072]{1,0:T(8,128)(2,1)}, bf16[256,3072]{1,0:T(8,128)(2,1)}, u32[]{:S(2)}, u32[]{:S(2)}) collective-permute-start(bf16[256,3072]{1,0:T(8,128)(2,1)} %get-tuple-element.355), channel_id=1, source_target_pairs={{0,16},{4,20},{8,24},{12,28},{16,0},{20,4},{24,8},{28,12},{1,17},{... | collective-permute-start | bytes 4718600 | tf_op jit(solution)/shard_map/ppermute | solution.py:673
  551.2 36.8 %collective-permute-start.68 = (bf16[256,3072]{1,0:T(8,128)(2,1)}, bf16[256,3072]{1,0:T(8,128)(2,1)}, u32[]{:S(2)}, u32[]{:S(2)}) collective-permute-start(bf16[256,3072]{1,0:T(8,128)(2,1)} %get-tuple-element.363), channel_id=1, source_target_pairs={{0,8},{4,12},{8,0},{12,4},{16,24},{20,28},{24,16},{28,20},{1,9},{5... | collective-permute-start | bytes 4718600 | tf_op jit(solution)/shard_map/ppermute | solution.py:673
  552.6 24.3 %collective-permute-start.71 = (bf16[512,1024]{1,0:T(8,128)(2,1)}, bf16[512,1024]{1,0:T(8,128)(2,1)}, u32[]{:S(2)}, u32[]{:S(2)}) collective-permute-start(bf16[512,1024]{1,0:T(8,128)(2,1)} %shard_map.262), channel_id=1, source_target_pairs={{0,4},{4,0},{8,12},{12,8},{16,20},{20,16},{24,28},{28,24},{1,5},{5... | collective-permute-start | bytes 3145736 | tf_op jit(solution)/shard_map/ppermute | solution.py:673
  558.1 25.7 %collective-permute-start.65 = (bf16[256,2048]{1,0:T(8,128)(2,1)}, bf16[256,2048]{1,0:T(8,128)(2,1)S(1)}, u32[]{:S(2)}, u32[]{:S(2)}) collective-permute-start(bf16[256,2048]{1,0:T(8,128)(2,1)} %add_convert_fusion.1), channel_id=1, source_target_pairs={{0,1},{1,0},{2,3},{3,2},{4,5},{5,4},{6,7},{7,6},{8,9},{9,8},{10,11... | collective-permute-start | bytes 3145736 | tf_op jit(solution)/shard_map/ppermute | solution.py:676
  558.2 25.7 %collective-permute-start.66 = (bf16[256,2048]{1,0:T(8,128)(2,1)}, bf16[256,2048]{1,0:T(8,128)(2,1)S(1)}, u32[]{:S(2)}, u32[]{:S(2)}) collective-permute-start(bf16[256,2048]{1,0:T(8,128)(2,1)} %add_convert_fusion), channel_id=1, source_target_pairs={{1,2},{2,1},{5,6},{6,5},{9,10},{10,9},{13,14},{14,13},{17,18},{18,... | collective-permute-start | bytes 3145736 | tf_op jit(solution)/shard_map/ppermute | solution.py:676
  594.8 30.1 %collective-permute-start.73 = (bf16[128,3072]{1,0:T(8,128)(2,1)}, bf16[128,3072]{1,0:T(8,128)(2,1)S(1)}, u32[]{:S(2)}, u32[]{:S(2)}) collective-permute-start(bf16[128,3072]{1,0:T(8,128)(2,1)} %get-tuple-element.380), channel_id=1, source_target_pairs={{0,8},{4,12},{8,0},{12,4},{16,24},{20,28},{24,16},{28,20},{1,9},{5... | collective-permute-start | bytes 2359304 | tf_op jit(solution)/shard_map/ppermute | solution.py:673
  595.5 29.4 %collective-permute-start.74 = (bf16[128,3072]{1,0:T(8,128)(2,1)}, bf16[128,3072]{1,0:T(8,128)(2,1)S(1)}, u32[]{:S(2)}, u32[]{:S(2)}) collective-permute-start(bf16[128,3072]{1,0:T(8,128)(2,1)} %get-tuple-element.383), channel_id=1, source_target_pairs={{0,16},{4,20},{8,24},{12,28},{16,0},{20,4},{24,8},{28,12},{1,17},{... | collective-permute-start | bytes 2359304 | tf_op jit(solution)/shard_map/ppermute | solution.py:673
  596.5 28.3 %collective-permute-start.72 = (bf16[256,2048]{1,0:T(8,128)(2,1)S(1)}, bf16[256,2048]{1,0:T(8,128)(2,1)S(1)}, u32[]{:S(2)}, u32[]{:S(2)}) collective-permute-start(bf16[256,2048]{1,0:T(8,128)(2,1)S(1)} %copy-done.99), channel_id=1, source_target_pairs={{0,1},{1,0},{2,3},{3,2},{4,5},{5,4},{6,7},{7,6},{8,9},{9,8},{10,11... | collective-permute-start | bytes 3145736 | tf_op jit(solution)/shard_map/ppermute | solution.py:676
  (147 other events, 1866.4 us)

commit v4 on v3

--- a/solution.py
+++ b/solution.py
@@ -306,11 +306,10 @@
 
 
 def mlp_kernel(pieces, units, own_ref, other_ref, own_grad_ref, other_grad_ref, *refs):
-    sources, outs = refs[:pieces], refs[pieces : pieces + 8]
-    gate_ref, up_ref, down_ref, semaphores = refs[pieces + 8 :]
-    rows = own_ref.shape[0]
+    sources, outs, weights = refs[:pieces], refs[pieces : pieces + 8], refs[pieces + 8 : pieces + 11]
+    semaphores = refs[pieces + 11]
     copies = []
-    for part, target in enumerate((gate_ref, up_ref, down_ref)):
+    for part, target in enumerate(weights):
         place = 0
         for index, source in enumerate(sources):
             height = source.shape[0]
@@ -322,17 +321,28 @@
             copy.start()
             copies.append(copy)
             place += height
-    third = pieces
+
+    def ready(part):
+        for copy in copies[part * pieces : (part + 1) * pieces]:
+            copy.wait()
+
+    mlp_body(ready, own_ref, other_ref, own_grad_ref, other_grad_ref, weights, outs)
+
+
+def mlp_again_kernel(own_ref, other_ref, own_grad_ref, other_grad_ref, *refs):
+    mlp_body(lambda part: None, own_ref, other_ref, own_grad_ref, other_grad_ref, refs[:3], refs[3:])
+
+
+def mlp_body(ready, own_ref, other_ref, own_grad_ref, other_grad_ref, weights, outs):
+    gate_ref, up_ref, down_ref = weights
+    rows = own_ref.shape[0]
     left = jnp.concatenate([own_ref[...], turn(other_ref[...])], 0)
     grad = jnp.concatenate([own_grad_ref[...], turn(other_grad_ref[...])], 0)
-    for copy in copies[:third]:
-        copy.wait()
+    ready(0)
     gate = times_plain(left, gate_ref[...])
-    for copy in copies[third : 2 * third]:
-        copy.wait()
+    ready(1)
     up = times_plain(left, up_ref[...])
-    for copy in copies[2 * third :]:
-        copy.wait()
+    ready(2)
     grad_hidden = times_plain(grad, down_ref[...])
     below = 0.5 + 0.5 * lax.erf(gate * (0.5**0.5))
     density = jnp.exp(-0.5 * gate * gate) * 0.3989422804014327
@@ -350,48 +360,49 @@
     outs[7][...] = turn(back[rows:]).astype(BF16)
 
 
-def mlp(own, other, own_grad, other_grad, pieces):
+def mlp(own, other, own_grad, other_grad, pieces, weights=None):
     rows, width = own.shape
-    units = pieces[0].shape[1] // 3
+    units = weights[0].shape[1] if weights else pieces[0].shape[1] // 3
     narrow = pl.BlockSpec((rows, units), lambda i: (0, 0))
     wide = pl.BlockSpec((rows, width), lambda i: (0, 0))
+    whole = pl.BlockSpec((width, units), lambda i: (0, 0))
     small, large = jax.ShapeDtypeStruct((rows, units), BF16), jax.ShapeDtypeStruct((rows, width), BF16)
-    return pl.pallas_call(
-        partial(mlp_kernel, len(pieces), units),
-        out_shape=[small] * 6 + [large] * 2,
+    handed = [] if weights else [jax.ShapeDtypeStruct((width, units), BF16)] * 3
+    return pl.pallas_call(
+        mlp_again_kernel if weights else partial(mlp_kernel, len(pieces), units),
+        out_shape=[small] * 6 + [large] * 2 + handed,
         grid=(1,),
-        in_specs=[wide] * 4 + [pl.BlockSpec(memory_space=pl.ANY)] * len(pieces),
-        out_specs=[narrow] * 6 + [wide] * 2,
-        scratch_shapes=[pltpu.VMEM((width, units), BF16)] * 3 + [pltpu.SemaphoreType.DMA((3, len(pieces)))],
+        in_specs=[wide] * 4
+        + ([whole] * 3 if weights else [pl.BlockSpec(memory_space=pl.ANY)] * len(pieces)),
+        out_specs=[narrow] * 6 + [wide] * 2 + [whole] * len(handed),
+        scratch_shapes=[] if weights else [pltpu.SemaphoreType.DMA((3, len(pieces)))],
         compiler_params=params(),
         cost_estimate=cost(2 * 2 * rows * width * units * 5, 6 * width * units),
-    )(own, other, own_grad, other_grad, *pieces)
-
-
-def down_kernel(pieces, *refs):
-    lefts, weights, outs = refs[:4], refs[4 : 4 + pieces], refs[4 + pieces :]
-    rows = lefts[0].shape[0]
-    weight = jnp.concatenate([ref[...] for ref in weights], 0)
+    )(own, other, own_grad, other_grad, *(weights or pieces))
+
+
+def down_kernel(*refs):
+    lefts, weight, outs = refs[:4], refs[4], refs[5:]
     for core in range(2):
         left = jnp.concatenate([lefts[2 * core][...], lefts[2 * core + 1][...]], 0)
-        result = times_right(left, weight)
+        result = times_right(left, weight[...])
         outs[core][...] = (turn(result) if core else result).astype(BF16)
 
 
-def mlp_down(hidden, pieces):
+def mlp_down(hidden, weight):
     rows, units = hidden[0].shape
-    width = sum(p.shape[0] for p in pieces)
+    width = weight.shape[0]
     whole = pl.BlockSpec((rows, units), lambda n: (0, 0))
     out = pl.BlockSpec((2 * rows, width), lambda n: (0, 0))
     return pl.pallas_call(
-        partial(down_kernel, len(pieces)),
+        down_kernel,
         out_shape=[jax.ShapeDtypeStruct((2 * rows, width), BF16)] * 2,
         grid=(1,),
-        in_specs=[whole] * 4 + [pl.BlockSpec((p.shape[0], units), lambda n: (0, 2)) for p in pieces],
+        in_specs=[whole] * 4 + [pl.BlockSpec((width, units), lambda n: (0, 0))],
         out_specs=[out] * 2,
         compiler_params=params(),
         cost_estimate=cost(8 * rows * width * units, 2 * width * units),
-    )(*hidden, *pieces)
+    )(*hidden, weight)
 
 
 def mlp_grad_kernel(*refs):
@@ -687,6 +698,7 @@
 
     top = tensor_size - 1
     to_even = [(pair(m | 1, t), pair(m, t)) for m in range(0, dp_size, 2) for t in range(tensor_size)]
+    stay = [(pair(m, t), pair(m, t)) for m in range(0, dp_size, 2) for t in range(tensor_size)]
     to_odd = [(pair(m, t), pair(m | 1, t ^ top)) for m in range(0, dp_size, 2) for t in range(tensor_size)]
     odd_turn = [(pair(m | 1, t), pair(m | 1, t ^ top)) for m in range(0, dp_size, 2) for t in range(tensor_size)]
     both = ("dp", "tensor")
@@ -776,6 +788,7 @@
     cosines, sines = jnp.asarray(np.cos(angles)), jnp.asarray(np.sin(angles))
 
     token = [mine_arg]
+    spans = slice(0, half_rows), slice(half_rows, shard_rows)
     proj_columns, out_columns = 2 * heads * (KEY + VPAD), heads * VPAD
     padded = -(-units // LANES) * LANES
 
@@ -811,13 +824,12 @@
     down_all = further([sent_down, down_one, down_two, down_three], down_bits)
     up_core = [core_one[0], core_two[0]] + [to_core(p) for p in up_all[2:]]
     down_core = [core_one[1], core_two[1]] + [to_core(p) for p in down_all[2:]]
-    turned = lax.ppermute(hold(local_two), both, odd_turn)
+    mlp_zero = [lax.ppermute(hold(local_two[span]), both, odd_turn + stay) for span in spans]
     grad_beside = swap_tensor(hold(grad_own), 1)
     close(*up_core, *down_core)
     attn_low = up_all + down_all + up_core + down_core
     first_slots = line_all(first_own, first_beside, first_middle, *first_far, first_last)
 
-    spans = slice(0, half_rows), slice(half_rows, shard_rows)
     orders = up_bits, down_bits
 
     def level_one(halves):
@@ -837,10 +849,9 @@
 
     grad_core = to_core(grad_own)
     projected = rows_times([hold(first_slots[0]), *first_slots[1:]], attn_low, 0, proj_columns)
-    close(turned, projected[0], grad_core)
-
-    mlp_zero = [jnp.where(odd, hold(turned)[span], local_two[span]) for span in spans]
-    zero_come = level_one(mlp_zero)
+    close(*mlp_zero, projected[0], grad_core)
+
+    zero_come = level_one([hold(half) for half in mlp_zero])
     mlp_one = [lax.ppermute(hold(local_two)[spans[0]], both, to_even + to_odd)]
     query, key, value, normed_head, scale_head, mixed = retain(
         [hold(projected[0]), *projected[1:]], place_arg, log_decay, cosines, sines, heads
@@ -877,7 +888,7 @@
 
     second_far = to_core(second_beside)
     second_rows = [second_own, second_beside, second_core, second_far]
-    second_part = mlp(hold(second_beside), second_far, grad_rows[1], grad_rows[3], mlp_pieces)
+    second_part = mlp(hold(second_beside), second_far, grad_rows[1], grad_rows[3], None, first_part[8:])
     far_core = swap_dp(second_part[7], 1)
     hidden, grad_gate, grad_up = (
         [first_part[2 * i], second_part[2 * i], first_part[2 * i + 1], second_part[2 * i + 1]] for i in range(3)
@@ -892,49 +903,53 @@
 
     second_back = swap_tensor(hold(far), 1)
     high = [mlp_grad(1, 0), mlp_grad(1, 1)]
-    down_own, down_other = mlp_down([hold(hidden[0]), *hidden[1:]], mlp_pieces)
+    down_own, down_other = mlp_down([hold(hidden[0]), *hidden[1:]], first_part[10])
     close(second_back, *high[0], *high[1], down_own)
 
     attn_own, grad_middle, grad_gain_two = middle_back(near, hold(second_back), middle, grad_own, gain_second)
     attn_beside = swap_tensor(attn_own, 1)
-    attn_middle = move_tensor(attn_own, across)
+    attn_second = swap_tensor(attn_own, 2)
     come = [[sum_start(high[0][0], up_bits), sum_start(high[0][1], down_bits)]]
+    come.append(
+        [sum_start(after(high[1][0], come[0][0]), up_bits), sum_start(after(high[1][1], come[0][1]), down_bits)]
+    )
     low = [mlp_grad(0, 0), mlp_grad(0, 1)]
-    close(attn_beside, attn_middle, *come[0], *low[0], *low[1])
-
-    attn_far = line_out(None, attn_beside, attn_middle)
-    come.append([sum_start(high[1][0], up_bits), sum_start(high[1][1], down_bits)])
     down_core = to_core(down_other)
-    splits = [[sum_split(low[0][part], hold(come[0][part])) for part in range(2)]]
-    close(*attn_far, *come[1], down_core, *splits[0][0], *splits[0][1])
-
-    attn_last = move_tensor(hold(attn_far[0]), outward)
+    splits = [[sum_split(low[0][part], come[0][part]) for part in range(2)]]
+    close(attn_beside, attn_second, *come[1], *low[1], down_core, *splits[0][0], *splits[0][1])
+
+    attn_middle = move_tensor(hold(attn_own), across)
+    attn_last = move_tensor(hold(attn_second), outward)
     splits.append([sum_split(low[1][part], hold(come[1][part])) for part in range(2)])
 
     def mlp_end(core):
-        return [add(*sum_end(*splits[core][part], orders[part])).astype(BF16) for part in range(2)]
-
-    mlp_total = [mlp_end(0)]
-    attn_third = attn_far[0], attn_far[1]
-    attn_second = jnp.where(inner, *attn_third)
+        return [sum_end(*splits[core][part], orders[part]) for part in range(2)]
+
+    def mlp_sum(ends):
+        return [add(*end).astype(BF16) for end in ends]
+
+    mlp_total = [mlp_sum(mlp_end(0))]
     grad_mixed = rows_times([hold(attn_own), attn_beside, attn_second], attn_low, proj_columns, out_columns)
     down_sum = add(down_own, hold(down_core))
     down_sent = down_sum[rows:].astype(BF16)
-    close(attn_last, *mlp_total[0], grad_mixed[0])
+    close(attn_middle, attn_last, *mlp_total[0], grad_mixed[0])
     attn_slots = attn_own, attn_beside, attn_second, jnp.where(inner, attn_middle, hold(attn_last))
 
-    grad_turn = lax.ppermute(jnp.concatenate([hold(t) for t in mlp_total[0]], 0), both, [(b, a) for a, b in odd_turn])
     grad_mixed = grad_mixed + rows_times([attn_slots[3]], attn_low, proj_columns, out_columns)
+    grad_turn = lax.ppermute(
+        jnp.concatenate([after(t, grad_mixed[3]) for t in mlp_total[0]], 0), both, [(b, a) for a, b in odd_turn]
+    )
     grad_proj = retain_back(
         grad_mixed, projected, normed_head, scale_head, query, key, value, place_arg, log_decay, cosines, sines, heads
     )
     back_third, gain_third = rows_back(grad_proj, (3,), attn_low, 0, first_slots[3:])
-    mlp_total.append(mlp_end(1))
-    close(grad_turn, back_third, *mlp_total[1])
+    mlp_ends = mlp_end(1)
+    close(grad_turn, back_third, mlp_ends[0][1], mlp_ends[1][1])
 
     from_ends = move_tensor(hold(back_third), inward)
     to_owner = [(b, a) for a, b in to_even + to_odd]
-    grad_core = [lax.ppermute(hold(mlp_total[1][0]), both, to_owner)]
+    mlp_total.append(mlp_sum([(low_part, hold(come_part)) for low_part, come_part in mlp_ends]))
+    grad_core = [lax.ppermute(mlp_total[1][0], both, to_owner)]
     other_high = attn_grads(1, first_slots, hold(grad_proj))
     back_second, gain_second_part = rows_back(after(grad_proj, other_high), (2,), attn_low, 0, first_slots[2:3])
     other_low = attn_grads(0, first_slots, after(grad_proj, back_second))
@@ -946,10 +961,10 @@
     core_high, core_low = to_core(other_high), to_core(other_low)
     out_other_high = attn_grads(1, attn_slots, hold(mixed))
     out_other_low = attn_grads(0, attn_slots, after(mixed, out_other_high))
-    up_high, down_high = attn_grads(1, first_slots, after(grad_proj, out_other_low), core_high)
+    back_own, back_first, gain_near = rows_back(after(grad_proj, out_other_low), (0, 1), attn_low, 0, first_slots[:2])
+    up_high, down_high = attn_grads(1, first_slots, after(grad_proj, back_own), core_high)
     proj_come = swap_dp(up_high, 1 << up_bits[-1]), swap_dp(down_high, 1 << down_bits[-1])
-    back_own, back_first, gain_near = rows_back(after(grad_proj, up_high), (0, 1), attn_low, 0, first_slots[:2])
-    close(from_inner, from_ends, back_own, core_low, out_other_low)
+    close(from_inner, from_ends, back_own, core_low, out_other_low, up_high)
 
     from_beside = swap_tensor(add(back_first, hold(from_inner)).astype(BF16), 1)
     from_middle = move_tensor(add(back_third, hold(from_ends)).astype(BF16), across)

time: 656 us -> 648 us (0.988)
  local copies, waits for them, and re-layouts: 22.4 us -> 39.7 us
  other arithmetic: 53.1 us -> 41.2 us
  waiting for transfers between devices: 233 us -> 224 us
    ppermute x53, waiting for transfers between devices: 135 us -> 87.9 us  [swap_dp(): return lax.ppermute(array, 'dp', [(i, i ^ mask) for i in range(dp_size)])]
    ppermute x27 -> x26, waiting for transfers between devices: 87.4 us -> 129 us  [move_tensor(): return lax.ppermute(array, 'tensor', pairs)]
    unnamed x220 -> x234, local copies, waits for them, and re-layouts: 14.5 us -> 32.4 us
    ppermute x27 -> x26, starting transfers between devices: 47.7 us -> 45.7 us  [move_tensor(): return lax.ppermute(array, 'tensor', pairs)]
  transfers between devices with their start and end apart: 86 -> 86, of which waited for: 39 -> 33; matrix products, arithmetic and copies ran while one was open for 8% -> 7% of each run, Pallas kernels for 32% -> 32%
where the time goes in v4:
time: 648 us; the launch traced here: 643 us
  Pallas kernels  236 us (36%)
  waiting for transfers between devices  224 us (35%)
  starting transfers between devices  98.8 us (15%)
  other arithmetic  41.2 us (6%)
  local copies, waits for them, and re-layouts  39.7 us (6%)
    ppermute x26, waiting for transfers between devices, move_tensor(): return lax.ppermute(array, 'tensor', pairs)  129 us
    ppermute x53, waiting for transfers between devices, swap_dp(): return lax.ppermute(array, 'dp', [(i, i ^ mask) for i in range(dp_size)])  87.9 us
    pallas_call x8, Pallas kernels, attn_grads(): pl.pallas_call(attn_grad_kernel if core else attn_grad_add_kernel, out_sh...  47.1 us
    ppermute x26, starting transfers between devices, move_tensor(): return lax.ppermute(array, 'tensor', pairs)  45.7 us
    pallas_call x5, Pallas kernels, rows_back(): pl.pallas_call(partial(rows_back_kernel, len(slots), len(pieces), 1 if we...  44.1 us
    pallas_call x2, Pallas kernels, mlp(): pl.pallas_call(mlp_again_kernel if weights else partial(mlp_kernel, len(p...  43.4 us
    ppermute x53, starting transfers between devices, swap_dp(): return lax.ppermute(array, 'dp', [(i, i ^ mask) for i in range(dp_size)])  41.8 us
    unnamed x234, local copies, waits for them, and re-layouts  32.4 us
  transfers between devices with their start and end apart: 86, of which 33 were waited for; matrix products, arithmetic and copies ran while one was open for 7% of the time, Pallas kernels for 32%

profile of v4, /device:TPU:0, one launch (start us, length us, event | category | flops | bytes accessed | tf_op | source)
XLA Modules:
  0.0 643.0 jit_solution(16134262490093975381)
XLA Ops:
  23.0 9.7 %collective-permute-done.2.refs_1_.refs_19_ = bf16[256,2048]{1,0:T(8,128)(2,1)} collective-permute-done((bf16[256,2048]{1,0:T(8,128)(2,1)}, bf16[256,2048]{1,0:T(8,128)(2,1)}, u32[]{:S(2)}, u32[]{:S(2)}) %collective-permute-start.2) | collective-permute-done | bytes 1048608 | tf_op jit(solution)/shard_map/ppermute | solution.py:687
  32.7 3.8 collective-permute-done.refs_5_.refs_2_.refs_4_.refs_3_
  42.0 25.1 %collective-permute-done.8 = bf16[256,2048]{1,0:T(8,128)(2,1)S(1)} collective-permute-done((bf16[256,2048]{1,0:T(8,128)(2,1)}, bf16[256,2048]{1,0:T(8,128)(2,1)S(1)}, u32[]{:S(2)}, u32[]{:S(2)}) %collective-permute-start.8) | collective-permute-done | bytes 1048608 | tf_op jit(solution)/shard_map/ppermute | solution.py:687
  73.1 24.6 %collective-permute-done.12 = bf16[256,2048]{1,0:T(8,128)(2,1)S(1)} collective-permute-done((bf16[256,2048]{1,0:T(8,128)(2,1)S(1)}, bf16[256,2048]{1,0:T(8,128)(2,1)S(1)}, u32[]{:S(2)}, u32[]{:S(2)}) %collective-permute-start.12) | collective-permute-done | bytes 1048608 | tf_op jit(solution)/shard_map/ppermute | solution.py:687
  105.3 3.5 collective-permute-start.21
  110.0 18.0 %shard_map.242 = (bf16[256,3072]{1,0:T(8,128)(2,1)}, bf16[256,3072]{1,0:T(8,128)(2,1)}, bf16[256,3072]{1,0:T(8,128)(2,1)}, bf16[256,3072]{1,0:T(8,128)(2,1)}) custom-call(bf16[256,2048]{1,0:T(8,128)(2,1)} %fusion.5.refs_0_.refs_18_, bf16[256,2048]{1,0:T(8,128)(2,1)} %collective-permute-done.2.refs_1_.refs_19_, ...), custom_call_target="tpu_custom_call" | custom-call | flops 201326592 | bytes 196608 | tf_op jit(solution)/shard_map/pallas_call | solution.py:245
  131.0 5.7 collective-permute-start.24
  139.9 10.3 %shard_map.243 = (bf16[1024,512]{1,0:T(8,128)(2,1)S(1)}, bf16[1024,512]{1,0:T(8,128)(2,1)S(1)}, bf16[1024,1024]{1,0:T(8,128)(2,1)}, bf16[1024,1024]{1,0:T(8,128)...) custom-call(s32[1]{0:T(128)} %bitcast.3.place_ref, f32[2]{0:T(128)S(1)} %subtract_log_fusion.decay_ref, ...), custom_call_target="tpu_custom_call" | custom-call | flops 25165824 | bytes 288000 | tf_op jit(solution)/shard_map/pallas_call | solution.py:125
  151.2 4.2 shard_map.244
  156.3 5.8 collective-permute-start.26
  168.7 6.6 %shard_map.245 = (bf16[256,2048]{1,0:T(8,128)(2,1)S(1)}, bf16[256,2048]{1,0:T(8,128)(2,1)S(1)}, bf16[256,2048]{1,0:T(8,128)(2,1)S(1)}) custom-call(bf16[1024,1024]{1,0:T(8,128)(2,1)} %get-tuple-element.379.refs_0_.refs_1_.refs_2_.refs_4_, bf16[1024,1024]{1,0:T(8,128)(2,1)} %get-tuple-element.379.refs_0_.refs_1_.refs_2_.refs_4_, ...), custom_call_target="tpu_custom_call" | custom-call | flops 50331648 | bytes 65536 | tf_op jit(solution)/shard_map/pallas_call | solution.py:288
  175.4 8.0 %collective-permute-done.26 = bf16[256,2048]{1,0:T(8,128)(2,1)S(1)} collective-permute-done((bf16[256,2048]{1,0:T(8,128)(2,1)S(1)}, bf16[256,2048]{1,0:T(8,128)(2,1)S(1)}, u32[]{:S(2)}, u32[]{:S(2)}) %collective-permute-start.26) | collective-permute-done | bytes 1048608 | tf_op jit(solution)/shard_map/ppermute | solution.py:687
  183.8 7.1 %collective-permute-done.27 = bf16[128,2688]{1,0:T(8,128)(2,1)S(1)} collective-permute-done((bf16[128,2688]{1,0:T(8,128)(2,1)}, bf16[128,2688]{1,0:T(8,128)(2,1)S(1)}, u32[]{:S(2)}, u32[]{:S(2)}) %collective-permute-start.27) | collective-permute-done | bytes 688160 | tf_op jit(solution)/shard_map/ppermute | solution.py:863
  190.9 4.3 collective-permute-done.29.refs_3_
  197.1 4.2 collective-permute-start.34
  202.5 14.5 %collective-permute-done.33 = bf16[128,2688]{1,0:T(8,128)(2,1)S(1)} collective-permute-done((bf16[128,2688]{1,0:T(8,128)(2,1)S(1)}, bf16[128,2688]{1,0:T(8,128)(2,1)S(1)}, u32[]{:S(2)}, u32[]{:S(2)}) %collective-permute-start.33) | collective-permute-done | bytes 688160 | tf_op jit(solution)/shard_map/ppermute | solution.py:684
  217.3 5.2 collective-permute-done.34
  228.1 18.3 %collective-permute-done.35 = bf16[256,2048]{1,0:T(8,128)(2,1)S(1)} collective-permute-done((bf16[256,2048]{1,0:T(8,128)(2,1)S(1)}, bf16[256,2048]{1,0:T(8,128)(2,1)S(1)}, u32[]{:S(2)}, u32[]{:S(2)}) %collective-permute-start.35) | collective-permute-done | bytes 1048608 | tf_op jit(solution)/shard_map/ppermute | solution.py:687
  248.5 7.8 %collective-permute-done.38.refs_7_ = bf16[256,2688]{1,0:T(8,128)(2,1)S(1)} collective-permute-done((bf16[256,2688]{1,0:T(8,128)(2,1)S(1)}, bf16[256,2688]{1,0:T(8,128)(2,1)S(1)}, u32[]{:S(2)}, u32[]{:S(2)}) %collective-permute-start.38) | collective-permute-done | bytes 1376288 | tf_op jit(solution)/shard_map/ppermute | solution.py:684
  260.5 15.9 %shard_map.246 = (bf16[256,896]{1,0:T(8,128)(2,1)S(1)}, bf16[256,896]{1,0:T(8,128)(2,1)S(1)}, bf16[256,896]{1,0:T(8,128)(2,1)S(1)}, bf16[256,896]{1,0:T(8,128)(2...) custom-call(bf16[256,2048]{1,0:T(8,128)(2,1)S(1)} %multiply_convert_, ...), custom_call_target="tpu_custom_call" | custom-call | flops 146800640 | bytes 172032 | tf_op jit(solution)/shard_map/pallas_call | solution.py:371
  276.6 5.9 collective-permute-done.40.own_ref.refs_1_
  286.2 27.6 %shard_map.247 = (bf16[256,896]{1,0:T(8,128)(2,1)S(1)}, bf16[256,896]{1,0:T(8,128)(2,1)S(1)}, bf16[256,896]{1,0:T(8,128)(2,1)S(1)}, bf16[256,896]{1,0:T(8,128)(2...) custom-call(bf16[256,2048]{1,0:T(8,128)(2,1)S(1)} %collective-permut, ...), custom_call_target="tpu_custom_call" | custom-call | flops 146800640 | bytes 172032 | tf_op jit(solution)/shard_map/pallas_call | solution.py:371
  318.5 6.8 %shard_map.250 = (bf16[256,2688]{1,0:T(8,128)(2,1)}, bf16[256,2688]{1,0:T(8,128)(2,1)}) custom-call(bf16[256,2048]{1,0:T(8,128)(2,1)} %copy-done.21, bf16[256,2048]{1,0:T(8,128)(2,1)} %copy-done.31, bf16[256,2048]{1,0:T(8,128)(2,1)} %copy-done.72, bf16[256,2048]{1,0:T(8,128)(2,1)} %copy-done.73, ...), custom_call_target="tpu_custom_call" | custom-call | flops 44040192 | bytes 57344 | tf_op jit(solution)/shard_map/pallas_call | solution.py:434
  325.3 6.9 %shard_map.249 = (bf16[256,2688]{1,0:T(8,128)(2,1)}, bf16[256,2688]{1,0:T(8,128)(2,1)}) custom-call(bf16[256,2048]{1,0:T(8,128)(2,1)} %copy-done.21, bf16[256,2048]{1,0:T(8,128)(2,1)} %copy-done.31, bf16[256,2048]{1,0:T(8,128)(2,1)} %copy-done.72, bf16[256,2048]{1,0:T(8,128)(2,1)} %copy-done.73, ...), custom_call_target="tpu_custom_call" | custom-call | flops 44040192 | bytes 57344 | tf_op jit(solution)/shard_map/pallas_call | solution.py:434
  332.3 6.8 %shard_map.248 = (bf16[512,2048]{1,0:T(8,128)(2,1)S(1)}, bf16[512,2048]{1,0:T(8,128)(2,1)S(1)}) custom-call(bf16[256,896]{1,0:T(8,128)(2,1)S(1)} %get-tuple-element.288.refs_0_.refs_16_, bf16[256,896]{1,0:T(8,128)(2,1)S(1)} %get-tuple-element.289.refs_1_.refs_17_, bf16[256,896]{1,0:T(8,128)(2,1)S(1)} %get-tuple-element.290.refs_2_.refs_18_, ...), custom_call_target="tpu_custom_call" | custom-call | flops 58720256 | bytes 57344 | tf_op jit(solution)/shard_map/pallas_call | solution.py:397
  343.9 4.1 shard_map.251
  352.3 6.9 %shard_map.253 = (bf16[256,2688]{1,0:T(8,128)(2,1)}, bf16[256,2688]{1,0:T(8,128)(2,1)}) custom-call(bf16[256,2048]{1,0:T(8,128)(2,1)} %copy-done.21, bf16[256,2048]{1,0:T(8,128)(2,1)} %copy-done.31, bf16[256,2048]{1,0:T(8,128)(2,1)} %copy-done.72, bf16[256,2048]{1,0:T(8,128)(2,1)} %copy-done.73, ...), custom_call_target="tpu_custom_call" | custom-call | flops 44040192 | bytes 57344 | tf_op jit(solution)/shard_map/pallas_call | solution.py:434
  359.2 7.3 %shard_map.252 = (bf16[256,2688]{1,0:T(8,128)(2,1)}, bf16[256,2688]{1,0:T(8,128)(2,1)}) custom-call(bf16[256,2048]{1,0:T(8,128)(2,1)} %copy-done.21, bf16[256,2048]{1,0:T(8,128)(2,1)} %copy-done.31, bf16[256,2048]{1,0:T(8,128)(2,1)} %copy-done.72, bf16[256,2048]{1,0:T(8,128)(2,1)} %copy-done.73, ...), custom_call_target="tpu_custom_call" | custom-call | flops 44040192 | bytes 57344 | tf_op jit(solution)/shard_map/pallas_call | solution.py:434
  366.5 7.4 %collective-permute-done.50 = bf16[256,2688]{1,0:T(8,128)(2,1)} collective-permute-done((bf16[256,2688]{1,0:T(8,128)(2,1)}, bf16[256,2688]{1,0:T(8,128)(2,1)}, u32[]{:S(2)}, u32[]{:S(2)}) %collective-permute-start.50) | collective-permute-done | bytes 1376288 | tf_op jit(solution)/shard_map/ppermute | solution.py:684
  380.8 16.6 %collective-permute-done.46.refs_1_ = bf16[256,2048]{1,0:T(8,128)(2,1)S(1)} collective-permute-done((bf16[256,2048]{1,0:T(8,128)(2,1)S(1)}, bf16[256,2048]{1,0:T(8,128)(2,1)S(1)}, u32[]{:S(2)}, u32[]{:S(2)}) %collective-permute-start.46) | collective-permute-done | bytes 1048608 | tf_op jit(solution)/shard_map/ppermute | solution.py:687
  397.4 7.2 %collective-permute-done.51 = bf16[256,2688]{1,0:T(8,128)(2,1)S(1)} collective-permute-done((bf16[256,2688]{1,0:T(8,128)(2,1)}, bf16[256,2688]{1,0:T(8,128)(2,1)S(1)}, u32[]{:S(2)}, u32[]{:S(2)}) %collective-permute-start.51) | collective-permute-done | bytes 1376288 | tf_op jit(solution)/shard_map/ppermute | solution.py:684
  408.8 5.4 shard_map.254
  414.3 6.0 collective-permute-done.55
  420.7 9.7 %collective-permute-done.53 = bf16[256,2048]{1,0:T(8,128)(2,1)S(1)} collective-permute-done((bf16[256,2048]{1,0:T(8,128)(2,1)S(1)}, bf16[256,2048]{1,0:T(8,128)(2,1)S(1)}, u32[]{:S(2)}, u32[]{:S(2)}) %collective-permute-start.53) | collective-permute-done | bytes 1048608 | tf_op jit(solution)/shard_map/ppermute | solution.py:687
  434.2 3.4 shard_map.255.refs_3_
  444.7 16.0 %shard_map.256.refs_0_.refs_4_.refs_1_ = bf16[1024,3072]{1,0:T(8,128)(2,1)} custom-call(s32[1]{0:T(128)} %bitcast.3.place_ref, f32[2]{0:T(128)S(1)} %subtract_log_fusion.decay_ref, bf16[256,1024]{1,0:T(8,128)(2,1)S(1)} %get-tuple-element.329.refs_0_, bf16[256,1024]{1,0:T(8,128)(2,1)S(1)} %get-tuple-element.334.refs_1_, ...), custom_call_target="tpu_custom_call" | custom-call | flops 58720256 | bytes 320000 | tf_op jit(solution)/shard_map/pallas_call | solution.py:212
  460.7 9.4 %shard_map.257 = (bf16[256,2048]{1,0:T(8,128)(2,1)S(1)}, f32[8,2048]{1,0:T(8,128)S(1)}) custom-call(bf16[1024,3072]{1,0:T(8,128)(2,1)} %shard_map.256.refs_0_.refs_4_.refs_1_, bf16[128,4096]{1,0:T(8,128)(2,1)S(1)} %get-tuple-element.225.refs_4_.refs_1_.refs_3_.refs_2_, bf16[128,4096]{1,0:T(8,128)(2,1)S(1)} %copy-done.3, ...), custom_call_target="tpu_custom_call" | custom-call | flops 50331648 | bytes 196608 | tf_op jit(solution)/shard_map/pallas_call | solution.py:288
  471.0 4.8 collective-permute-start.59
  476.1 8.0 %shard_map.258 = bf16[512,3072]{1,0:T(8,128)(2,1)} custom-call(bf16[256,2048]{1,0:T(8,128)(2,1)} %fusion.5.refs_0_.refs_18_, bf16[256,2048]{1,0:T(8,128)(2,1)} %collective-permute-done.2.refs_1_.refs_19_, bf16[256,2048]{1,0:T(8,128)(2,1)S(1)} %broadcast_select_fusion.3.refs_2_.refs_17_, bf16[256,2048]{1,0:T(8,128)(2,1)S(1)} %copy-done.11, ...), custom_call_target="tpu_custom_call" | custom-call | flops 50331648 | bytes 98304 | tf_op jit(solution)/shard_map/pallas_call | solution.py:468
  484.2 10.3 %shard_map.259 = (bf16[256,2048]{1,0:T(8,128)(2,1)}, f32[8,2048]{1,0:T(8,128)S(1)}) custom-call(bf16[1024,3072]{1,0:T(8,128)(2,1)} %shard_map.256.refs_0_.refs_4_.refs_1_, bf16[128,4096]{1,0:T(8,128)(2,1)S(1)} %get-tuple-element.225.refs_4_.refs_1_.refs_3_.refs_2_, bf16[128,4096]{1,0:T(8,128)(2,1)S(1)} %copy-done.3, ...), custom_call_target="tpu_custom_call" | custom-call | flops 50331648 | bytes 196608 | tf_op jit(solution)/shard_map/pallas_call | solution.py:288
  494.4 7.8 %shard_map.260 = bf16[512,3072]{1,0:T(8,128)(2,1)} custom-call(bf16[256,2048]{1,0:T(8,128)(2,1)} %fusion.5.refs_0_.refs_18_, bf16[256,2048]{1,0:T(8,128)(2,1)} %collective-permute-done.2.refs_1_.refs_19_, bf16[256,2048]{1,0:T(8,128)(2,1)S(1)} %copy-done.8, bf16[256,2048]{1,0:T(8,128)(2,1)S(1)} %copy-done.11, ...), custom_call_target="tpu_custom_call" | custom-call | flops 50331648 | bytes 98304 | tf_op jit(solution)/shard_map/pallas_call | solution.py:468
  521.4 13.6 %shard_map.263 = (bf16[256,2048]{1,0:T(8,128)(2,1)S(1)}, bf16[256,2048]{1,0:T(8,128)(2,1)S(1)}, f32[8,2048]{1,0:T(8,128)S(1)}) custom-call(bf16[1024,3072]{1,0:T(8,128)(2,1)} %shard_map.256.refs_0_.refs_4_.refs_1_, bf16[1024,3072]{1,0:T(8,128)(2,1)} %shard_map.256.refs_0_.refs_4_.refs_1_, ...), custom_call_target="tpu_custom_call" | custom-call | flops 100663296 | bytes 196608 | tf_op jit(solution)/shard_map/pallas_call | solution.py:288
  535.1 9.2 %shard_map.264 = (bf16[256,3072]{1,0:T(8,128)(2,1)}, bf16[256,3072]{1,0:T(8,128)(2,1)}) custom-call(bf16[256,2048]{1,0:T(8,128)(2,1)} %fusion.5.refs_0_.refs_18_, bf16[256,2048]{1,0:T(8,128)(2,1)} %collective-permute-done.2.refs_1_.refs_19_, bf16[256,2048]{1,0:T(8,128)(2,1)S(1)} %copy-done.9, bf16[256,2048]{1,0:T(8,128)(2,1)S(1)} %copy-done.12, ...), custom_call_target="tpu_custom_call" | custom-call | flops 50331648 | bytes 98304 | tf_op jit(solution)/shard_map/pallas_call | solution.py:468
  560.2 8.7 %shard_map.266 = (bf16[256,3072]{1,0:T(8,128)(2,1)S(1)}, bf16[256,3072]{1,0:T(8,128)(2,1)}) custom-call(bf16[256,2048]{1,0:T(8,128)(2,1)} %fusion.5.refs_0_.refs_18_, bf16[256,2048]{1,0:T(8,128)(2,1)} %collective-permute-done.2.refs_1_.refs_19_, bf16[256,2048]{1,0:T(8,128)(2,1)S(1)} %copy-done.9, bf16[256,2048]{1,0:T(8,128)(2,1)S(1)} %copy-done.12, ...), custom_call_target="tpu_custom_call" | custom-call | flops 50331648 | bytes 98304 | tf_op jit(solution)/shard_map/pallas_call | solution.py:468
  569.0 3.5 shard_map.267
  572.5 3.6 shard_map.268
  591.8 5.7 collective-permute-done.75
  602.2 16.4 %collective-permute-done.76 = bf16[256,1024]{1,0:T(8,128)(2,1)} collective-permute-done((bf16[256,1024]{1,0:T(8,128)(2,1)S(1)}, bf16[256,1024]{1,0:T(8,128)(2,1)}, u32[]{:S(2)}, u32[]{:S(2)}) %collective-permute-start.76) | collective-permute-done | bytes 524320 | tf_op jit(solution)/shard_map/ppermute | solution.py:684
  (452 shorter events, 192.3 us)
Async XLA Ops:
  6.2 26.5 %collective-permute-start.2 = (bf16[256,2048]{1,0:T(8,128)(2,1)}, bf16[256,2048]{1,0:T(8,128)(2,1)}, u32[]{:S(2)}, u32[]{:S(2)}) collective-permute-start(bf16[256,2048]{1,0:T(8,128)(2,1)} %fusion.5.refs_0_.refs_18_), channel_id=1, source_target_pairs={{0,1},{1,0},{2,3},{3,2},{4,5},{5,4},{6,7},{7,6},{8,9},{9,8},{10,11... | collective-permute-start | bytes 3145736 | tf_op jit(solution)/shard_map/ppermute | solution.py:687
  11.0 25.6 %collective-permute-start = (bf16[128,4096]{1,0:T(8,128)(2,1)S(1)}, bf16[128,4096]{1,0:T(8,128)(2,1)S(1)}, u32[]{:S(2)}, u32[]{:S(2)}) collective-permute-start(bf16[128,4096]{1,0:T(8,128)(2,1)S(1)} %get-tuple-element.225.refs_4_.refs_1_.refs_3_.refs_2_), channel_id=1, source_target_pairs={{0,8},{4,12},{8,0},{12,4},{16,24},{20,28},{24,16},{28,20},{1,9},{5... | collective-permute-start | bytes 3145736 | tf_op jit(solution)/shard_map/ppermute | solution.py:684
  12.5 25.4 %collective-permute-start.1 = (bf16[128,4096]{1,0:T(8,128)(2,1)S(1)}, bf16[128,4096]{1,0:T(8,128)(2,1)}, u32[]{:S(2)}, u32[]{:S(2)}) collective-permute-start(bf16[128,4096]{1,0:T(8,128)(2,1)S(1)} %get-tuple-element.226.refs_8_.refs_5_.refs_7_.refs_6_), channel_id=1, source_target_pairs={{0,16},{4,20},{8,24},{12,28},{16,0},{20,4},{24,8},{28,12},{1,17},{... | collective-permute-start | bytes 3145736 | tf_op jit(solution)/shard_map/ppermute | solution.py:684
  37.8 29.3 %collective-permute-start.6 = (bf16[128,4096]{1,0:T(8,128)(2,1)S(1)}, bf16[128,4096]{1,0:T(8,128)(2,1)}, u32[]{:S(2)}, u32[]{:S(2)}) collective-permute-start(bf16[128,4096]{1,0:T(8,128)(2,1)S(1)} %get-tuple-element.226.refs_8_.refs_5_.refs_7_.refs_6_), channel_id=1, source_target_pairs={{0,8},{4,12},{8,0},{12,4},{16,24},{20,28},{24,16},{28,20},{1,9},{5... | collective-permute-start | bytes 3145736 | tf_op jit(solution)/shard_map/ppermute | solution.py:684
  38.4 28.7 %collective-permute-start.9 = (bf16[128,4096]{1,0:T(8,128)(2,1)S(1)}, bf16[128,4096]{1,0:T(8,128)(2,1)S(1)}, u32[]{:S(2)}, u32[]{:S(2)}) collective-permute-start(bf16[128,4096]{1,0:T(8,128)(2,1)S(1)} %get-tuple-element.226.refs_8_.refs_5_.refs_7_.refs_6_), channel_id=1, source_target_pairs={{0,4},{4,0},{8,12},{12,8},{16,20},{20,16},{24,28},{28,24},{1,5},{5... | collective-permute-start | bytes 3145736 | tf_op jit(solution)/shard_map/ppermute | solution.py:684
  38.4 28.7 %collective-permute-start.8 = (bf16[256,2048]{1,0:T(8,128)(2,1)}, bf16[256,2048]{1,0:T(8,128)(2,1)S(1)}, u32[]{:S(2)}, u32[]{:S(2)}) collective-permute-start(bf16[256,2048]{1,0:T(8,128)(2,1)} %collective-permute-done.3), channel_id=1, source_target_pairs={{1,0},{2,3},{5,4},{6,7},{9,8},{10,11},{13,12},{14,15},{17,16},{18,... | collective-permute-start | bytes 3145736 | tf_op jit(solution)/shard_map/ppermute | solution.py:687
  39.7 27.4 %collective-permute-start.7 = (bf16[256,2048]{1,0:T(8,128)(2,1)}, bf16[256,2048]{1,0:T(8,128)(2,1)S(1)}, u32[]{:S(2)}, u32[]{:S(2)}) collective-permute-start(bf16[256,2048]{1,0:T(8,128)(2,1)} %collective-permute-done.2.refs_1_.refs_19_), channel_id=1, source_target_pairs={{1,2},{2,1},{5,6},{6,5},{9,10},{10,9},{13,14},{14,13},{17,18},{18,... | collective-permute-start | bytes 3145736 | tf_op jit(solution)/shard_map/ppermute | solution.py:687
  40.4 26.7 %collective-permute-start.5 = (bf16[128,4096]{1,0:T(8,128)(2,1)S(1)}, bf16[128,4096]{1,0:T(8,128)(2,1)}, u32[]{:S(2)}, u32[]{:S(2)}) collective-permute-start(bf16[128,4096]{1,0:T(8,128)(2,1)S(1)} %get-tuple-element.225.refs_4_.refs_1_.refs_3_.refs_2_), channel_id=1, source_target_pairs={{0,16},{4,20},{8,24},{12,28},{16,0},{20,4},{24,8},{28,12},{1,17},{... | collective-permute-start | bytes 3145736 | tf_op jit(solution)/shard_map/ppermute | solution.py:684
  68.5 29.1 %collective-permute-start.11 = (bf16[128,4096]{1,0:T(8,128)(2,1)}, bf16[128,4096]{1,0:T(8,128)(2,1)}, u32[]{:S(2)}, u32[]{:S(2)}) collective-permute-start(bf16[128,4096]{1,0:T(8,128)(2,1)} %collective-permute-done.1.refs_9_.refs_6_.refs_8_.refs_7_), channel_id=1, source_target_pairs={{0,8},{4,12},{8,0},{12,4},{16,24},{20,28},{24,16},{28,20},{1,9},{5... | collective-permute-start | bytes 3145736 | tf_op jit(solution)/shard_map/ppermute | solution.py:684
  70.0 27.7 %collective-permute-start.14 = (bf16[128,4096]{1,0:T(8,128)(2,1)}, bf16[128,4096]{1,0:T(8,128)(2,1)S(1)}, u32[]{:S(2)}, u32[]{:S(2)}) collective-permute-start(bf16[128,4096]{1,0:T(8,128)(2,1)} %collective-permute-done.1.refs_9_.refs_6_.refs_8_.refs_7_), channel_id=1, source_target_pairs={{0,4},{4,0},{8,12},{12,8},{16,20},{20,16},{24,28},{28,24},{1,5},{5... | collective-permute-start | bytes 3145736 | tf_op jit(solution)/shard_map/ppermute | solution.py:684
  70.0 27.7 %collective-permute-start.12 = (bf16[256,2048]{1,0:T(8,128)(2,1)S(1)}, bf16[256,2048]{1,0:T(8,128)(2,1)S(1)}, u32[]{:S(2)}, u32[]{:S(2)}) collective-permute-start(bf16[256,2048]{1,0:T(8,128)(2,1)S(1)} %collective-permute-done.7), channel_id=1, source_target_pairs={{1,0},{2,3},{5,4},{6,7},{9,8},{10,11},{13,12},{14,15},{17,16},{18,... | collective-permute-start | bytes 3145736 | tf_op jit(solution)/shard_map/ppermute | solution.py:687
  71.3 26.4 %collective-permute-start.10 = (bf16[128,4096]{1,0:T(8,128)(2,1)S(1)}, bf16[128,4096]{1,0:T(8,128)(2,1)S(1)}, u32[]{:S(2)}, u32[]{:S(2)}) collective-permute-start(bf16[128,4096]{1,0:T(8,128)(2,1)S(1)} %collective-permute-done.refs_5_.refs_2_.refs_4_.refs_3_), channel_id=1, source_target_pairs={{0,16},{4,20},{8,24},{12,28},{16,0},{20,4},{24,8},{28,12},{1,17},{... | collective-permute-start | bytes 3145736 | tf_op jit(solution)/shard_map/ppermute | solution.py:684
  101.0 27.0 %collective-permute-start.19 = (bf16[128,2688]{1,0:T(8,128)(2,1)S(1)}, bf16[128,2688]{1,0:T(8,128)(2,1)}, u32[]{:S(2)}, u32[]{:S(2)}) collective-permute-start(bf16[128,2688]{1,0:T(8,128)(2,1)S(1)} %get-tuple-element.241), channel_id=1, source_target_pairs={{4,7},{5,6},{6,5},{7,4},{12,15},{13,14},{14,13},{15,12},{20,23},{2... | collective-permute-start | bytes 2064392 | tf_op jit(solution)/shard_map/ppermute | solution.py:827
  102.5 25.5 %collective-permute-start.20 = (bf16[128,2688]{1,0:T(8,128)(2,1)S(1)}, bf16[128,2688]{1,0:T(8,128)(2,1)}, u32[]{:S(2)}, u32[]{:S(2)}) collective-permute-start(bf16[128,2688]{1,0:T(8,128)(2,1)S(1)} %get-tuple-element.242), channel_id=1, source_target_pairs={{4,7},{5,6},{6,5},{7,4},{12,15},{13,14},{14,13},{15,12},{20,23},{2... | collective-permute-start | bytes 2064392 | tf_op jit(solution)/shard_map/ppermute | solution.py:827
  109.1 46.4 %collective-permute-start.25 = (bf16[256,2048]{1,0:T(8,128)(2,1)S(1)}, bf16[256,2048]{1,0:T(8,128)(2,1)}, u32[]{:S(2)}, u32[]{:S(2)}) collective-permute-start(bf16[256,2048]{1,0:T(8,128)(2,1)S(1)} %copy-done.13), channel_id=1, source_target_pairs={{0,1},{1,0},{2,3},{3,2},{4,5},{5,4},{6,7},{7,6},{8,9},{9,8},{10,11... | collective-permute-start | bytes 3145736 | tf_op jit(solution)/shard_map/ppermute | solution.py:687
  128.0 27.5 %collective-permute-start.23 = (bf16[128,2688]{1,0:T(8,128)(2,1)}, bf16[128,2688]{1,0:T(8,128)(2,1)S(1)}, u32[]{:S(2)}, u32[]{:S(2)}) collective-permute-start(bf16[128,2688]{1,0:T(8,128)(2,1)} %collective-permute-done.20), channel_id=1, source_target_pairs={{0,16},{4,20},{8,24},{12,28},{16,0},{20,4},{24,8},{28,12},{1,17},{... | collective-permute-start | bytes 2064392 | tf_op jit(solution)/shard_map/ppermute | solution.py:684
  129.6 25.9 %collective-permute-start.22 = (bf16[128,2688]{1,0:T(8,128)(2,1)}, bf16[128,2688]{1,0:T(8,128)(2,1)S(1)}, u32[]{:S(2)}, u32[]{:S(2)}) collective-permute-start(bf16[128,2688]{1,0:T(8,128)(2,1)} %collective-permute-done.19), channel_id=1, source_target_pairs={{0,8},{4,12},{8,0},{12,4},{16,24},{20,28},{24,16},{28,20},{1,9},{5... | collective-permute-start | bytes 2064392 | tf_op jit(solution)/shard_map/ppermute | solution.py:684
  131.0 25.3 %collective-permute-start.24 = (bf16[128,2688]{1,0:T(8,128)(2,1)}, bf16[128,2688]{1,0:T(8,128)(2,1)S(1)}, u32[]{:S(2)}, u32[]{:S(2)}) collective-permute-start(bf16[128,2688]{1,0:T(8,128)(2,1)} %slice.132), channel_id=1, source_target_pairs={{4,0},{5,1},{6,2},{7,3},{12,8},{13,9},{14,10},{15,11},{20,16},{21,... | collective-permute-start | bytes 2064392 | tf_op jit(solution)/shard_map/ppermute | solution.py:855
  156.3 27.1 %collective-permute-start.26 = (bf16[256,2048]{1,0:T(8,128)(2,1)S(1)}, bf16[256,2048]{1,0:T(8,128)(2,1)S(1)}, u32[]{:S(2)}, u32[]{:S(2)}) collective-permute-start(bf16[256,2048]{1,0:T(8,128)(2,1)S(1)} %shard_map.244), channel_id=1, source_target_pairs={{0,1},{3,2},{4,5},{7,6},{8,9},{11,10},{12,13},{15,14},{16,17},{19,... | collective-permute-start | bytes 3145736 | tf_op jit(solution)/shard_map/ppermute | solution.py:687
  164.1 31.1 %collective-permute-start.29 = (bf16[256,2688]{1,0:T(8,128)(2,1)}, bf16[256,2688]{1,0:T(8,128)(2,1)S(1)}, u32[]{:S(2)}, u32[]{:S(2)}) collective-permute-start(bf16[256,2688]{1,0:T(8,128)(2,1)} %constant_dynamic-update-slice_fusion.2.refs_2_), channel_id=1, source_target_pairs={{0,8},{4,12},{8,0},{12,4},{16,24},{20,28},{24,16},{28,20},{1,9},{5... | collective-permute-start | bytes 4128776 | tf_op jit(solution)/shard_map/ppermute | solution.py:684
  165.7 30.6 %collective-permute-start.28 = (bf16[256,2688]{1,0:T(8,128)(2,1)S(1)}, bf16[256,2688]{1,0:T(8,128)(2,1)S(1)}, u32[]{:S(2)}, u32[]{:S(2)}) collective-permute-start(bf16[256,2688]{1,0:T(8,128)(2,1)S(1)} %constant_dynamic-update-slice_fusion.refs_0_), channel_id=1, source_target_pairs={{0,16},{4,20},{8,24},{12,28},{16,0},{20,4},{24,8},{28,12},{1,17},{... | collective-permute-start | bytes 4128776 | tf_op jit(solution)/shard_map/ppermute | solution.py:684
  197.1 25.3 %collective-permute-start.34 = (bf16[256,2048]{1,0:T(8,128)(2,1)S(1)}, bf16[256,2048]{1,0:T(8,128)(2,1)S(1)}, u32[]{:S(2)}, u32[]{:S(2)}) collective-permute-start(bf16[256,2048]{1,0:T(8,128)(2,1)S(1)} %get-tuple-element.268), channel_id=1, source_target_pairs={{0,1},{3,2},{4,5},{7,6},{8,9},{11,10},{12,13},{15,14},{16,17},{19,... | collective-permute-start | bytes 3145736 | tf_op jit(solution)/shard_map/ppermute | solution.py:687
  226.7 29.5 %collective-permute-start.38 = (bf16[256,2688]{1,0:T(8,128)(2,1)S(1)}, bf16[256,2688]{1,0:T(8,128)(2,1)S(1)}, u32[]{:S(2)}, u32[]{:S(2)}) collective-permute-start(bf16[256,2688]{1,0:T(8,128)(2,1)S(1)} %constant_dynamic-update-slice_fusion.6.refs_6_), channel_id=1, source_target_pairs={{0,8},{4,12},{8,0},{12,4},{16,24},{20,28},{24,16},{28,20},{1,9},{5... | collective-permute-start | bytes 4128776 | tf_op jit(solution)/shard_map/ppermute | solution.py:684
  227.5 29.4 %collective-permute-start.37 = (bf16[256,2688]{1,0:T(8,128)(2,1)S(1)}, bf16[256,2688]{1,0:T(8,128)(2,1)S(1)}, u32[]{:S(2)}, u32[]{:S(2)}) collective-permute-start(bf16[256,2688]{1,0:T(8,128)(2,1)S(1)} %constant_dynamic-update-slice_fusion.4.refs_4_), channel_id=1, source_target_pairs={{0,16},{4,20},{8,24},{12,28},{16,0},{20,4},{24,8},{28,12},{1,17},{... | collective-permute-start | bytes 4128776 | tf_op jit(solution)/shard_map/ppermute | solution.py:684
  256.9 25.6 %collective-permute-start.40 = (bf16[256,2048]{1,0:T(8,128)(2,1)S(1)}, bf16[256,2048]{1,0:T(8,128)(2,1)S(1)}, u32[]{:S(2)}, u32[]{:S(2)}) collective-permute-start(bf16[256,2048]{1,0:T(8,128)(2,1)S(1)} %multiply_convert_fusion.own_ref.refs_0_), channel_id=1, source_target_pairs={{0,1},{1,0},{2,3},{3,2},{4,5},{5,4},{6,7},{7,6},{8,9},{9,8},{10,11... | collective-permute-start | bytes 3145736 | tf_op jit(solution)/shard_map/ppermute | solution.py:687
  316.9 25.3 %collective-permute-start.44 = (bf16[256,2048]{1,0:T(8,128)(2,1)S(1)}, bf16[256,2048]{1,0:T(8,128)(2,1)S(1)}, u32[]{:S(2)}, u32[]{:S(2)}) collective-permute-start(bf16[256,2048]{1,0:T(8,128)(2,1)S(1)} %add_convert_fusion.3), channel_id=1, source_target_pairs={{0,1},{1,0},{2,3},{3,2},{4,5},{5,4},{6,7},{7,6},{8,9},{9,8},{10,11... | collective-permute-start | bytes 3145736 | tf_op jit(solution)/shard_map/ppermute | solution.py:687
  342.2 31.7 %collective-permute-start.50 = (bf16[256,2688]{1,0:T(8,128)(2,1)}, bf16[256,2688]{1,0:T(8,128)(2,1)}, u32[]{:S(2)}, u32[]{:S(2)}) collective-permute-start(bf16[256,2688]{1,0:T(8,128)(2,1)} %get-tuple-element.315), channel_id=1, source_target_pairs={{0,8},{4,12},{8,0},{12,4},{16,24},{20,28},{24,16},{28,20},{1,9},{5... | collective-permute-start | bytes 4128776 | tf_op jit(solution)/shard_map/ppermute | solution.py:684
  343.4 31.7 %collective-permute-start.48 = (bf16[256,2688]{1,0:T(8,128)(2,1)}, bf16[256,2688]{1,0:T(8,128)(2,1)}, u32[]{:S(2)}, u32[]{:S(2)}) collective-permute-start(bf16[256,2688]{1,0:T(8,128)(2,1)} %get-tuple-element.312), channel_id=1, source_target_pairs={{0,16},{4,20},{8,24},{12,28},{16,0},{20,4},{24,8},{28,12},{1,17},{... | collective-permute-start | bytes 4128776 | tf_op jit(solution)/shard_map/ppermute | solution.py:684
  343.9 53.5 %collective-permute-start.45 = (bf16[512,2048]{1,0:T(8,128)(2,1)S(1)}, bf16[512,2048]{1,0:T(8,128)(2,1)}, u32[]{:S(2)}, u32[]{:S(2)}) collective-permute-start(bf16[512,2048]{1,0:T(8,128)(2,1)S(1)} %get-tuple-element.309), channel_id=1, source_target_pairs={{0,4},{4,0},{8,12},{12,8},{16,20},{20,16},{24,28},{28,24},{1,5},{5... | collective-permute-start | bytes 6291464 | tf_op jit(solution)/shard_map/ppermute | solution.py:684
  349.4 48.0 %collective-permute-start.46 = (bf16[256,2048]{1,0:T(8,128)(2,1)S(1)}, bf16[256,2048]{1,0:T(8,128)(2,1)S(1)}, u32[]{:S(2)}, u32[]{:S(2)}) collective-permute-start(bf16[256,2048]{1,0:T(8,128)(2,1)S(1)} %get-tuple-element.325.refs_0_), channel_id=1, source_target_pairs={{0,1},{1,0},{2,3},{3,2},{4,5},{5,4},{6,7},{7,6},{8,9},{9,8},{10,11... | collective-permute-start | bytes 3145736 | tf_op jit(solution)/shard_map/ppermute | solution.py:687
  350.8 46.6 %collective-permute-start.47 = (bf16[256,2048]{1,0:T(8,128)(2,1)S(1)}, bf16[256,2048]{1,0:T(8,128)(2,1)S(1)}, u32[]{:S(2)}, u32[]{:S(2)}) collective-permute-start(bf16[256,2048]{1,0:T(8,128)(2,1)S(1)} %get-tuple-element.325.refs_0_), channel_id=1, source_target_pairs={{0,2},{1,3},{2,0},{3,1},{4,6},{5,7},{6,4},{7,5},{8,10},{9,11},{10,... | collective-permute-start | bytes 3145736 | tf_op jit(solution)/shard_map/ppermute | solution.py:687
  373.9 30.7 %collective-permute-start.51 = (bf16[256,2688]{1,0:T(8,128)(2,1)}, bf16[256,2688]{1,0:T(8,128)(2,1)S(1)}, u32[]{:S(2)}, u32[]{:S(2)}) collective-permute-start(bf16[256,2688]{1,0:T(8,128)(2,1)} %get-tuple-element.317), channel_id=1, source_target_pairs={{0,8},{4,12},{8,0},{12,4},{16,24},{20,28},{24,16},{28,20},{1,9},{5... | collective-permute-start | bytes 4128776 | tf_op jit(solution)/shard_map/ppermute | solution.py:684
  375.1 30.4 %collective-permute-start.49 = (bf16[256,2688]{1,0:T(8,128)(2,1)}, bf16[256,2688]{1,0:T(8,128)(2,1)S(1)}, u32[]{:S(2)}, u32[]{:S(2)}) collective-permute-start(bf16[256,2688]{1,0:T(8,128)(2,1)} %get-tuple-element.314), channel_id=1, source_target_pairs={{0,16},{4,20},{8,24},{12,28},{16,0},{20,4},{24,8},{28,12},{1,17},{... | collective-permute-start | bytes 4128776 | tf_op jit(solution)/shard_map/ppermute | solution.py:684
  437.8 32.3 %collective-permute-start.56 = (bf16[256,2688]{1,0:T(8,128)(2,1)S(1)}, bf16[256,2688]{1,0:T(8,128)(2,1)S(1)}, u32[]{:S(2)}, u32[]{:S(2)}) collective-permute-start(bf16[256,2688]{1,0:T(8,128)(2,1)S(1)} %pad_maximum_fusion), channel_id=1, source_target_pairs={{7,4},{6,5},{5,6},{4,7},{15,12},{14,13},{13,14},{12,15},{23,20},{2... | collective-permute-start | bytes 4128776 | tf_op jit(solution)/shard_map/ppermute | solution.py:939
  441.9 28.2 %collective-permute-start.58 = (bf16[128,2688]{1,0:T(8,128)(2,1)}, bf16[128,2688]{1,0:T(8,128)(2,1)S(1)}, u32[]{:S(2)}, u32[]{:S(2)}) collective-permute-start(bf16[128,2688]{1,0:T(8,128)(2,1)} %get-tuple-element.345), channel_id=1, source_target_pairs={{0,16},{4,20},{8,24},{12,28},{16,0},{20,4},{24,8},{28,12},{1,17},{... | collective-permute-start | bytes 2064392 | tf_op jit(solution)/shard_map/ppermute | solution.py:684
  443.5 26.6 %collective-permute-start.57 = (bf16[128,2688]{1,0:T(8,128)(2,1)S(1)}, bf16[128,2688]{1,0:T(8,128)(2,1)S(1)}, u32[]{:S(2)}, u32[]{:S(2)}) collective-permute-start(bf16[128,2688]{1,0:T(8,128)(2,1)S(1)} %get-tuple-element.343), channel_id=1, source_target_pairs={{0,8},{4,12},{8,0},{12,4},{16,24},{20,28},{24,16},{28,20},{1,9},{5... | collective-permute-start | bytes 2064392 | tf_op jit(solution)/shard_map/ppermute | solution.py:684
  471.0 31.3 %collective-permute-start.59 = (bf16[256,2048]{1,0:T(8,128)(2,1)S(1)}, bf16[256,2048]{1,0:T(8,128)(2,1)S(1)}, u32[]{:S(2)}, u32[]{:S(2)}) collective-permute-start(bf16[256,2048]{1,0:T(8,128)(2,1)S(1)} %get-tuple-element.350), channel_id=1, source_target_pairs={{0,1},{3,2},{4,5},{7,6},{8,9},{11,10},{12,13},{15,14},{16,17},{19,... | collective-permute-start | bytes 3145736 | tf_op jit(solution)/shard_map/ppermute | solution.py:687
  476.0 28.8 %collective-permute-start.60 = (bf16[128,2688]{1,0:T(8,128)(2,1)S(1)}, bf16[128,2688]{1,0:T(8,128)(2,1)}, u32[]{:S(2)}, u32[]{:S(2)}) collective-permute-start(bf16[128,2688]{1,0:T(8,128)(2,1)S(1)} %add_convert_fusion.13), channel_id=1, source_target_pairs={{0,4},{1,5},{2,6},{3,7},{8,12},{9,13},{10,14},{11,15},{16,20},{17,... | collective-permute-start | bytes 2064392 | tf_op jit(solution)/shard_map/ppermute | solution.py:952
  504.9 30.2 %collective-permute-start.64 = (bf16[512,3072]{1,0:T(8,128)(2,1)}, bf16[512,3072]{1,0:T(8,128)(2,1)}, u32[]{:S(2)}, u32[]{:S(2)}) collective-permute-start(bf16[512,3072]{1,0:T(8,128)(2,1)} %shard_map.258), channel_id=1, source_target_pairs={{0,4},{4,0},{8,12},{12,8},{16,20},{20,16},{24,28},{28,24},{1,5},{5... | collective-permute-start | bytes 9437192 | tf_op jit(solution)/shard_map/ppermute | solution.py:684
  507.3 36.9 %collective-permute-start.63 = (bf16[512,3072]{1,0:T(8,128)(2,1)}, bf16[512,3072]{1,0:T(8,128)(2,1)}, u32[]{:S(2)}, u32[]{:S(2)}) collective-permute-start(bf16[512,3072]{1,0:T(8,128)(2,1)} %shard_map.260), channel_id=1, source_target_pairs={{0,4},{4,0},{8,12},{12,8},{16,20},{20,16},{24,28},{28,24},{1,5},{5... | collective-permute-start | bytes 9437192 | tf_op jit(solution)/shard_map/ppermute | solution.py:684
  507.4 36.9 %collective-permute-start.62 = (bf16[256,2048]{1,0:T(8,128)(2,1)}, bf16[256,2048]{1,0:T(8,128)(2,1)}, u32[]{:S(2)}, u32[]{:S(2)}) collective-permute-start(bf16[256,2048]{1,0:T(8,128)(2,1)} %get-tuple-element.355), channel_id=1, source_target_pairs={{0,1},{3,2},{4,5},{7,6},{8,9},{11,10},{12,13},{15,14},{16,17},{19,... | collective-permute-start | bytes 3145736 | tf_op jit(solution)/shard_map/ppermute | solution.py:687
  509.7 34.6 %collective-permute-start.61 = (bf16[256,2048]{1,0:T(8,128)(2,1)}, bf16[256,2048]{1,0:T(8,128)(2,1)}, u32[]{:S(2)}, u32[]{:S(2)}) collective-permute-start(bf16[256,2048]{1,0:T(8,128)(2,1)} %add_convert_fusion.2), channel_id=1, source_target_pairs={{1,2},{2,1},{5,6},{6,5},{9,10},{10,9},{13,14},{14,13},{17,18},{18,... | collective-permute-start | bytes 3145736 | tf_op jit(solution)/shard_map/ppermute | solution.py:687
  544.3 37.2 %collective-permute-start.67 = (bf16[256,3072]{1,0:T(8,128)(2,1)}, bf16[256,3072]{1,0:T(8,128)(2,1)}, u32[]{:S(2)}, u32[]{:S(2)}) collective-permute-start(bf16[256,3072]{1,0:T(8,128)(2,1)} %get-tuple-element.363), channel_id=1, source_target_pairs={{0,16},{4,20},{8,24},{12,28},{16,0},{20,4},{24,8},{28,12},{1,17},{... | collective-permute-start | bytes 4718600 | tf_op jit(solution)/shard_map/ppermute | solution.py:684
  544.8 27.7 %collective-permute-start.71 = (bf16[512,1024]{1,0:T(8,128)(2,1)S(1)}, bf16[512,1024]{1,0:T(8,128)(2,1)}, u32[]{:S(2)}, u32[]{:S(2)}) collective-permute-start(bf16[512,1024]{1,0:T(8,128)(2,1)S(1)} %shard_map.262), channel_id=1, source_target_pairs={{0,4},{4,0},{8,12},{12,8},{16,20},{20,16},{24,28},{28,24},{1,5},{5... | collective-permute-start | bytes 3145736 | tf_op jit(solution)/shard_map/ppermute | solution.py:684
  545.7 36.9 %collective-permute-start.68 = (bf16[256,3072]{1,0:T(8,128)(2,1)}, bf16[256,3072]{1,0:T(8,128)(2,1)}, u32[]{:S(2)}, u32[]{:S(2)}) collective-permute-start(bf16[256,3072]{1,0:T(8,128)(2,1)} %get-tuple-element.368), channel_id=1, source_target_pairs={{0,8},{4,12},{8,0},{12,4},{16,24},{20,28},{24,16},{28,20},{1,9},{5... | collective-permute-start | bytes 4718600 | tf_op jit(solution)/shard_map/ppermute | solution.py:684
  586.1 32.5 %collective-permute-start.74 = (bf16[128,3072]{1,0:T(8,128)(2,1)S(1)}, bf16[128,3072]{1,0:T(8,128)(2,1)S(1)}, u32[]{:S(2)}, u32[]{:S(2)}) collective-permute-start(bf16[128,3072]{1,0:T(8,128)(2,1)S(1)} %get-tuple-element.388), channel_id=1, source_target_pairs={{0,16},{4,20},{8,24},{12,28},{16,0},{20,4},{24,8},{28,12},{1,17},{... | collective-permute-start | bytes 2359304 | tf_op jit(solution)/shard_map/ppermute | solution.py:684
  588.7 29.9 %collective-permute-start.73 = (bf16[128,3072]{1,0:T(8,128)(2,1)S(1)}, bf16[128,3072]{1,0:T(8,128)(2,1)S(1)}, u32[]{:S(2)}, u32[]{:S(2)}) collective-permute-start(bf16[128,3072]{1,0:T(8,128)(2,1)S(1)} %get-tuple-element.385), channel_id=1, source_target_pairs={{0,8},{4,12},{8,0},{12,4},{16,24},{20,28},{24,16},{28,20},{1,9},{5... | collective-permute-start | bytes 2359304 | tf_op jit(solution)/shard_map/ppermute | solution.py:684
  589.6 31.1 %collective-permute-start.72 = (bf16[256,2048]{1,0:T(8,128)(2,1)S(1)}, bf16[256,2048]{1,0:T(8,128)(2,1)S(1)}, u32[]{:S(2)}, u32[]{:S(2)}) collective-permute-start(bf16[256,2048]{1,0:T(8,128)(2,1)S(1)} %copy-done.99), channel_id=1, source_target_pairs={{0,1},{1,0},{2,3},{3,2},{4,5},{5,4},{6,7},{7,6},{8,9},{9,8},{10,11... | collective-permute-start | bytes 3145736 | tf_op jit(solution)/shard_map/ppermute | solution.py:687
  (153 other events, 2147.9 us)

commit v5 on v4

--- a/solution.py
+++ b/solution.py
@@ -836,10 +836,11 @@
         return [first_level(half, order) for half, order in zip(halves, orders)]
 
     def level_two(halves, come):
+        firsts = [second_level(half, order) for half, order in zip(halves, orders)]
         found = []
-        for half, other, order in zip(halves, come, orders):
-            both_pieces = jnp.concatenate([half, hold(other)], 0)
-            found += further_two([both_pieces, swap_dp(both_pieces, 1 << order[1])], order)
+        for half, other, first, order in zip(halves, come, firsts, orders):
+            last = swap_dp(after(hold(other), first), 1 << order[1])
+            found += further_two([half, other, first, last], order)
         return found
 
     def further_two(pieces, order):
@@ -936,15 +937,15 @@
     attn_slots = attn_own, attn_beside, attn_second, jnp.where(inner, attn_middle, hold(attn_last))
 
     grad_mixed = grad_mixed + rows_times([attn_slots[3]], attn_low, proj_columns, out_columns)
-    grad_turn = lax.ppermute(
-        jnp.concatenate([after(t, grad_mixed[3]) for t in mlp_total[0]], 0), both, [(b, a) for a, b in odd_turn]
-    )
+    grad_turn = [
+        lax.ppermute(after(t, grad_mixed[3]), both, [(b, a) for a, b in odd_turn]) for t in mlp_total[0]
+    ]
     grad_proj = retain_back(
         grad_mixed, projected, normed_head, scale_head, query, key, value, place_arg, log_decay, cosines, sines, heads
     )
     back_third, gain_third = rows_back(grad_proj, (3,), attn_low, 0, first_slots[3:])
     mlp_ends = mlp_end(1)
-    close(grad_turn, back_third, mlp_ends[0][1], mlp_ends[1][1])
+    close(*grad_turn, back_third, mlp_ends[0][1], mlp_ends[1][1])
 
     from_ends = move_tensor(hold(back_third), inward)
     to_owner = [(b, a) for a, b in to_even + to_odd]
@@ -992,15 +993,17 @@
     sum_mgate, sum_mup, sum_down = receive_mlp(
         (mine & 1).astype(jnp.int32).reshape(1),
         jnp.concatenate([hold(t) for t in mlp_total[0]], 0),
-        grad_turn,
+        jnp.concatenate(grad_turn, 0),
         jnp.concatenate(grad_core, 0),
         units,
     )
     out_up = sum_end(*sum_split(out_up_low, hold(out_come[0])), up_bits)
     out_down = sum_end(*sum_split(out_down_low, hold(out_come[1])), down_bits)
     gains = hold(gains)
-    gains = gains + sum(swap_dp(gains, 2 * chip) for chip in range(1, dp_size // 2))
-    gains = gains + sum(swap_tensor(gains, other) for other in range(1, tensor_size))
+    for other in (1, 2):
+        gains = gains + swap_tensor(gains, other)
+    for bit in range(1, bits):
+        gains = gains + swap_dp(gains, 1 << bit)
     sum_query, sum_key, sum_value, sum_gate = receive_attn(
         (hold(proj_up[0]), proj_up[1], *proj_down), 2, 2, heads
     )

time: 648 us -> 647 us (level)
  local copies, waits for them, and re-layouts: 39.7 us -> 28.3 us
  Pallas kernels: 236 us -> 228 us
    ppermute x53 -> x56, waiting for transfers between devices: 87.9 us -> 109 us  [swap_dp(): return lax.ppermute(array, 'dp', [(i, i ^ mask) for i in range(dp_size)])]
    ppermute x26 -> x25, waiting for transfers between devices: 129 us -> 113 us  [move_tensor(): return lax.ppermute(array, 'tensor', pairs)]
    unnamed x234 -> x210, local copies, waits for them, and re-layouts: 32.4 us -> 24.1 us
    pallas_call x2, Pallas kernels: 43.4 us -> 35.3 us  [mlp(): pl.pallas_call(mlp_again_kernel if weights else partial(mlp_kernel, len(p...]
    ppermute x53 -> x56, starting transfers between devices: 41.8 us -> 43.5 us  [swap_dp(): return lax.ppermute(array, 'dp', [(i, i ^ mask) for i in range(dp_size)])]
    ppermute x26 -> x25, starting transfers between devices: 45.7 us -> 47.1 us  [move_tensor(): return lax.ppermute(array, 'tensor', pairs)]
  transfers between devices with their start and end apart: 86 -> 89, of which waited for: 33 -> 40; matrix products, arithmetic and copies ran while one was open for 7% -> 7% of each run, Pallas kernels for 32% -> 32%
where the time goes in v5:
time: 647 us; the launch traced here: 637 us
  Pallas kernels  228 us (35%)
  waiting for transfers between devices  228 us (35%)
  starting transfers between devices  104 us (16%)
  other arithmetic  44.5 us (7%)
  local copies, waits for them, and re-layouts  28.3 us (4%)
    ppermute x25, waiting for transfers between devices, move_tensor(): return lax.ppermute(array, 'tensor', pairs)  113 us
    ppermute x56, waiting for transfers between devices, swap_dp(): return lax.ppermute(array, 'dp', [(i, i ^ mask) for i in range(dp_size)])  109 us
    ppermute x25, starting transfers between devices, move_tensor(): return lax.ppermute(array, 'tensor', pairs)  47.1 us
    pallas_call x8, Pallas kernels, attn_grads(): pl.pallas_call(attn_grad_kernel if core else attn_grad_add_kernel, out_sh...  46.8 us
    ppermute x56, starting transfers between devices, swap_dp(): return lax.ppermute(array, 'dp', [(i, i ^ mask) for i in range(dp_size)])  43.5 us
    pallas_call x5, Pallas kernels, rows_back(): pl.pallas_call(partial(rows_back_kernel, len(slots), len(pieces), 1 if we...  43.5 us
    pallas_call x2, Pallas kernels, mlp(): pl.pallas_call(mlp_again_kernel if weights else partial(mlp_kernel, len(p...  35.3 us
    pallas_call x4, Pallas kernels, mlp_grads(): pl.pallas_call(mlp_grad_kernel, out_shape=[jax.ShapeDtypeStruct((tile, 3...  27.9 us
  transfers between devices with their start and end apart: 89, of which 40 were waited for; matrix products, arithmetic and copies ran while one was open for 7% of the time, Pallas kernels for 32%

profile of v5, /device:TPU:0, one launch (start us, length us, event | category | flops | bytes accessed | tf_op | source)
XLA Modules:
  0.0 636.5 jit_solution(13704010926158996016)
XLA Ops:
  22.5 10.2 %collective-permute-done.2.refs_1_.refs_19_ = bf16[256,2048]{1,0:T(8,128)(2,1)} collective-permute-done((bf16[256,2048]{1,0:T(8,128)(2,1)}, bf16[256,2048]{1,0:T(8,128)(2,1)}, u32[]{:S(2)}, u32[]{:S(2)}) %collective-permute-start.2) | collective-permute-done | bytes 1048608 | tf_op jit(solution)/shard_map/ppermute | solution.py:687
  32.7 3.8 collective-permute-done.refs_5_.refs_2_.refs_4_.refs_3_
  42.0 25.1 %collective-permute-done.8 = bf16[256,2048]{1,0:T(8,128)(2,1)S(1)} collective-permute-done((bf16[256,2048]{1,0:T(8,128)(2,1)}, bf16[256,2048]{1,0:T(8,128)(2,1)S(1)}, u32[]{:S(2)}, u32[]{:S(2)}) %collective-permute-start.8) | collective-permute-done | bytes 1048608 | tf_op jit(solution)/shard_map/ppermute | solution.py:687
  73.1 24.6 %collective-permute-done.12 = bf16[256,2048]{1,0:T(8,128)(2,1)S(1)} collective-permute-done((bf16[256,2048]{1,0:T(8,128)(2,1)S(1)}, bf16[256,2048]{1,0:T(8,128)(2,1)S(1)}, u32[]{:S(2)}, u32[]{:S(2)}) %collective-permute-start.12) | collective-permute-done | bytes 1048608 | tf_op jit(solution)/shard_map/ppermute | solution.py:687
  105.3 3.5 collective-permute-start.21
  109.1 18.1 %shard_map.242 = (bf16[256,3072]{1,0:T(8,128)(2,1)}, bf16[256,3072]{1,0:T(8,128)(2,1)}, bf16[256,3072]{1,0:T(8,128)(2,1)}, bf16[256,3072]{1,0:T(8,128)(2,1)}) custom-call(bf16[256,2048]{1,0:T(8,128)(2,1)} %fusion.5.refs_0_.refs_18_, bf16[256,2048]{1,0:T(8,128)(2,1)} %collective-permute-done.2.refs_1_.refs_19_, ...), custom_call_target="tpu_custom_call" | custom-call | flops 201326592 | bytes 196608 | tf_op jit(solution)/shard_map/pallas_call | solution.py:245
  130.3 7.0 %collective-permute-start.24 = (bf16[128,2688]{1,0:T(8,128)(2,1)}, bf16[128,2688]{1,0:T(8,128)(2,1)}, u32[]{:S(2)}, u32[]{:S(2)}) collective-permute-start(bf16[128,2688]{1,0:T(8,128)(2,1)} %slice.132), channel_id=1, source_target_pairs={{4,0},{5,1},{6,2},{7,3},{12,8},{13,9},{14,10},{15,11},{20,16},{21,... | collective-permute-start | bytes 2064392 | tf_op jit(solution)/shard_map/ppermute | solution.py:856
  138.8 10.3 %shard_map.243 = (bf16[1024,512]{1,0:T(8,128)(2,1)S(1)}, bf16[1024,512]{1,0:T(8,128)(2,1)S(1)}, bf16[1024,1024]{1,0:T(8,128)(2,1)}, bf16[1024,1024]{1,0:T(8,128)...) custom-call(s32[1]{0:T(128)} %bitcast.3.place_ref, f32[2]{0:T(128)S(1)} %subtract_log_fusion.decay_ref, ...), custom_call_target="tpu_custom_call" | custom-call | flops 25165824 | bytes 288000 | tf_op jit(solution)/shard_map/pallas_call | solution.py:125
  150.1 3.5 shard_map.244
  153.7 5.1 collective-permute-start.26
  163.0 12.5 %collective-permute-done.30.refs_6_ = bf16[128,2688]{1,0:T(8,128)(2,1)S(1)} collective-permute-done((bf16[128,2688]{1,0:T(8,128)(2,1)}, bf16[128,2688]{1,0:T(8,128)(2,1)S(1)}, u32[]{:S(2)}, u32[]{:S(2)}) %collective-permute-start.30) | collective-permute-done | bytes 688160 | tf_op jit(solution)/shard_map/ppermute | solution.py:684
  177.4 6.6 %shard_map.245 = (bf16[256,2048]{1,0:T(8,128)(2,1)S(1)}, bf16[256,2048]{1,0:T(8,128)(2,1)S(1)}, bf16[256,2048]{1,0:T(8,128)(2,1)S(1)}) custom-call(bf16[1024,1024]{1,0:T(8,128)(2,1)} %get-tuple-element.395.refs_0_.refs_1_.refs_2_.refs_4_, bf16[1024,1024]{1,0:T(8,128)(2,1)} %get-tuple-element.395.refs_0_.refs_1_.refs_2_.refs_4_, ...), custom_call_target="tpu_custom_call" | custom-call | flops 50331648 | bytes 65536 | tf_op jit(solution)/shard_map/pallas_call | solution.py:288
  184.5 3.5 collective-permute-done.27.refs_12_
  193.0 6.6 %collective-permute-start.36 = (bf16[256,2048]{1,0:T(8,128)(2,1)S(1)}, bf16[256,2048]{1,0:T(8,128)(2,1)S(1)}, u32[]{:S(2)}, u32[]{:S(2)}) collective-permute-start(bf16[256,2048]{1,0:T(8,128)(2,1)S(1)} %get-tuple-element.280), channel_id=1, source_target_pairs={{0,1},{3,2},{4,5},{7,6},{8,9},{11,10},{12,13},{15,14},{16,17},{19,... | collective-permute-start | bytes 3145736 | tf_op jit(solution)/shard_map/ppermute | solution.py:687
  201.3 13.9 %collective-permute-done.35.refs_13_ = bf16[128,2688]{1,0:T(8,128)(2,1)S(1)} collective-permute-done((bf16[128,2688]{1,0:T(8,128)(2,1)S(1)}, bf16[128,2688]{1,0:T(8,128)(2,1)S(1)}, u32[]{:S(2)}, u32[]{:S(2)}) %collective-permute-start.35) | collective-permute-done | bytes 688160 | tf_op jit(solution)/shard_map/ppermute | solution.py:684
  215.6 4.9 collective-permute-done.36
  226.7 13.3 %collective-permute-done.41.refs_14_ = bf16[128,2688]{1,0:T(8,128)(2,1)S(1)} collective-permute-done((bf16[128,2688]{1,0:T(8,128)(2,1)S(1)}, bf16[128,2688]{1,0:T(8,128)(2,1)S(1)}, u32[]{:S(2)}, u32[]{:S(2)}) %collective-permute-start.41) | collective-permute-done | bytes 688160 | tf_op jit(solution)/shard_map/ppermute | solution.py:684
  246.4 7.6 %collective-permute-done.42.refs_15_ = bf16[128,2688]{1,0:T(8,128)(2,1)S(1)} collective-permute-done((bf16[128,2688]{1,0:T(8,128)(2,1)S(1)}, bf16[128,2688]{1,0:T(8,128)(2,1)S(1)}, u32[]{:S(2)}, u32[]{:S(2)}) %collective-permute-start.42) | collective-permute-done | bytes 688160 | tf_op jit(solution)/shard_map/ppermute | solution.py:684
  259.4 18.7 %shard_map.246 = (bf16[256,896]{1,0:T(8,128)(2,1)S(1)}, bf16[256,896]{1,0:T(8,128)(2,1)S(1)}, bf16[256,896]{1,0:T(8,128)(2,1)S(1)}, bf16[256,896]{1,0:T(8,128)(2...) custom-call(bf16[256,2048]{1,0:T(8,128)(2,1)} %copy-done.60, ...), custom_call_target="tpu_custom_call" | custom-call | flops 146800640 | bytes 172032 | tf_op jit(solution)/shard_map/pallas_call | solution.py:371
  285.0 16.6 %shard_map.247 = (bf16[256,896]{1,0:T(8,128)(2,1)S(1)}, bf16[256,896]{1,0:T(8,128)(2,1)S(1)}, bf16[256,896]{1,0:T(8,128)(2,1)S(1)}, bf16[256,896]{1,0:T(8,128)(2...) custom-call(bf16[256,2048]{1,0:T(8,128)(2,1)S(1)} %collective-permut, ...), custom_call_target="tpu_custom_call" | custom-call | flops 146800640 | bytes 172032 | tf_op jit(solution)/shard_map/pallas_call | solution.py:371
  306.5 6.8 %shard_map.250 = (bf16[256,2688]{1,0:T(8,128)(2,1)}, bf16[256,2688]{1,0:T(8,128)(2,1)}) custom-call(bf16[256,2048]{1,0:T(8,128)(2,1)} %copy-done.60, bf16[256,2048]{1,0:T(8,128)(2,1)} %copy-done.26, bf16[256,2048]{1,0:T(8,128)(2,1)} %copy-done.62, bf16[256,2048]{1,0:T(8,128)(2,1)} %copy-done.63, ...), custom_call_target="tpu_custom_call" | custom-call | flops 44040192 | bytes 57344 | tf_op jit(solution)/shard_map/pallas_call | solution.py:434
  313.3 6.9 %shard_map.249 = (bf16[256,2688]{1,0:T(8,128)(2,1)}, bf16[256,2688]{1,0:T(8,128)(2,1)}) custom-call(bf16[256,2048]{1,0:T(8,128)(2,1)} %copy-done.60, bf16[256,2048]{1,0:T(8,128)(2,1)} %copy-done.26, bf16[256,2048]{1,0:T(8,128)(2,1)} %copy-done.62, bf16[256,2048]{1,0:T(8,128)(2,1)} %copy-done.63, ...), custom_call_target="tpu_custom_call" | custom-call | flops 44040192 | bytes 57344 | tf_op jit(solution)/shard_map/pallas_call | solution.py:434
  320.2 7.8 %shard_map.248 = (bf16[512,2048]{1,0:T(8,128)(2,1)S(1)}, bf16[512,2048]{1,0:T(8,128)(2,1)}) custom-call(bf16[256,896]{1,0:T(8,128)(2,1)S(1)} %get-tuple-element.304.refs_0_.refs_16_, bf16[256,896]{1,0:T(8,128)(2,1)S(1)} %get-tuple-element.305.refs_1_.refs_17_, bf16[256,896]{1,0:T(8,128)(2,1)S(1)} %get-tuple-element.306.refs_2_.refs_18_, ...), custom_call_target="tpu_custom_call" | custom-call | flops 58720256 | bytes 57344 | tf_op jit(solution)/shard_map/pallas_call | solution.py:397
  331.4 4.2 shard_map.251
  339.9 7.2 %shard_map.253 = (bf16[256,2688]{1,0:T(8,128)(2,1)}, bf16[256,2688]{1,0:T(8,128)(2,1)}) custom-call(bf16[256,2048]{1,0:T(8,128)(2,1)} %copy-done.60, bf16[256,2048]{1,0:T(8,128)(2,1)} %copy-done.26, bf16[256,2048]{1,0:T(8,128)(2,1)} %copy-done.62, bf16[256,2048]{1,0:T(8,128)(2,1)} %copy-done.63, ...), custom_call_target="tpu_custom_call" | custom-call | flops 44040192 | bytes 57344 | tf_op jit(solution)/shard_map/pallas_call | solution.py:434
  347.1 7.0 %shard_map.252 = (bf16[256,2688]{1,0:T(8,128)(2,1)}, bf16[256,2688]{1,0:T(8,128)(2,1)}) custom-call(bf16[256,2048]{1,0:T(8,128)(2,1)} %copy-done.60, bf16[256,2048]{1,0:T(8,128)(2,1)} %copy-done.26, bf16[256,2048]{1,0:T(8,128)(2,1)} %copy-done.62, bf16[256,2048]{1,0:T(8,128)(2,1)} %copy-done.63, ...), custom_call_target="tpu_custom_call" | custom-call | flops 44040192 | bytes 57344 | tf_op jit(solution)/shard_map/pallas_call | solution.py:434
  354.1 7.6 %collective-permute-done.54 = bf16[256,2688]{1,0:T(8,128)(2,1)} collective-permute-done((bf16[256,2688]{1,0:T(8,128)(2,1)}, bf16[256,2688]{1,0:T(8,128)(2,1)}, u32[]{:S(2)}, u32[]{:S(2)}) %collective-permute-start.54) | collective-permute-done | bytes 1376288 | tf_op jit(solution)/shard_map/ppermute | solution.py:684
  368.1 16.6 %collective-permute-done.50.refs_1_ = bf16[256,2048]{1,0:T(8,128)(2,1)S(1)} collective-permute-done((bf16[256,2048]{1,0:T(8,128)(2,1)S(1)}, bf16[256,2048]{1,0:T(8,128)(2,1)S(1)}, u32[]{:S(2)}, u32[]{:S(2)}) %collective-permute-start.50) | collective-permute-done | bytes 1048608 | tf_op jit(solution)/shard_map/ppermute | solution.py:687
  387.4 4.9 collective-permute-done.55
  397.6 5.3 shard_map.254
  410.7 7.5 %collective-permute-done.57 = bf16[256,2048]{1,0:T(8,128)(2,1)S(1)} collective-permute-done((bf16[256,2048]{1,0:T(8,128)(2,1)S(1)}, bf16[256,2048]{1,0:T(8,128)(2,1)S(1)}, u32[]{:S(2)}, u32[]{:S(2)}) %collective-permute-start.57) | collective-permute-done | bytes 1048608 | tf_op jit(solution)/shard_map/ppermute | solution.py:687
  418.4 3.3 shard_map.255.refs_3_
  425.7 16.0 %shard_map.256.refs_0_.refs_4_.refs_1_ = bf16[1024,3072]{1,0:T(8,128)(2,1)} custom-call(s32[1]{0:T(128)} %bitcast.3.place_ref, f32[2]{0:T(128)S(1)} %subtract_log_fusion.decay_ref, bf16[256,1024]{1,0:T(8,128)(2,1)S(1)} %get-tuple-element.345.refs_0_, bf16[256,1024]{1,0:T(8,128)(2,1)S(1)} %get-tuple-element.350.refs_1_, ...), custom_call_target="tpu_custom_call" | custom-call | flops 58720256 | bytes 320000 | tf_op jit(solution)/shard_map/pallas_call | solution.py:212
  441.7 9.4 %shard_map.257 = (bf16[256,2048]{1,0:T(8,128)(2,1)S(1)}, f32[8,2048]{1,0:T(8,128)S(1)}) custom-call(bf16[1024,3072]{1,0:T(8,128)(2,1)} %shard_map.256.refs_0_.refs_4_.refs_1_, bf16[128,4096]{1,0:T(8,128)(2,1)S(1)} %get-tuple-element.233.refs_4_.refs_1_.refs_3_.refs_2_, bf16[128,4096]{1,0:T(8,128)(2,1)S(1)} %copy-done.3, ...), custom_call_target="tpu_custom_call" | custom-call | flops 50331648 | bytes 196608 | tf_op jit(solution)/shard_map/pallas_call | solution.py:288
  452.0 7.3 %collective-permute-start.64 = (bf16[256,2048]{1,0:T(8,128)(2,1)S(1)}, bf16[256,2048]{1,0:T(8,128)(2,1)S(1)}, u32[]{:S(2)}, u32[]{:S(2)}) collective-permute-start(bf16[256,2048]{1,0:T(8,128)(2,1)S(1)} %get-tuple-element.366), channel_id=1, source_target_pairs={{0,1},{3,2},{4,5},{7,6},{8,9},{11,10},{12,13},{15,14},{16,17},{19,... | collective-permute-start | bytes 3145736 | tf_op jit(solution)/shard_map/ppermute | solution.py:687
  460.7 7.8 %shard_map.258 = bf16[512,3072]{1,0:T(8,128)(2,1)} custom-call(bf16[256,2048]{1,0:T(8,128)(2,1)} %fusion.5.refs_0_.refs_18_, bf16[256,2048]{1,0:T(8,128)(2,1)} %collective-permute-done.2.refs_1_.refs_19_, bf16[256,2048]{1,0:T(8,128)(2,1)S(1)} %copy-done.8, bf16[256,2048]{1,0:T(8,128)(2,1)S(1)} %copy-done.12, ...), custom_call_target="tpu_custom_call" | custom-call | flops 50331648 | bytes 98304 | tf_op jit(solution)/shard_map/pallas_call | solution.py:468
  468.5 10.3 %shard_map.259 = (bf16[256,2048]{1,0:T(8,128)(2,1)}, f32[8,2048]{1,0:T(8,128)S(1)}) custom-call(bf16[1024,3072]{1,0:T(8,128)(2,1)} %shard_map.256.refs_0_.refs_4_.refs_1_, bf16[128,4096]{1,0:T(8,128)(2,1)S(1)} %get-tuple-element.233.refs_4_.refs_1_.refs_3_.refs_2_, bf16[128,4096]{1,0:T(8,128)(2,1)S(1)} %copy-done.3, ...), custom_call_target="tpu_custom_call" | custom-call | flops 50331648 | bytes 196608 | tf_op jit(solution)/shard_map/pallas_call | solution.py:288
  478.9 7.8 %shard_map.260 = bf16[512,3072]{1,0:T(8,128)(2,1)} custom-call(bf16[256,2048]{1,0:T(8,128)(2,1)} %fusion.5.refs_0_.refs_18_, bf16[256,2048]{1,0:T(8,128)(2,1)} %collective-permute-done.2.refs_1_.refs_19_, bf16[256,2048]{1,0:T(8,128)(2,1)S(1)} %copy-done.9, bf16[256,2048]{1,0:T(8,128)(2,1)S(1)} %copy-done.12, ...), custom_call_target="tpu_custom_call" | custom-call | flops 50331648 | bytes 98304 | tf_op jit(solution)/shard_map/pallas_call | solution.py:468
  502.0 3.2 shard_map.261
  509.4 13.6 %shard_map.263 = (bf16[256,2048]{1,0:T(8,128)(2,1)S(1)}, bf16[256,2048]{1,0:T(8,128)(2,1)S(1)}, f32[8,2048]{1,0:T(8,128)S(1)}) custom-call(bf16[1024,3072]{1,0:T(8,128)(2,1)} %shard_map.256.refs_0_.refs_4_.refs_1_, bf16[1024,3072]{1,0:T(8,128)(2,1)} %shard_map.256.refs_0_.refs_4_.refs_1_, ...), custom_call_target="tpu_custom_call" | custom-call | flops 100663296 | bytes 196608 | tf_op jit(solution)/shard_map/pallas_call | solution.py:288
  524.1 9.2 %shard_map.264 = (bf16[256,3072]{1,0:T(8,128)(2,1)}, bf16[256,3072]{1,0:T(8,128)(2,1)}) custom-call(bf16[256,2048]{1,0:T(8,128)(2,1)} %fusion.5.refs_0_.refs_18_, bf16[256,2048]{1,0:T(8,128)(2,1)} %collective-permute-done.2.refs_1_.refs_19_, bf16[256,2048]{1,0:T(8,128)(2,1)S(1)} %copy-done.10, bf16[256,2048]{1,0:T(8,128)(2,1)S(1)} %copy-done.13, ...), custom_call_target="tpu_custom_call" | custom-call | flops 50331648 | bytes 98304 | tf_op jit(solution)/shard_map/pallas_call | solution.py:468
  544.6 8.6 %shard_map.266 = (bf16[256,3072]{1,0:T(8,128)(2,1)S(1)}, bf16[256,3072]{1,0:T(8,128)(2,1)}) custom-call(bf16[256,2048]{1,0:T(8,128)(2,1)} %fusion.5.refs_0_.refs_18_, bf16[256,2048]{1,0:T(8,128)(2,1)} %collective-permute-done.2.refs_1_.refs_19_, bf16[256,2048]{1,0:T(8,128)(2,1)S(1)} %copy-done.10, bf16[256,2048]{1,0:T(8,128)(2,1)S(1)} %copy-done.13, ...), custom_call_target="tpu_custom_call" | custom-call | flops 50331648 | bytes 98304 | tf_op jit(solution)/shard_map/pallas_call | solution.py:468
  553.2 3.5 shard_map.267
  556.8 3.6 shard_map.268
  560.4 7.4 %collective-permute-done.70 = bf16[256,2048]{1,0:T(8,128)(2,1)S(1)} collective-permute-done((bf16[256,2048]{1,0:T(8,128)(2,1)}, bf16[256,2048]{1,0:T(8,128)(2,1)S(1)}, u32[]{:S(2)}, u32[]{:S(2)}) %collective-permute-start.70) | collective-permute-done | bytes 1048608 | tf_op jit(solution)/shard_map/ppermute | solution.py:687
  580.6 6.1 collective-permute-done.80
  591.4 17.3 %collective-permute-done.81 = bf16[256,1024]{1,0:T(8,128)(2,1)} collective-permute-done((bf16[256,1024]{1,0:T(8,128)(2,1)S(1)}, bf16[256,1024]{1,0:T(8,128)(2,1)}, u32[]{:S(2)}, u32[]{:S(2)}) %collective-permute-start.81) | collective-permute-done | bytes 524320 | tf_op jit(solution)/shard_map/ppermute | solution.py:684
  619.0 3.8 collective-permute-done.84
  (432 shorter events, 197.7 us)
Async XLA Ops:
  6.2 26.5 %collective-permute-start.2 = (bf16[256,2048]{1,0:T(8,128)(2,1)}, bf16[256,2048]{1,0:T(8,128)(2,1)}, u32[]{:S(2)}, u32[]{:S(2)}) collective-permute-start(bf16[256,2048]{1,0:T(8,128)(2,1)} %fusion.5.refs_0_.refs_18_), channel_id=1, source_target_pairs={{0,1},{1,0},{2,3},{3,2},{4,5},{5,4},{6,7},{7,6},{8,9},{9,8},{10,11... | collective-permute-start | bytes 3145736 | tf_op jit(solution)/shard_map/ppermute | solution.py:687
  11.0 25.6 %collective-permute-start = (bf16[128,4096]{1,0:T(8,128)(2,1)S(1)}, bf16[128,4096]{1,0:T(8,128)(2,1)S(1)}, u32[]{:S(2)}, u32[]{:S(2)}) collective-permute-start(bf16[128,4096]{1,0:T(8,128)(2,1)S(1)} %get-tuple-element.233.refs_4_.refs_1_.refs_3_.refs_2_), channel_id=1, source_target_pairs={{0,8},{4,12},{8,0},{12,4},{16,24},{20,28},{24,16},{28,20},{1,9},{5... | collective-permute-start | bytes 3145736 | tf_op jit(solution)/shard_map/ppermute | solution.py:684
  12.4 25.4 %collective-permute-start.1 = (bf16[128,4096]{1,0:T(8,128)(2,1)S(1)}, bf16[128,4096]{1,0:T(8,128)(2,1)}, u32[]{:S(2)}, u32[]{:S(2)}) collective-permute-start(bf16[128,4096]{1,0:T(8,128)(2,1)S(1)} %get-tuple-element.234.refs_8_.refs_5_.refs_7_.refs_6_), channel_id=1, source_target_pairs={{0,16},{4,20},{8,24},{12,28},{16,0},{20,4},{24,8},{28,12},{1,17},{... | collective-permute-start | bytes 3145736 | tf_op jit(solution)/shard_map/ppermute | solution.py:684
  37.8 29.3 %collective-permute-start.6 = (bf16[128,4096]{1,0:T(8,128)(2,1)S(1)}, bf16[128,4096]{1,0:T(8,128)(2,1)}, u32[]{:S(2)}, u32[]{:S(2)}) collective-permute-start(bf16[128,4096]{1,0:T(8,128)(2,1)S(1)} %get-tuple-element.234.refs_8_.refs_5_.refs_7_.refs_6_), channel_id=1, source_target_pairs={{0,8},{4,12},{8,0},{12,4},{16,24},{20,28},{24,16},{28,20},{1,9},{5... | collective-permute-start | bytes 3145736 | tf_op jit(solution)/shard_map/ppermute | solution.py:684
  38.4 28.7 %collective-permute-start.9 = (bf16[128,4096]{1,0:T(8,128)(2,1)S(1)}, bf16[128,4096]{1,0:T(8,128)(2,1)S(1)}, u32[]{:S(2)}, u32[]{:S(2)}) collective-permute-start(bf16[128,4096]{1,0:T(8,128)(2,1)S(1)} %get-tuple-element.234.refs_8_.refs_5_.refs_7_.refs_6_), channel_id=1, source_target_pairs={{0,4},{4,0},{8,12},{12,8},{16,20},{20,16},{24,28},{28,24},{1,5},{5... | collective-permute-start | bytes 3145736 | tf_op jit(solution)/shard_map/ppermute | solution.py:684
  38.4 28.7 %collective-permute-start.8 = (bf16[256,2048]{1,0:T(8,128)(2,1)}, bf16[256,2048]{1,0:T(8,128)(2,1)S(1)}, u32[]{:S(2)}, u32[]{:S(2)}) collective-permute-start(bf16[256,2048]{1,0:T(8,128)(2,1)} %collective-permute-done.3), channel_id=1, source_target_pairs={{1,0},{2,3},{5,4},{6,7},{9,8},{10,11},{13,12},{14,15},{17,16},{18,... | collective-permute-start | bytes 3145736 | tf_op jit(solution)/shard_map/ppermute | solution.py:687
  39.7 27.4 %collective-permute-start.7 = (bf16[256,2048]{1,0:T(8,128)(2,1)}, bf16[256,2048]{1,0:T(8,128)(2,1)S(1)}, u32[]{:S(2)}, u32[]{:S(2)}) collective-permute-start(bf16[256,2048]{1,0:T(8,128)(2,1)} %collective-permute-done.2.refs_1_.refs_19_), channel_id=1, source_target_pairs={{1,2},{2,1},{5,6},{6,5},{9,10},{10,9},{13,14},{14,13},{17,18},{18,... | collective-permute-start | bytes 3145736 | tf_op jit(solution)/shard_map/ppermute | solution.py:687
  40.4 26.7 %collective-permute-start.5 = (bf16[128,4096]{1,0:T(8,128)(2,1)S(1)}, bf16[128,4096]{1,0:T(8,128)(2,1)}, u32[]{:S(2)}, u32[]{:S(2)}) collective-permute-start(bf16[128,4096]{1,0:T(8,128)(2,1)S(1)} %get-tuple-element.233.refs_4_.refs_1_.refs_3_.refs_2_), channel_id=1, source_target_pairs={{0,16},{4,20},{8,24},{12,28},{16,0},{20,4},{24,8},{28,12},{1,17},{... | collective-permute-start | bytes 3145736 | tf_op jit(solution)/shard_map/ppermute | solution.py:684
  68.5 29.2 %collective-permute-start.11 = (bf16[128,4096]{1,0:T(8,128)(2,1)}, bf16[128,4096]{1,0:T(8,128)(2,1)}, u32[]{:S(2)}, u32[]{:S(2)}) collective-permute-start(bf16[128,4096]{1,0:T(8,128)(2,1)} %collective-permute-done.1.refs_9_.refs_6_.refs_8_.refs_7_), channel_id=1, source_target_pairs={{0,8},{4,12},{8,0},{12,4},{16,24},{20,28},{24,16},{28,20},{1,9},{5... | collective-permute-start | bytes 3145736 | tf_op jit(solution)/shard_map/ppermute | solution.py:684
  69.9 27.7 %collective-permute-start.14 = (bf16[128,4096]{1,0:T(8,128)(2,1)}, bf16[128,4096]{1,0:T(8,128)(2,1)S(1)}, u32[]{:S(2)}, u32[]{:S(2)}) collective-permute-start(bf16[128,4096]{1,0:T(8,128)(2,1)} %collective-permute-done.1.refs_9_.refs_6_.refs_8_.refs_7_), channel_id=1, source_target_pairs={{0,4},{4,0},{8,12},{12,8},{16,20},{20,16},{24,28},{28,24},{1,5},{5... | collective-permute-start | bytes 3145736 | tf_op jit(solution)/shard_map/ppermute | solution.py:684
  69.9 27.7 %collective-permute-start.12 = (bf16[256,2048]{1,0:T(8,128)(2,1)S(1)}, bf16[256,2048]{1,0:T(8,128)(2,1)S(1)}, u32[]{:S(2)}, u32[]{:S(2)}) collective-permute-start(bf16[256,2048]{1,0:T(8,128)(2,1)S(1)} %collective-permute-done.7), channel_id=1, source_target_pairs={{1,0},{2,3},{5,4},{6,7},{9,8},{10,11},{13,12},{14,15},{17,16},{18,... | collective-permute-start | bytes 3145736 | tf_op jit(solution)/shard_map/ppermute | solution.py:687
  71.2 26.4 %collective-permute-start.10 = (bf16[128,4096]{1,0:T(8,128)(2,1)S(1)}, bf16[128,4096]{1,0:T(8,128)(2,1)S(1)}, u32[]{:S(2)}, u32[]{:S(2)}) collective-permute-start(bf16[128,4096]{1,0:T(8,128)(2,1)S(1)} %collective-permute-done.refs_5_.refs_2_.refs_4_.refs_3_), channel_id=1, source_target_pairs={{0,16},{4,20},{8,24},{12,28},{16,0},{20,4},{24,8},{28,12},{1,17},{... | collective-permute-start | bytes 3145736 | tf_op jit(solution)/shard_map/ppermute | solution.py:684
  72.8 24.8 %collective-permute-start.13 = (bf16[128,4096]{1,0:T(8,128)(2,1)S(1)}, bf16[128,4096]{1,0:T(8,128)(2,1)S(1)}, u32[]{:S(2)}, u32[]{:S(2)}) collective-permute-start(bf16[128,4096]{1,0:T(8,128)(2,1)S(1)} %collective-permute-done.refs_5_.refs_2_.refs_4_.refs_3_), channel_id=1, source_target_pairs={{0,4},{4,0},{8,12},{12,8},{16,20},{20,16},{24,28},{28,24},{1,5},{5... | collective-permute-start | bytes 3145736 | tf_op jit(solution)/shard_map/ppermute | solution.py:684
  100.9 26.4 %collective-permute-start.19 = (bf16[128,2688]{1,0:T(8,128)(2,1)S(1)}, bf16[128,2688]{1,0:T(8,128)(2,1)}, u32[]{:S(2)}, u32[]{:S(2)}) collective-permute-start(bf16[128,2688]{1,0:T(8,128)(2,1)S(1)} %get-tuple-element.249), channel_id=1, source_target_pairs={{4,7},{5,6},{6,5},{7,4},{12,15},{13,14},{14,13},{15,12},{20,23},{2... | collective-permute-start | bytes 2064392 | tf_op jit(solution)/shard_map/ppermute | solution.py:827
  102.6 24.7 %collective-permute-start.20 = (bf16[128,2688]{1,0:T(8,128)(2,1)S(1)}, bf16[128,2688]{1,0:T(8,128)(2,1)}, u32[]{:S(2)}, u32[]{:S(2)}) collective-permute-start(bf16[128,2688]{1,0:T(8,128)(2,1)S(1)} %get-tuple-element.250), channel_id=1, source_target_pairs={{4,7},{5,6},{6,5},{7,4},{12,15},{13,14},{14,13},{15,12},{20,23},{2... | collective-permute-start | bytes 2064392 | tf_op jit(solution)/shard_map/ppermute | solution.py:827
  108.9 44.8 %collective-permute-start.25 = (bf16[256,2048]{1,0:T(8,128)(2,1)}, bf16[256,2048]{1,0:T(8,128)(2,1)}, u32[]{:S(2)}, u32[]{:S(2)}) collective-permute-start(bf16[256,2048]{1,0:T(8,128)(2,1)} %broadcast_select_fusion.own_grad_ref.refs_4_.grad_final), channel_id=1, source_target_pairs={{0,1},{1,0},{2,3},{3,2},{4,5},{5,4},{6,7},{7,6},{8,9},{9,8},{10,11... | collective-permute-start | bytes 3145736 | tf_op jit(solution)/shard_map/ppermute | solution.py:687
  127.3 26.4 %collective-permute-start.23 = (bf16[128,2688]{1,0:T(8,128)(2,1)}, bf16[128,2688]{1,0:T(8,128)(2,1)}, u32[]{:S(2)}, u32[]{:S(2)}) collective-permute-start(bf16[128,2688]{1,0:T(8,128)(2,1)} %collective-permute-done.20.refs_4_), channel_id=1, source_target_pairs={{0,16},{4,20},{8,24},{12,28},{16,0},{20,4},{24,8},{28,12},{1,17},{... | collective-permute-start | bytes 2064392 | tf_op jit(solution)/shard_map/ppermute | solution.py:684
  128.9 24.8 %collective-permute-start.22 = (bf16[128,2688]{1,0:T(8,128)(2,1)}, bf16[128,2688]{1,0:T(8,128)(2,1)}, u32[]{:S(2)}, u32[]{:S(2)}) collective-permute-start(bf16[128,2688]{1,0:T(8,128)(2,1)} %collective-permute-done.19.refs_0_), channel_id=1, source_target_pairs={{0,8},{4,12},{8,0},{12,4},{16,24},{20,28},{24,16},{28,20},{1,9},{5... | collective-permute-start | bytes 2064392 | tf_op jit(solution)/shard_map/ppermute | solution.py:684
  153.7 30.4 %collective-permute-start.26 = (bf16[256,2048]{1,0:T(8,128)(2,1)S(1)}, bf16[256,2048]{1,0:T(8,128)(2,1)S(1)}, u32[]{:S(2)}, u32[]{:S(2)}) collective-permute-start(bf16[256,2048]{1,0:T(8,128)(2,1)S(1)} %shard_map.244), channel_id=1, source_target_pairs={{0,1},{3,2},{4,5},{7,6},{8,9},{11,10},{12,13},{15,14},{16,17},{19,... | collective-permute-start | bytes 3145736 | tf_op jit(solution)/shard_map/ppermute | solution.py:687
  160.9 27.1 %collective-permute-start.32 = (bf16[256,2048]{1,0:T(8,128)(2,1)}, bf16[256,2048]{1,0:T(8,128)(2,1)S(1)}, u32[]{:S(2)}, u32[]{:S(2)}) collective-permute-start(bf16[256,2048]{1,0:T(8,128)(2,1)} %collective-permute-done.25.own_grad_ref.refs_5_), channel_id=1, source_target_pairs={{0,4},{4,0},{8,12},{12,8},{16,20},{20,16},{24,28},{28,24},{1,5},{5... | collective-permute-start | bytes 3145736 | tf_op jit(solution)/shard_map/ppermute | solution.py:684
  160.9 27.0 %collective-permute-start.27 = (bf16[128,2688]{1,0:T(8,128)(2,1)S(1)}, bf16[128,2688]{1,0:T(8,128)(2,1)S(1)}, u32[]{:S(2)}, u32[]{:S(2)}) collective-permute-start(bf16[128,2688]{1,0:T(8,128)(2,1)S(1)} %slice.133), channel_id=1, source_target_pairs={{4,0},{5,1},{6,2},{7,3},{12,8},{13,9},{14,10},{15,11},{20,16},{21,... | collective-permute-start | bytes 2064392 | tf_op jit(solution)/shard_map/ppermute | solution.py:864
  193.0 27.5 %collective-permute-start.36 = (bf16[256,2048]{1,0:T(8,128)(2,1)S(1)}, bf16[256,2048]{1,0:T(8,128)(2,1)S(1)}, u32[]{:S(2)}, u32[]{:S(2)}) collective-permute-start(bf16[256,2048]{1,0:T(8,128)(2,1)S(1)} %get-tuple-element.280), channel_id=1, source_target_pairs={{0,1},{3,2},{4,5},{7,6},{8,9},{11,10},{12,13},{15,14},{16,17},{19,... | collective-permute-start | bytes 3145736 | tf_op jit(solution)/shard_map/ppermute | solution.py:687
  255.7 25.6 %collective-permute-start.44 = (bf16[256,2048]{1,0:T(8,128)(2,1)S(1)}, bf16[256,2048]{1,0:T(8,128)(2,1)S(1)}, u32[]{:S(2)}, u32[]{:S(2)}) collective-permute-start(bf16[256,2048]{1,0:T(8,128)(2,1)S(1)} %multiply_convert_fusion.own_ref.refs_0_), channel_id=1, source_target_pairs={{0,1},{1,0},{2,3},{3,2},{4,5},{5,4},{6,7},{7,6},{8,9},{9,8},{10,11... | collective-permute-start | bytes 3145736 | tf_op jit(solution)/shard_map/ppermute | solution.py:687
  304.7 25.3 %collective-permute-start.48 = (bf16[256,2048]{1,0:T(8,128)(2,1)S(1)}, bf16[256,2048]{1,0:T(8,128)(2,1)S(1)}, u32[]{:S(2)}, u32[]{:S(2)}) collective-permute-start(bf16[256,2048]{1,0:T(8,128)(2,1)S(1)} %add_convert_fusion.3), channel_id=1, source_target_pairs={{0,1},{1,0},{2,3},{3,2},{4,5},{5,4},{6,7},{7,6},{8,9},{9,8},{10,11... | collective-permute-start | bytes 3145736 | tf_op jit(solution)/shard_map/ppermute | solution.py:687
  330.0 31.7 %collective-permute-start.54 = (bf16[256,2688]{1,0:T(8,128)(2,1)}, bf16[256,2688]{1,0:T(8,128)(2,1)}, u32[]{:S(2)}, u32[]{:S(2)}) collective-permute-start(bf16[256,2688]{1,0:T(8,128)(2,1)} %get-tuple-element.331), channel_id=1, source_target_pairs={{0,8},{4,12},{8,0},{12,4},{16,24},{20,28},{24,16},{28,20},{1,9},{5... | collective-permute-start | bytes 4128776 | tf_op jit(solution)/shard_map/ppermute | solution.py:684
  330.9 31.7 %collective-permute-start.52 = (bf16[256,2688]{1,0:T(8,128)(2,1)}, bf16[256,2688]{1,0:T(8,128)(2,1)}, u32[]{:S(2)}, u32[]{:S(2)}) collective-permute-start(bf16[256,2688]{1,0:T(8,128)(2,1)} %get-tuple-element.328), channel_id=1, source_target_pairs={{0,16},{4,20},{8,24},{12,28},{16,0},{20,4},{24,8},{28,12},{1,17},{... | collective-permute-start | bytes 4128776 | tf_op jit(solution)/shard_map/ppermute | solution.py:684
  331.4 56.0 %collective-permute-start.49 = (bf16[512,2048]{1,0:T(8,128)(2,1)}, bf16[512,2048]{1,0:T(8,128)(2,1)}, u32[]{:S(2)}, u32[]{:S(2)}) collective-permute-start(bf16[512,2048]{1,0:T(8,128)(2,1)} %get-tuple-element.325), channel_id=1, source_target_pairs={{0,4},{4,0},{8,12},{12,8},{16,20},{20,16},{24,28},{28,24},{1,5},{5... | collective-permute-start | bytes 6291464 | tf_op jit(solution)/shard_map/ppermute | solution.py:684
  337.0 47.8 %collective-permute-start.50 = (bf16[256,2048]{1,0:T(8,128)(2,1)S(1)}, bf16[256,2048]{1,0:T(8,128)(2,1)S(1)}, u32[]{:S(2)}, u32[]{:S(2)}) collective-permute-start(bf16[256,2048]{1,0:T(8,128)(2,1)S(1)} %get-tuple-element.341.refs_0_), channel_id=1, source_target_pairs={{0,1},{1,0},{2,3},{3,2},{4,5},{5,4},{6,7},{7,6},{8,9},{9,8},{10,11... | collective-permute-start | bytes 3145736 | tf_op jit(solution)/shard_map/ppermute | solution.py:687
  338.7 48.7 %collective-permute-start.51 = (bf16[256,2048]{1,0:T(8,128)(2,1)S(1)}, bf16[256,2048]{1,0:T(8,128)(2,1)S(1)}, u32[]{:S(2)}, u32[]{:S(2)}) collective-permute-start(bf16[256,2048]{1,0:T(8,128)(2,1)S(1)} %get-tuple-element.341.refs_0_), channel_id=1, source_target_pairs={{0,2},{1,3},{2,0},{3,1},{4,6},{5,7},{6,4},{7,5},{8,10},{9,11},{10,... | collective-permute-start | bytes 3145736 | tf_op jit(solution)/shard_map/ppermute | solution.py:687
  361.7 30.7 %collective-permute-start.55 = (bf16[256,2688]{1,0:T(8,128)(2,1)}, bf16[256,2688]{1,0:T(8,128)(2,1)S(1)}, u32[]{:S(2)}, u32[]{:S(2)}) collective-permute-start(bf16[256,2688]{1,0:T(8,128)(2,1)} %get-tuple-element.333), channel_id=1, source_target_pairs={{0,8},{4,12},{8,0},{12,4},{16,24},{20,28},{24,16},{28,20},{1,9},{5... | collective-permute-start | bytes 4128776 | tf_op jit(solution)/shard_map/ppermute | solution.py:684
  362.6 30.4 %collective-permute-start.53 = (bf16[256,2688]{1,0:T(8,128)(2,1)}, bf16[256,2688]{1,0:T(8,128)(2,1)S(1)}, u32[]{:S(2)}, u32[]{:S(2)}) collective-permute-start(bf16[256,2688]{1,0:T(8,128)(2,1)} %get-tuple-element.330), channel_id=1, source_target_pairs={{0,16},{4,20},{8,24},{12,28},{16,0},{20,4},{24,8},{28,12},{1,17},{... | collective-permute-start | bytes 4128776 | tf_op jit(solution)/shard_map/ppermute | solution.py:684
  421.7 29.4 %collective-permute-start.63 = (bf16[128,2688]{1,0:T(8,128)(2,1)}, bf16[128,2688]{1,0:T(8,128)(2,1)S(1)}, u32[]{:S(2)}, u32[]{:S(2)}) collective-permute-start(bf16[128,2688]{1,0:T(8,128)(2,1)} %get-tuple-element.361), channel_id=1, source_target_pairs={{0,16},{4,20},{8,24},{12,28},{16,0},{20,4},{24,8},{28,12},{1,17},{... | collective-permute-start | bytes 2064392 | tf_op jit(solution)/shard_map/ppermute | solution.py:684
  423.3 27.8 %collective-permute-start.62 = (bf16[128,2688]{1,0:T(8,128)(2,1)}, bf16[128,2688]{1,0:T(8,128)(2,1)}, u32[]{:S(2)}, u32[]{:S(2)}) collective-permute-start(bf16[128,2688]{1,0:T(8,128)(2,1)} %get-tuple-element.359), channel_id=1, source_target_pairs={{0,8},{4,12},{8,0},{12,4},{16,24},{20,28},{24,16},{28,20},{1,9},{5... | collective-permute-start | bytes 2064392 | tf_op jit(solution)/shard_map/ppermute | solution.py:684
  424.2 26.9 %collective-permute-start.61 = (bf16[128,2688]{1,0:T(8,128)(2,1)S(1)}, bf16[128,2688]{1,0:T(8,128)(2,1)S(1)}, u32[]{:S(2)}, u32[]{:S(2)}) collective-permute-start(bf16[128,2688]{1,0:T(8,128)(2,1)S(1)} %add_convert_fusion.17), channel_id=1, source_target_pairs={{7,4},{6,5},{5,6},{4,7},{15,12},{14,13},{13,14},{12,15},{23,20},{2... | collective-permute-start | bytes 2064392 | tf_op jit(solution)/shard_map/ppermute | solution.py:941
  424.9 26.2 %collective-permute-start.60 = (bf16[128,2688]{1,0:T(8,128)(2,1)S(1)}, bf16[128,2688]{1,0:T(8,128)(2,1)S(1)}, u32[]{:S(2)}, u32[]{:S(2)}) collective-permute-start(bf16[128,2688]{1,0:T(8,128)(2,1)S(1)} %add_convert_fusion.18), channel_id=1, source_target_pairs={{7,4},{6,5},{5,6},{4,7},{15,12},{14,13},{13,14},{12,15},{23,20},{2... | collective-permute-start | bytes 2064392 | tf_op jit(solution)/shard_map/ppermute | solution.py:941
  452.0 34.7 %collective-permute-start.64 = (bf16[256,2048]{1,0:T(8,128)(2,1)S(1)}, bf16[256,2048]{1,0:T(8,128)(2,1)S(1)}, u32[]{:S(2)}, u32[]{:S(2)}) collective-permute-start(bf16[256,2048]{1,0:T(8,128)(2,1)S(1)} %get-tuple-element.366), channel_id=1, source_target_pairs={{0,1},{3,2},{4,5},{7,6},{8,9},{11,10},{12,13},{15,14},{16,17},{19,... | collective-permute-start | bytes 3145736 | tf_op jit(solution)/shard_map/ppermute | solution.py:687
  460.6 30.2 %collective-permute-start.65 = (bf16[128,2688]{1,0:T(8,128)(2,1)S(1)}, bf16[128,2688]{1,0:T(8,128)(2,1)}, u32[]{:S(2)}, u32[]{:S(2)}) collective-permute-start(bf16[128,2688]{1,0:T(8,128)(2,1)S(1)} %add_convert_fusion.13), channel_id=1, source_target_pairs={{0,4},{1,5},{2,6},{3,7},{8,12},{9,13},{10,14},{11,15},{16,20},{17,... | collective-permute-start | bytes 2064392 | tf_op jit(solution)/shard_map/ppermute | solution.py:953
  490.8 33.3 %collective-permute-start.69 = (bf16[512,3072]{1,0:T(8,128)(2,1)}, bf16[512,3072]{1,0:T(8,128)(2,1)}, u32[]{:S(2)}, u32[]{:S(2)}) collective-permute-start(bf16[512,3072]{1,0:T(8,128)(2,1)} %shard_map.258), channel_id=1, source_target_pairs={{0,4},{4,0},{8,12},{12,8},{16,20},{20,16},{24,28},{28,24},{1,5},{5... | collective-permute-start | bytes 9437192 | tf_op jit(solution)/shard_map/ppermute | solution.py:684
  491.7 41.6 %collective-permute-start.68 = (bf16[512,3072]{1,0:T(8,128)(2,1)}, bf16[512,3072]{1,0:T(8,128)(2,1)}, u32[]{:S(2)}, u32[]{:S(2)}) collective-permute-start(bf16[512,3072]{1,0:T(8,128)(2,1)} %shard_map.260), channel_id=1, source_target_pairs={{0,4},{4,0},{8,12},{12,8},{16,20},{20,16},{24,28},{28,24},{1,5},{5... | collective-permute-start | bytes 9437192 | tf_op jit(solution)/shard_map/ppermute | solution.py:684
  491.7 41.6 %collective-permute-start.67 = (bf16[256,2048]{1,0:T(8,128)(2,1)}, bf16[256,2048]{1,0:T(8,128)(2,1)}, u32[]{:S(2)}, u32[]{:S(2)}) collective-permute-start(bf16[256,2048]{1,0:T(8,128)(2,1)} %get-tuple-element.371), channel_id=1, source_target_pairs={{0,1},{3,2},{4,5},{7,6},{8,9},{11,10},{12,13},{15,14},{16,17},{19,... | collective-permute-start | bytes 3145736 | tf_op jit(solution)/shard_map/ppermute | solution.py:687
  493.9 39.4 %collective-permute-start.66 = (bf16[256,2048]{1,0:T(8,128)(2,1)}, bf16[256,2048]{1,0:T(8,128)(2,1)}, u32[]{:S(2)}, u32[]{:S(2)}) collective-permute-start(bf16[256,2048]{1,0:T(8,128)(2,1)} %add_convert_fusion.2), channel_id=1, source_target_pairs={{1,2},{2,1},{5,6},{6,5},{9,10},{10,9},{13,14},{14,13},{17,18},{18,... | collective-permute-start | bytes 3145736 | tf_op jit(solution)/shard_map/ppermute | solution.py:687
  533.3 37.2 %collective-permute-start.72 = (bf16[256,3072]{1,0:T(8,128)(2,1)}, bf16[256,3072]{1,0:T(8,128)(2,1)}, u32[]{:S(2)}, u32[]{:S(2)}) collective-permute-start(bf16[256,3072]{1,0:T(8,128)(2,1)} %get-tuple-element.379), channel_id=1, source_target_pairs={{0,16},{4,20},{8,24},{12,28},{16,0},{20,4},{24,8},{28,12},{1,17},{... | collective-permute-start | bytes 4718600 | tf_op jit(solution)/shard_map/ppermute | solution.py:684
  534.9 36.9 %collective-permute-start.73 = (bf16[256,3072]{1,0:T(8,128)(2,1)}, bf16[256,3072]{1,0:T(8,128)(2,1)}, u32[]{:S(2)}, u32[]{:S(2)}) collective-permute-start(bf16[256,3072]{1,0:T(8,128)(2,1)} %get-tuple-element.384), channel_id=1, source_target_pairs={{0,8},{4,12},{8,0},{12,4},{16,24},{20,28},{24,16},{28,20},{1,9},{5... | collective-permute-start | bytes 4718600 | tf_op jit(solution)/shard_map/ppermute | solution.py:684
  542.4 25.3 %collective-permute-start.70 = (bf16[256,2048]{1,0:T(8,128)(2,1)}, bf16[256,2048]{1,0:T(8,128)(2,1)S(1)}, u32[]{:S(2)}, u32[]{:S(2)}) collective-permute-start(bf16[256,2048]{1,0:T(8,128)(2,1)} %add_convert_fusion.1), channel_id=1, source_target_pairs={{0,1},{1,0},{2,3},{3,2},{4,5},{5,4},{6,7},{7,6},{8,9},{9,8},{10,11... | collective-permute-start | bytes 3145736 | tf_op jit(solution)/shard_map/ppermute | solution.py:687
  575.2 33.5 %collective-permute-start.79 = (bf16[128,3072]{1,0:T(8,128)(2,1)S(1)}, bf16[128,3072]{1,0:T(8,128)(2,1)S(1)}, u32[]{:S(2)}, u32[]{:S(2)}) collective-permute-start(bf16[128,3072]{1,0:T(8,128)(2,1)S(1)} %get-tuple-element.404), channel_id=1, source_target_pairs={{0,16},{4,20},{8,24},{12,28},{16,0},{20,4},{24,8},{28,12},{1,17},{... | collective-permute-start | bytes 2359304 | tf_op jit(solution)/shard_map/ppermute | solution.py:684
  578.7 29.9 %collective-permute-start.78 = (bf16[128,3072]{1,0:T(8,128)(2,1)}, bf16[128,3072]{1,0:T(8,128)(2,1)S(1)}, u32[]{:S(2)}, u32[]{:S(2)}) collective-permute-start(bf16[128,3072]{1,0:T(8,128)(2,1)} %get-tuple-element.401), channel_id=1, source_target_pairs={{0,8},{4,12},{8,0},{12,4},{16,24},{20,28},{24,16},{28,20},{1,9},{5... | collective-permute-start | bytes 2359304 | tf_op jit(solution)/shard_map/ppermute | solution.py:684
  579.7 31.3 %collective-permute-start.77 = (bf16[256,2048]{1,0:T(8,128)(2,1)}, bf16[256,2048]{1,0:T(8,128)(2,1)S(1)}, u32[]{:S(2)}, u32[]{:S(2)}) collective-permute-start(bf16[256,2048]{1,0:T(8,128)(2,1)} %slice.226), channel_id=1, source_target_pairs={{0,1},{1,0},{2,3},{3,2},{4,5},{5,4},{6,7},{7,6},{8,9},{9,8},{10,11... | collective-permute-start | bytes 3145736 | tf_op jit(solution)/shard_map/ppermute | solution.py:687
  586.7 24.3 %collective-permute-start.82 = (bf16[128,2688]{1,0:T(8,128)(2,1)}, bf16[128,2688]{1,0:T(8,128)(2,1)}, u32[]{:S(2)}, u32[]{:S(2)}) collective-permute-start(bf16[128,2688]{1,0:T(8,128)(2,1)} %add_convert_fusion.11), channel_id=1, source_target_pairs={{0,4},{1,5},{2,6},{3,7},{8,12},{9,13},{10,14},{11,15},{16,20},{17,... | collective-permute-start | bytes 2064392 | tf_op jit(solution)/shard_map/ppermute | solution.py:985
  (146 other events, 1784.9 us)

commit v6 on v5

--- a/solution.py
+++ b/solution.py
@@ -836,11 +836,10 @@
         return [first_level(half, order) for half, order in zip(halves, orders)]
 
     def level_two(halves, come):
-        firsts = [second_level(half, order) for half, order in zip(halves, orders)]
         found = []
-        for half, other, first, order in zip(halves, come, firsts, orders):
-            last = swap_dp(after(hold(other), first), 1 << order[1])
-            found += further_two([half, other, first, last], order)
+        for half, other, order in zip(halves, come, orders):
+            both_pieces = jnp.concatenate([half, hold(other)], 0)
+            found += further_two([both_pieces, swap_dp(both_pieces, 1 << order[1])], order)
         return found
 
     def further_two(pieces, order):

time: 647 us -> 657 us (1.015)
  Pallas kernels: 228 us -> 238 us
  local copies, waits for them, and re-layouts: 28.3 us -> 38.3 us
  starting transfers between devices: 104 us -> 95.4 us
  waiting for transfers between devices: 228 us -> 235 us
    ppermute x25, waiting for transfers between devices: 113 us -> 137 us  [move_tensor(): return lax.ppermute(array, 'tensor', pairs)]
    ppermute x56 -> x52, waiting for transfers between devices: 109 us -> 86.8 us  [swap_dp(): return lax.ppermute(array, 'dp', [(i, i ^ mask) for i in range(dp_size)])]
    pallas_call x2, Pallas kernels: 35.3 us -> 43.5 us  [mlp(): pl.pallas_call(mlp_again_kernel if weights else partial(mlp_kernel, len(p...]
    unnamed x210 -> x222, local copies, waits for them, and re-layouts: 24.1 us -> 30.9 us
    ppermute x56 -> x52, starting transfers between devices: 43.5 us -> 39.6 us  [swap_dp(): return lax.ppermute(array, 'dp', [(i, i ^ mask) for i in range(dp_size)])]
  transfers between devices with their start and end apart: 89 -> 85, of which waited for: 40 -> 37; matrix products, arithmetic and copies ran while one was open for 7% -> 8% of each run, Pallas kernels for 32% -> 31%
where the time goes in v6:
time: 657 us; the launch traced here: 653 us
  Pallas kernels  238 us (36%)
  waiting for transfers between devices  235 us (36%)
  starting transfers between devices  95.4 us (15%)
  other arithmetic  43.2 us (7%)
  local copies, waits for them, and re-layouts  38.3 us (6%)
    ppermute x25, waiting for transfers between devices, move_tensor(): return lax.ppermute(array, 'tensor', pairs)  137 us
    ppermute x52, waiting for transfers between devices, swap_dp(): return lax.ppermute(array, 'dp', [(i, i ^ mask) for i in range(dp_size)])  86.8 us
    pallas_call x8, Pallas kernels, attn_grads(): pl.pallas_call(attn_grad_kernel if core else attn_grad_add_kernel, out_sh...  47.3 us
    pallas_call x5, Pallas kernels, rows_back(): pl.pallas_call(partial(rows_back_kernel, len(slots), len(pieces), 1 if we...  44.1 us
    pallas_call x2, Pallas kernels, mlp(): pl.pallas_call(mlp_again_kernel if weights else partial(mlp_kernel, len(p...  43.5 us
    ppermute x25, starting transfers between devices, move_tensor(): return lax.ppermute(array, 'tensor', pairs)  43.1 us
    ppermute x52, starting transfers between devices, swap_dp(): return lax.ppermute(array, 'dp', [(i, i ^ mask) for i in range(dp_size)])  39.6 us
    unnamed x222, local copies, waits for them, and re-layouts  30.9 us
  transfers between devices with their start and end apart: 85, of which 37 were waited for; matrix products, arithmetic and copies ran while one was open for 8% of the time, Pallas kernels for 31%

profile of v6, /device:TPU:0, one launch (start us, length us, event | category | flops | bytes accessed | tf_op | source)
XLA Modules:
  0.0 652.7 jit_solution(11285480844939671413)
XLA Ops:
  23.1 9.6 %collective-permute-done.2.refs_1_.refs_19_ = bf16[256,2048]{1,0:T(8,128)(2,1)} collective-permute-done((bf16[256,2048]{1,0:T(8,128)(2,1)}, bf16[256,2048]{1,0:T(8,128)(2,1)}, u32[]{:S(2)}, u32[]{:S(2)}) %collective-permute-start.2) | collective-permute-done | bytes 1048608 | tf_op jit(solution)/shard_map/ppermute | solution.py:687
  32.7 3.8 collective-permute-done.refs_5_.refs_2_.refs_4_.refs_3_
  42.0 25.1 %collective-permute-done.8 = bf16[256,2048]{1,0:T(8,128)(2,1)S(1)} collective-permute-done((bf16[256,2048]{1,0:T(8,128)(2,1)}, bf16[256,2048]{1,0:T(8,128)(2,1)S(1)}, u32[]{:S(2)}, u32[]{:S(2)}) %collective-permute-start.8) | collective-permute-done | bytes 1048608 | tf_op jit(solution)/shard_map/ppermute | solution.py:687
  73.1 24.6 %collective-permute-done.12 = bf16[256,2048]{1,0:T(8,128)(2,1)S(1)} collective-permute-done((bf16[256,2048]{1,0:T(8,128)(2,1)S(1)}, bf16[256,2048]{1,0:T(8,128)(2,1)S(1)}, u32[]{:S(2)}, u32[]{:S(2)}) %collective-permute-start.12) | collective-permute-done | bytes 1048608 | tf_op jit(solution)/shard_map/ppermute | solution.py:687
  105.3 3.5 collective-permute-start.21
  110.0 18.0 %shard_map.242 = (bf16[256,3072]{1,0:T(8,128)(2,1)}, bf16[256,3072]{1,0:T(8,128)(2,1)}, bf16[256,3072]{1,0:T(8,128)(2,1)}, bf16[256,3072]{1,0:T(8,128)(2,1)}) custom-call(bf16[256,2048]{1,0:T(8,128)(2,1)} %fusion.5.refs_0_.refs_18_, bf16[256,2048]{1,0:T(8,128)(2,1)} %collective-permute-done.2.refs_1_.refs_19_, ...), custom_call_target="tpu_custom_call" | custom-call | flops 201326592 | bytes 196608 | tf_op jit(solution)/shard_map/pallas_call | solution.py:245
  131.0 5.6 collective-permute-start.24
  139.8 10.3 %shard_map.243 = (bf16[1024,512]{1,0:T(8,128)(2,1)S(1)}, bf16[1024,512]{1,0:T(8,128)(2,1)S(1)}, bf16[1024,1024]{1,0:T(8,128)(2,1)}, bf16[1024,1024]{1,0:T(8,128)...) custom-call(s32[1]{0:T(128)} %bitcast.3.place_ref, f32[2]{0:T(128)S(1)} %subtract_log_fusion.decay_ref, ...), custom_call_target="tpu_custom_call" | custom-call | flops 25165824 | bytes 288000 | tf_op jit(solution)/shard_map/pallas_call | solution.py:125
  151.2 4.2 shard_map.244
  156.4 6.1 collective-permute-start.26
  169.1 6.6 %shard_map.245 = (bf16[256,2048]{1,0:T(8,128)(2,1)S(1)}, bf16[256,2048]{1,0:T(8,128)(2,1)S(1)}, bf16[256,2048]{1,0:T(8,128)(2,1)S(1)}) custom-call(bf16[1024,1024]{1,0:T(8,128)(2,1)} %get-tuple-element.379.refs_0_.refs_1_.refs_2_.refs_4_, bf16[1024,1024]{1,0:T(8,128)(2,1)} %get-tuple-element.379.refs_0_.refs_1_.refs_2_.refs_4_, ...), custom_call_target="tpu_custom_call" | custom-call | flops 50331648 | bytes 65536 | tf_op jit(solution)/shard_map/pallas_call | solution.py:288
  175.7 8.0 %collective-permute-done.26 = bf16[256,2048]{1,0:T(8,128)(2,1)S(1)} collective-permute-done((bf16[256,2048]{1,0:T(8,128)(2,1)S(1)}, bf16[256,2048]{1,0:T(8,128)(2,1)S(1)}, u32[]{:S(2)}, u32[]{:S(2)}) %collective-permute-start.26) | collective-permute-done | bytes 1048608 | tf_op jit(solution)/shard_map/ppermute | solution.py:687
  184.1 7.1 %collective-permute-done.27 = bf16[128,2688]{1,0:T(8,128)(2,1)} collective-permute-done((bf16[128,2688]{1,0:T(8,128)(2,1)}, bf16[128,2688]{1,0:T(8,128)(2,1)}, u32[]{:S(2)}, u32[]{:S(2)}) %collective-permute-start.27) | collective-permute-done | bytes 688160 | tf_op jit(solution)/shard_map/ppermute | solution.py:863
  191.2 4.3 collective-permute-done.29.refs_3_
  197.4 4.3 collective-permute-start.34
  204.5 13.1 %collective-permute-done.33 = bf16[128,2688]{1,0:T(8,128)(2,1)S(1)} collective-permute-done((bf16[128,2688]{1,0:T(8,128)(2,1)}, bf16[128,2688]{1,0:T(8,128)(2,1)S(1)}, u32[]{:S(2)}, u32[]{:S(2)}) %collective-permute-start.33) | collective-permute-done | bytes 688160 | tf_op jit(solution)/shard_map/ppermute | solution.py:684
  217.9 4.9 collective-permute-done.34
  229.9 16.9 %collective-permute-done.35 = bf16[256,2048]{1,0:T(8,128)(2,1)S(1)} collective-permute-done((bf16[256,2048]{1,0:T(8,128)(2,1)S(1)}, bf16[256,2048]{1,0:T(8,128)(2,1)S(1)}, u32[]{:S(2)}, u32[]{:S(2)}) %collective-permute-start.35) | collective-permute-done | bytes 1048608 | tf_op jit(solution)/shard_map/ppermute | solution.py:687
  248.9 8.8 %collective-permute-done.38.refs_7_ = bf16[256,2688]{1,0:T(8,128)(2,1)S(1)} collective-permute-done((bf16[256,2688]{1,0:T(8,128)(2,1)S(1)}, bf16[256,2688]{1,0:T(8,128)(2,1)S(1)}, u32[]{:S(2)}, u32[]{:S(2)}) %collective-permute-start.38) | collective-permute-done | bytes 1376288 | tf_op jit(solution)/shard_map/ppermute | solution.py:684
  263.1 15.9 %shard_map.246 = (bf16[256,896]{1,0:T(8,128)(2,1)S(1)}, bf16[256,896]{1,0:T(8,128)(2,1)S(1)}, bf16[256,896]{1,0:T(8,128)(2,1)S(1)}, bf16[256,896]{1,0:T(8,128)(2...) custom-call(bf16[256,2048]{1,0:T(8,128)(2,1)S(1)} %multiply_convert_, ...), custom_call_target="tpu_custom_call" | custom-call | flops 146800640 | bytes 172032 | tf_op jit(solution)/shard_map/pallas_call | solution.py:371
  279.2 5.9 collective-permute-done.40.own_ref.refs_1_
  288.8 27.6 %shard_map.247 = (bf16[256,896]{1,0:T(8,128)(2,1)S(1)}, bf16[256,896]{1,0:T(8,128)(2,1)S(1)}, bf16[256,896]{1,0:T(8,128)(2,1)S(1)}, bf16[256,896]{1,0:T(8,128)(2...) custom-call(bf16[256,2048]{1,0:T(8,128)(2,1)S(1)} %collective-permut, ...), custom_call_target="tpu_custom_call" | custom-call | flops 146800640 | bytes 172032 | tf_op jit(solution)/shard_map/pallas_call | solution.py:371
  321.1 6.8 %shard_map.250 = (bf16[256,2688]{1,0:T(8,128)(2,1)}, bf16[256,2688]{1,0:T(8,128)(2,1)}) custom-call(bf16[256,2048]{1,0:T(8,128)(2,1)} %copy-done.21, bf16[256,2048]{1,0:T(8,128)(2,1)} %copy-done.28, bf16[256,2048]{1,0:T(8,128)(2,1)} %copy-done.67, bf16[256,2048]{1,0:T(8,128)(2,1)} %copy-done.68, ...), custom_call_target="tpu_custom_call" | custom-call | flops 44040192 | bytes 57344 | tf_op jit(solution)/shard_map/pallas_call | solution.py:434
  327.9 6.9 %shard_map.249 = (bf16[256,2688]{1,0:T(8,128)(2,1)}, bf16[256,2688]{1,0:T(8,128)(2,1)}) custom-call(bf16[256,2048]{1,0:T(8,128)(2,1)} %copy-done.21, bf16[256,2048]{1,0:T(8,128)(2,1)} %copy-done.28, bf16[256,2048]{1,0:T(8,128)(2,1)} %copy-done.67, bf16[256,2048]{1,0:T(8,128)(2,1)} %copy-done.68, ...), custom_call_target="tpu_custom_call" | custom-call | flops 44040192 | bytes 57344 | tf_op jit(solution)/shard_map/pallas_call | solution.py:434
  334.7 8.1 %shard_map.248 = (bf16[512,2048]{1,0:T(8,128)(2,1)S(1)}, bf16[512,2048]{1,0:T(8,128)(2,1)}) custom-call(bf16[256,896]{1,0:T(8,128)(2,1)S(1)} %get-tuple-element.288.refs_0_.refs_16_, bf16[256,896]{1,0:T(8,128)(2,1)S(1)} %get-tuple-element.289.refs_1_.refs_17_, bf16[256,896]{1,0:T(8,128)(2,1)S(1)} %get-tuple-element.290.refs_2_.refs_18_, ...), custom_call_target="tpu_custom_call" | custom-call | flops 58720256 | bytes 57344 | tf_op jit(solution)/shard_map/pallas_call | solution.py:397
  348.7 4.1 shard_map.251
  357.1 6.9 %shard_map.253 = (bf16[256,2688]{1,0:T(8,128)(2,1)}, bf16[256,2688]{1,0:T(8,128)(2,1)}) custom-call(bf16[256,2048]{1,0:T(8,128)(2,1)} %copy-done.21, bf16[256,2048]{1,0:T(8,128)(2,1)} %copy-done.28, bf16[256,2048]{1,0:T(8,128)(2,1)} %copy-done.67, bf16[256,2048]{1,0:T(8,128)(2,1)} %copy-done.68, ...), custom_call_target="tpu_custom_call" | custom-call | flops 44040192 | bytes 57344 | tf_op jit(solution)/shard_map/pallas_call | solution.py:434
  364.0 7.5 %shard_map.252 = (bf16[256,2688]{1,0:T(8,128)(2,1)}, bf16[256,2688]{1,0:T(8,128)(2,1)}) custom-call(bf16[256,2048]{1,0:T(8,128)(2,1)} %copy-done.21, bf16[256,2048]{1,0:T(8,128)(2,1)} %copy-done.28, bf16[256,2048]{1,0:T(8,128)(2,1)} %copy-done.67, bf16[256,2048]{1,0:T(8,128)(2,1)} %copy-done.68, ...), custom_call_target="tpu_custom_call" | custom-call | flops 44040192 | bytes 57344 | tf_op jit(solution)/shard_map/pallas_call | solution.py:434
  371.5 6.0 collective-permute-done.50
  384.3 17.9 %collective-permute-done.46.refs_1_ = bf16[256,2048]{1,0:T(8,128)(2,1)S(1)} collective-permute-done((bf16[256,2048]{1,0:T(8,128)(2,1)S(1)}, bf16[256,2048]{1,0:T(8,128)(2,1)S(1)}, u32[]{:S(2)}, u32[]{:S(2)}) %collective-permute-start.46) | collective-permute-done | bytes 1048608 | tf_op jit(solution)/shard_map/ppermute | solution.py:687
  402.2 5.9 collective-permute-done.51
  413.6 5.4 shard_map.254
  426.8 7.6 %collective-permute-done.53 = bf16[256,2048]{1,0:T(8,128)(2,1)S(1)} collective-permute-done((bf16[256,2048]{1,0:T(8,128)(2,1)S(1)}, bf16[256,2048]{1,0:T(8,128)(2,1)S(1)}, u32[]{:S(2)}, u32[]{:S(2)}) %collective-permute-start.53) | collective-permute-done | bytes 1048608 | tf_op jit(solution)/shard_map/ppermute | solution.py:687
  444.5 15.9 %shard_map.256.refs_0_.refs_4_.refs_1_ = bf16[1024,3072]{1,0:T(8,128)(2,1)} custom-call(s32[1]{0:T(128)} %bitcast.3.place_ref, f32[2]{0:T(128)S(1)} %subtract_log_fusion.decay_ref, bf16[256,1024]{1,0:T(8,128)(2,1)S(1)} %get-tuple-element.329.refs_0_, bf16[256,1024]{1,0:T(8,128)(2,1)S(1)} %get-tuple-element.334.refs_1_, ...), custom_call_target="tpu_custom_call" | custom-call | flops 58720256 | bytes 320000 | tf_op jit(solution)/shard_map/pallas_call | solution.py:212
  460.5 9.4 %shard_map.257 = (bf16[256,2048]{1,0:T(8,128)(2,1)S(1)}, f32[8,2048]{1,0:T(8,128)S(1)}) custom-call(bf16[1024,3072]{1,0:T(8,128)(2,1)} %shard_map.256.refs_0_.refs_4_.refs_1_, bf16[128,4096]{1,0:T(8,128)(2,1)S(1)} %get-tuple-element.225.refs_4_.refs_1_.refs_3_.refs_2_, bf16[128,4096]{1,0:T(8,128)(2,1)S(1)} %copy-done.3, ...), custom_call_target="tpu_custom_call" | custom-call | flops 50331648 | bytes 196608 | tf_op jit(solution)/shard_map/pallas_call | solution.py:288
  469.9 5.1 collective-permute-start.60
  476.4 8.0 %shard_map.258 = bf16[512,3072]{1,0:T(8,128)(2,1)} custom-call(bf16[256,2048]{1,0:T(8,128)(2,1)} %fusion.5.refs_0_.refs_18_, bf16[256,2048]{1,0:T(8,128)(2,1)} %collective-permute-done.2.refs_1_.refs_19_, bf16[256,2048]{1,0:T(8,128)(2,1)S(1)} %broadcast_select_fusion.3.refs_2_.refs_17_, bf16[256,2048]{1,0:T(8,128)(2,1)S(1)} %copy-done.11, ...), custom_call_target="tpu_custom_call" | custom-call | flops 50331648 | bytes 98304 | tf_op jit(solution)/shard_map/pallas_call | solution.py:468
  484.5 10.3 %shard_map.259 = (bf16[256,2048]{1,0:T(8,128)(2,1)}, f32[8,2048]{1,0:T(8,128)S(1)}) custom-call(bf16[1024,3072]{1,0:T(8,128)(2,1)} %shard_map.256.refs_0_.refs_4_.refs_1_, bf16[128,4096]{1,0:T(8,128)(2,1)S(1)} %get-tuple-element.225.refs_4_.refs_1_.refs_3_.refs_2_, bf16[128,4096]{1,0:T(8,128)(2,1)S(1)} %copy-done.3, ...), custom_call_target="tpu_custom_call" | custom-call | flops 50331648 | bytes 196608 | tf_op jit(solution)/shard_map/pallas_call | solution.py:288
  494.7 7.8 %shard_map.260 = bf16[512,3072]{1,0:T(8,128)(2,1)} custom-call(bf16[256,2048]{1,0:T(8,128)(2,1)} %fusion.5.refs_0_.refs_18_, bf16[256,2048]{1,0:T(8,128)(2,1)} %collective-permute-done.2.refs_1_.refs_19_, bf16[256,2048]{1,0:T(8,128)(2,1)S(1)} %copy-done.8, bf16[256,2048]{1,0:T(8,128)(2,1)S(1)} %copy-done.11, ...), custom_call_target="tpu_custom_call" | custom-call | flops 50331648 | bytes 98304 | tf_op jit(solution)/shard_map/pallas_call | solution.py:468
  505.0 3.8 collective-permute-done.61
  522.7 4.0 shard_map.262
  526.7 13.6 %shard_map.263 = (bf16[256,2048]{1,0:T(8,128)(2,1)S(1)}, bf16[256,2048]{1,0:T(8,128)(2,1)S(1)}, f32[8,2048]{1,0:T(8,128)S(1)}) custom-call(bf16[1024,3072]{1,0:T(8,128)(2,1)} %shard_map.256.refs_0_.refs_4_.refs_1_, bf16[1024,3072]{1,0:T(8,128)(2,1)} %shard_map.256.refs_0_.refs_4_.refs_1_, ...), custom_call_target="tpu_custom_call" | custom-call | flops 100663296 | bytes 196608 | tf_op jit(solution)/shard_map/pallas_call | solution.py:288
  541.4 8.7 %shard_map.264 = (bf16[256,3072]{1,0:T(8,128)(2,1)S(1)}, bf16[256,3072]{1,0:T(8,128)(2,1)}) custom-call(bf16[256,2048]{1,0:T(8,128)(2,1)} %fusion.5.refs_0_.refs_18_, bf16[256,2048]{1,0:T(8,128)(2,1)} %collective-permute-done.2.refs_1_.refs_19_, bf16[256,2048]{1,0:T(8,128)(2,1)S(1)} %copy-done.9, bf16[256,2048]{1,0:T(8,128)(2,1)S(1)} %copy-done.12, ...), custom_call_target="tpu_custom_call" | custom-call | flops 50331648 | bytes 98304 | tf_op jit(solution)/shard_map/pallas_call | solution.py:468
  560.7 8.6 %shard_map.266 = (bf16[256,3072]{1,0:T(8,128)(2,1)S(1)}, bf16[256,3072]{1,0:T(8,128)(2,1)}) custom-call(bf16[256,2048]{1,0:T(8,128)(2,1)} %fusion.5.refs_0_.refs_18_, bf16[256,2048]{1,0:T(8,128)(2,1)} %collective-permute-done.2.refs_1_.refs_19_, bf16[256,2048]{1,0:T(8,128)(2,1)S(1)} %copy-done.9, bf16[256,2048]{1,0:T(8,128)(2,1)S(1)} %copy-done.12, ...), custom_call_target="tpu_custom_call" | custom-call | flops 50331648 | bytes 98304 | tf_op jit(solution)/shard_map/pallas_call | solution.py:468
  572.8 3.6 shard_map.268
  576.4 8.1 %collective-permute-done.66 = bf16[256,2048]{1,0:T(8,128)(2,1)S(1)} collective-permute-done((bf16[256,2048]{1,0:T(8,128)(2,1)}, bf16[256,2048]{1,0:T(8,128)(2,1)S(1)}, u32[]{:S(2)}, u32[]{:S(2)}) %collective-permute-start.66) | collective-permute-done | bytes 1048608 | tf_op jit(solution)/shard_map/ppermute | solution.py:687
  598.2 5.1 collective-permute-done.76
  606.8 19.5 %collective-permute-done.77 = bf16[256,1024]{1,0:T(8,128)(2,1)S(1)} collective-permute-done((bf16[256,1024]{1,0:T(8,128)(2,1)S(1)}, bf16[256,1024]{1,0:T(8,128)(2,1)S(1)}, u32[]{:S(2)}, u32[]{:S(2)}) %collective-permute-start.77) | collective-permute-done | bytes 524320 | tf_op jit(solution)/shard_map/ppermute | solution.py:684
  (440 shorter events, 201.0 us)
Async XLA Ops:
  6.2 26.5 %collective-permute-start.2 = (bf16[256,2048]{1,0:T(8,128)(2,1)}, bf16[256,2048]{1,0:T(8,128)(2,1)}, u32[]{:S(2)}, u32[]{:S(2)}) collective-permute-start(bf16[256,2048]{1,0:T(8,128)(2,1)} %fusion.5.refs_0_.refs_18_), channel_id=1, source_target_pairs={{0,1},{1,0},{2,3},{3,2},{4,5},{5,4},{6,7},{7,6},{8,9},{9,8},{10,11... | collective-permute-start | bytes 3145736 | tf_op jit(solution)/shard_map/ppermute | solution.py:687
  11.0 25.6 %collective-permute-start = (bf16[128,4096]{1,0:T(8,128)(2,1)S(1)}, bf16[128,4096]{1,0:T(8,128)(2,1)S(1)}, u32[]{:S(2)}, u32[]{:S(2)}) collective-permute-start(bf16[128,4096]{1,0:T(8,128)(2,1)S(1)} %get-tuple-element.225.refs_4_.refs_1_.refs_3_.refs_2_), channel_id=1, source_target_pairs={{0,8},{4,12},{8,0},{12,4},{16,24},{20,28},{24,16},{28,20},{1,9},{5... | collective-permute-start | bytes 3145736 | tf_op jit(solution)/shard_map/ppermute | solution.py:684
  12.4 25.4 %collective-permute-start.1 = (bf16[128,4096]{1,0:T(8,128)(2,1)S(1)}, bf16[128,4096]{1,0:T(8,128)(2,1)}, u32[]{:S(2)}, u32[]{:S(2)}) collective-permute-start(bf16[128,4096]{1,0:T(8,128)(2,1)S(1)} %get-tuple-element.226.refs_8_.refs_5_.refs_7_.refs_6_), channel_id=1, source_target_pairs={{0,16},{4,20},{8,24},{12,28},{16,0},{20,4},{24,8},{28,12},{1,17},{... | collective-permute-start | bytes 3145736 | tf_op jit(solution)/shard_map/ppermute | solution.py:684
  37.8 29.3 %collective-permute-start.6 = (bf16[128,4096]{1,0:T(8,128)(2,1)S(1)}, bf16[128,4096]{1,0:T(8,128)(2,1)}, u32[]{:S(2)}, u32[]{:S(2)}) collective-permute-start(bf16[128,4096]{1,0:T(8,128)(2,1)S(1)} %get-tuple-element.226.refs_8_.refs_5_.refs_7_.refs_6_), channel_id=1, source_target_pairs={{0,8},{4,12},{8,0},{12,4},{16,24},{20,28},{24,16},{28,20},{1,9},{5... | collective-permute-start | bytes 3145736 | tf_op jit(solution)/shard_map/ppermute | solution.py:684
  38.4 28.7 %collective-permute-start.9 = (bf16[128,4096]{1,0:T(8,128)(2,1)S(1)}, bf16[128,4096]{1,0:T(8,128)(2,1)S(1)}, u32[]{:S(2)}, u32[]{:S(2)}) collective-permute-start(bf16[128,4096]{1,0:T(8,128)(2,1)S(1)} %get-tuple-element.226.refs_8_.refs_5_.refs_7_.refs_6_), channel_id=1, source_target_pairs={{0,4},{4,0},{8,12},{12,8},{16,20},{20,16},{24,28},{28,24},{1,5},{5... | collective-permute-start | bytes 3145736 | tf_op jit(solution)/shard_map/ppermute | solution.py:684
  38.4 28.7 %collective-permute-start.8 = (bf16[256,2048]{1,0:T(8,128)(2,1)}, bf16[256,2048]{1,0:T(8,128)(2,1)S(1)}, u32[]{:S(2)}, u32[]{:S(2)}) collective-permute-start(bf16[256,2048]{1,0:T(8,128)(2,1)} %collective-permute-done.3), channel_id=1, source_target_pairs={{1,0},{2,3},{5,4},{6,7},{9,8},{10,11},{13,12},{14,15},{17,16},{18,... | collective-permute-start | bytes 3145736 | tf_op jit(solution)/shard_map/ppermute | solution.py:687
  39.7 27.4 %collective-permute-start.7 = (bf16[256,2048]{1,0:T(8,128)(2,1)}, bf16[256,2048]{1,0:T(8,128)(2,1)S(1)}, u32[]{:S(2)}, u32[]{:S(2)}) collective-permute-start(bf16[256,2048]{1,0:T(8,128)(2,1)} %collective-permute-done.2.refs_1_.refs_19_), channel_id=1, source_target_pairs={{1,2},{2,1},{5,6},{6,5},{9,10},{10,9},{13,14},{14,13},{17,18},{18,... | collective-permute-start | bytes 3145736 | tf_op jit(solution)/shard_map/ppermute | solution.py:687
  40.4 26.7 %collective-permute-start.5 = (bf16[128,4096]{1,0:T(8,128)(2,1)S(1)}, bf16[128,4096]{1,0:T(8,128)(2,1)}, u32[]{:S(2)}, u32[]{:S(2)}) collective-permute-start(bf16[128,4096]{1,0:T(8,128)(2,1)S(1)} %get-tuple-element.225.refs_4_.refs_1_.refs_3_.refs_2_), channel_id=1, source_target_pairs={{0,16},{4,20},{8,24},{12,28},{16,0},{20,4},{24,8},{28,12},{1,17},{... | collective-permute-start | bytes 3145736 | tf_op jit(solution)/shard_map/ppermute | solution.py:684
  68.5 29.2 %collective-permute-start.11 = (bf16[128,4096]{1,0:T(8,128)(2,1)}, bf16[128,4096]{1,0:T(8,128)(2,1)}, u32[]{:S(2)}, u32[]{:S(2)}) collective-permute-start(bf16[128,4096]{1,0:T(8,128)(2,1)} %collective-permute-done.1.refs_9_.refs_6_.refs_8_.refs_7_), channel_id=1, source_target_pairs={{0,8},{4,12},{8,0},{12,4},{16,24},{20,28},{24,16},{28,20},{1,9},{5... | collective-permute-start | bytes 3145736 | tf_op jit(solution)/shard_map/ppermute | solution.py:684
  69.9 27.7 %collective-permute-start.14 = (bf16[128,4096]{1,0:T(8,128)(2,1)}, bf16[128,4096]{1,0:T(8,128)(2,1)S(1)}, u32[]{:S(2)}, u32[]{:S(2)}) collective-permute-start(bf16[128,4096]{1,0:T(8,128)(2,1)} %collective-permute-done.1.refs_9_.refs_6_.refs_8_.refs_7_), channel_id=1, source_target_pairs={{0,4},{4,0},{8,12},{12,8},{16,20},{20,16},{24,28},{28,24},{1,5},{5... | collective-permute-start | bytes 3145736 | tf_op jit(solution)/shard_map/ppermute | solution.py:684
  70.0 27.7 %collective-permute-start.12 = (bf16[256,2048]{1,0:T(8,128)(2,1)S(1)}, bf16[256,2048]{1,0:T(8,128)(2,1)S(1)}, u32[]{:S(2)}, u32[]{:S(2)}) collective-permute-start(bf16[256,2048]{1,0:T(8,128)(2,1)S(1)} %collective-permute-done.7), channel_id=1, source_target_pairs={{1,0},{2,3},{5,4},{6,7},{9,8},{10,11},{13,12},{14,15},{17,16},{18,... | collective-permute-start | bytes 3145736 | tf_op jit(solution)/shard_map/ppermute | solution.py:687
  71.2 26.4 %collective-permute-start.10 = (bf16[128,4096]{1,0:T(8,128)(2,1)S(1)}, bf16[128,4096]{1,0:T(8,128)(2,1)S(1)}, u32[]{:S(2)}, u32[]{:S(2)}) collective-permute-start(bf16[128,4096]{1,0:T(8,128)(2,1)S(1)} %collective-permute-done.refs_5_.refs_2_.refs_4_.refs_3_), channel_id=1, source_target_pairs={{0,16},{4,20},{8,24},{12,28},{16,0},{20,4},{24,8},{28,12},{1,17},{... | collective-permute-start | bytes 3145736 | tf_op jit(solution)/shard_map/ppermute | solution.py:684
  100.9 27.0 %collective-permute-start.19 = (bf16[128,2688]{1,0:T(8,128)(2,1)S(1)}, bf16[128,2688]{1,0:T(8,128)(2,1)}, u32[]{:S(2)}, u32[]{:S(2)}) collective-permute-start(bf16[128,2688]{1,0:T(8,128)(2,1)S(1)} %get-tuple-element.241), channel_id=1, source_target_pairs={{4,7},{5,6},{6,5},{7,4},{12,15},{13,14},{14,13},{15,12},{20,23},{2... | collective-permute-start | bytes 2064392 | tf_op jit(solution)/shard_map/ppermute | solution.py:827
  102.5 25.5 %collective-permute-start.20 = (bf16[128,2688]{1,0:T(8,128)(2,1)S(1)}, bf16[128,2688]{1,0:T(8,128)(2,1)}, u32[]{:S(2)}, u32[]{:S(2)}) collective-permute-start(bf16[128,2688]{1,0:T(8,128)(2,1)S(1)} %get-tuple-element.242), channel_id=1, source_target_pairs={{4,7},{5,6},{6,5},{7,4},{12,15},{13,14},{14,13},{15,12},{20,23},{2... | collective-permute-start | bytes 2064392 | tf_op jit(solution)/shard_map/ppermute | solution.py:827
  109.0 46.4 %collective-permute-start.25 = (bf16[256,2048]{1,0:T(8,128)(2,1)S(1)}, bf16[256,2048]{1,0:T(8,128)(2,1)S(1)}, u32[]{:S(2)}, u32[]{:S(2)}) collective-permute-start(bf16[256,2048]{1,0:T(8,128)(2,1)S(1)} %copy-done.13), channel_id=1, source_target_pairs={{0,1},{1,0},{2,3},{3,2},{4,5},{5,4},{6,7},{7,6},{8,9},{9,8},{10,11... | collective-permute-start | bytes 3145736 | tf_op jit(solution)/shard_map/ppermute | solution.py:687
  128.0 27.5 %collective-permute-start.23 = (bf16[128,2688]{1,0:T(8,128)(2,1)}, bf16[128,2688]{1,0:T(8,128)(2,1)}, u32[]{:S(2)}, u32[]{:S(2)}) collective-permute-start(bf16[128,2688]{1,0:T(8,128)(2,1)} %collective-permute-done.20), channel_id=1, source_target_pairs={{0,16},{4,20},{8,24},{12,28},{16,0},{20,4},{24,8},{28,12},{1,17},{... | collective-permute-start | bytes 2064392 | tf_op jit(solution)/shard_map/ppermute | solution.py:684
  129.6 25.9 %collective-permute-start.22 = (bf16[128,2688]{1,0:T(8,128)(2,1)}, bf16[128,2688]{1,0:T(8,128)(2,1)S(1)}, u32[]{:S(2)}, u32[]{:S(2)}) collective-permute-start(bf16[128,2688]{1,0:T(8,128)(2,1)} %collective-permute-done.19), channel_id=1, source_target_pairs={{0,8},{4,12},{8,0},{12,4},{16,24},{20,28},{24,16},{28,20},{1,9},{5... | collective-permute-start | bytes 2064392 | tf_op jit(solution)/shard_map/ppermute | solution.py:684
  156.4 27.4 %collective-permute-start.26 = (bf16[256,2048]{1,0:T(8,128)(2,1)S(1)}, bf16[256,2048]{1,0:T(8,128)(2,1)S(1)}, u32[]{:S(2)}, u32[]{:S(2)}) collective-permute-start(bf16[256,2048]{1,0:T(8,128)(2,1)S(1)} %shard_map.244), channel_id=1, source_target_pairs={{0,1},{3,2},{4,5},{7,6},{8,9},{11,10},{12,13},{15,14},{16,17},{19,... | collective-permute-start | bytes 3145736 | tf_op jit(solution)/shard_map/ppermute | solution.py:687
  164.5 31.1 %collective-permute-start.29 = (bf16[256,2688]{1,0:T(8,128)(2,1)}, bf16[256,2688]{1,0:T(8,128)(2,1)S(1)}, u32[]{:S(2)}, u32[]{:S(2)}) collective-permute-start(bf16[256,2688]{1,0:T(8,128)(2,1)} %constant_dynamic-update-slice_fusion.2.refs_2_), channel_id=1, source_target_pairs={{0,8},{4,12},{8,0},{12,4},{16,24},{20,28},{24,16},{28,20},{1,9},{5... | collective-permute-start | bytes 4128776 | tf_op jit(solution)/shard_map/ppermute | solution.py:684
  166.1 30.6 %collective-permute-start.28 = (bf16[256,2688]{1,0:T(8,128)(2,1)S(1)}, bf16[256,2688]{1,0:T(8,128)(2,1)S(1)}, u32[]{:S(2)}, u32[]{:S(2)}) collective-permute-start(bf16[256,2688]{1,0:T(8,128)(2,1)S(1)} %constant_dynamic-update-slice_fusion.refs_0_), channel_id=1, source_target_pairs={{0,16},{4,20},{8,24},{12,28},{16,0},{20,4},{24,8},{28,12},{1,17},{... | collective-permute-start | bytes 4128776 | tf_op jit(solution)/shard_map/ppermute | solution.py:684
  197.4 25.4 %collective-permute-start.34 = (bf16[256,2048]{1,0:T(8,128)(2,1)S(1)}, bf16[256,2048]{1,0:T(8,128)(2,1)S(1)}, u32[]{:S(2)}, u32[]{:S(2)}) collective-permute-start(bf16[256,2048]{1,0:T(8,128)(2,1)S(1)} %get-tuple-element.268), channel_id=1, source_target_pairs={{0,1},{3,2},{4,5},{7,6},{8,9},{11,10},{12,13},{15,14},{16,17},{19,... | collective-permute-start | bytes 3145736 | tf_op jit(solution)/shard_map/ppermute | solution.py:687
  228.1 29.6 %collective-permute-start.38 = (bf16[256,2688]{1,0:T(8,128)(2,1)S(1)}, bf16[256,2688]{1,0:T(8,128)(2,1)S(1)}, u32[]{:S(2)}, u32[]{:S(2)}) collective-permute-start(bf16[256,2688]{1,0:T(8,128)(2,1)S(1)} %constant_dynamic-update-slice_fusion.6.refs_6_), channel_id=1, source_target_pairs={{0,8},{4,12},{8,0},{12,4},{16,24},{20,28},{24,16},{28,20},{1,9},{5... | collective-permute-start | bytes 4128776 | tf_op jit(solution)/shard_map/ppermute | solution.py:684
  229.0 29.4 %collective-permute-start.37 = (bf16[256,2688]{1,0:T(8,128)(2,1)S(1)}, bf16[256,2688]{1,0:T(8,128)(2,1)S(1)}, u32[]{:S(2)}, u32[]{:S(2)}) collective-permute-start(bf16[256,2688]{1,0:T(8,128)(2,1)S(1)} %constant_dynamic-update-slice_fusion.4.refs_4_), channel_id=1, source_target_pairs={{0,16},{4,20},{8,24},{12,28},{16,0},{20,4},{24,8},{28,12},{1,17},{... | collective-permute-start | bytes 4128776 | tf_op jit(solution)/shard_map/ppermute | solution.py:684
  259.5 25.6 %collective-permute-start.40 = (bf16[256,2048]{1,0:T(8,128)(2,1)S(1)}, bf16[256,2048]{1,0:T(8,128)(2,1)S(1)}, u32[]{:S(2)}, u32[]{:S(2)}) collective-permute-start(bf16[256,2048]{1,0:T(8,128)(2,1)S(1)} %multiply_convert_fusion.own_ref.refs_0_), channel_id=1, source_target_pairs={{0,1},{1,0},{2,3},{3,2},{4,5},{5,4},{6,7},{7,6},{8,9},{9,8},{10,11... | collective-permute-start | bytes 3145736 | tf_op jit(solution)/shard_map/ppermute | solution.py:687
  345.7 31.7 %collective-permute-start.50 = (bf16[256,2688]{1,0:T(8,128)(2,1)}, bf16[256,2688]{1,0:T(8,128)(2,1)}, u32[]{:S(2)}, u32[]{:S(2)}) collective-permute-start(bf16[256,2688]{1,0:T(8,128)(2,1)} %get-tuple-element.315), channel_id=1, source_target_pairs={{0,8},{4,12},{8,0},{12,4},{16,24},{20,28},{24,16},{28,20},{1,9},{5... | collective-permute-start | bytes 4128776 | tf_op jit(solution)/shard_map/ppermute | solution.py:684
  347.0 31.7 %collective-permute-start.48 = (bf16[256,2688]{1,0:T(8,128)(2,1)}, bf16[256,2688]{1,0:T(8,128)(2,1)}, u32[]{:S(2)}, u32[]{:S(2)}) collective-permute-start(bf16[256,2688]{1,0:T(8,128)(2,1)} %get-tuple-element.312), channel_id=1, source_target_pairs={{0,16},{4,20},{8,24},{12,28},{16,0},{20,4},{24,8},{28,12},{1,17},{... | collective-permute-start | bytes 4128776 | tf_op jit(solution)/shard_map/ppermute | solution.py:684
  347.5 54.8 %collective-permute-start.45 = (bf16[512,2048]{1,0:T(8,128)(2,1)}, bf16[512,2048]{1,0:T(8,128)(2,1)}, u32[]{:S(2)}, u32[]{:S(2)}) collective-permute-start(bf16[512,2048]{1,0:T(8,128)(2,1)} %get-tuple-element.309), channel_id=1, source_target_pairs={{0,4},{4,0},{8,12},{12,8},{16,20},{20,16},{24,28},{28,24},{1,5},{5... | collective-permute-start | bytes 6291464 | tf_op jit(solution)/shard_map/ppermute | solution.py:684
  354.2 48.0 %collective-permute-start.46 = (bf16[256,2048]{1,0:T(8,128)(2,1)S(1)}, bf16[256,2048]{1,0:T(8,128)(2,1)S(1)}, u32[]{:S(2)}, u32[]{:S(2)}) collective-permute-start(bf16[256,2048]{1,0:T(8,128)(2,1)S(1)} %get-tuple-element.325.refs_0_), channel_id=1, source_target_pairs={{0,1},{1,0},{2,3},{3,2},{4,5},{5,4},{6,7},{7,6},{8,9},{9,8},{10,11... | collective-permute-start | bytes 3145736 | tf_op jit(solution)/shard_map/ppermute | solution.py:687
  355.6 46.6 %collective-permute-start.47 = (bf16[256,2048]{1,0:T(8,128)(2,1)S(1)}, bf16[256,2048]{1,0:T(8,128)(2,1)S(1)}, u32[]{:S(2)}, u32[]{:S(2)}) collective-permute-start(bf16[256,2048]{1,0:T(8,128)(2,1)S(1)} %get-tuple-element.325.refs_0_), channel_id=1, source_target_pairs={{0,2},{1,3},{2,0},{3,1},{4,6},{5,7},{6,4},{7,5},{8,10},{9,11},{10,... | collective-permute-start | bytes 3145736 | tf_op jit(solution)/shard_map/ppermute | solution.py:687
  377.5 30.7 %collective-permute-start.51 = (bf16[256,2688]{1,0:T(8,128)(2,1)}, bf16[256,2688]{1,0:T(8,128)(2,1)S(1)}, u32[]{:S(2)}, u32[]{:S(2)}) collective-permute-start(bf16[256,2688]{1,0:T(8,128)(2,1)} %get-tuple-element.317), channel_id=1, source_target_pairs={{0,8},{4,12},{8,0},{12,4},{16,24},{20,28},{24,16},{28,20},{1,9},{5... | collective-permute-start | bytes 4128776 | tf_op jit(solution)/shard_map/ppermute | solution.py:684
  378.7 30.4 %collective-permute-start.49 = (bf16[256,2688]{1,0:T(8,128)(2,1)}, bf16[256,2688]{1,0:T(8,128)(2,1)S(1)}, u32[]{:S(2)}, u32[]{:S(2)}) collective-permute-start(bf16[256,2688]{1,0:T(8,128)(2,1)} %get-tuple-element.314), channel_id=1, source_target_pairs={{0,16},{4,20},{8,24},{12,28},{16,0},{20,4},{24,8},{28,12},{1,17},{... | collective-permute-start | bytes 4128776 | tf_op jit(solution)/shard_map/ppermute | solution.py:684
  440.6 29.2 %collective-permute-start.59 = (bf16[128,2688]{1,0:T(8,128)(2,1)}, bf16[128,2688]{1,0:T(8,128)(2,1)S(1)}, u32[]{:S(2)}, u32[]{:S(2)}) collective-permute-start(bf16[128,2688]{1,0:T(8,128)(2,1)} %get-tuple-element.345), channel_id=1, source_target_pairs={{0,16},{4,20},{8,24},{12,28},{16,0},{20,4},{24,8},{28,12},{1,17},{... | collective-permute-start | bytes 2064392 | tf_op jit(solution)/shard_map/ppermute | solution.py:684
  441.9 28.0 %collective-permute-start.58 = (bf16[128,2688]{1,0:T(8,128)(2,1)}, bf16[128,2688]{1,0:T(8,128)(2,1)S(1)}, u32[]{:S(2)}, u32[]{:S(2)}) collective-permute-start(bf16[128,2688]{1,0:T(8,128)(2,1)} %get-tuple-element.343), channel_id=1, source_target_pairs={{0,8},{4,12},{8,0},{12,4},{16,24},{20,28},{24,16},{28,20},{1,9},{5... | collective-permute-start | bytes 2064392 | tf_op jit(solution)/shard_map/ppermute | solution.py:684
  443.1 26.8 %collective-permute-start.57 = (bf16[128,2688]{1,0:T(8,128)(2,1)S(1)}, bf16[128,2688]{1,0:T(8,128)(2,1)S(1)}, u32[]{:S(2)}, u32[]{:S(2)}) collective-permute-start(bf16[128,2688]{1,0:T(8,128)(2,1)S(1)} %add_convert_fusion.17), channel_id=1, source_target_pairs={{7,4},{6,5},{5,6},{4,7},{15,12},{14,13},{13,14},{12,15},{23,20},{2... | collective-permute-start | bytes 2064392 | tf_op jit(solution)/shard_map/ppermute | solution.py:940
  443.8 26.1 %collective-permute-start.56 = (bf16[128,2688]{1,0:T(8,128)(2,1)S(1)}, bf16[128,2688]{1,0:T(8,128)(2,1)S(1)}, u32[]{:S(2)}, u32[]{:S(2)}) collective-permute-start(bf16[128,2688]{1,0:T(8,128)(2,1)S(1)} %add_convert_fusion.18), channel_id=1, source_target_pairs={{7,4},{6,5},{5,6},{4,7},{15,12},{14,13},{13,14},{12,15},{23,20},{2... | collective-permute-start | bytes 2064392 | tf_op jit(solution)/shard_map/ppermute | solution.py:940
  469.9 32.6 %collective-permute-start.60 = (bf16[256,2048]{1,0:T(8,128)(2,1)S(1)}, bf16[256,2048]{1,0:T(8,128)(2,1)S(1)}, u32[]{:S(2)}, u32[]{:S(2)}) collective-permute-start(bf16[256,2048]{1,0:T(8,128)(2,1)S(1)} %get-tuple-element.350), channel_id=1, source_target_pairs={{0,1},{3,2},{4,5},{7,6},{8,9},{11,10},{12,13},{15,14},{16,17},{19,... | collective-permute-start | bytes 3145736 | tf_op jit(solution)/shard_map/ppermute | solution.py:687
  475.3 33.5 %collective-permute-start.61 = (bf16[128,2688]{1,0:T(8,128)(2,1)S(1)}, bf16[128,2688]{1,0:T(8,128)(2,1)}, u32[]{:S(2)}, u32[]{:S(2)}) collective-permute-start(bf16[128,2688]{1,0:T(8,128)(2,1)S(1)} %add_convert_fusion.13), channel_id=1, source_target_pairs={{0,4},{1,5},{2,6},{3,7},{8,12},{9,13},{10,14},{11,15},{16,20},{17,... | collective-permute-start | bytes 2064392 | tf_op jit(solution)/shard_map/ppermute | solution.py:952
  508.8 32.5 %collective-permute-start.65 = (bf16[512,3072]{1,0:T(8,128)(2,1)}, bf16[512,3072]{1,0:T(8,128)(2,1)}, u32[]{:S(2)}, u32[]{:S(2)}) collective-permute-start(bf16[512,3072]{1,0:T(8,128)(2,1)} %shard_map.258), channel_id=1, source_target_pairs={{0,4},{4,0},{8,12},{12,8},{16,20},{20,16},{24,28},{28,24},{1,5},{5... | collective-permute-start | bytes 9437192 | tf_op jit(solution)/shard_map/ppermute | solution.py:684
  508.8 41.2 %collective-permute-start.64 = (bf16[512,3072]{1,0:T(8,128)(2,1)}, bf16[512,3072]{1,0:T(8,128)(2,1)}, u32[]{:S(2)}, u32[]{:S(2)}) collective-permute-start(bf16[512,3072]{1,0:T(8,128)(2,1)} %shard_map.260), channel_id=1, source_target_pairs={{0,4},{4,0},{8,12},{12,8},{16,20},{20,16},{24,28},{28,24},{1,5},{5... | collective-permute-start | bytes 9437192 | tf_op jit(solution)/shard_map/ppermute | solution.py:684
  509.3 40.7 %collective-permute-start.63 = (bf16[256,2048]{1,0:T(8,128)(2,1)}, bf16[256,2048]{1,0:T(8,128)(2,1)}, u32[]{:S(2)}, u32[]{:S(2)}) collective-permute-start(bf16[256,2048]{1,0:T(8,128)(2,1)} %get-tuple-element.355), channel_id=1, source_target_pairs={{0,1},{3,2},{4,5},{7,6},{8,9},{11,10},{12,13},{15,14},{16,17},{19,... | collective-permute-start | bytes 3145736 | tf_op jit(solution)/shard_map/ppermute | solution.py:687
  511.6 38.4 %collective-permute-start.62 = (bf16[256,2048]{1,0:T(8,128)(2,1)}, bf16[256,2048]{1,0:T(8,128)(2,1)}, u32[]{:S(2)}, u32[]{:S(2)}) collective-permute-start(bf16[256,2048]{1,0:T(8,128)(2,1)} %add_convert_fusion.2), channel_id=1, source_target_pairs={{1,2},{2,1},{5,6},{6,5},{9,10},{10,9},{13,14},{14,13},{17,18},{18,... | collective-permute-start | bytes 3145736 | tf_op jit(solution)/shard_map/ppermute | solution.py:687
  550.0 36.5 %collective-permute-start.68 = (bf16[256,3072]{1,0:T(8,128)(2,1)S(1)}, bf16[256,3072]{1,0:T(8,128)(2,1)}, u32[]{:S(2)}, u32[]{:S(2)}) collective-permute-start(bf16[256,3072]{1,0:T(8,128)(2,1)S(1)} %get-tuple-element.363), channel_id=1, source_target_pairs={{0,16},{4,20},{8,24},{12,28},{16,0},{20,4},{24,8},{28,12},{1,17},{... | collective-permute-start | bytes 4718600 | tf_op jit(solution)/shard_map/ppermute | solution.py:684
  551.4 37.1 %collective-permute-start.69 = (bf16[256,3072]{1,0:T(8,128)(2,1)}, bf16[256,3072]{1,0:T(8,128)(2,1)}, u32[]{:S(2)}, u32[]{:S(2)}) collective-permute-start(bf16[256,3072]{1,0:T(8,128)(2,1)} %get-tuple-element.368), channel_id=1, source_target_pairs={{0,8},{4,12},{8,0},{12,4},{16,24},{20,28},{24,16},{28,20},{1,9},{5... | collective-permute-start | bytes 4718600 | tf_op jit(solution)/shard_map/ppermute | solution.py:684
  559.0 25.5 %collective-permute-start.66 = (bf16[256,2048]{1,0:T(8,128)(2,1)}, bf16[256,2048]{1,0:T(8,128)(2,1)S(1)}, u32[]{:S(2)}, u32[]{:S(2)}) collective-permute-start(bf16[256,2048]{1,0:T(8,128)(2,1)} %add_convert_fusion.1), channel_id=1, source_target_pairs={{0,1},{1,0},{2,3},{3,2},{4,5},{5,4},{6,7},{7,6},{8,9},{9,8},{10,11... | collective-permute-start | bytes 3145736 | tf_op jit(solution)/shard_map/ppermute | solution.py:687
  592.8 33.4 %collective-permute-start.75 = (bf16[128,3072]{1,0:T(8,128)(2,1)}, bf16[128,3072]{1,0:T(8,128)(2,1)S(1)}, u32[]{:S(2)}, u32[]{:S(2)}) collective-permute-start(bf16[128,3072]{1,0:T(8,128)(2,1)} %get-tuple-element.388), channel_id=1, source_target_pairs={{0,16},{4,20},{8,24},{12,28},{16,0},{20,4},{24,8},{28,12},{1,17},{... | collective-permute-start | bytes 2359304 | tf_op jit(solution)/shard_map/ppermute | solution.py:684
  596.2 30.0 %collective-permute-start.74 = (bf16[128,3072]{1,0:T(8,128)(2,1)}, bf16[128,3072]{1,0:T(8,128)(2,1)S(1)}, u32[]{:S(2)}, u32[]{:S(2)}) collective-permute-start(bf16[128,3072]{1,0:T(8,128)(2,1)} %get-tuple-element.385), channel_id=1, source_target_pairs={{0,8},{4,12},{8,0},{12,4},{16,24},{20,28},{24,16},{28,20},{1,9},{5... | collective-permute-start | bytes 2359304 | tf_op jit(solution)/shard_map/ppermute | solution.py:684
  597.3 31.6 %collective-permute-start.73 = (bf16[256,2048]{1,0:T(8,128)(2,1)}, bf16[256,2048]{1,0:T(8,128)(2,1)}, u32[]{:S(2)}, u32[]{:S(2)}) collective-permute-start(bf16[256,2048]{1,0:T(8,128)(2,1)} %slice.226), channel_id=1, source_target_pairs={{0,1},{1,0},{2,3},{3,2},{4,5},{5,4},{6,7},{7,6},{8,9},{9,8},{10,11... | collective-permute-start | bytes 3145736 | tf_op jit(solution)/shard_map/ppermute | solution.py:687
  603.4 25.5 %collective-permute-start.78 = (bf16[128,2688]{1,0:T(8,128)(2,1)}, bf16[128,2688]{1,0:T(8,128)(2,1)}, u32[]{:S(2)}, u32[]{:S(2)}) collective-permute-start(bf16[128,2688]{1,0:T(8,128)(2,1)} %add_convert_fusion.11), channel_id=1, source_target_pairs={{0,4},{1,5},{2,6},{3,7},{8,12},{9,13},{10,14},{11,15},{16,20},{17,... | collective-permute-start | bytes 2064392 | tf_op jit(solution)/shard_map/ppermute | solution.py:984
  (146 other events, 2080.2 us)
